TPU v7x, 128 devices: a whole 4x4x4 slice. The times are simulated.
128 devices in a mesh: row: 8 (over y, core), col: 16 (over z, x).
Axes of the slice: x: 4, y: 4, z: 4, core: 2. Of those that a mesh axis runs over, the one named last changes fastest.
Arguments:
- queries: bfloat16 [16384, 1024], P(('row', 'col')), may hold values from -3 to 3
- passages: bfloat16 [16384, 1024], P('col', 'row'), may hold values from -3 to 3
- positive: int32 [16384], P('row'), may hold values from 0 to 16383, as said below
Outputs:
- loss: float32 [], replicated
- grad_queries: float32 [16384, 1024], P(('row', 'col'))
- grad_passages: float32 [16384, 1024], P('col', 'row')
Inputs may be any that keep to these rules, and one draw needn't show every extreme that they name: A permutation: every passage is the positive of exactly one query.
All inputs are finite; a program needn't handle non-finite values.
Results may differ from a plain program's by a relative error of at most 0.015.
Values may be sent and summed in bfloat16 or wider, within the bound.
No kernel may reach another device: no remote copies, remote signals or barrier semaphores. Data moves between devices by JAX's collectives and lax.ppermute only.
A program may use at most 64 MiB of HBM per device.

v0:
```python
import jax
import jax.numpy as jnp
from jax import lax
from jax.sharding import PartitionSpec as P

logit_scale = 40.0


def score_block(query_rows, passage_all):
    return logit_scale * lax.dot_general(
        query_rows, passage_all, (((1,), (1,)), ((), ())), preferred_element_type=jnp.float32
    )


def slope_block(scores, row_lse, col_lse, targets, col_start):
    columns = col_start + lax.broadcasted_iota(jnp.int32, scores.shape, 1)
    onehot = (columns == targets[:, None]).astype(jnp.float32)
    slope = (
        0.5 * jnp.exp(scores - row_lse[:, None]) + 0.5 * jnp.exp(scores - col_lse[None, :]) - onehot
    )
    return (slope.astype(jnp.bfloat16), onehot)


def shards(queries, passages, positive):
    query_all = lax.all_gather(queries, "col", axis=0, tiled=True)
    passage_all = lax.all_gather(passages, "row", axis=1, tiled=True)
    total_rows = query_all.shape[0]
    total_cols = passage_all.shape[0]
    width = passage_all.shape[1]
    col_start = lax.axis_index("col") * total_cols
    block_rows = min(512, total_rows)
    block_count = total_rows // block_rows

    def first_pass(carry, block_index):
        col_top, col_sum = carry
        offset = block_index * block_rows
        scores = score_block(
            lax.dynamic_slice_in_dim(query_all, offset, block_rows, 0), passage_all
        )
        row_top = jnp.max(scores, axis=1)
        row_sum = jnp.sum(jnp.exp(scores - row_top[:, None]), axis=1)
        new_top = jnp.maximum(col_top, jnp.max(scores, axis=0))
        col_sum = col_sum * jnp.exp(col_top - new_top) + jnp.sum(
            jnp.exp(scores - new_top[None, :]), axis=0
        )
        return ((new_top, col_sum), (row_top, row_sum))

    start_top = jnp.full((total_cols,), -1e30, jnp.float32)
    start_sum = jnp.zeros((total_cols,), jnp.float32)
    (col_top, col_sum), (row_top, row_sum) = lax.scan(
        first_pass, (start_top, start_sum), jnp.arange(block_count)
    )
    row_top = row_top.reshape(total_rows)
    row_sum = row_sum.reshape(total_rows)
    row_peak = lax.pmax(row_top, "col")
    row_sum = lax.psum(row_sum * jnp.exp(row_top - row_peak), "col")
    row_top = row_peak
    col_peak = lax.pmax(col_top, "row")
    col_sum = lax.psum(col_sum * jnp.exp(col_top - col_peak), "row")
    col_top = col_peak
    row_lse = row_top + jnp.log(row_sum)
    col_lse = col_top + jnp.log(col_sum)

    def second_pass(carry, block_index):
        passage_grad, loss_part = carry
        offset = block_index * block_rows
        query_rows = lax.dynamic_slice_in_dim(query_all, offset, block_rows, 0)
        targets = lax.dynamic_slice_in_dim(positive, offset, block_rows, 0)
        lse_rows = lax.dynamic_slice_in_dim(row_lse, offset, block_rows, 0)
        scores = score_block(query_rows, passage_all)
        slope, onehot = slope_block(scores, lse_rows, col_lse, targets, col_start)
        loss_part = loss_part + jnp.sum(
            onehot * (lse_rows[:, None] + col_lse[None, :] - 2.0 * scores)
        )
        passage_grad = passage_grad + logit_scale * lax.dot_general(
            slope, query_rows, (((0,), (0,)), ((), ())), preferred_element_type=jnp.float32
        )
        query_term = logit_scale * jnp.dot(slope, passage_all, preferred_element_type=jnp.float32)
        return ((passage_grad, loss_part), query_term)

    start_grad = jnp.zeros((total_cols, width), jnp.float32)
    start_loss = jnp.zeros((), jnp.float32)
    (passage_grad, loss_part), query_terms = lax.scan(
        second_pass, (start_grad, start_loss), jnp.arange(block_count)
    )
    grad_queries = lax.psum_scatter(
        query_terms.reshape(total_rows, width).astype(jnp.bfloat16),
        "col",
        scatter_dimension=0,
        tiled=True,
    ).astype(jnp.float32)
    grad_passages = lax.psum_scatter(
        passage_grad.astype(jnp.bfloat16), "row", scatter_dimension=1, tiled=True
    ).astype(jnp.float32)
    loss = lax.psum(loss_part, ("row", "col")) / (2.0 * total_rows * lax.axis_size("row"))
    return (loss, grad_queries, grad_passages)


def solution(mesh):
    in_specs = (P(("row", "col"), None), P("col", "row"), P("row"))
    out_specs = (P(), P(("row", "col"), None), P("col", "row"))
    return jax.shard_map(shards, mesh=mesh, in_specs=in_specs, out_specs=out_specs, check_vma=False)
```

profile of v0, /device:TPU:1, one launch (start us, length us, event | category | flops | bytes accessed | tf_op | source)
XLA Modules:
  0.0 408.7 jit_solution(5121061964453657462)
XLA Ops:
  7.2 0.7 all-gather.5.cloned.1.call-update
  7.9 0.7 all-gather.3.cloned.1.call-update
  8.8 31.8 %all-gather.5.cloned.1.call-done = bf16[1024,1024]{1,0:T(8,128)(2,1)} async-done(((bf16[1024,128]{1,0:T(8,128)(2,1)}), bf16[1024,1024]{1,0:T(8,128)(2,1)}) %all-gather.5.cloned.1.call-update) | async-done | bytes 2097168 | tf_op jit(solution)/shard_map/all_gather | solution.py:26
  40.6 54.4 %all-gather.3.cloned.1.call-done = bf16[2048,1024]{1,0:T(8,128)(2,1)} async-done(((bf16[128,1024]{1,0:T(8,128)(2,1)}), bf16[2048,1024]{1,0:T(8,128)(2,1)}) %all-gather.3.cloned.1.call-update) | async-done | bytes 4194320 | tf_op jit(solution)/shard_map/all_gather | solution.py:25
  95.0 22.7 %while.34 = (s32[]{:T(128)}, f32[1024]{0:T(1024)S(1)}, f32[1024]{0:T(1024)S(1)}, f32[4,512]{1,0:T(4,128)S(1)}, f32[4,512]{1,0:T(4,128)S(1)}, /*index=5*/s32[4]{0...) while((s32[]{:T(128)}, f32[1024]{0:T(1024)S(1)}, ...), condition=%wide.region_5.6_spmd.clone, body=%wide.region_0.5_spmd.clone.sunk | while | flops 1077940224 | bytes 7407822 | solution.py:50
  96.4 3.3 multiply_reduce_fusion.3
  99.7 0.9 exponential_reduce_fusion.3
  100.7 0.7 dynamic_slice.55
  102.0 3.3 multiply_reduce_fusion.3
  105.4 0.9 exponential_reduce_fusion.3
  106.4 0.7 dynamic_slice.55
  107.7 3.3 multiply_reduce_fusion.3
  111.0 0.9 exponential_reduce_fusion.3
  112.0 0.7 dynamic_slice.55
  113.4 3.3 multiply_reduce_fusion.3
  116.7 0.9 exponential_reduce_fusion.3
  117.7 12.5 %pmax.15 = f32[1024]{0:T(1024)S(1)} all-reduce(f32[1024]{0:T(1024)S(1)} %get-tuple-element.189), channel_id=1, replica_groups=mesh['row'=8,'col'=16] {'row'}, use_global_device_ids=true, to_apply=%region_8.9 | all-reduce | flops 1024 | bytes 8192 | tf_op jit(solution)/shard_map/pmax | solution.py:58
  130.2 14.6 %psum.22 = f32[1024]{0:T(1024)S(1)} all-reduce(f32[1024]{0:T(1024)S(1)} %exponential_multiply_fusion.1), channel_id=1, replica_groups=mesh['row'=8,'col'=16] {'row'}, use_global_device_ids=true, to_apply=%region_9.10 | all-reduce | flops 1024 | bytes 8192 | tf_op jit(solution)/shard_map/psum | solution.py:59
  144.8 32.0 %pmax.14 = f32[2048]{0:T(1024)S(1)} all-reduce(f32[2048]{0:T(1024)S(1)} %bitcast.37), channel_id=1, replica_groups=mesh['row'=8,'col'=16] {'col'}, use_global_device_ids=true, to_apply=%region_6.7 | all-reduce | flops 2048 | bytes 16384 | tf_op jit(solution)/shard_map/pmax | solution.py:55
  176.9 29.0 %psum.21 = f32[2048]{0:T(1024)S(1)} all-reduce(f32[2048]{0:T(1024)S(1)} %exponential_multiply_fusion), channel_id=1, replica_groups=mesh['row'=8,'col'=16] {'col'}, use_global_device_ids=true, to_apply=%region_7.8 | all-reduce | flops 2048 | bytes 16384 | tf_op jit(solution)/shard_map/psum | solution.py:56
  205.9 66.6 %while.35 = (s32[]{:T(128)}, f32[1024,1024]{1,0:T(8,128)}, f32[]{:T(128)}, bf16[4,512,1024]{2,1,0:T(8,128)(2,1)}, s32[4]{0:T(128)S(1)}, /*index=5*/bf16[2048,102...) while((s32[]{:T(128)}, f32[1024,1024]{1,0:T(8,128)}, ...), condition=%wide.region_12.13_spmd.clone, body=%wide.region_10.12_spmd.clone.sunk | while | flops 3237479424 | bytes 65061204 | solution.py:83
  207.2 0.8 dynamic_slice.60
  208.0 4.0 fusion.32
  212.7 5.2 %select_add_fusion.2 = f32[1024,1024]{1,0:T(8,128)} fusion(f32[1024,1024]{1,0:T(8,128)} %get-tuple-element.484, pred[]{:T(512)S(6)} %compare.7, bf16[2048,1024]{1,0:T(8,128)(2,1)} %get-tuple-element.503, s32[]{:T(128)S(6)} %select_n.16, f32[512,1024]{1,0:T(8,128)S(1)} %get-tuple-element.430, s32[1024]{0:T(1024)S(1)} %iota_add_fusion.2, ...), kind=kOutput, calls=%fused_computation.10.clone.1 | convolution fusion | flops 1081606144 | bytes 11546629 | tf_op jit(solution)/shard_map/while/body/eval_jaxpr/dot_general | solution.py:75
  217.9 1.7 bitcast_dynamic-update-slice_fusion.2
  219.6 2.0 copy-done.1
  222.8 0.8 dynamic_slice.60
  223.7 4.0 fusion.32
  228.3 6.5 %select_add_fusion.2 = f32[1024,1024]{1,0:T(8,128)} fusion(f32[1024,1024]{1,0:T(8,128)} %get-tuple-element.484, pred[]{:T(512)S(6)} %compare.7, bf16[2048,1024]{1,0:T(8,128)(2,1)} %get-tuple-element.503, s32[]{:T(128)S(6)} %select_n.16, f32[512,1024]{1,0:T(8,128)S(1)} %get-tuple-element.430, s32[1024]{0:T(1024)S(1)} %iota_add_fusion.2, ...), kind=kOutput, calls=%fused_computation.10.clone.1 | convolution fusion | flops 1081606144 | bytes 11546629 | tf_op jit(solution)/shard_map/while/body/eval_jaxpr/dot_general | solution.py:75
  234.8 1.7 bitcast_dynamic-update-slice_fusion.2
  236.6 2.0 copy-done.1
  239.8 0.8 dynamic_slice.60
  240.7 4.0 fusion.32
  245.3 6.5 %select_add_fusion.2 = f32[1024,1024]{1,0:T(8,128)} fusion(f32[1024,1024]{1,0:T(8,128)} %get-tuple-element.484, pred[]{:T(512)S(6)} %compare.7, bf16[2048,1024]{1,0:T(8,128)(2,1)} %get-tuple-element.503, s32[]{:T(128)S(6)} %select_n.16, f32[512,1024]{1,0:T(8,128)S(1)} %get-tuple-element.430, s32[1024]{0:T(1024)S(1)} %iota_add_fusion.2, ...), kind=kOutput, calls=%fused_computation.10.clone.1 | convolution fusion | flops 1081606144 | bytes 11546629 | tf_op jit(solution)/shard_map/while/body/eval_jaxpr/dot_general | solution.py:75
  251.8 1.7 bitcast_dynamic-update-slice_fusion.2
  253.6 2.0 copy-done.1
  256.8 0.8 dynamic_slice.60
  257.6 4.0 fusion.32
  262.3 6.5 %select_add_fusion.2 = f32[1024,1024]{1,0:T(8,128)} fusion(f32[1024,1024]{1,0:T(8,128)} %get-tuple-element.484, pred[]{:T(512)S(6)} %compare.7, bf16[2048,1024]{1,0:T(8,128)(2,1)} %get-tuple-element.503, s32[]{:T(128)S(6)} %select_n.16, f32[512,1024]{1,0:T(8,128)S(1)} %get-tuple-element.430, s32[1024]{0:T(1024)S(1)} %iota_add_fusion.2, ...), kind=kOutput, calls=%fused_computation.10.clone.1 | convolution fusion | flops 1081606144 | bytes 11546629 | tf_op jit(solution)/shard_map/while/body/eval_jaxpr/dot_general | solution.py:75
  268.8 1.7 bitcast_dynamic-update-slice_fusion.2
  270.5 2.0 copy-done.1
  272.5 2.5 convert_element_type.30
  275.0 2.6 copy.6
  278.2 77.2 %psum.23 = f32[]{:T(128)} all-reduce(f32[]{:T(128)} %get-tuple-element.191), channel_id=1, replica_groups=mesh['row'=8,'col'=16] {'row','col'}, use_global_device_ids=true, to_apply=%region_13.14 | all-reduce | flops 1 | bytes 8 | tf_op jit(solution)/shard_map/psum | solution.py:95
  356.1 1.1 copy.7
  357.2 0.8 convert_element_type.31
  358.1 41.2 %reduce-scatter.5.cloned.1.call-done = bf16[128,1024]{1,0:T(8,128)(2,1)} async-done(((bf16[2048,1024]{1,0:T(8,128)(2,1)}), bf16[128,1024]{1,0:T(8,128)(2,1)}) %reduce-scatter.5.cloned.1.call-update) | async-done | bytes 262160 | tf_op jit(solution)/shard_map/reduce_scatter | solution.py:86
  399.3 1.8 convert_element_type.29
  (74 shorter events, 4.6 us)
Async XLA Ops:
  7.2 33.4 %all-gather.5.cloned.1.call-start = ((), (), s32[]{:S(2)}) async-start(), calls=%async_computation.3 | async-start | bytes 2359296 | tf_op jit(solution)/shard_map/all_gather | solution.py:26
  7.9 87.1 %all-gather.3.cloned.1.call-start = ((), (), s32[]{:S(2)}) async-start(), calls=%async_computation.2 | async-start | bytes 4456448 | tf_op jit(solution)/shard_map/all_gather | solution.py:25
  8.6 347.5 %reduce-scatter.7.cloned.1.call-start = ((), (), s32[]{:S(2)}) async-start(), calls=%async_computation.5 | async-start | bytes 2359296
  212.6 5.2 %copy-start = (bf16[4,512,1024]{2,1,0:T(8,128)(2,1)S(1)}, bf16[4,512,1024]{2,1,0:T(8,128)(2,1)}, u32[]{:S(2)}) copy-start(bf16[4,512,1024]{2,1,0:T(8,128)(2,1)} %get-tuple-element.486) | copy-start | bytes 12582916 | tf_op jit(solution)/shard_map/while
  212.6 5.2 %copy-start.2 = (bf16[1024,1024]{1,0:T(8,128)(2,1)S(1)}, bf16[1024,1024]{1,0:T(8,128)(2,1)}, u32[]{:S(2)}) copy-start(bf16[1024,1024]{1,0:T(8,128)(2,1)} %get-tuple-element.504) | copy-start | bytes 6291460 | tf_op jit(solution)/shard_map/while
  219.6 2.0 copy-start.1
  228.3 6.5 %copy-start = (bf16[4,512,1024]{2,1,0:T(8,128)(2,1)S(1)}, bf16[4,512,1024]{2,1,0:T(8,128)(2,1)}, u32[]{:S(2)}) copy-start(bf16[4,512,1024]{2,1,0:T(8,128)(2,1)} %get-tuple-element.486) | copy-start | bytes 12582916 | tf_op jit(solution)/shard_map/while
  228.3 6.5 %copy-start.2 = (bf16[1024,1024]{1,0:T(8,128)(2,1)S(1)}, bf16[1024,1024]{1,0:T(8,128)(2,1)}, u32[]{:S(2)}) copy-start(bf16[1024,1024]{1,0:T(8,128)(2,1)} %get-tuple-element.504) | copy-start | bytes 6291460 | tf_op jit(solution)/shard_map/while
  236.6 2.0 copy-start.1
  245.3 6.5 %copy-start = (bf16[4,512,1024]{2,1,0:T(8,128)(2,1)S(1)}, bf16[4,512,1024]{2,1,0:T(8,128)(2,1)}, u32[]{:S(2)}) copy-start(bf16[4,512,1024]{2,1,0:T(8,128)(2,1)} %get-tuple-element.486) | copy-start | bytes 12582916 | tf_op jit(solution)/shard_map/while
  245.3 6.5 %copy-start.2 = (bf16[1024,1024]{1,0:T(8,128)(2,1)S(1)}, bf16[1024,1024]{1,0:T(8,128)(2,1)}, u32[]{:S(2)}) copy-start(bf16[1024,1024]{1,0:T(8,128)(2,1)} %get-tuple-element.504) | copy-start | bytes 6291460 | tf_op jit(solution)/shard_map/while
  253.6 2.0 copy-start.1
  262.3 6.5 %copy-start = (bf16[4,512,1024]{2,1,0:T(8,128)(2,1)S(1)}, bf16[4,512,1024]{2,1,0:T(8,128)(2,1)}, u32[]{:S(2)}) copy-start(bf16[4,512,1024]{2,1,0:T(8,128)(2,1)} %get-tuple-element.486) | copy-start | bytes 12582916 | tf_op jit(solution)/shard_map/while
  262.3 6.5 %copy-start.2 = (bf16[1024,1024]{1,0:T(8,128)(2,1)S(1)}, bf16[1024,1024]{1,0:T(8,128)(2,1)}, u32[]{:S(2)}) copy-start(bf16[1024,1024]{1,0:T(8,128)(2,1)} %get-tuple-element.504) | copy-start | bytes 6291460 | tf_op jit(solution)/shard_map/while
  270.5 2.0 copy-start.1
  277.6 121.6 %reduce-scatter.5.cloned.1.call-start = ((), (), s32[]{:S(2)}) async-start(), calls=%async_computation.4 | async-start | bytes 4456448 | tf_op jit(solution)/shard_map/reduce_scatter | solution.py:86
Sparse Core Ops, SparseCore 0:
  9.7 30.8 all-gather.4
  42.7 52.2 all-gather.2
  277.8 39.8 reduce-scatter.6
  320.9 78.3 reduce-scatter.4
where the time goes:
time: 410 us; the launch traced here: 409 us
  blocking collectives  165 us (40%)
  waiting for transfers between devices  129 us (31%)
  matrix products  60.8 us (15%)
  local copies, waits for them, and re-layouts  20.4 us (5%)
  between operations  15.7 us (4%)
  other arithmetic  8.7 us (2%)
  loops' own time  8.34 us (2%)
    psum x1, blocking collectives, shards(): lax.psum(loss_part, ('row', 'col'))  77.2 us
    all_gather x1, waiting for transfers between devices, shards(): query_all = lax.all_gather(queries, 'col', axis=0, tiled=True)  54.4 us
    reduce_scatter x1, waiting for transfers between devices, shards(): lax.psum_scatter(query_terms.reshape(total_rows, width).astype(jnp.bfloat...  41.2 us
    pmax x1, blocking collectives, shards(): row_peak = lax.pmax(row_top, 'col')  32 us
    all_gather x1, waiting for transfers between devices, shards(): passage_all = lax.all_gather(passages, 'row', axis=1, tiled=True)  31.8 us
    dot_general x8, matrix products, score_block(): lax.dot_general(query_rows, passage_all, (((1,), (1,)), ((), ())), prefer...  29.1 us
    psum x1, blocking collectives, shards(): row_sum = lax.psum(row_sum * jnp.exp(row_top - row_peak), 'col')  29 us
    dot_general x4, matrix products, second_pass(): lax.dot_general(slope, query_rows, (((0,), (0,)), ((), ())), preferred_el...  24.7 us
  transfers between devices with their start and end apart: 4, of which 3 were waited for; matrix products, arithmetic and copies ran while one was open for 0% of the time, Pallas kernels for 0%

commit v1 on v0

v1 whole, which is shorter than its diff:
```python
import functools

import jax
import jax.numpy as jnp
from jax import lax
from jax.experimental import pallas as pl
from jax.experimental.pallas import tpu as pltpu
from jax.sharding import PartitionSpec as P

logit_scale = 40.0
low = -1e30
AX = ("row", "col")
f32, bf16 = jnp.float32, jnp.bfloat16
MIB = 1024 * 1024


def lin(y, c, z, x):
    return ((y * 2 + c) * 4 + z) * 4 + x


def moves(step):
    pairs = []
    for y in range(4):
        for z in range(4):
            for x in range(4):
                pairs.append((lin(y, 0, z, x), lin(y, 0, *step(z, x, x ^ 1))))
                far_y, far_x = step(y, x, 3 - x)
                pairs.append((lin(y, 1, z, x), lin(far_y, 1, z, far_x)))
    return pairs


def hop(a, d, flip):
    return lax.ppermute(a, AX, moves(lambda r, x, other: ((r + d) % 4, other if flip else x)))


def hop_xor(a):
    return lax.ppermute(a, AX, moves(lambda r, x, other: (r ^ 1, x)))


def swap(a):
    return lax.ppermute(a, "row", [(i, i ^ 1) for i in range(8)])


def place():
    row, col = lax.axis_index("row"), lax.axis_index("col")
    return row // 2, row % 2, col // 4, col % 4


OFFSETS = [(0, 0), (0, 1), (1, 0), (3, 0), (2, 0), (1, 1), (3, 1), (2, 1)]


def load_copies(core, y, z, x, mine, theirs, q_dst, p_dst, sems):
    out = []
    for k, (d, flip) in enumerate(OFFSETS):
        slot = ((x % 2) ^ flip) * 4 + (z - d + 4) % 4
        far_y = (y - d + 4) % 4
        rank = (x // 2) ^ flip
        for which in range(2):
            copies = []
            q_src, p_src = (mine[k], theirs[k]) if which == 0 else (theirs[k], mine[k])
            if q_dst is not None:
                rows = pl.ds(pl.multiple_of(slot * 128, 128), 128)
                copies.append(pltpu.make_async_copy(q_src.at[which], q_dst.at[rows], sems.at[k, 0]))
            if p_dst is not None:
                for part in range(2):
                    rows = pl.ds(pl.multiple_of(far_y * 256 + (1 - part) * 128, 128), 128)
                    copies.append(
                        pltpu.make_async_copy(p_src.at[part], p_dst.at[rank, rows], sems.at[k, 1 + part])
                    )
            out.append((which, copies))
    return out


def run_copies(core, groups, start):
    for which in range(2):

        @pl.when(core == which)
        def _():
            for w, copies in groups:
                if w == which:
                    for copy in copies:
                        copy.start() if start else copy.wait()


TILE = 16


def score_kernel(*refs):
    mine, theirs, (target, scores_out, keep, send, qv, pt, sv, row_top, row_sum, col_top, sems, out_sem) = (
        refs[:8],
        refs[8:16],
        refs[16:],
    )
    y, core, z, x = place()
    groups = load_copies(core, y, z, x, mine, theirs, qv, pt, sems)
    run_copies(core, groups, True)
    run_copies(core, groups, False)
    for h in range(2):
        for n in range(4):
            cols = slice(n * 256, n * 256 + 256)
            s = logit_scale * jnp.dot(qv[...], pt[h, :, cols], preferred_element_type=f32)
            sv[h, :, cols] = s
            col_top[:, h * 1024 + n * 256 : h * 1024 + n * 256 + 256] = jnp.broadcast_to(
                jnp.max(s, axis=0, keepdims=True), (8, 256)
            )
    write = pltpu.make_async_copy(sv, scores_out, out_sem)
    write.start()
    lanes = lax.broadcasted_iota(jnp.int32, (TILE, 1024), 1)

    def step(i, carry):
        col_acc, hit_acc = carry
        rows = pl.ds(pl.multiple_of(i * TILE, TILE), TILE)
        parts = [sv[h, rows, :] for h in range(2)]
        aim = target[rows, :1]
        top = jnp.maximum(
            jnp.max(parts[0], axis=1, keepdims=True), jnp.max(parts[1], axis=1, keepdims=True)
        )
        total = jnp.zeros((TILE, 1), f32)
        cols, hits = [], jnp.zeros((TILE, 1024), f32)
        for h in range(2):
            t = parts[h]
            total = total + jnp.sum(jnp.exp(t - top), axis=1, keepdims=True)
            e = jnp.exp(t - col_top[:1, h * 1024 : h * 1024 + 1024])
            cols.append(sum(e[r : r + 8] for r in range(0, TILE, 8)))
            hits = hits + jnp.where(lanes == aim - h * 1024, t, 0.0)
        row_top[rows, :] = jnp.broadcast_to(top, (TILE, 128))
        row_sum[rows, :] = jnp.broadcast_to(total, (TILE, 128))
        hit_acc = hit_acc + sum(hits[r : r + 8] for r in range(0, TILE, 8))
        return (col_acc[0] + cols[0], col_acc[1] + cols[1]), hit_acc

    zero = jnp.zeros((8, 1024), f32)
    col_acc, hit_acc = lax.fori_loop(0, 1024 // TILE, step, ((zero, zero), zero))
    hits = jnp.sum(hit_acc, axis=0, keepdims=True)

    def fill(rows_ref, cols_ref, first):
        off = 0 if first else 1024
        for s in range(8):
            at = slice(off + s * 128, off + s * 128 + 128)
            rows_ref[0:1, at] = row_top[s * 128 : s * 128 + 128, :].T[0:1]
            rows_ref[1:2, at] = row_sum[s * 128 : s * 128 + 128, :].T[0:1]
        gap = slice(1024 - off, 2048 - off)
        rows_ref[0:1, gap] = jnp.full((1, 1024), low, f32)
        rows_ref[1:2, gap] = jnp.zeros((1, 1024), f32)
        rows_ref[2:3, :1024] = hits
        rows_ref[2:3, 1024:] = jnp.zeros((1, 1024), f32)
        cols_ref[0:1, :] = col_top[0:1, :]
        for h in range(2):
            cols_ref[1:2, h * 1024 : h * 1024 + 1024] = jnp.sum(col_acc[h], axis=0, keepdims=True)
        cols_ref[2:3, :] = jnp.zeros((1, 2048), f32)

    @pl.when(core == 0)
    def _():
        fill(keep, send, True)

    @pl.when(core == 1)
    def _():
        fill(send, keep, False)

    write.wait()


def flip_kernel(*refs):
    mine, theirs, (_, out, qv, sems) = refs[:8], refs[8:16], refs[16:]
    y, core, z, x = place()
    groups = load_copies(core, y, z, x, mine, theirs, qv, None, sems)
    run_copies(core, groups, True)
    run_copies(core, groups, False)
    for m in range(8):
        out[:, m * 128 : m * 128 + 128] = qv[m * 128 : m * 128 + 128, :].T


def grad_kernel(flip, order, with_slope, *refs):
    n = len(order)
    mine, theirs, refs = refs[:8], refs[8:16], refs[16:]
    if with_slope:
        (scores, target, own_lse, got_lse, q_flip), refs = refs[:5], refs[5:]
        keeps, sends, slope_out, refs = refs[:n], refs[n : 2 * n], refs[2 * n], refs[2 * n + 1 :]
        (pt, qt, slope, gq, gp, zeros, sems, in_sem, q_sem, out_sems, sl_sem, sv, row_lse) = refs
    else:
        (slope_in, q_flip), refs = refs[:2], refs[2:]
        keeps, sends, refs = refs[:n], refs[n : 2 * n], refs[2 * n :]
        (pt, qt, slope, gq, gp, zeros, sems, in_sem, q_sem, out_sems) = refs
    y, core, z, x = place()
    groups = load_copies(core, y, z, x, mine, theirs, None, pt, sems)
    q_copy = pltpu.make_async_copy(q_flip, qt, q_sem)
    zeros[...] = jnp.zeros(zeros.shape, bf16)
    if with_slope:
        reads = [
            pltpu.make_async_copy(
                scores.at[:, pl.ds(s * 128, 128)], sv.at[:, pl.ds(s * 128, 128)], in_sem.at[s]
            )
            for s in range(8)
        ]
        for read in reads:
            read.start()
        q_copy.start()
        run_copies(core, groups, True)
        first = core == 0
        mine_lse, their_lse = own_lse[...], got_lse[...]
        rows_lse = jnp.where(first, mine_lse[:, :1024], their_lse[:, 1024:])
        cols_lse = jnp.where(first, their_lse, mine_lse)
        for s in range(8):
            row_lse[s * 128 : s * 128 + 128, :] = jnp.broadcast_to(
                rows_lse[:, s * 128 : s * 128 + 128], (128, 128)
            ).T
        lanes = lax.broadcasted_iota(jnp.int32, (TILE, 1024), 1)

        for s in range(8):
            reads[s].wait()

            def step(i, carry, s=s):
                rows = pl.ds(pl.multiple_of(s * 128 + i * TILE, TILE), TILE)
                aim = target[rows, :1]
                lse = row_lse[rows, :1]
                for h in range(2):
                    t = sv[h, rows, :]
                    e = 0.5 * jnp.exp(t - lse) + 0.5 * jnp.exp(t - cols_lse[:, h * 1024 : h * 1024 + 1024])
                    e = e - jnp.where(lanes == aim - h * 1024, 1.0, 0.0)
                    slope[h, rows, :] = e.astype(bf16)
                return carry

            lax.fori_loop(0, 128 // TILE, step, 0)
        slope_copy = pltpu.make_async_copy(slope, slope_out, sl_sem)
        slope_copy.start()
    else:
        slope_copy = pltpu.make_async_copy(slope_in, slope, in_sem.at[0])
        slope_copy.start()
        q_copy.start()
        run_copies(core, groups, True)
        slope_copy.wait()
    run_copies(core, groups, False)
    half = (x % 2) ^ flip
    rank = (x // 2) ^ flip
    rows = pl.ds(pl.multiple_of(half * 512, 512), 512)
    for m in range(4):
        cut = slice(m * 256, m * 256 + 256)
        g = sum(
            lax.dot_general(
                slope[h, rows, :], pt[h, cut, :], (((1,), (1,)), ((), ())), preferred_element_type=f32
            )
            for h in range(2)
        )
        gq[:, cut] = (logit_scale * g).astype(bf16)
    q_copy.wait()
    for m in range(4):
        cut = slice(m * 256, m * 256 + 256)
        g = jnp.dot(qt[...], slope[rank, :, cut], preferred_element_type=f32)
        gp[:, cut] = (logit_scale * g).astype(bf16)

    def outs(which):
        copies = []
        for k, d in enumerate(order):
            q_rows = pl.ds(pl.multiple_of((z + d) % 4 * 128, 128), 128)
            far_y = (y + d) % 4
            q_from = gq.at[q_rows]
            p_to, q_to = (sends[k], keeps[k]) if which == 0 else (keeps[k], sends[k])
            for part in range(2):
                p_rows = pl.ds(pl.multiple_of(far_y * 256 + (1 - part) * 128, 128), 128)
                copies.append(pltpu.make_async_copy(gp.at[p_rows], p_to.at[part], out_sems.at[k, part]))
            copies.append(pltpu.make_async_copy(q_from, q_to.at[which], out_sems.at[k, 2]))
            copies.append(pltpu.make_async_copy(zeros, q_to.at[1 - which], out_sems.at[k, 3]))
        return copies

    for which in range(2):

        @pl.when(core == which)
        def _():
            copies = outs(which)
            for copy in copies:
                copy.start()
            for copy in copies:
                copy.wait()

    if with_slope:
        slope_copy.wait()


ANY = pl.BlockSpec(memory_space=pl.ANY)
VM = pl.BlockSpec(memory_space=pltpu.VMEM)


def arr(shape, dtype):
    return jax.ShapeDtypeStruct(shape, dtype)


def cost(flops, nbytes):
    return pl.CostEstimate(flops=flops, bytes_accessed=nbytes, transcendentals=0)


def scores_of(mine, theirs, target):
    return pl.pallas_call(
        score_kernel,
        out_shape=(arr((2, 1024, 1024), f32), arr((3, 2048), f32), arr((3, 2048), f32)),
        in_specs=[ANY] * 16 + [VM],
        out_specs=(ANY, VM, VM),
        scratch_shapes=[
            pltpu.VMEM((1024, 1024), bf16),
            pltpu.VMEM((2, 1024, 1024), bf16),
            pltpu.VMEM((2, 1024, 1024), f32),
            pltpu.VMEM((1024, 128), f32),
            pltpu.VMEM((1024, 128), f32),
            pltpu.VMEM((8, 2048), f32),
            pltpu.SemaphoreType.DMA((8, 3)),
            pltpu.SemaphoreType.DMA,
        ],
        compiler_params=pltpu.CompilerParams(vmem_limit_bytes=40 * MIB),
        cost_estimate=cost(2 * 1024**2 * 2048, 16 * MIB),
        name="scores",
    )(*mine, *theirs, target)


def flipped(mine, theirs, after):
    return pl.pallas_call(
        flip_kernel,
        out_shape=arr((1024, 1024), bf16),
        in_specs=[ANY] * 17,
        out_specs=VM,
        scratch_shapes=[pltpu.VMEM((1024, 1024), bf16), pltpu.SemaphoreType.DMA((8, 3))],
        compiler_params=pltpu.CompilerParams(vmem_limit_bytes=16 * MIB),
        cost_estimate=cost(0, 4 * MIB),
        name="flip",
    )(*mine, *theirs, after)


def grads_of(flip, order, mine, theirs, operands, in_specs, with_slope):
    n = len(order)
    chunk = arr((2, 128, 1024), bf16)
    out_shape = [chunk] * (2 * n) + ([arr((2, 1024, 1024), bf16)] if with_slope else [])
    scratch = [
        pltpu.VMEM((2, 1024, 1024), bf16),
        pltpu.VMEM((1024, 1024), bf16),
        pltpu.VMEM((2, 1024, 1024), bf16),
        pltpu.VMEM((512, 1024), bf16),
        pltpu.VMEM((1024, 1024), bf16),
        pltpu.VMEM((128, 1024), bf16),
        pltpu.SemaphoreType.DMA((8, 3)),
        pltpu.SemaphoreType.DMA((8,)),
        pltpu.SemaphoreType.DMA,
        pltpu.SemaphoreType.DMA((n, 4)),
    ]
    if with_slope:
        scratch += [
            pltpu.SemaphoreType.DMA,
            pltpu.VMEM((2, 1024, 1024), f32),
            pltpu.VMEM((1024, 128), f32),
        ]
    return pl.pallas_call(
        functools.partial(grad_kernel, flip, order, with_slope),
        out_shape=out_shape,
        in_specs=[ANY] * 16 + in_specs,
        out_specs=[ANY] * len(out_shape),
        scratch_shapes=scratch,
        compiler_params=pltpu.CompilerParams(vmem_limit_bytes=48 * MIB),
        cost_estimate=cost(2 * 1024**2 * 2048, 20 * MIB),
        name="grads_far" if flip else "grads_near",
    )(*mine, *theirs, *operands)


def merge(a, b):
    top = jnp.maximum(a[0], b[0])
    total = a[1] * jnp.exp(a[0] - top) + b[1] * jnp.exp(b[0] - top)
    return jnp.stack([top, total, a[2] + b[2]])


def shards(queries, passages, positive):
    y, core, z, x = place()
    first = core == 0
    flat = passages.T
    got = swap(jnp.where(first, flat, queries))
    own = jnp.stack([jnp.where(first, queries, flat), got])
    across = hop(own, 0, True)
    up, down, far = hop(own, 1, False), hop(own, 3, False), hop(own, 2, False)
    chunks = [own, across, up, down, far, hop(up, 0, True), hop(down, 0, True), hop(across, 2, False)]
    others = [swap(c) for c in chunks]

    aims = positive.reshape(4, 2, 2, 128)
    aims = jnp.where(x // 2 == 0, aims[:, 0], aims[:, 1]).transpose(1, 0, 2).reshape(1024)
    block = aims // 1024
    in_tile = (block // 4 == z) & ((block % 4 + 1) % 4 // 2 == (x + 1) % 4 // 2)
    aims = jnp.where(in_tile, block % 4 // 2 * 1024 + aims % 1024, -1)
    aims = jnp.broadcast_to(aims[:, None], (1024, 128))

    scores, keep, send = scores_of(chunks, others, aims)
    q_flip = flipped(chunks, others, keep)
    stats = merge(keep, swap(send))
    stats = merge(stats, hop(stats, 0, True))
    stats = merge(stats, hop_xor(stats))
    stats = merge(stats, hop(stats, 2, False))
    own_lse = (stats[0] + jnp.log(stats[1])).reshape(1, 2048)
    got_lse = swap(own_lse)

    far_order, near_order = (1, 3, 2, 0), (1, 3, 2, 0)
    outs = grads_of(1, far_order, chunks, others, (scores, aims, own_lse, got_lse, q_flip), [ANY, VM, VM, VM, ANY], True)
    keeps, sends, slope = outs[:4], outs[4:8], outs[8]

    def add(a, b):
        return (a.astype(f32) + b.astype(f32)).astype(bf16)

    total = []
    for d, k, s in zip(far_order, keeps, sends):
        total.append(hop(add(k, swap(s)), d, True))
    outs = grads_of(0, near_order, chunks, others, (slope, q_flip), [ANY, ANY], False)
    for d, k, s in zip(near_order, outs[:4], outs[4:]):
        part = add(k, swap(s))
        total.append(hop(part, d, False) if d else part)
    grads = sum(t.astype(f32) for t in total)
    other = swap(grads[1])
    grad_queries = jnp.where(first, grads[0], other)
    grad_passages = jnp.where(first, other, grads[0]).T

    part = jnp.sum(own_lse) - 2.0 * jnp.sum(stats[2])
    part = swap(part)
    part = part + hop(part, 0, True)
    part = part + hop_xor(part)
    part = part + hop(part, 2, False)
    loss = (part + swap(part)) / 32768.0
    return loss, grad_queries, grad_passages


def solution(mesh):
    in_specs = (P(("row", "col"), None), P("col", "row"), P("row"))
    out_specs = (P(), P(("row", "col"), None), P("col", "row"))
    return jax.shard_map(shards, mesh=mesh, in_specs=in_specs, out_specs=out_specs, check_vma=False)
```

time: 410 us -> 170 us (0.41)
  blocking collectives: 165 us -> 0 us
  waiting for transfers between devices: 129 us -> 40.2 us
  matrix products: 60.8 us -> 0 us
  starting transfers between devices: 0.16 us -> 60.9 us
  Pallas kernels: 0 us -> 48.2 us
  local copies, waits for them, and re-layouts: 20.4 us -> 7.29 us
  between operations: 15.7 us -> 6.69 us
  loops' own time: 8.34 us -> 0 us
    psum x3 -> x0, blocking collectives: 121 us -> none  [the longest x1 77.2 us: shards(): lax.psum(loss_part, ('row', 'col'))]
    all_gather x2 -> x0, waiting for transfers between devices: 86.2 us -> none  [the longest x1 54.4 us: shards(): query_all = lax.all_gather(queries, 'col', axis=0, tiled=True)]
    ppermute x0 -> x42, starting transfers between devices: none -> 60.9 us  [the longest x18 37.3 us: hop(): lax.ppermute(a, AX, moves(lambda r, x, other: ((r + d) % 4, other if flip...]
    dot_general x16 -> x0, matrix products: 60.8 us -> none  [the longest x8 29.1 us: score_block(): lax.dot_general(query_rows, passage_all, (((1,), (1,)), ((), ())), prefer...]
    pallas_call x0 -> x4, Pallas kernels: none -> 48.2 us  [the longest x2 24.4 us: grads_of(): pl.pallas_call(functools.partial(grad_kernel, flip, order, with_slope), o...]
    pmax x2 -> x0, blocking collectives: 44.5 us -> none  [the longest x1 32 us: shards(): row_peak = lax.pmax(row_top, 'col')]
    reduce_scatter x1 -> x0, waiting for transfers between devices: 41.2 us -> none  [shards(): lax.psum_scatter(query_terms.reshape(total_rows, width).astype(jnp.bfloat...]
    ppermute x0 -> x42, waiting for transfers between devices: none -> 40.2 us  [the longest x18 34.6 us: hop(): lax.ppermute(a, AX, moves(lambda r, x, other: ((r + d) % 4, other if flip...]
  transfers between devices with their start and end apart: 4 -> 42, of which waited for: 3 -> 19; matrix products, arithmetic and copies ran while one was open for 0% -> 1% of each run, Pallas kernels for 0% -> 7%
where the time goes in v1:
time: 170 us; the launch traced here: 169 us
  starting transfers between devices  60.9 us (36%)
  Pallas kernels  48.2 us (28%)
  waiting for transfers between devices  40.2 us (24%)
  local copies, waits for them, and re-layouts  7.29 us (4%)
  between operations  6.69 us (4%)
  other arithmetic  5.92 us (3%)
    ppermute x18, starting transfers between devices, hop(): lax.ppermute(a, AX, moves(lambda r, x, other: ((r + d) % 4, other if flip...  37.3 us
    ppermute x18, waiting for transfers between devices, hop(): lax.ppermute(a, AX, moves(lambda r, x, other: ((r + d) % 4, other if flip...  34.6 us
    pallas_call x2, Pallas kernels, grads_of(): pl.pallas_call(functools.partial(grad_kernel, flip, order, with_slope), o...  24.4 us
    pallas_call x1, Pallas kernels, scores_of(): pl.pallas_call(score_kernel, out_shape=(arr((2, 1024, 1024), f32), arr((3...  21.6 us
    ppermute x22, starting transfers between devices, swap(): return lax.ppermute(a, 'row', [(i, i ^ 1) for i in range(8)])  17.1 us
    unnamed x20, local copies, waits for them, and re-layouts  7.06 us
    ppermute x2, starting transfers between devices, hop_xor(): return lax.ppermute(a, AX, moves(lambda r, x, other: (r ^ 1, x)))  6.42 us
    ppermute x22, waiting for transfers between devices, swap(): return lax.ppermute(a, 'row', [(i, i ^ 1) for i in range(8)])  3.83 us
  transfers between devices with their start and end apart: 42, of which 19 were waited for; matrix products, arithmetic and copies ran while one was open for 1% of the time, Pallas kernels for 7%

profile of v1, /device:TPU:1, one launch (start us, length us, event | category | flops | bytes accessed | tf_op | source)
XLA Modules:
  0.0 169.2 jit_solution(14964584900280968872)
XLA Ops:
  0.6 1.1 copy.10
  1.7 1.0 fusion.1
  2.7 1.5 collective-permute-start
  4.2 1.2 collective-permute-done
  5.4 3.1 %collective-permute-start.4 = (bf16[2,128,1024]{2,1,0:T(8,128)(2,1)S(1)}, bf16[2,128,1024]{2,1,0:T(8,128)(2,1)S(1)}, u32[]{:S(2)}, u32[]{:S(2)}) collective-permute-start(bf16[2,128,1024]{2,1,0:T(8,128)(2,1)S(1)} %pad_maximum_fusion.refs_0_), channel_id=1, source_target_pairs={{0,8},{16,80},{1,9},{17,81},{2,10},{18,82},{3,11},{19,83},{4,12},{... | collective-permute-start | bytes 1572872 | tf_op jit(solution)/shard_map/ppermute | solution.py:33
  9.3 1.3 collective-permute-start.8
  10.6 1.3 collective-permute-start.2
  11.9 2.5 %collective-permute-start.1 = (bf16[2,128,1024]{2,1,0:T(8,128)(2,1)S(1)}, bf16[2,128,1024]{2,1,0:T(8,128)(2,1)S(1)}, u32[]{:S(2)}, u32[]{:S(2)}) collective-permute-start(bf16[2,128,1024]{2,1,0:T(8,128)(2,1)S(1)} %pad_maximum_fusion.refs_0_), channel_id=1, source_target_pairs={{0,1},{16,19},{1,0},{17,18},{2,3},{18,17},{3,2},{19,16},{4,5},{20,... | collective-permute-start | bytes 1572872 | tf_op jit(solution)/shard_map/ppermute | solution.py:33
  14.3 1.0 collective-permute-done.4.refs_4_
  15.4 1.7 %collective-permute-start.12 = (bf16[2,128,1024]{2,1,0:T(8,128)(2,1)S(1)}, bf16[2,128,1024]{2,1,0:T(8,128)(2,1)S(1)}, u32[]{:S(2)}, u32[]{:S(2)}) collective-permute-start(bf16[2,128,1024]{2,1,0:T(8,128)(2,1)S(1)} %collective-permute-done.4.refs_4_), channel_id=1, source_target_pairs={{0,16},{16,0},{32,48},{48,32},{64,80},{80,64},{96,112},{112,96},{1... | collective-permute-start | bytes 1572872 | tf_op jit(solution)/shard_map/ppermute | solution.py:41
  17.1 4.3 %collective-permute-done.3.refs_3_ = bf16[2,128,1024]{2,1,0:T(8,128)(2,1)S(1)} collective-permute-done((bf16[2,128,1024]{2,1,0:T(8,128)(2,1)S(1)}, bf16[2,128,1024]{2,1,0:T(8,128)(2,1)S(1)}, u32[]{:S(2)}, u32[]{:S(2)}) %collective-permute-start.3) | collective-permute-done | bytes 524320 | tf_op jit(solution)/shard_map/ppermute | solution.py:33
  21.4 2.3 %collective-permute-start.11 = (bf16[2,128,1024]{2,1,0:T(8,128)(2,1)S(1)}, bf16[2,128,1024]{2,1,0:T(8,128)(2,1)S(1)}, u32[]{:S(2)}, u32[]{:S(2)}) collective-permute-start(bf16[2,128,1024]{2,1,0:T(8,128)(2,1)S(1)} %collective-permute-done.3.refs_3_), channel_id=1, source_target_pairs={{0,16},{16,0},{32,48},{48,32},{64,80},{80,64},{96,112},{112,96},{1... | collective-permute-start | bytes 1572872 | tf_op jit(solution)/shard_map/ppermute | solution.py:41
  23.7 2.5 %collective-permute-start.6 = (bf16[2,128,1024]{2,1,0:T(8,128)(2,1)S(1)}, bf16[2,128,1024]{2,1,0:T(8,128)(2,1)}, u32[]{:S(2)}, u32[]{:S(2)}) collective-permute-start(bf16[2,128,1024]{2,1,0:T(8,128)(2,1)S(1)} %collective-permute-done.3.refs_3_), channel_id=1, source_target_pairs={{0,1},{16,19},{1,0},{17,18},{2,3},{18,17},{3,2},{19,16},{4,5},{20,... | collective-permute-start | bytes 1572872 | tf_op jit(solution)/shard_map/ppermute | solution.py:33
  26.4 2.9 %collective-permute-start.7 = (bf16[2,128,1024]{2,1,0:T(8,128)(2,1)S(1)}, bf16[2,128,1024]{2,1,0:T(8,128)(2,1)}, u32[]{:S(2)}, u32[]{:S(2)}) collective-permute-start(bf16[2,128,1024]{2,1,0:T(8,128)(2,1)S(1)} %collective-permute-done.1.refs_1_), channel_id=1, source_target_pairs={{0,8},{16,80},{1,9},{17,81},{2,10},{18,82},{3,11},{19,83},{4,12},{... | collective-permute-start | bytes 1572872 | tf_op jit(solution)/shard_map/ppermute | solution.py:33
  31.4 1.9 %collective-permute-done.6.refs_6_ = bf16[2,128,1024]{2,1,0:T(8,128)(2,1)} collective-permute-done((bf16[2,128,1024]{2,1,0:T(8,128)(2,1)S(1)}, bf16[2,128,1024]{2,1,0:T(8,128)(2,1)}, u32[]{:S(2)}, u32[]{:S(2)}) %collective-permute-start.6) | collective-permute-done | bytes 524320 | tf_op jit(solution)/shard_map/ppermute | solution.py:33
  33.3 5.3 %collective-permute-done.5.refs_5_ = bf16[2,128,1024]{2,1,0:T(8,128)(2,1)} collective-permute-done((bf16[2,128,1024]{2,1,0:T(8,128)(2,1)S(1)}, bf16[2,128,1024]{2,1,0:T(8,128)(2,1)}, u32[]{:S(2)}, u32[]{:S(2)}) %collective-permute-start.5) | collective-permute-done | bytes 524320 | tf_op jit(solution)/shard_map/ppermute | solution.py:33
  41.9 1.0 copy-done.5
  42.9 1.0 copy-done.7
  44.0 21.6 %scores.1 = (f32[2,1024,1024]{2,1,0:T(8,128)}, f32[3,2048]{1,0:T(4,128)S(1)}, f32[3,2048]{1,0:T(4,128)S(1)}) custom-call(bf16[2,128,1024]{2,1,0:T(8,128)(2,1)S(1)} %pad_maximum_fusion.refs_0_, bf16[2,128,1024]{2,1,0:T(8,128)(2,1)S(1)} %collective-permute-done.1.refs_1_, bf16[2,128,1024]{2,1,0:T(8,128)(2,1)S(1)} %collective-permute-done.2.refs_2_, ...), custom_call_target="tpu_custom_call" | custom-call | flops 4294967296 | bytes 16777216 | tf_op jit(solution)/shard_map/scores/pallas_call | solution.py:291
  67.0 2.6 %collective-permute-start.17 = (f32[3,2048]{1,0:T(4,128)S(1)}, f32[3,2048]{1,0:T(4,128)S(1)}, u32[]{:S(2)}, u32[]{:S(2)}) collective-permute-start(f32[3,2048]{1,0:T(4,128)S(1)} %pad_maximum_fusion.1), channel_id=1, source_target_pairs={{0,1},{16,19},{1,0},{17,18},{2,3},{18,17},{3,2},{19,16},{4,5},{20,... | collective-permute-start | bytes 73736 | tf_op jit(solution)/shard_map/ppermute | solution.py:33
  69.5 1.5 collective-permute-done.17
  71.1 1.4 collective-permute-start.18
  72.5 1.5 collective-permute-done.18
  74.0 3.0 %collective-permute-start.19 = (f32[3,2048]{1,0:T(4,128)S(1)}, f32[3,2048]{1,0:T(4,128)S(1)}, u32[]{:S(2)}, u32[]{:S(2)}) collective-permute-start(f32[3,2048]{1,0:T(4,128)S(1)} %pad_maximum_fusion.3), channel_id=1, source_target_pairs={{0,8},{16,80},{1,9},{17,81},{2,10},{18,82},{3,11},{19,83},{4,12},{... | collective-permute-start | bytes 73736 | tf_op jit(solution)/shard_map/ppermute | solution.py:33
  77.0 1.4 collective-permute-done.19
  79.1 2.5 %collective-permute-start.25 = (f32[1,2048]{1,0:T(1,128)S(1)}, f32[1,2048]{1,0:T(1,128)S(1)}, u32[]{:S(2)}, u32[]{:S(2)}) collective-permute-start(f32[1,2048]{1,0:T(1,128)S(1)} %get-tuple-element.53.refs_18_), channel_id=1, source_target_pairs={{0,16},{16,0},{32,48},{48,32},{64,80},{80,64},{96,112},{112,96},{1... | collective-permute-start | bytes 24584 | tf_op jit(solution)/shard_map/ppermute | solution.py:41
  81.6 2.2 %flip.1.refs_20_.refs_17_ = bf16[1024,1024]{1,0:T(8,128)(2,1)S(1)} custom-call(bf16[2,128,1024]{2,1,0:T(8,128)(2,1)S(1)} %pad_maximum_fusion.refs_0_, bf16[2,128,1024]{2,1,0:T(8,128)(2,1)S(1)} %collective-permute-done.1.refs_1_, bf16[2,128,1024]{2,1,0:T(8,128)(2,1)S(1)} %collective-permute-done.2.refs_2_, ...), custom_call_target="tpu_custom_call" | custom-call | bytes 4194304 | tf_op jit(solution)/shard_map/flip/pallas_call | solution.py:313
  83.9 1.3 copy-done
  85.2 15.3 %grads_far.1 = (bf16[2,128,1024]{2,1,0:T(8,128)(2,1)S(1)}, bf16[2,128,1024]{2,1,0:T(8,128)(2,1)S(1)}, bf16[2,128,1024]{2,1,0:T(8,128)(2,1)S(1)}, bf16[2,128,1024...) custom-call(bf16[2,128,1024]{2,1,0:T(8,128)(2,1)S(1)} %pad_maximum_f, ...), custom_call_target="tpu_custom_call" | custom-call | flops 4294967296 | bytes 20971520 | tf_op jit(solution)/shard_map/grads_far/pallas_call | solution.py:347
  101.6 9.1 %grads_near.1 = (bf16[2,128,1024]{2,1,0:T(8,128)(2,1)S(1)}, bf16[2,128,1024]{2,1,0:T(8,128)(2,1)S(1)}, bf16[2,128,1024]{2,1,0:T(8,128)(2,1)S(1)}, bf16[2,128,102...) custom-call(bf16[2,128,1024]{2,1,0:T(8,128)(2,1)S(1)} %pad_maximum_f, ...), custom_call_target="tpu_custom_call" | custom-call | flops 4294967296 | bytes 20971520 | tf_op jit(solution)/shard_map/grads_near/pallas_call | solution.py:347
  112.9 3.6 %collective-permute-start.27 = (bf16[2,128,1024]{2,1,0:T(8,128)(2,1)S(1)}, bf16[2,128,1024]{2,1,0:T(8,128)(2,1)S(1)}, u32[]{:S(2)}, u32[]{:S(2)}) collective-permute-start(bf16[2,128,1024]{2,1,0:T(8,128)(2,1)S(1)} %add_convert_fusion.7), channel_id=1, source_target_pairs={{0,5},{16,51},{1,4},{17,50},{2,7},{18,49},{3,6},{19,48},{4,9},{20,... | collective-permute-start | bytes 1572872 | tf_op jit(solution)/shard_map/ppermute | solution.py:33
  116.7 1.5 collective-permute-start.29
  118.4 3.8 %collective-permute-start.31 = (bf16[2,128,1024]{2,1,0:T(8,128)(2,1)S(1)}, bf16[2,128,1024]{2,1,0:T(8,128)(2,1)S(1)}, u32[]{:S(2)}, u32[]{:S(2)}) collective-permute-start(bf16[2,128,1024]{2,1,0:T(8,128)(2,1)S(1)} %add_convert_fusion.5), channel_id=1, source_target_pairs={{0,9},{16,83},{1,8},{17,82},{2,11},{18,81},{3,10},{19,80},{4,13},{... | collective-permute-start | bytes 1572872 | tf_op jit(solution)/shard_map/ppermute | solution.py:33
  123.4 1.1 collective-permute-done.27
  124.5 1.7 collective-permute-start.37
  126.2 3.8 %collective-permute-done.29 = bf16[2,128,1024]{2,1,0:T(8,128)(2,1)S(1)} collective-permute-done((bf16[2,128,1024]{2,1,0:T(8,128)(2,1)S(1)}, bf16[2,128,1024]{2,1,0:T(8,128)(2,1)S(1)}, u32[]{:S(2)}, u32[]{:S(2)}) %collective-permute-start.29) | collective-permute-done | bytes 524320 | tf_op jit(solution)/shard_map/ppermute | solution.py:33
  130.0 1.4 collective-permute-start.39
  131.4 5.6 %collective-permute-done.31 = bf16[2,128,1024]{2,1,0:T(8,128)(2,1)S(1)} collective-permute-done((bf16[2,128,1024]{2,1,0:T(8,128)(2,1)S(1)}, bf16[2,128,1024]{2,1,0:T(8,128)(2,1)S(1)}, u32[]{:S(2)}, u32[]{:S(2)}) %collective-permute-start.31) | collective-permute-done | bytes 524320 | tf_op jit(solution)/shard_map/ppermute | solution.py:33
  137.0 3.4 %collective-permute-done.33 = bf16[2,128,1024]{2,1,0:T(8,128)(2,1)S(1)} collective-permute-done((bf16[2,128,1024]{2,1,0:T(8,128)(2,1)S(1)}, bf16[2,128,1024]{2,1,0:T(8,128)(2,1)S(1)}, u32[]{:S(2)}, u32[]{:S(2)}) %collective-permute-start.33) | collective-permute-done | bytes 524320 | tf_op jit(solution)/shard_map/ppermute | solution.py:33
  140.4 3.0 %collective-permute-done.35 = bf16[2,128,1024]{2,1,0:T(8,128)(2,1)S(1)} collective-permute-done((bf16[2,128,1024]{2,1,0:T(8,128)(2,1)S(1)}, bf16[2,128,1024]{2,1,0:T(8,128)(2,1)S(1)}, u32[]{:S(2)}, u32[]{:S(2)}) %collective-permute-start.35) | collective-permute-done | bytes 524320 | tf_op jit(solution)/shard_map/ppermute | solution.py:33
  143.5 1.0 convert_add_fusion
  145.9 1.4 collective-permute-start.20
  147.3 2.5 %collective-permute-start.21 = (f32[]{:T(128)}, f32[]{:T(128)}, u32[]{:S(2)}, u32[]{:S(2)}) collective-permute-start(f32[]{:T(128)} %collective-permute-done.20), channel_id=1, source_target_pairs={{0,1},{16,19},{1,0},{17,18},{2,3},{18,17},{3,2},{19,16},{4,5},{20,... | collective-permute-start | bytes 20 | tf_op jit(solution)/shard_map/ppermute | solution.py:33
  149.8 1.4 collective-permute-done.21
  152.5 5.0 %collective-permute-start.22 = (f32[]{:T(128)}, f32[]{:T(128)}, u32[]{:S(2)}, u32[]{:S(2)}) collective-permute-start(f32[]{:T(128)} %add.202), channel_id=1, source_target_pairs={{0,4},{16,48},{1,5},{17,49},{2,6},{18,50},{3,7},{19,51},{4,0},{20,... | collective-permute-start | bytes 20 | tf_op jit(solution)/shard_map/ppermute | solution.py:37
  158.5 3.4 %collective-permute-start.23 = (f32[]{:T(128)}, f32[]{:T(128)}, u32[]{:S(2)}, u32[]{:S(2)}) collective-permute-start(f32[]{:T(128)} %add.203), channel_id=1, source_target_pairs={{0,8},{16,80},{1,9},{17,81},{2,10},{18,82},{3,11},{19,83},{4,12},{... | collective-permute-start | bytes 20 | tf_op jit(solution)/shard_map/ppermute | solution.py:33
  163.3 2.3 %collective-permute-start.24 = (f32[]{:T(128)}, f32[]{:T(128)}, u32[]{:S(2)}, u32[]{:S(2)}) collective-permute-start(f32[]{:T(128)} %add.204), channel_id=1, source_target_pairs={{0,16},{16,0},{32,48},{48,32},{64,80},{80,64},{96,112},{112,96},{1... | collective-permute-start | bytes 20 | tf_op jit(solution)/shard_map/ppermute | solution.py:41
  167.1 1.0 copy.12
  (83 shorter events, 15.4 us)
Async XLA Ops:
  2.7 2.7 %collective-permute-start = (bf16[128,1024]{1,0:T(8,128)(2,1)S(1)}, bf16[128,1024]{1,0:T(8,128)(2,1)S(1)}, u32[]{:S(2)}, u32[]{:S(2)}) collective-permute-start(bf16[128,1024]{1,0:T(8,128)(2,1)S(1)} %get-tuple-element.63), channel_id=1, source_target_pairs={{0,16},{16,0},{32,48},{48,32},{64,80},{80,64},{96,112},{112,96},{1... | collective-permute-start | bytes 786440 | tf_op jit(solution)/shard_map/ppermute | solution.py:41
  5.4 9.9 %collective-permute-start.4 = (bf16[2,128,1024]{2,1,0:T(8,128)(2,1)S(1)}, bf16[2,128,1024]{2,1,0:T(8,128)(2,1)S(1)}, u32[]{:S(2)}, u32[]{:S(2)}) collective-permute-start(bf16[2,128,1024]{2,1,0:T(8,128)(2,1)S(1)} %pad_maximum_fusion.refs_0_), channel_id=1, source_target_pairs={{0,8},{16,80},{1,9},{17,81},{2,10},{18,82},{3,11},{19,83},{4,12},{... | collective-permute-start | bytes 1572872 | tf_op jit(solution)/shard_map/ppermute | solution.py:33
  8.5 12.9 %collective-permute-start.3 = (bf16[2,128,1024]{2,1,0:T(8,128)(2,1)S(1)}, bf16[2,128,1024]{2,1,0:T(8,128)(2,1)S(1)}, u32[]{:S(2)}, u32[]{:S(2)}) collective-permute-start(bf16[2,128,1024]{2,1,0:T(8,128)(2,1)S(1)} %pad_maximum_fusion.refs_0_), channel_id=1, source_target_pairs={{0,12},{16,112},{1,13},{17,113},{2,14},{18,114},{3,15},{19,115},{4... | collective-permute-start | bytes 1572872 | tf_op jit(solution)/shard_map/ppermute | solution.py:33
  9.3 14.4 %collective-permute-start.8 = (bf16[2,128,1024]{2,1,0:T(8,128)(2,1)S(1)}, bf16[2,128,1024]{2,1,0:T(8,128)(2,1)S(1)}, u32[]{:S(2)}, u32[]{:S(2)}) collective-permute-start(bf16[2,128,1024]{2,1,0:T(8,128)(2,1)S(1)} %pad_maximum_fusion.refs_0_), channel_id=1, source_target_pairs={{0,16},{16,0},{32,48},{48,32},{64,80},{80,64},{96,112},{112,96},{1... | collective-permute-start | bytes 1572872 | tf_op jit(solution)/shard_map/ppermute | solution.py:41
  10.6 15.6 %collective-permute-start.2 = (bf16[2,128,1024]{2,1,0:T(8,128)(2,1)S(1)}, bf16[2,128,1024]{2,1,0:T(8,128)(2,1)S(1)}, u32[]{:S(2)}, u32[]{:S(2)}) collective-permute-start(bf16[2,128,1024]{2,1,0:T(8,128)(2,1)S(1)} %pad_maximum_fusion.refs_0_), channel_id=1, source_target_pairs={{0,4},{16,48},{1,5},{17,49},{2,6},{18,50},{3,7},{19,51},{4,8},{20,... | collective-permute-start | bytes 1572872 | tf_op jit(solution)/shard_map/ppermute | solution.py:33
  11.9 14.5 %collective-permute-start.1 = (bf16[2,128,1024]{2,1,0:T(8,128)(2,1)S(1)}, bf16[2,128,1024]{2,1,0:T(8,128)(2,1)S(1)}, u32[]{:S(2)}, u32[]{:S(2)}) collective-permute-start(bf16[2,128,1024]{2,1,0:T(8,128)(2,1)S(1)} %pad_maximum_fusion.refs_0_), channel_id=1, source_target_pairs={{0,1},{16,19},{1,0},{17,18},{2,3},{18,17},{3,2},{19,16},{4,5},{20,... | collective-permute-start | bytes 1572872 | tf_op jit(solution)/shard_map/ppermute | solution.py:33
  15.4 66.2 %copy-start.1 = (bf16[2,128,1024]{2,1,0:T(8,128)(2,1)}, bf16[2,128,1024]{2,1,0:T(8,128)(2,1)S(1)}, u32[]{:S(2)}) copy-start(bf16[2,128,1024]{2,1,0:T(8,128)(2,1)S(1)} %collective-permute-done.4.refs_4_) | copy-start | bytes 1572868
  15.4 13.9 %collective-permute-start.12 = (bf16[2,128,1024]{2,1,0:T(8,128)(2,1)S(1)}, bf16[2,128,1024]{2,1,0:T(8,128)(2,1)S(1)}, u32[]{:S(2)}, u32[]{:S(2)}) collective-permute-start(bf16[2,128,1024]{2,1,0:T(8,128)(2,1)S(1)} %collective-permute-done.4.refs_4_), channel_id=1, source_target_pairs={{0,16},{16,0},{32,48},{48,32},{64,80},{80,64},{96,112},{112,96},{1... | collective-permute-start | bytes 1572872 | tf_op jit(solution)/shard_map/ppermute | solution.py:41
  21.4 60.2 %copy-start.2 = (bf16[2,128,1024]{2,1,0:T(8,128)(2,1)}, bf16[2,128,1024]{2,1,0:T(8,128)(2,1)S(1)}, u32[]{:S(2)}) copy-start(bf16[2,128,1024]{2,1,0:T(8,128)(2,1)S(1)} %collective-permute-done.3.refs_3_) | copy-start | bytes 1572868
  21.4 8.7 %collective-permute-start.11 = (bf16[2,128,1024]{2,1,0:T(8,128)(2,1)S(1)}, bf16[2,128,1024]{2,1,0:T(8,128)(2,1)S(1)}, u32[]{:S(2)}, u32[]{:S(2)}) collective-permute-start(bf16[2,128,1024]{2,1,0:T(8,128)(2,1)S(1)} %collective-permute-done.3.refs_3_), channel_id=1, source_target_pairs={{0,16},{16,0},{32,48},{48,32},{64,80},{80,64},{96,112},{112,96},{1... | collective-permute-start | bytes 1572872 | tf_op jit(solution)/shard_map/ppermute | solution.py:41
  23.7 57.9 %copy-start.3 = (bf16[2,128,1024]{2,1,0:T(8,128)(2,1)}, bf16[2,128,1024]{2,1,0:T(8,128)(2,1)S(1)}, u32[]{:S(2)}) copy-start(bf16[2,128,1024]{2,1,0:T(8,128)(2,1)S(1)} %collective-permute-done.8.refs_8_) | copy-start | bytes 1572868
  23.7 9.6 %collective-permute-start.6 = (bf16[2,128,1024]{2,1,0:T(8,128)(2,1)S(1)}, bf16[2,128,1024]{2,1,0:T(8,128)(2,1)}, u32[]{:S(2)}, u32[]{:S(2)}) collective-permute-start(bf16[2,128,1024]{2,1,0:T(8,128)(2,1)S(1)} %collective-permute-done.3.refs_3_), channel_id=1, source_target_pairs={{0,1},{16,19},{1,0},{17,18},{2,3},{18,17},{3,2},{19,16},{4,5},{20,... | collective-permute-start | bytes 1572872 | tf_op jit(solution)/shard_map/ppermute | solution.py:33
  26.2 12.5 %collective-permute-start.5 = (bf16[2,128,1024]{2,1,0:T(8,128)(2,1)S(1)}, bf16[2,128,1024]{2,1,0:T(8,128)(2,1)}, u32[]{:S(2)}, u32[]{:S(2)}) collective-permute-start(bf16[2,128,1024]{2,1,0:T(8,128)(2,1)S(1)} %collective-permute-done.2.refs_2_), channel_id=1, source_target_pairs={{0,1},{16,19},{1,0},{17,18},{2,3},{18,17},{3,2},{19,16},{4,5},{20,... | collective-permute-start | bytes 1572872 | tf_op jit(solution)/shard_map/ppermute | solution.py:33
  26.4 12.3 %collective-permute-start.7 = (bf16[2,128,1024]{2,1,0:T(8,128)(2,1)S(1)}, bf16[2,128,1024]{2,1,0:T(8,128)(2,1)}, u32[]{:S(2)}, u32[]{:S(2)}) collective-permute-start(bf16[2,128,1024]{2,1,0:T(8,128)(2,1)S(1)} %collective-permute-done.1.refs_1_), channel_id=1, source_target_pairs={{0,8},{16,80},{1,9},{17,81},{2,10},{18,82},{3,11},{19,83},{4,12},{... | collective-permute-start | bytes 1572872 | tf_op jit(solution)/shard_map/ppermute | solution.py:33
  30.1 9.8 %collective-permute-start.10 = (bf16[2,128,1024]{2,1,0:T(8,128)(2,1)S(1)}, bf16[2,128,1024]{2,1,0:T(8,128)(2,1)}, u32[]{:S(2)}, u32[]{:S(2)}) collective-permute-start(bf16[2,128,1024]{2,1,0:T(8,128)(2,1)S(1)} %collective-permute-done.2.refs_2_), channel_id=1, source_target_pairs={{0,16},{16,0},{32,48},{48,32},{64,80},{80,64},{96,112},{112,96},{1... | collective-permute-start | bytes 1572872 | tf_op jit(solution)/shard_map/ppermute | solution.py:41
  30.9 9.0 %collective-permute-start.9 = (bf16[2,128,1024]{2,1,0:T(8,128)(2,1)S(1)}, bf16[2,128,1024]{2,1,0:T(8,128)(2,1)}, u32[]{:S(2)}, u32[]{:S(2)}) collective-permute-start(bf16[2,128,1024]{2,1,0:T(8,128)(2,1)S(1)} %collective-permute-done.1.refs_1_), channel_id=1, source_target_pairs={{0,16},{16,0},{32,48},{48,32},{64,80},{80,64},{96,112},{112,96},{1... | collective-permute-start | bytes 1572872 | tf_op jit(solution)/shard_map/ppermute | solution.py:41
  33.3 6.6 %collective-permute-start.14 = (bf16[2,128,1024]{2,1,0:T(8,128)(2,1)}, bf16[2,128,1024]{2,1,0:T(8,128)(2,1)}, u32[]{:S(2)}, u32[]{:S(2)}) collective-permute-start(bf16[2,128,1024]{2,1,0:T(8,128)(2,1)} %collective-permute-done.6.refs_6_), channel_id=1, source_target_pairs={{0,16},{16,0},{32,48},{48,32},{64,80},{80,64},{96,112},{112,96},{1... | collective-permute-start | bytes 1572872 | tf_op jit(solution)/shard_map/ppermute | solution.py:41
  38.7 2.3 %collective-permute-start.13 = (bf16[2,128,1024]{2,1,0:T(8,128)(2,1)}, bf16[2,128,1024]{2,1,0:T(8,128)(2,1)}, u32[]{:S(2)}, u32[]{:S(2)}) collective-permute-start(bf16[2,128,1024]{2,1,0:T(8,128)(2,1)} %collective-permute-done.5.refs_5_), channel_id=1, source_target_pairs={{0,16},{16,0},{32,48},{48,32},{64,80},{80,64},{96,112},{112,96},{1... | collective-permute-start | bytes 1572872 | tf_op jit(solution)/shard_map/ppermute | solution.py:41
  38.7 3.0 %collective-permute-start.15 = (bf16[2,128,1024]{2,1,0:T(8,128)(2,1)}, bf16[2,128,1024]{2,1,0:T(8,128)(2,1)}, u32[]{:S(2)}, u32[]{:S(2)}) collective-permute-start(bf16[2,128,1024]{2,1,0:T(8,128)(2,1)} %collective-permute-done.7.refs_7_), channel_id=1, source_target_pairs={{0,16},{16,0},{32,48},{48,32},{64,80},{80,64},{96,112},{112,96},{1... | collective-permute-start | bytes 1572872 | tf_op jit(solution)/shard_map/ppermute | solution.py:41
  41.9 1.0 copy-start.5
  44.0 21.6 %copy-start.8 = (s32[1024,128]{1,0:T(8,128)}, s32[1024,128]{1,0:T(8,128)S(1)}, u32[]{:S(2)}) copy-start(s32[1024,128]{1,0:T(8,128)S(1)} %broadcast_in_dim.4.refs_16_.refs_17_) | copy-start | bytes 1572868
  65.6 1.3 collective-permute-start.16
  67.0 4.1 %collective-permute-start.17 = (f32[3,2048]{1,0:T(4,128)S(1)}, f32[3,2048]{1,0:T(4,128)S(1)}, u32[]{:S(2)}, u32[]{:S(2)}) collective-permute-start(f32[3,2048]{1,0:T(4,128)S(1)} %pad_maximum_fusion.1), channel_id=1, source_target_pairs={{0,1},{16,19},{1,0},{17,18},{2,3},{18,17},{3,2},{19,16},{4,5},{20,... | collective-permute-start | bytes 73736 | tf_op jit(solution)/shard_map/ppermute | solution.py:33
  71.1 2.8 %collective-permute-start.18 = (f32[3,2048]{1,0:T(4,128)S(1)}, f32[3,2048]{1,0:T(4,128)S(1)}, u32[]{:S(2)}, u32[]{:S(2)}) collective-permute-start(f32[3,2048]{1,0:T(4,128)S(1)} %pad_maximum_fusion.2), channel_id=1, source_target_pairs={{0,4},{16,48},{1,5},{17,49},{2,6},{18,50},{3,7},{19,51},{4,0},{20,... | collective-permute-start | bytes 73736 | tf_op jit(solution)/shard_map/ppermute | solution.py:37
  74.0 4.3 %collective-permute-start.19 = (f32[3,2048]{1,0:T(4,128)S(1)}, f32[3,2048]{1,0:T(4,128)S(1)}, u32[]{:S(2)}, u32[]{:S(2)}) collective-permute-start(f32[3,2048]{1,0:T(4,128)S(1)} %pad_maximum_fusion.3), channel_id=1, source_target_pairs={{0,8},{16,80},{1,9},{17,81},{2,10},{18,82},{3,11},{19,83},{4,12},{... | collective-permute-start | bytes 73736 | tf_op jit(solution)/shard_map/ppermute | solution.py:33
  79.1 6.1 %collective-permute-start.25 = (f32[1,2048]{1,0:T(1,128)S(1)}, f32[1,2048]{1,0:T(1,128)S(1)}, u32[]{:S(2)}, u32[]{:S(2)}) collective-permute-start(f32[1,2048]{1,0:T(1,128)S(1)} %get-tuple-element.53.refs_18_), channel_id=1, source_target_pairs={{0,16},{16,0},{32,48},{48,32},{64,80},{80,64},{96,112},{112,96},{1... | collective-permute-start | bytes 24584 | tf_op jit(solution)/shard_map/ppermute | solution.py:41
  83.9 1.3 copy-start
  100.5 10.8 %collective-permute-start.26 = (bf16[2,128,1024]{2,1,0:T(8,128)(2,1)S(1)}, bf16[2,128,1024]{2,1,0:T(8,128)(2,1)S(1)}, u32[]{:S(2)}, u32[]{:S(2)}) collective-permute-start(bf16[2,128,1024]{2,1,0:T(8,128)(2,1)S(1)} %get-tuple-element.27), channel_id=1, source_target_pairs={{0,16},{16,0},{32,48},{48,32},{64,80},{80,64},{96,112},{112,96},{1... | collective-permute-start | bytes 1572872 | tf_op jit(solution)/shard_map/ppermute | solution.py:41
  100.6 11.0 %collective-permute-start.28 = (bf16[2,128,1024]{2,1,0:T(8,128)(2,1)S(1)}, bf16[2,128,1024]{2,1,0:T(8,128)(2,1)S(1)}, u32[]{:S(2)}, u32[]{:S(2)}) collective-permute-start(bf16[2,128,1024]{2,1,0:T(8,128)(2,1)S(1)} %get-tuple-element.29), channel_id=1, source_target_pairs={{0,16},{16,0},{32,48},{48,32},{64,80},{80,64},{96,112},{112,96},{1... | collective-permute-start | bytes 1572872 | tf_op jit(solution)/shard_map/ppermute | solution.py:41
  101.1 11.5 %collective-permute-start.30 = (bf16[2,128,1024]{2,1,0:T(8,128)(2,1)S(1)}, bf16[2,128,1024]{2,1,0:T(8,128)(2,1)S(1)}, u32[]{:S(2)}, u32[]{:S(2)}) collective-permute-start(bf16[2,128,1024]{2,1,0:T(8,128)(2,1)S(1)} %get-tuple-element.31), channel_id=1, source_target_pairs={{0,16},{16,0},{32,48},{48,32},{64,80},{80,64},{96,112},{112,96},{1... | collective-permute-start | bytes 1572872 | tf_op jit(solution)/shard_map/ppermute | solution.py:41
  101.2 11.8 %collective-permute-start.32 = (bf16[2,128,1024]{2,1,0:T(8,128)(2,1)S(1)}, bf16[2,128,1024]{2,1,0:T(8,128)(2,1)S(1)}, u32[]{:S(2)}, u32[]{:S(2)}) collective-permute-start(bf16[2,128,1024]{2,1,0:T(8,128)(2,1)S(1)} %get-tuple-element.33), channel_id=1, source_target_pairs={{0,16},{16,0},{32,48},{48,32},{64,80},{80,64},{96,112},{112,96},{1... | collective-permute-start | bytes 1572872 | tf_op jit(solution)/shard_map/ppermute | solution.py:41
  110.7 6.0 %collective-permute-start.34 = (bf16[2,128,1024]{2,1,0:T(8,128)(2,1)S(1)}, bf16[2,128,1024]{2,1,0:T(8,128)(2,1)S(1)}, u32[]{:S(2)}, u32[]{:S(2)}) collective-permute-start(bf16[2,128,1024]{2,1,0:T(8,128)(2,1)S(1)} %get-tuple-element.36), channel_id=1, source_target_pairs={{0,16},{16,0},{32,48},{48,32},{64,80},{80,64},{96,112},{112,96},{1... | collective-permute-start | bytes 1572872 | tf_op jit(solution)/shard_map/ppermute | solution.py:41
  111.3 7.1 %collective-permute-start.36 = (bf16[2,128,1024]{2,1,0:T(8,128)(2,1)S(1)}, bf16[2,128,1024]{2,1,0:T(8,128)(2,1)S(1)}, u32[]{:S(2)}, u32[]{:S(2)}) collective-permute-start(bf16[2,128,1024]{2,1,0:T(8,128)(2,1)S(1)} %get-tuple-element.38), channel_id=1, source_target_pairs={{0,16},{16,0},{32,48},{48,32},{64,80},{80,64},{96,112},{112,96},{1... | collective-permute-start | bytes 1572872 | tf_op jit(solution)/shard_map/ppermute | solution.py:41
  111.6 10.8 %collective-permute-start.38 = (bf16[2,128,1024]{2,1,0:T(8,128)(2,1)S(1)}, bf16[2,128,1024]{2,1,0:T(8,128)(2,1)S(1)}, u32[]{:S(2)}, u32[]{:S(2)}) collective-permute-start(bf16[2,128,1024]{2,1,0:T(8,128)(2,1)S(1)} %get-tuple-element.40), channel_id=1, source_target_pairs={{0,16},{16,0},{32,48},{48,32},{64,80},{80,64},{96,112},{112,96},{1... | collective-permute-start | bytes 1572872 | tf_op jit(solution)/shard_map/ppermute | solution.py:41
  112.5 10.4 %collective-permute-start.40 = (bf16[2,128,1024]{2,1,0:T(8,128)(2,1)S(1)}, bf16[2,128,1024]{2,1,0:T(8,128)(2,1)S(1)}, u32[]{:S(2)}, u32[]{:S(2)}) collective-permute-start(bf16[2,128,1024]{2,1,0:T(8,128)(2,1)S(1)} %get-tuple-element.42), channel_id=1, source_target_pairs={{0,16},{16,0},{32,48},{48,32},{64,80},{80,64},{96,112},{112,96},{1... | collective-permute-start | bytes 1572872 | tf_op jit(solution)/shard_map/ppermute | solution.py:41
  112.9 11.6 %collective-permute-start.27 = (bf16[2,128,1024]{2,1,0:T(8,128)(2,1)S(1)}, bf16[2,128,1024]{2,1,0:T(8,128)(2,1)S(1)}, u32[]{:S(2)}, u32[]{:S(2)}) collective-permute-start(bf16[2,128,1024]{2,1,0:T(8,128)(2,1)S(1)} %add_convert_fusion.7), channel_id=1, source_target_pairs={{0,5},{16,51},{1,4},{17,50},{2,7},{18,49},{3,6},{19,48},{4,9},{20,... | collective-permute-start | bytes 1572872 | tf_op jit(solution)/shard_map/ppermute | solution.py:33
  116.7 13.3 %collective-permute-start.29 = (bf16[2,128,1024]{2,1,0:T(8,128)(2,1)S(1)}, bf16[2,128,1024]{2,1,0:T(8,128)(2,1)S(1)}, u32[]{:S(2)}, u32[]{:S(2)}) collective-permute-start(bf16[2,128,1024]{2,1,0:T(8,128)(2,1)S(1)} %add_convert_fusion.6), channel_id=1, source_target_pairs={{0,13},{16,115},{1,12},{17,114},{2,15},{18,113},{3,14},{19,112},{4... | collective-permute-start | bytes 1572872 | tf_op jit(solution)/shard_map/ppermute | solution.py:33
  118.4 18.6 %collective-permute-start.31 = (bf16[2,128,1024]{2,1,0:T(8,128)(2,1)S(1)}, bf16[2,128,1024]{2,1,0:T(8,128)(2,1)S(1)}, u32[]{:S(2)}, u32[]{:S(2)}) collective-permute-start(bf16[2,128,1024]{2,1,0:T(8,128)(2,1)S(1)} %add_convert_fusion.5), channel_id=1, source_target_pairs={{0,9},{16,83},{1,8},{17,82},{2,11},{18,81},{3,10},{19,80},{4,13},{... | collective-permute-start | bytes 1572872 | tf_op jit(solution)/shard_map/ppermute | solution.py:33
  122.4 18.0 %collective-permute-start.33 = (bf16[2,128,1024]{2,1,0:T(8,128)(2,1)S(1)}, bf16[2,128,1024]{2,1,0:T(8,128)(2,1)S(1)}, u32[]{:S(2)}, u32[]{:S(2)}) collective-permute-start(bf16[2,128,1024]{2,1,0:T(8,128)(2,1)S(1)} %add_convert_fusion.4), channel_id=1, source_target_pairs={{0,1},{16,19},{1,0},{17,18},{2,3},{18,17},{3,2},{19,16},{4,5},{20,... | collective-permute-start | bytes 1572872 | tf_op jit(solution)/shard_map/ppermute | solution.py:33
  122.9 20.5 %collective-permute-start.35 = (bf16[2,128,1024]{2,1,0:T(8,128)(2,1)S(1)}, bf16[2,128,1024]{2,1,0:T(8,128)(2,1)S(1)}, u32[]{:S(2)}, u32[]{:S(2)}) collective-permute-start(bf16[2,128,1024]{2,1,0:T(8,128)(2,1)S(1)} %add_convert_fusion.3), channel_id=1, source_target_pairs={{0,4},{16,48},{1,5},{17,49},{2,6},{18,50},{3,7},{19,51},{4,8},{20,... | collective-permute-start | bytes 1572872 | tf_op jit(solution)/shard_map/ppermute | solution.py:33
  124.5 19.0 %collective-permute-start.37 = (bf16[2,128,1024]{2,1,0:T(8,128)(2,1)S(1)}, bf16[2,128,1024]{2,1,0:T(8,128)(2,1)S(1)}, u32[]{:S(2)}, u32[]{:S(2)}) collective-permute-start(bf16[2,128,1024]{2,1,0:T(8,128)(2,1)S(1)} %add_convert_fusion.2), channel_id=1, source_target_pairs={{0,12},{16,112},{1,13},{17,113},{2,14},{18,114},{3,15},{19,115},{4... | collective-permute-start | bytes 1572872 | tf_op jit(solution)/shard_map/ppermute | solution.py:33
  130.0 13.5 %collective-permute-start.39 = (bf16[2,128,1024]{2,1,0:T(8,128)(2,1)S(1)}, bf16[2,128,1024]{2,1,0:T(8,128)(2,1)S(1)}, u32[]{:S(2)}, u32[]{:S(2)}) collective-permute-start(bf16[2,128,1024]{2,1,0:T(8,128)(2,1)S(1)} %add_convert_fusion.1), channel_id=1, source_target_pairs={{0,8},{16,80},{1,9},{17,81},{2,10},{18,82},{3,11},{19,83},{4,12},{... | collective-permute-start | bytes 1572872 | tf_op jit(solution)/shard_map/ppermute | solution.py:33
  144.5 21.7 %collective-permute-start.41 = (f32[128,1024]{1,0:T(8,128)S(1)}, f32[128,1024]{1,0:T(8,128)S(1)}, u32[]{:S(2)}, u32[]{:S(2)}) collective-permute-start(f32[128,1024]{1,0:T(8,128)S(1)} %slice_bitcast_fusion), channel_id=1, source_target_pairs={{0,16},{16,0},{32,48},{48,32},{64,80},{80,64},{96,112},{112,96},{1... | collective-permute-start | bytes 1572872 | tf_op jit(solution)/shard_map/ppermute | solution.py:41
  145.9 1.4 collective-permute-start.20
  147.3 3.9 %collective-permute-start.21 = (f32[]{:T(128)}, f32[]{:T(128)}, u32[]{:S(2)}, u32[]{:S(2)}) collective-permute-start(f32[]{:T(128)} %collective-permute-done.20), channel_id=1, source_target_pairs={{0,1},{16,19},{1,0},{17,18},{2,3},{18,17},{3,2},{19,16},{4,5},{20,... | collective-permute-start | bytes 20 | tf_op jit(solution)/shard_map/ppermute | solution.py:33
  152.5 5.4 %collective-permute-start.22 = (f32[]{:T(128)}, f32[]{:T(128)}, u32[]{:S(2)}, u32[]{:S(2)}) collective-permute-start(f32[]{:T(128)} %add.202), channel_id=1, source_target_pairs={{0,4},{16,48},{1,5},{17,49},{2,6},{18,50},{3,7},{19,51},{4,0},{20,... | collective-permute-start | bytes 20 | tf_op jit(solution)/shard_map/ppermute | solution.py:37
  158.5 4.1 %collective-permute-start.23 = (f32[]{:T(128)}, f32[]{:T(128)}, u32[]{:S(2)}, u32[]{:S(2)}) collective-permute-start(f32[]{:T(128)} %add.203), channel_id=1, source_target_pairs={{0,8},{16,80},{1,9},{17,81},{2,10},{18,82},{3,11},{19,83},{4,12},{... | collective-permute-start | bytes 20 | tf_op jit(solution)/shard_map/ppermute | solution.py:33
  163.3 2.3 %collective-permute-start.24 = (f32[]{:T(128)}, f32[]{:T(128)}, u32[]{:S(2)}, u32[]{:S(2)}) collective-permute-start(f32[]{:T(128)} %add.204), channel_id=1, source_target_pairs={{0,16},{16,0},{32,48},{48,32},{64,80},{80,64},{96,112},{112,96},{1... | collective-permute-start | bytes 20 | tf_op jit(solution)/shard_map/ppermute | solution.py:41
  (3 other events, 2.6 us)

commit v2 on v1

v2 whole, which is shorter than its diff:
```python
import functools

import jax
import jax.numpy as jnp
from jax import lax
from jax.experimental import pallas as pl
from jax.experimental.pallas import tpu as pltpu
from jax.sharding import PartitionSpec as P

logit_scale = 40.0
log2_e = 1.4426950408889634
score_scale = logit_scale * log2_e
low = -1e30
AX = ("row", "col")
f32, bf16 = jnp.float32, jnp.bfloat16
MIB = 1024 * 1024


def lin(y, c, z, x):
    return ((y * 2 + c) * 4 + z) * 4 + x


def moves(step):
    pairs = []
    for y in range(4):
        for z in range(4):
            for x in range(4):
                pairs.append((lin(y, 0, z, x), lin(y, 0, *step(z, x, x ^ 1))))
                far_y, far_x = step(y, x, 3 - x)
                pairs.append((lin(y, 1, z, x), lin(far_y, 1, z, far_x)))
    return pairs


def hop(a, d, flip):
    return lax.ppermute(a, AX, moves(lambda r, x, other: ((r + d) % 4, other if flip else x)))


def hop_xor(a):
    return lax.ppermute(a, AX, moves(lambda r, x, other: (r ^ 1, x)))


def swap(a):
    return lax.ppermute(a, "row", [(i, i ^ 1) for i in range(8)])


def place():
    row, col = lax.axis_index("row"), lax.axis_index("col")
    return row // 2, row % 2, col // 4, col % 4


OFFSETS = [(0, 0), (0, 1), (1, 0), (3, 0), (2, 0), (1, 1), (3, 1), (2, 1)]


def load_copies(core, y, z, x, mine, theirs, q_dst, p_dst, sems):
    out = []
    for k, (d, flip) in enumerate(OFFSETS):
        slot = ((x % 2) ^ flip) * 4 + (z - d + 4) % 4
        far_y = (y - d + 4) % 4
        rank = (x // 2) ^ flip
        for which in range(2):
            copies = []
            q_src, p_src = (mine[k], theirs[k]) if which == 0 else (theirs[k], mine[k])
            if q_dst is not None:
                rows = pl.ds(pl.multiple_of(slot * 128, 128), 128)
                copies.append(pltpu.make_async_copy(q_src.at[which], q_dst.at[rows], sems.at[k, 0]))
            if p_dst is not None:
                for part in range(2):
                    rows = pl.ds(pl.multiple_of(far_y * 256 + (1 - part) * 128, 128), 128)
                    copies.append(
                        pltpu.make_async_copy(p_src.at[part], p_dst.at[rank, rows], sems.at[k, 1 + part])
                    )
            out.append((which, copies))
    return out


def run_copies(core, groups, start):
    for which in range(2):

        @pl.when(core == which)
        def _():
            for w, copies in groups:
                if w == which:
                    for copy in copies:
                        copy.start() if start else copy.wait()


TILE = 32


def lane_groups():
    return [(g // 8, slice(g % 8 * 128, g % 8 * 128 + 128)) for g in range(16)]


def fold(a):
    return sum(a[r : r + 8] for r in range(0, a.shape[0], 8))


def score_kernel(*refs):
    mine, theirs, (target, sv, keep, send, qv, pt, row_top, row_sum, col_top, sems) = (
        refs[:8],
        refs[8:16],
        refs[16:],
    )
    y, core, z, x = place()
    groups = load_copies(core, y, z, x, mine, theirs, qv, pt, sems)
    run_copies(core, groups, True)
    run_copies(core, groups, False)
    for h in range(2):
        for n in range(2):
            cols = slice(n * 512, n * 512 + 512)
            s = score_scale * jnp.dot(qv[...], pt[h, :, cols], preferred_element_type=f32)
            sv[h, :, cols] = s
            col_top[h, :, cols] = jnp.broadcast_to(jnp.max(s, axis=0, keepdims=True), (8, 512))
            top = jnp.maximum(
                jnp.maximum(s[:, :128], s[:, 128:256]), jnp.maximum(s[:, 256:384], s[:, 384:])
            )
            row_top[...] = top if h == n == 0 else jnp.maximum(row_top[...], top)
    tops = []
    for s in range(8):
        rows = slice(s * 128, s * 128 + 128)
        top = jnp.max(row_top[rows, :].T, axis=0, keepdims=True)
        tops.append(top)
        row_top[rows, :] = jnp.broadcast_to(top, (128, 128)).T
    lanes = lax.broadcasted_iota(jnp.int32, (TILE, 128), 1)

    def step(i, carry):
        col_acc, hits = carry
        rows = pl.ds(pl.multiple_of(i * TILE, TILE), TILE)
        top, aim = row_top[rows, :], target[rows, :]
        total, cols = jnp.zeros((TILE, 128), f32), []
        for g, (h, at) in enumerate(lane_groups()):
            t = sv[h, rows, at]
            total = total + jnp.exp2(t - top)
            cols.append(col_acc[g] + fold(jnp.exp2(t - col_top[h, 0:1, at])))
            hits = hits + fold(jnp.where(lanes == aim - g * 128, t, 0.0))
        row_sum[rows, :] = total
        return tuple(cols), hits

    zero = jnp.zeros((8, 128), f32)
    col_acc, hits = lax.fori_loop(0, 1024 // TILE, step, ((zero,) * 16, zero))
    hits = jnp.sum(hits, axis=0, keepdims=True)

    def fill(rows_ref, cols_ref, first):
        off = 0 if first else 1024
        for s in range(8):
            at = slice(off + s * 128, off + s * 128 + 128)
            rows_ref[0:1, at] = tops[s]
            rows_ref[1:2, at] = jnp.sum(row_sum[s * 128 : s * 128 + 128, :].T, axis=0, keepdims=True)
        gap = slice(1024 - off, 2048 - off)
        rows_ref[0:1, gap] = jnp.full((1, 1024), low, f32)
        rows_ref[1:2, gap] = jnp.zeros((1, 1024), f32)
        rows_ref[2:3, :] = jnp.zeros((1, 2048), f32)
        rows_ref[2:3, :128] = hits
        for h in range(2):
            cols_ref[0:1, h * 1024 : h * 1024 + 1024] = col_top[h, 0:1, :]
        for g in range(16):
            cols_ref[1:2, g * 128 : g * 128 + 128] = jnp.sum(col_acc[g], axis=0, keepdims=True)
        cols_ref[2:3, :] = jnp.zeros((1, 2048), f32)

    @pl.when(core == 0)
    def _():
        fill(keep, send, True)

    @pl.when(core == 1)
    def _():
        fill(send, keep, False)


def flip_kernel(*refs):
    mine, theirs, (_, out, qv, sems) = refs[:8], refs[8:16], refs[16:]
    y, core, z, x = place()
    groups = load_copies(core, y, z, x, mine, theirs, qv, None, sems)
    run_copies(core, groups, True)
    run_copies(core, groups, False)
    for m in range(8):
        out[:, m * 128 : m * 128 + 128] = qv[m * 128 : m * 128 + 128, :].T


def grad_kernel(flip, order, with_slope, n_ties, *refs):
    n = len(order)
    mine, theirs, refs = refs[:8], refs[8:16], refs[16:]
    steps = [(g, i, d) for g, group in enumerate(order) for i, d in enumerate(group)]
    if with_slope:
        (sv, target, own_lse, got_lse, q_flip), refs = refs[:5], refs[5 + n_ties :]
        keeps, sends, slope_out, refs = refs[:n], refs[n : 2 * n], refs[2 * n], refs[2 * n + 1 :]
        (pt, qt, slope, gq, gp, zeros, sems, in_sem, q_sem, out_sems, sl_sem, row_lse) = refs
    else:
        (slope_in, q_flip), refs = refs[:2], refs[2 + n_ties :]
        keeps, sends, refs = refs[:n], refs[n : 2 * n], refs[2 * n :]
        (pt, qt, slope, gq, gp, zeros, sems, in_sem, q_sem, out_sems) = refs
    y, core, z, x = place()
    groups = load_copies(core, y, z, x, mine, theirs, None, pt, sems)
    q_copy = pltpu.make_async_copy(q_flip, qt, q_sem)
    zeros[...] = jnp.zeros(zeros.shape, bf16)
    if with_slope:
        q_copy.start()
        run_copies(core, groups, True)
        first = core == 0
        mine_lse, their_lse = own_lse[...], got_lse[...]
        rows_lse = jnp.where(first, mine_lse[:, :1024], their_lse[:, 1024:])
        cols_lse = jnp.where(first, their_lse, mine_lse)
        for s in range(8):
            row_lse[s * 128 : s * 128 + 128, :] = jnp.broadcast_to(
                rows_lse[:, s * 128 : s * 128 + 128], (128, 128)
            ).T
        lanes = lax.broadcasted_iota(jnp.int32, (TILE, 128), 1)

        def step(i, carry):
            rows = pl.ds(pl.multiple_of(i * TILE, TILE), TILE)
            aim, lse = target[rows, :], row_lse[rows, :]
            for g, (h, at) in enumerate(lane_groups()):
                t = sv[h, rows, at]
                e = 0.5 * (jnp.exp2(t - lse) + jnp.exp2(t - cols_lse[:, g * 128 : g * 128 + 128]))
                slope[h, rows, at] = jnp.where(lanes == aim - g * 128, e - 1.0, e).astype(bf16)
            return carry

        lax.fori_loop(0, 1024 // TILE, step, 0)
        slope_copy = pltpu.make_async_copy(slope, slope_out, sl_sem)
        slope_copy.start()
    else:
        slope_copy = pltpu.make_async_copy(slope_in, slope, in_sem.at[0])
        slope_copy.start()
        q_copy.start()
        run_copies(core, groups, True)
        slope_copy.wait()
    run_copies(core, groups, False)
    half = (x % 2) ^ flip
    rank = (x // 2) ^ flip
    rows = pl.ds(pl.multiple_of(half * 512, 512), 512)
    for m in range(4):
        cut = slice(m * 256, m * 256 + 256)
        g = sum(
            lax.dot_general(
                slope[h, rows, :], pt[h, cut, :], (((1,), (1,)), ((), ())), preferred_element_type=f32
            )
            for h in range(2)
        )
        gq[:, cut] = (logit_scale * g).astype(bf16)
    q_copy.wait()
    for m in range(4):
        cut = slice(m * 256, m * 256 + 256)
        g = jnp.dot(qt[...], slope[rank, :, cut], preferred_element_type=f32)
        gp[:, cut] = (logit_scale * g).astype(bf16)

    def outs(which):
        copies = []
        for k, (g, i, d) in enumerate(steps):
            q_rows = pl.ds(pl.multiple_of((z + d) % 4 * 128, 128), 128)
            far_y = (y + d) % 4
            q_from = gq.at[q_rows]
            p_to, q_to = (sends[g], keeps[g]) if which == 0 else (keeps[g], sends[g])
            p_to, q_to = p_to.at[i], q_to.at[i]
            for part in range(2):
                p_rows = pl.ds(pl.multiple_of(far_y * 256 + (1 - part) * 128, 128), 128)
                copies.append(pltpu.make_async_copy(gp.at[p_rows], p_to.at[part], out_sems.at[k, part]))
            copies.append(pltpu.make_async_copy(q_from, q_to.at[which], out_sems.at[k, 2]))
            copies.append(pltpu.make_async_copy(zeros, q_to.at[1 - which], out_sems.at[k, 3]))
        return copies

    for which in range(2):

        @pl.when(core == which)
        def _():
            copies = outs(which)
            for copy in copies:
                copy.start()
            for copy in copies:
                copy.wait()

    if with_slope:
        slope_copy.wait()


ANY = pl.BlockSpec(memory_space=pl.ANY)
VM = pl.BlockSpec(memory_space=pltpu.VMEM)


def arr(shape, dtype):
    return jax.ShapeDtypeStruct(shape, dtype)


def cost(flops, nbytes):
    return pl.CostEstimate(flops=flops, bytes_accessed=nbytes, transcendentals=0)


def scores_of(mine, theirs, target):
    return pl.pallas_call(
        score_kernel,
        out_shape=(arr((2, 1024, 1024), f32), arr((3, 2048), f32), arr((3, 2048), f32)),
        in_specs=[ANY] * 16 + [VM],
        out_specs=(VM, VM, VM),
        scratch_shapes=[
            pltpu.VMEM((1024, 1024), bf16),
            pltpu.VMEM((2, 1024, 1024), bf16),
            pltpu.VMEM((1024, 128), f32),
            pltpu.VMEM((1024, 128), f32),
            pltpu.VMEM((2, 8, 1024), f32),
            pltpu.SemaphoreType.DMA((8, 3)),
        ],
        compiler_params=pltpu.CompilerParams(vmem_limit_bytes=32 * MIB),
        cost_estimate=cost(2 * 1024**2 * 2048, 16 * MIB),
        name="scores",
    )(*mine, *theirs, target)


def flipped(mine, theirs, after):
    return pl.pallas_call(
        flip_kernel,
        out_shape=arr((1024, 1024), bf16),
        in_specs=[ANY] * 17,
        out_specs=VM,
        scratch_shapes=[pltpu.VMEM((1024, 1024), bf16), pltpu.SemaphoreType.DMA((8, 3))],
        compiler_params=pltpu.CompilerParams(vmem_limit_bytes=16 * MIB),
        cost_estimate=cost(0, 4 * MIB),
        name="flip",
    )(*mine, *theirs, after)


def grads_of(flip, order, mine, theirs, operands, in_specs, with_slope, ties=()):
    n = len(order)
    chunks = [arr((len(group), 2, 128, 1024), bf16) for group in order]
    out_shape = chunks * 2 + ([arr((2, 1024, 1024), bf16)] if with_slope else [])
    scratch = [
        pltpu.VMEM((2, 1024, 1024), bf16),
        pltpu.VMEM((1024, 1024), bf16),
        pltpu.VMEM((2, 1024, 1024), bf16),
        pltpu.VMEM((512, 1024), bf16),
        pltpu.VMEM((1024, 1024), bf16),
        pltpu.VMEM((128, 1024), bf16),
        pltpu.SemaphoreType.DMA((8, 3)),
        pltpu.SemaphoreType.DMA((8,)),
        pltpu.SemaphoreType.DMA,
        pltpu.SemaphoreType.DMA((4, 4)),
    ]
    if with_slope:
        scratch += [
            pltpu.SemaphoreType.DMA,
            pltpu.VMEM((1024, 128), f32),
        ]
    return pl.pallas_call(
        functools.partial(grad_kernel, flip, order, with_slope, len(ties)),
        out_shape=out_shape,
        in_specs=[ANY] * 16 + in_specs + [ANY] * len(ties),
        out_specs=[ANY] * len(out_shape),
        scratch_shapes=scratch,
        compiler_params=pltpu.CompilerParams(vmem_limit_bytes=32 * MIB),
        cost_estimate=cost(2 * 1024**2 * 2048, 20 * MIB),
        name="grads_far" if flip else "grads_near",
    )(*mine, *theirs, *operands, *ties)


def join_kernel(picks, *refs):
    out = refs[-1]
    parts = [r[...] if p is None else r[p : p + 1] for p, r in zip(picks, refs)]
    out[...] = sum(p.astype(f32) for p in parts).astype(bf16)


def join(terms, ties=(), pick=None):
    a, n = terms[0], len(terms)
    return pl.pallas_call(
        functools.partial(join_kernel, [None] * (n - 1) + [pick]),
        out_shape=arr(a.shape, bf16),
        in_specs=[VM] * n + [ANY] * len(ties),
        out_specs=VM,
        compiler_params=pltpu.CompilerParams(vmem_limit_bytes=16 * MIB),
        cost_estimate=cost(a.size, 6 * a.size),
        name="join",
    )(*terms, *ties)


def total_kernel(n, *refs):
    mine, other = refs[-2:]
    mine[...] = sum(r[0, 0].astype(f32) for r in refs[:n])
    other[...] = sum(r[0, 1].astype(f32) for r in refs[:n])


def total(terms, ties=()):
    return pl.pallas_call(
        functools.partial(total_kernel, len(terms)),
        out_shape=[arr((128, 1024), f32)] * 2,
        in_specs=[VM] * len(terms) + [ANY] * len(ties),
        out_specs=[VM] * 2,
        compiler_params=pltpu.CompilerParams(vmem_limit_bytes=16 * MIB),
        cost_estimate=cost(5 * 2**18, 4 * MIB),
        name="total",
    )(*terms, *ties)


def merge_kernel(last, a, b, *refs):
    top = jnp.maximum(a[0:1], b[0:1])
    total = a[1:2] * jnp.exp2(a[0:1] - top) + b[1:2] * jnp.exp2(b[0:1] - top)
    hits = a[2:3] + b[2:3]
    if last:
        lse, part = refs[-2:]
        lse[...] = top + jnp.log2(total)
        figure = jnp.sum(lse[...] - 2.0 * hits, axis=1, keepdims=True)
        part[...] = jnp.broadcast_to(figure, (8, 128))
    else:
        out = refs[-1]
        out[0:1] = top
        out[1:2] = total
        out[2:3] = hits


def merge(a, b, ties=(), last=False):
    return pl.pallas_call(
        functools.partial(merge_kernel, last),
        out_shape=[arr((1, 2048), f32), arr((8, 128), f32)] if last else arr((3, 2048), f32),
        in_specs=[VM, VM] + [ANY] * len(ties),
        out_specs=[VM, VM] if last else VM,
        compiler_params=pltpu.CompilerParams(vmem_limit_bytes=4 * MIB),
        cost_estimate=cost(0, 2**16),
        name="merge",
    )(a, b, *ties)


def shards(queries, passages, positive):
    y, core, z, x = place()
    first = core == 0
    flat = passages.T
    got = swap(jnp.where(first, flat, queries))
    own = jnp.stack([jnp.where(first, queries, flat), got])
    down, up, far = hop(own, 3, False), hop(own, 1, False), hop(own, 2, False)
    across = hop(own, 0, True)
    down_across, up_across = hop(down, 0, True), hop(up, 0, True)
    far_across = hop(across, 2, False)
    chunks = [own, across, up, down, far, up_across, down_across, far_across]
    others = [swap(c) for c in chunks]

    aims = positive.reshape(4, 2, 2, 128)
    aims = jnp.where(x // 2 == 0, aims[:, 0], aims[:, 1]).transpose(1, 0, 2).reshape(1024)
    block = aims // 1024
    in_tile = (block // 4 == z) & ((block % 4 + 1) % 4 // 2 == (x + 1) % 4 // 2)
    aims = jnp.where(in_tile, block % 4 // 2 * 1024 + aims % 1024, -1)
    aims = jnp.broadcast_to(aims[:, None], (1024, 128))

    scores, keep, send = scores_of(chunks, others, aims)
    q_flip = flipped(chunks, others, keep)
    stats = merge(keep, swap(send))
    stats = merge(stats, hop(stats, 0, True), (q_flip,))
    stats = merge(stats, hop_xor(stats))
    own_lse, part = merge(stats, hop(stats, 2, False), last=True)
    got_lse, part = swap(own_lse), swap(part)

    outs = grads_of(
        1, ((1, 3), (2,), (0,)), chunks, others, (scores, aims, own_lse, got_lse, q_flip), [VM, VM, VM, VM, ANY], True, (part,)
    )
    keeps, recvs, slope = outs[:3], [swap(s) for s in outs[3:6]], outs[6]
    sides, beyond = join([keeps[0], recvs[0]]), join([keeps[1], recvs[1]])
    part = part + hop(part, 0, True)
    ties = (sides, beyond, part)
    sides, beyond = hop(sides, 0, True), hop(beyond, 2, False)
    across = [keeps[2], recvs[2]]
    outs = grads_of(0, ((1,), (3,), (2,), (0,)), chunks, others, (slope, q_flip), [ANY, ANY], False, ties)
    part = part + hop_xor(part)
    keeps, recvs = outs[:4], [swap(s) for s in outs[4:]]
    up = hop(join([keeps[0], recvs[0], sides], pick=0), 1, False)
    down = hop(join([keeps[1], recvs[1], sides], pick=1), 3, False)
    across = hop(join([*across, beyond]), 0, True)
    far = hop(join([keeps[2], recvs[2]], (part,)), 2, False)
    home = join([keeps[3], recvs[3]], (part,))
    part = part + hop(part, 2, False)
    mine, other = total([home, far, across, up, down], (part,))
    other = swap(other)
    grad_queries = jnp.where(first, mine, other)
    grad_passages = jnp.where(first, other, mine).T
    loss = (part + swap(part))[0, 0] / (32768.0 * log2_e)
    return loss, grad_queries, grad_passages


def solution(mesh):
    in_specs = (P(("row", "col"), None), P("col", "row"), P("row"))
    out_specs = (P(), P(("row", "col"), None), P("col", "row"))
    return jax.shard_map(shards, mesh=mesh, in_specs=in_specs, out_specs=out_specs, check_vma=False)
```

time: 170 us -> 143 us (0.84)
  Pallas kernels: 48.2 us -> 34.6 us
  starting transfers between devices: 60.9 us -> 53.2 us
  between operations: 6.69 us -> 2.69 us
  other arithmetic: 5.92 us -> 2.68 us
  waiting for transfers between devices: 40.2 us -> 42.7 us
    pallas_call x1, Pallas kernels: 21.6 us -> 10.1 us  [scores_of(): pl.pallas_call(score_kernel, out_shape=(arr((2, 1024, 1024), f32), arr((3...]
    ppermute x22 -> x21, waiting for transfers between devices: 3.83 us -> 7.83 us  [swap(): return lax.ppermute(a, 'row', [(i, i ^ 1) for i in range(8)])]
    ppermute x2, starting transfers between devices: 6.42 us -> 2.69 us  [hop_xor(): return lax.ppermute(a, AX, moves(lambda r, x, other: (r ^ 1, x)))]
    ppermute x18 -> x17, starting transfers between devices: 37.3 us -> 35.2 us  [hop(): lax.ppermute(a, AX, moves(lambda r, x, other: ((r + d) % 4, other if flip...]
    pallas_call x2 -> x14, Pallas kernels: 24.4 us -> 22.3 us  [the longest x2 20.7 us: grads_of(): pl.pallas_call(functools.partial(grad_kernel, flip, order, with_slope, le...]
    ppermute x22 -> x21, starting transfers between devices: 17.1 us -> 15.3 us  [swap(): return lax.ppermute(a, 'row', [(i, i ^ 1) for i in range(8)])]
    unnamed x20 -> x12, local copies, waits for them, and re-layouts: 7.06 us -> 5.75 us
    ppermute x18 -> x17, waiting for transfers between devices: 34.6 us -> 33.4 us  [hop(): lax.ppermute(a, AX, moves(lambda r, x, other: ((r + d) % 4, other if flip...]
  transfers between devices with their start and end apart: 42 -> 40, of which waited for: 19 -> 18; matrix products, arithmetic and copies ran while one was open for 1% -> 1% of each run, Pallas kernels for 7% -> 8%
where the time goes in v2:
time: 143 us; the launch traced here: 142 us
  starting transfers between devices  53.2 us (37%)
  waiting for transfers between devices  42.7 us (30%)
  Pallas kernels  34.6 us (24%)
  local copies, waits for them, and re-layouts  6.46 us (5%)
  between operations  2.69 us (2%)
  other arithmetic  2.68 us (2%)
    ppermute x17, starting transfers between devices, hop(): lax.ppermute(a, AX, moves(lambda r, x, other: ((r + d) % 4, other if flip...  35.2 us
    ppermute x17, waiting for transfers between devices, hop(): lax.ppermute(a, AX, moves(lambda r, x, other: ((r + d) % 4, other if flip...  33.4 us
    pallas_call x2, Pallas kernels, grads_of(): pl.pallas_call(functools.partial(grad_kernel, flip, order, with_slope, le...  20.7 us
    ppermute x21, starting transfers between devices, swap(): return lax.ppermute(a, 'row', [(i, i ^ 1) for i in range(8)])  15.3 us
    pallas_call x1, Pallas kernels, scores_of(): pl.pallas_call(score_kernel, out_shape=(arr((2, 1024, 1024), f32), arr((3...  10.1 us
    ppermute x21, waiting for transfers between devices, swap(): return lax.ppermute(a, 'row', [(i, i ^ 1) for i in range(8)])  7.83 us
    unnamed x12, local copies, waits for them, and re-layouts  5.75 us
  transfers between devices with their start and end apart: 40, of which 18 were waited for; matrix products, arithmetic and copies ran while one was open for 1% of the time, Pallas kernels for 8%

profile of v2, /device:TPU:1, one launch (start us, length us, event | category | flops | bytes accessed | tf_op | source)
XLA Modules:
  0.0 142.3 jit_solution(10129241406141373643)
XLA Ops:
  0.6 1.1 copy.10
  1.7 1.0 fusion
  2.7 1.5 %collective-permute-start = (bf16[128,1024]{1,0:T(8,128)(2,1)S(1)}, bf16[128,1024]{1,0:T(8,128)(2,1)S(1)}, u32[]{:S(2)}, u32[]{:S(2)}) collective-permute-start(bf16[128,1024]{1,0:T(8,128)(2,1)S(1)} %get-tuple-element.59), channel_id=1, source_target_pairs={{0,16},{16,0},{32,48},{48,32},{64,80},{80,64},{96,112},{112,96},{1... | collective-permute-start | bytes 786440 | tf_op jit(solution)/shard_map/ppermute | solution.py:43
  4.2 1.2 collective-permute-done
  5.4 1.4 %collective-permute-start.2 = (bf16[2,128,1024]{2,1,0:T(8,128)(2,1)S(1)}, bf16[2,128,1024]{2,1,0:T(8,128)(2,1)S(1)}, u32[]{:S(2)}, u32[]{:S(2)}) collective-permute-start(bf16[2,128,1024]{2,1,0:T(8,128)(2,1)S(1)} %pad_maximum_fusion.refs_0_), channel_id=1, source_target_pairs={{0,4},{16,48},{1,5},{17,49},{2,6},{18,50},{3,7},{19,51},{4,8},{20,... | collective-permute-start | bytes 1572872 | tf_op jit(solution)/shard_map/ppermute | solution.py:35
  6.9 1.5 %collective-permute-start.3 = (bf16[2,128,1024]{2,1,0:T(8,128)(2,1)S(1)}, bf16[2,128,1024]{2,1,0:T(8,128)(2,1)S(1)}, u32[]{:S(2)}, u32[]{:S(2)}) collective-permute-start(bf16[2,128,1024]{2,1,0:T(8,128)(2,1)S(1)} %pad_maximum_fusion.refs_0_), channel_id=1, source_target_pairs={{0,12},{16,112},{1,13},{17,113},{2,14},{18,114},{3,15},{19,115},{4... | collective-permute-start | bytes 1572872 | tf_op jit(solution)/shard_map/ppermute | solution.py:35
  8.4 2.5 %collective-permute-start.1 = (bf16[2,128,1024]{2,1,0:T(8,128)(2,1)S(1)}, bf16[2,128,1024]{2,1,0:T(8,128)(2,1)S(1)}, u32[]{:S(2)}, u32[]{:S(2)}) collective-permute-start(bf16[2,128,1024]{2,1,0:T(8,128)(2,1)S(1)} %pad_maximum_fusion.refs_0_), channel_id=1, source_target_pairs={{0,1},{16,19},{1,0},{17,18},{2,3},{18,17},{3,2},{19,16},{4,5},{20,... | collective-permute-start | bytes 1572872 | tf_op jit(solution)/shard_map/ppermute | solution.py:35
  10.9 1.6 %collective-permute-start.4 = (bf16[2,128,1024]{2,1,0:T(8,128)(2,1)S(1)}, bf16[2,128,1024]{2,1,0:T(8,128)(2,1)S(1)}, u32[]{:S(2)}, u32[]{:S(2)}) collective-permute-start(bf16[2,128,1024]{2,1,0:T(8,128)(2,1)S(1)} %pad_maximum_fusion.refs_0_), channel_id=1, source_target_pairs={{0,8},{16,80},{1,9},{17,81},{2,10},{18,82},{3,11},{19,83},{4,12},{... | collective-permute-start | bytes 1572872 | tf_op jit(solution)/shard_map/ppermute | solution.py:35
  12.5 0.9 collective-permute-start.8
  13.4 1.8 %collective-permute-done.2.refs_2_ = bf16[2,128,1024]{2,1,0:T(8,128)(2,1)S(1)} collective-permute-done((bf16[2,128,1024]{2,1,0:T(8,128)(2,1)S(1)}, bf16[2,128,1024]{2,1,0:T(8,128)(2,1)S(1)}, u32[]{:S(2)}, u32[]{:S(2)}) %collective-permute-start.2) | collective-permute-done | bytes 524320 | tf_op jit(solution)/shard_map/ppermute | solution.py:35
  15.2 2.5 %collective-permute-start.5 = (bf16[2,128,1024]{2,1,0:T(8,128)(2,1)S(1)}, bf16[2,128,1024]{2,1,0:T(8,128)(2,1)}, u32[]{:S(2)}, u32[]{:S(2)}) collective-permute-start(bf16[2,128,1024]{2,1,0:T(8,128)(2,1)S(1)} %collective-permute-done.2.refs_2_), channel_id=1, source_target_pairs={{0,1},{16,19},{1,0},{17,18},{2,3},{18,17},{3,2},{19,16},{4,5},{20,... | collective-permute-start | bytes 1572872 | tf_op jit(solution)/shard_map/ppermute | solution.py:35
  17.7 2.5 %collective-permute-done.3.refs_3_ = bf16[2,128,1024]{2,1,0:T(8,128)(2,1)S(1)} collective-permute-done((bf16[2,128,1024]{2,1,0:T(8,128)(2,1)S(1)}, bf16[2,128,1024]{2,1,0:T(8,128)(2,1)S(1)}, u32[]{:S(2)}, u32[]{:S(2)}) %collective-permute-start.3) | collective-permute-done | bytes 524320 | tf_op jit(solution)/shard_map/ppermute | solution.py:35
  20.2 2.5 %collective-permute-start.6 = (bf16[2,128,1024]{2,1,0:T(8,128)(2,1)S(1)}, bf16[2,128,1024]{2,1,0:T(8,128)(2,1)}, u32[]{:S(2)}, u32[]{:S(2)}) collective-permute-start(bf16[2,128,1024]{2,1,0:T(8,128)(2,1)S(1)} %collective-permute-done.3.refs_3_), channel_id=1, source_target_pairs={{0,1},{16,19},{1,0},{17,18},{2,3},{18,17},{3,2},{19,16},{4,5},{20,... | collective-permute-start | bytes 1572872 | tf_op jit(solution)/shard_map/ppermute | solution.py:35
  22.6 2.5 %collective-permute-start.7 = (bf16[2,128,1024]{2,1,0:T(8,128)(2,1)S(1)}, bf16[2,128,1024]{2,1,0:T(8,128)(2,1)}, u32[]{:S(2)}, u32[]{:S(2)}) collective-permute-start(bf16[2,128,1024]{2,1,0:T(8,128)(2,1)S(1)} %collective-permute-done.1.refs_1_), channel_id=1, source_target_pairs={{0,8},{16,80},{1,9},{17,81},{2,10},{18,82},{3,11},{19,83},{4,12},{... | collective-permute-start | bytes 1572872 | tf_op jit(solution)/shard_map/ppermute | solution.py:35
  25.1 1.5 %collective-permute-start.10 = (bf16[2,128,1024]{2,1,0:T(8,128)(2,1)S(1)}, bf16[2,128,1024]{2,1,0:T(8,128)(2,1)S(1)}, u32[]{:S(2)}, u32[]{:S(2)}) collective-permute-start(bf16[2,128,1024]{2,1,0:T(8,128)(2,1)S(1)} %collective-permute-done.2.refs_2_), channel_id=1, source_target_pairs={{0,16},{16,0},{32,48},{48,32},{64,80},{80,64},{96,112},{112,96},{1... | collective-permute-start | bytes 1572872 | tf_op jit(solution)/shard_map/ppermute | solution.py:43
  27.2 3.3 %collective-permute-done.6.refs_6_ = bf16[2,128,1024]{2,1,0:T(8,128)(2,1)} collective-permute-done((bf16[2,128,1024]{2,1,0:T(8,128)(2,1)S(1)}, bf16[2,128,1024]{2,1,0:T(8,128)(2,1)}, u32[]{:S(2)}, u32[]{:S(2)}) %collective-permute-start.6) | collective-permute-done | bytes 524320 | tf_op jit(solution)/shard_map/ppermute | solution.py:35
  30.5 1.6 %collective-permute-start.12 = (bf16[2,128,1024]{2,1,0:T(8,128)(2,1)S(1)}, bf16[2,128,1024]{2,1,0:T(8,128)(2,1)}, u32[]{:S(2)}, u32[]{:S(2)}) collective-permute-start(bf16[2,128,1024]{2,1,0:T(8,128)(2,1)S(1)} %collective-permute-done.4.refs_4_), channel_id=1, source_target_pairs={{0,16},{16,0},{32,48},{48,32},{64,80},{80,64},{96,112},{112,96},{1... | collective-permute-start | bytes 1572872 | tf_op jit(solution)/shard_map/ppermute | solution.py:43
  32.6 2.1 %collective-permute-start.13 = (bf16[2,128,1024]{2,1,0:T(8,128)(2,1)}, bf16[2,128,1024]{2,1,0:T(8,128)(2,1)}, u32[]{:S(2)}, u32[]{:S(2)}) collective-permute-start(bf16[2,128,1024]{2,1,0:T(8,128)(2,1)} %collective-permute-done.5.refs_5_), channel_id=1, source_target_pairs={{0,16},{16,0},{32,48},{48,32},{64,80},{80,64},{96,112},{112,96},{1... | collective-permute-start | bytes 1572872 | tf_op jit(solution)/shard_map/ppermute | solution.py:43
  37.8 0.9 collective-permute-done.15.refs_15_
  38.9 1.0 copy-done.2
  40.0 1.0 copy-done.4
  41.0 10.1 %scores.1 = (f32[2,1024,1024]{2,1,0:T(8,128)S(1)}, f32[3,2048]{1,0:T(4,128)S(1)}, f32[3,2048]{1,0:T(4,128)S(1)}) custom-call(bf16[2,128,1024]{2,1,0:T(8,128)(2,1)S(1)} %pad_maximum_fusion.refs_0_, bf16[2,128,1024]{2,1,0:T(8,128)(2,1)S(1)} %collective-permute-done.1.refs_1_, bf16[2,128,1024]{2,1,0:T(8,128)(2,1)S(1)} %collective-permute-done.2.refs_2_, ...), custom_call_target="tpu_custom_call" | custom-call | flops 4294967296 | bytes 16777216 | tf_op jit(solution)/shard_map/scores/pallas_call | solution.py:287
  52.5 1.9 %collective-permute-start.17 = (f32[3,2048]{1,0:T(4,128)S(1)}, f32[3,2048]{1,0:T(4,128)S(1)}, u32[]{:S(2)}, u32[]{:S(2)}) collective-permute-start(f32[3,2048]{1,0:T(4,128)S(1)} %merge.4.a), channel_id=1, source_target_pairs={{0,1},{16,19},{1,0},{17,18},{2,3},{18,17},{3,2},{19,16},{4,5},{20,... | collective-permute-start | bytes 73736 | tf_op jit(solution)/shard_map/ppermute | solution.py:35
  54.4 2.2 %flip.1.refs_0_.refs_20_.refs_17_ = bf16[1024,1024]{1,0:T(8,128)(2,1)S(1)} custom-call(bf16[2,128,1024]{2,1,0:T(8,128)(2,1)S(1)} %pad_maximum_fusion.refs_0_, bf16[2,128,1024]{2,1,0:T(8,128)(2,1)S(1)} %collective-permute-done.1.refs_1_, bf16[2,128,1024]{2,1,0:T(8,128)(2,1)S(1)} %collective-permute-done.2.refs_2_, ...), custom_call_target="tpu_custom_call" | custom-call | bytes 4194304 | tf_op jit(solution)/shard_map/flip/pallas_call | solution.py:307
  56.7 1.4 collective-permute-start.18
  58.1 1.5 %collective-permute-done.18.b = f32[3,2048]{1,0:T(4,128)S(1)} collective-permute-done((f32[3,2048]{1,0:T(4,128)S(1)}, f32[3,2048]{1,0:T(4,128)S(1)}, u32[]{:S(2)}, u32[]{:S(2)}) %collective-permute-start.18) | collective-permute-done | bytes 24608 | tf_op jit(solution)/shard_map/ppermute | solution.py:39
  59.5 4.2 %collective-permute-start.19 = (f32[3,2048]{1,0:T(4,128)S(1)}, f32[3,2048]{1,0:T(4,128)S(1)}, u32[]{:S(2)}, u32[]{:S(2)}) collective-permute-start(f32[3,2048]{1,0:T(4,128)S(1)} %merge.6.a), channel_id=1, source_target_pairs={{0,8},{16,80},{1,9},{17,81},{2,10},{18,82},{3,11},{19,83},{4,12},{... | collective-permute-start | bytes 73736 | tf_op jit(solution)/shard_map/ppermute | solution.py:35
  63.8 1.3 collective-permute-done.19.b
  65.2 2.9 %collective-permute-start.25 = (f32[1,2048]{1,0:T(1,128)S(1)}, f32[1,2048]{1,0:T(1,128)S(1)}, u32[]{:S(2)}, u32[]{:S(2)}) collective-permute-start(f32[1,2048]{1,0:T(1,128)S(1)} %get-tuple-element.29.refs_18_), channel_id=1, source_target_pairs={{0,16},{16,0},{32,48},{48,32},{64,80},{80,64},{96,112},{112,96},{1... | collective-permute-start | bytes 24584 | tf_op jit(solution)/shard_map/ppermute | solution.py:43
  68.2 1.1 collective-permute-done.20.refs_21_
  69.3 13.2 %grads_far.1 = (bf16[2,2,128,1024]{3,2,1,0:T(8,128)(2,1)S(1)}, bf16[1,2,128,1024]{3,2,1,0:T(8,128)(2,1)S(1)}, bf16[1,2,128,1024]{3,2,1,0:T(8,128)(2,1)S(1)}, bf1...) custom-call(bf16[2,128,1024]{2,1,0:T(8,128)(2,1)S(1)} %pad_maximum_f, ...), custom_call_target="tpu_custom_call" | custom-call | flops 4294967296 | bytes 20971520 | tf_op jit(solution)/shard_map/grads_far/pallas_call | solution.py:340
  83.1 2.1 %collective-permute-done.26.refs_1_ = bf16[2,2,128,1024]{3,2,1,0:T(8,128)(2,1)S(1)} collective-permute-done((bf16[2,2,128,1024]{3,2,1,0:T(8,128)(2,1)S(1)}, bf16[2,2,128,1024]{3,2,1,0:T(8,128)(2,1)S(1)}, u32[]{:S(2)}, u32[]{:S(2)}) %collective-permute-start.26) | collective-permute-done | bytes 1048608 | tf_op jit(solution)/shard_map/ppermute | solution.py:43
  85.5 2.6 %collective-permute-start.35 = (bf16[2,2,128,1024]{3,2,1,0:T(8,128)(2,1)S(1)}, bf16[2,2,128,1024]{3,2,1,0:T(8,128)(2,1)S(1)}, u32[]{:S(2)}, u32[]{:S(2)}) collective-permute-start(bf16[2,2,128,1024]{3,2,1,0:T(8,128)(2,1)S(1)} %join.7.refs_18_), channel_id=1, source_target_pairs={{0,1},{16,19},{1,0},{17,18},{2,3},{18,17},{3,2},{19,16},{4,5},{20,... | collective-permute-start | bytes 3145736 | tf_op jit(solution)/shard_map/ppermute | solution.py:35
  88.0 1.0 collective-permute-start.21
  89.0 11.4 %collective-permute-done.21 = f32[8,128]{1,0:T(8,128)S(1)} collective-permute-done((f32[8,128]{1,0:T(8,128)S(1)}, f32[8,128]{1,0:T(8,128)S(1)}, u32[]{:S(2)}, u32[]{:S(2)}) %collective-permute-start.21) | collective-permute-done | bytes 4128 | tf_op jit(solution)/shard_map/ppermute | solution.py:35
  100.5 1.3 collective-permute-start.22
  101.9 2.7 %collective-permute-start.32 = (bf16[1,2,128,1024]{3,2,1,0:T(8,128)(2,1)S(1)}, bf16[1,2,128,1024]{3,2,1,0:T(8,128)(2,1)S(1)}, u32[]{:S(2)}, u32[]{:S(2)}) collective-permute-start(bf16[1,2,128,1024]{3,2,1,0:T(8,128)(2,1)S(1)} %join.8.refs_19_), channel_id=1, source_target_pairs={{0,8},{16,80},{1,9},{17,81},{2,10},{18,82},{3,11},{19,83},{4,12},{... | collective-permute-start | bytes 1572872 | tf_op jit(solution)/shard_map/ppermute | solution.py:35
  104.6 7.5 %grads_near.1 = (bf16[1,2,128,1024]{3,2,1,0:T(8,128)(2,1)S(1)}, bf16[1,2,128,1024]{3,2,1,0:T(8,128)(2,1)S(1)}, bf16[1,2,128,1024]{3,2,1,0:T(8,128)(2,1)S(1)}, bf...) custom-call(bf16[2,128,1024]{2,1,0:T(8,128)(2,1)S(1)} %pad_maximum_f, ...), custom_call_target="tpu_custom_call" | custom-call | flops 4294967296 | bytes 20971520 | tf_op jit(solution)/shard_map/grads_near/pallas_call | solution.py:340
  113.0 3.4 %collective-permute-start.23 = (f32[8,128]{1,0:T(8,128)S(1)}, f32[8,128]{1,0:T(8,128)S(1)}, u32[]{:S(2)}, u32[]{:S(2)}) collective-permute-start(f32[8,128]{1,0:T(8,128)S(1)} %add.101.refs_2_), channel_id=1, source_target_pairs={{0,8},{16,80},{1,9},{17,81},{2,10},{18,82},{3,11},{19,83},{4,12},{... | collective-permute-start | bytes 12296 | tf_op jit(solution)/shard_map/ppermute | solution.py:35
  116.6 2.6 %collective-permute-start.33 = (bf16[1,2,128,1024]{3,2,1,0:T(8,128)(2,1)S(1)}, bf16[1,2,128,1024]{3,2,1,0:T(8,128)(2,1)S(1)}, u32[]{:S(2)}, u32[]{:S(2)}) collective-permute-start(bf16[1,2,128,1024]{3,2,1,0:T(8,128)(2,1)S(1)} %join.11), channel_id=1, source_target_pairs={{0,1},{16,19},{1,0},{17,18},{2,3},{18,17},{3,2},{19,16},{4,5},{20,... | collective-permute-start | bytes 1572872 | tf_op jit(solution)/shard_map/ppermute | solution.py:35
  120.4 1.2 collective-permute-start.38
  122.4 3.9 %collective-permute-done.33.refs_2_ = bf16[1,2,128,1024]{3,2,1,0:T(8,128)(2,1)S(1)} collective-permute-done((bf16[1,2,128,1024]{3,2,1,0:T(8,128)(2,1)S(1)}, bf16[1,2,128,1024]{3,2,1,0:T(8,128)(2,1)S(1)}, u32[]{:S(2)}, u32[]{:S(2)}) %collective-permute-start.33) | collective-permute-done | bytes 524320 | tf_op jit(solution)/shard_map/ppermute | solution.py:35
  126.2 3.1 %collective-permute-done.30.refs_1_ = bf16[1,2,128,1024]{3,2,1,0:T(8,128)(2,1)S(1)} collective-permute-done((bf16[1,2,128,1024]{3,2,1,0:T(8,128)(2,1)S(1)}, bf16[1,2,128,1024]{3,2,1,0:T(8,128)(2,1)S(1)}, u32[]{:S(2)}, u32[]{:S(2)}) %collective-permute-start.30) | collective-permute-done | bytes 524320 | tf_op jit(solution)/shard_map/ppermute | solution.py:35
  129.3 3.4 %collective-permute-done.38.refs_4_ = bf16[1,2,128,1024]{3,2,1,0:T(8,128)(2,1)S(1)} collective-permute-done((bf16[1,2,128,1024]{3,2,1,0:T(8,128)(2,1)S(1)}, bf16[1,2,128,1024]{3,2,1,0:T(8,128)(2,1)S(1)}, u32[]{:S(2)}, u32[]{:S(2)}) %collective-permute-start.38) | collective-permute-done | bytes 524320 | tf_op jit(solution)/shard_map/ppermute | solution.py:35
  132.8 2.1 %collective-permute-done.36.refs_3_ = bf16[1,2,128,1024]{3,2,1,0:T(8,128)(2,1)S(1)} collective-permute-done((bf16[1,2,128,1024]{3,2,1,0:T(8,128)(2,1)S(1)}, bf16[1,2,128,1024]{3,2,1,0:T(8,128)(2,1)S(1)}, u32[]{:S(2)}, u32[]{:S(2)}) %collective-permute-start.36) | collective-permute-done | bytes 524320 | tf_op jit(solution)/shard_map/ppermute | solution.py:35
  135.2 1.3 collective-permute-start.39
  136.7 1.4 %collective-permute-done.24 = f32[8,128]{1,0:T(8,128)S(1)} collective-permute-done((f32[8,128]{1,0:T(8,128)S(1)}, f32[8,128]{1,0:T(8,128)S(1)}, u32[]{:S(2)}, u32[]{:S(2)}) %collective-permute-start.24) | collective-permute-done | bytes 4128 | tf_op jit(solution)/shard_map/ppermute | solution.py:43
  140.2 1.0 copy.12
  (72 shorter events, 11.7 us)
Async XLA Ops:
  2.7 2.7 %collective-permute-start = (bf16[128,1024]{1,0:T(8,128)(2,1)S(1)}, bf16[128,1024]{1,0:T(8,128)(2,1)S(1)}, u32[]{:S(2)}, u32[]{:S(2)}) collective-permute-start(bf16[128,1024]{1,0:T(8,128)(2,1)S(1)} %get-tuple-element.59), channel_id=1, source_target_pairs={{0,16},{16,0},{32,48},{48,32},{64,80},{80,64},{96,112},{112,96},{1... | collective-permute-start | bytes 786440 | tf_op jit(solution)/shard_map/ppermute | solution.py:43
  5.4 9.8 %collective-permute-start.2 = (bf16[2,128,1024]{2,1,0:T(8,128)(2,1)S(1)}, bf16[2,128,1024]{2,1,0:T(8,128)(2,1)S(1)}, u32[]{:S(2)}, u32[]{:S(2)}) collective-permute-start(bf16[2,128,1024]{2,1,0:T(8,128)(2,1)S(1)} %pad_maximum_fusion.refs_0_), channel_id=1, source_target_pairs={{0,4},{16,48},{1,5},{17,49},{2,6},{18,50},{3,7},{19,51},{4,8},{20,... | collective-permute-start | bytes 1572872 | tf_op jit(solution)/shard_map/ppermute | solution.py:35
  6.9 13.3 %collective-permute-start.3 = (bf16[2,128,1024]{2,1,0:T(8,128)(2,1)S(1)}, bf16[2,128,1024]{2,1,0:T(8,128)(2,1)S(1)}, u32[]{:S(2)}, u32[]{:S(2)}) collective-permute-start(bf16[2,128,1024]{2,1,0:T(8,128)(2,1)S(1)} %pad_maximum_fusion.refs_0_), channel_id=1, source_target_pairs={{0,12},{16,112},{1,13},{17,113},{2,14},{18,114},{3,15},{19,115},{4... | collective-permute-start | bytes 1572872 | tf_op jit(solution)/shard_map/ppermute | solution.py:35
  8.4 14.2 %collective-permute-start.1 = (bf16[2,128,1024]{2,1,0:T(8,128)(2,1)S(1)}, bf16[2,128,1024]{2,1,0:T(8,128)(2,1)S(1)}, u32[]{:S(2)}, u32[]{:S(2)}) collective-permute-start(bf16[2,128,1024]{2,1,0:T(8,128)(2,1)S(1)} %pad_maximum_fusion.refs_0_), channel_id=1, source_target_pairs={{0,1},{16,19},{1,0},{17,18},{2,3},{18,17},{3,2},{19,16},{4,5},{20,... | collective-permute-start | bytes 1572872 | tf_op jit(solution)/shard_map/ppermute | solution.py:35
  10.9 14.3 %collective-permute-start.4 = (bf16[2,128,1024]{2,1,0:T(8,128)(2,1)S(1)}, bf16[2,128,1024]{2,1,0:T(8,128)(2,1)S(1)}, u32[]{:S(2)}, u32[]{:S(2)}) collective-permute-start(bf16[2,128,1024]{2,1,0:T(8,128)(2,1)S(1)} %pad_maximum_fusion.refs_0_), channel_id=1, source_target_pairs={{0,8},{16,80},{1,9},{17,81},{2,10},{18,82},{3,11},{19,83},{4,12},{... | collective-permute-start | bytes 1572872 | tf_op jit(solution)/shard_map/ppermute | solution.py:35
  12.5 14.2 %collective-permute-start.8 = (bf16[2,128,1024]{2,1,0:T(8,128)(2,1)S(1)}, bf16[2,128,1024]{2,1,0:T(8,128)(2,1)S(1)}, u32[]{:S(2)}, u32[]{:S(2)}) collective-permute-start(bf16[2,128,1024]{2,1,0:T(8,128)(2,1)S(1)} %pad_maximum_fusion.refs_0_), channel_id=1, source_target_pairs={{0,16},{16,0},{32,48},{48,32},{64,80},{80,64},{96,112},{112,96},{1... | collective-permute-start | bytes 1572872 | tf_op jit(solution)/shard_map/ppermute | solution.py:43
  15.2 11.6 %collective-permute-start.5 = (bf16[2,128,1024]{2,1,0:T(8,128)(2,1)S(1)}, bf16[2,128,1024]{2,1,0:T(8,128)(2,1)}, u32[]{:S(2)}, u32[]{:S(2)}) collective-permute-start(bf16[2,128,1024]{2,1,0:T(8,128)(2,1)S(1)} %collective-permute-done.2.refs_2_), channel_id=1, source_target_pairs={{0,1},{16,19},{1,0},{17,18},{2,3},{18,17},{3,2},{19,16},{4,5},{20,... | collective-permute-start | bytes 1572872 | tf_op jit(solution)/shard_map/ppermute | solution.py:35
  20.2 10.3 %collective-permute-start.6 = (bf16[2,128,1024]{2,1,0:T(8,128)(2,1)S(1)}, bf16[2,128,1024]{2,1,0:T(8,128)(2,1)}, u32[]{:S(2)}, u32[]{:S(2)}) collective-permute-start(bf16[2,128,1024]{2,1,0:T(8,128)(2,1)S(1)} %collective-permute-done.3.refs_3_), channel_id=1, source_target_pairs={{0,1},{16,19},{1,0},{17,18},{2,3},{18,17},{3,2},{19,16},{4,5},{20,... | collective-permute-start | bytes 1572872 | tf_op jit(solution)/shard_map/ppermute | solution.py:35
  22.6 9.9 %collective-permute-start.7 = (bf16[2,128,1024]{2,1,0:T(8,128)(2,1)S(1)}, bf16[2,128,1024]{2,1,0:T(8,128)(2,1)}, u32[]{:S(2)}, u32[]{:S(2)}) collective-permute-start(bf16[2,128,1024]{2,1,0:T(8,128)(2,1)S(1)} %collective-permute-done.1.refs_1_), channel_id=1, source_target_pairs={{0,8},{16,80},{1,9},{17,81},{2,10},{18,82},{3,11},{19,83},{4,12},{... | collective-permute-start | bytes 1572872 | tf_op jit(solution)/shard_map/ppermute | solution.py:35
  25.1 9.6 %collective-permute-start.10 = (bf16[2,128,1024]{2,1,0:T(8,128)(2,1)S(1)}, bf16[2,128,1024]{2,1,0:T(8,128)(2,1)S(1)}, u32[]{:S(2)}, u32[]{:S(2)}) collective-permute-start(bf16[2,128,1024]{2,1,0:T(8,128)(2,1)S(1)} %collective-permute-done.2.refs_2_), channel_id=1, source_target_pairs={{0,16},{16,0},{32,48},{48,32},{64,80},{80,64},{96,112},{112,96},{1... | collective-permute-start | bytes 1572872 | tf_op jit(solution)/shard_map/ppermute | solution.py:43
  26.7 8.8 %collective-permute-start.11 = (bf16[2,128,1024]{2,1,0:T(8,128)(2,1)S(1)}, bf16[2,128,1024]{2,1,0:T(8,128)(2,1)S(1)}, u32[]{:S(2)}, u32[]{:S(2)}) collective-permute-start(bf16[2,128,1024]{2,1,0:T(8,128)(2,1)S(1)} %collective-permute-done.3.refs_3_), channel_id=1, source_target_pairs={{0,16},{16,0},{32,48},{48,32},{64,80},{80,64},{96,112},{112,96},{1... | collective-permute-start | bytes 1572872 | tf_op jit(solution)/shard_map/ppermute | solution.py:43
  26.8 10.8 %collective-permute-start.9 = (bf16[2,128,1024]{2,1,0:T(8,128)(2,1)S(1)}, bf16[2,128,1024]{2,1,0:T(8,128)(2,1)}, u32[]{:S(2)}, u32[]{:S(2)}) collective-permute-start(bf16[2,128,1024]{2,1,0:T(8,128)(2,1)S(1)} %collective-permute-done.1.refs_1_), channel_id=1, source_target_pairs={{0,16},{16,0},{32,48},{48,32},{64,80},{80,64},{96,112},{112,96},{1... | collective-permute-start | bytes 1572872 | tf_op jit(solution)/shard_map/ppermute | solution.py:43
  30.5 7.1 %collective-permute-start.12 = (bf16[2,128,1024]{2,1,0:T(8,128)(2,1)S(1)}, bf16[2,128,1024]{2,1,0:T(8,128)(2,1)}, u32[]{:S(2)}, u32[]{:S(2)}) collective-permute-start(bf16[2,128,1024]{2,1,0:T(8,128)(2,1)S(1)} %collective-permute-done.4.refs_4_), channel_id=1, source_target_pairs={{0,16},{16,0},{32,48},{48,32},{64,80},{80,64},{96,112},{112,96},{1... | collective-permute-start | bytes 1572872 | tf_op jit(solution)/shard_map/ppermute | solution.py:43
  32.6 5.0 %collective-permute-start.13 = (bf16[2,128,1024]{2,1,0:T(8,128)(2,1)}, bf16[2,128,1024]{2,1,0:T(8,128)(2,1)}, u32[]{:S(2)}, u32[]{:S(2)}) collective-permute-start(bf16[2,128,1024]{2,1,0:T(8,128)(2,1)} %collective-permute-done.5.refs_5_), channel_id=1, source_target_pairs={{0,16},{16,0},{32,48},{48,32},{64,80},{80,64},{96,112},{112,96},{1... | collective-permute-start | bytes 1572872 | tf_op jit(solution)/shard_map/ppermute | solution.py:43
  34.7 0.8 copy-start.1
  35.5 2.3 %collective-permute-start.14 = (bf16[2,128,1024]{2,1,0:T(8,128)(2,1)}, bf16[2,128,1024]{2,1,0:T(8,128)(2,1)}, u32[]{:S(2)}, u32[]{:S(2)}) collective-permute-start(bf16[2,128,1024]{2,1,0:T(8,128)(2,1)} %collective-permute-done.6.refs_6_), channel_id=1, source_target_pairs={{0,16},{16,0},{32,48},{48,32},{64,80},{80,64},{96,112},{112,96},{1... | collective-permute-start | bytes 1572872 | tf_op jit(solution)/shard_map/ppermute | solution.py:43
  35.5 0.8 copy-start.3
  36.3 2.4 %collective-permute-start.15 = (bf16[2,128,1024]{2,1,0:T(8,128)(2,1)}, bf16[2,128,1024]{2,1,0:T(8,128)(2,1)}, u32[]{:S(2)}, u32[]{:S(2)}) collective-permute-start(bf16[2,128,1024]{2,1,0:T(8,128)(2,1)} %collective-permute-done.7.refs_7_), channel_id=1, source_target_pairs={{0,16},{16,0},{32,48},{48,32},{64,80},{80,64},{96,112},{112,96},{1... | collective-permute-start | bytes 1572872 | tf_op jit(solution)/shard_map/ppermute | solution.py:43
  38.9 1.0 copy-start.2
  40.0 1.0 copy-start.4
  51.1 5.5 %copy-start = (f32[2,1024,1024]{2,1,0:T(8,128)}, f32[2,1024,1024]{2,1,0:T(8,128)S(1)}, u32[]{:S(2)}) copy-start(f32[2,1024,1024]{2,1,0:T(8,128)S(1)} %get-tuple-element.28.refs_16_) | copy-start | bytes 25165828
  51.1 1.4 collective-permute-start.16
  52.5 4.1 %collective-permute-start.17 = (f32[3,2048]{1,0:T(4,128)S(1)}, f32[3,2048]{1,0:T(4,128)S(1)}, u32[]{:S(2)}, u32[]{:S(2)}) collective-permute-start(f32[3,2048]{1,0:T(4,128)S(1)} %merge.4.a), channel_id=1, source_target_pairs={{0,1},{16,19},{1,0},{17,18},{2,3},{18,17},{3,2},{19,16},{4,5},{20,... | collective-permute-start | bytes 73736 | tf_op jit(solution)/shard_map/ppermute | solution.py:35
  56.7 2.8 %collective-permute-start.18 = (f32[3,2048]{1,0:T(4,128)S(1)}, f32[3,2048]{1,0:T(4,128)S(1)}, u32[]{:S(2)}, u32[]{:S(2)}) collective-permute-start(f32[3,2048]{1,0:T(4,128)S(1)} %merge.5.a), channel_id=1, source_target_pairs={{0,4},{16,48},{1,5},{17,49},{2,6},{18,50},{3,7},{19,51},{4,0},{20,... | collective-permute-start | bytes 73736 | tf_op jit(solution)/shard_map/ppermute | solution.py:39
  59.5 5.5 %collective-permute-start.19 = (f32[3,2048]{1,0:T(4,128)S(1)}, f32[3,2048]{1,0:T(4,128)S(1)}, u32[]{:S(2)}, u32[]{:S(2)}) collective-permute-start(f32[3,2048]{1,0:T(4,128)S(1)} %merge.6.a), channel_id=1, source_target_pairs={{0,8},{16,80},{1,9},{17,81},{2,10},{18,82},{3,11},{19,83},{4,12},{... | collective-permute-start | bytes 73736 | tf_op jit(solution)/shard_map/ppermute | solution.py:35
  65.2 4.1 %collective-permute-start.25 = (f32[1,2048]{1,0:T(1,128)S(1)}, f32[1,2048]{1,0:T(1,128)S(1)}, u32[]{:S(2)}, u32[]{:S(2)}) collective-permute-start(f32[1,2048]{1,0:T(1,128)S(1)} %get-tuple-element.29.refs_18_), channel_id=1, source_target_pairs={{0,16},{16,0},{32,48},{48,32},{64,80},{80,64},{96,112},{112,96},{1... | collective-permute-start | bytes 24584 | tf_op jit(solution)/shard_map/ppermute | solution.py:43
  68.1 1.2 collective-permute-start.20
  82.5 2.7 %collective-permute-start.26 = (bf16[2,2,128,1024]{3,2,1,0:T(8,128)(2,1)S(1)}, bf16[2,2,128,1024]{3,2,1,0:T(8,128)(2,1)S(1)}, u32[]{:S(2)}, u32[]{:S(2)}) collective-permute-start(bf16[2,2,128,1024]{3,2,1,0:T(8,128)(2,1)S(1)} %get-tuple-element.32), channel_id=1, source_target_pairs={{0,16},{16,0},{32,48},{48,32},{64,80},{80,64},{96,112},{112,96},{1... | collective-permute-start | bytes 3145736 | tf_op jit(solution)/shard_map/ppermute | solution.py:43
  82.6 19.1 %collective-permute-start.27 = (bf16[1,2,128,1024]{3,2,1,0:T(8,128)(2,1)S(1)}, bf16[1,2,128,1024]{3,2,1,0:T(8,128)(2,1)S(1)}, u32[]{:S(2)}, u32[]{:S(2)}) collective-permute-start(bf16[1,2,128,1024]{3,2,1,0:T(8,128)(2,1)S(1)} %get-tuple-element.34), channel_id=1, source_target_pairs={{0,16},{16,0},{32,48},{48,32},{64,80},{80,64},{96,112},{112,96},{1... | collective-permute-start | bytes 1572872 | tf_op jit(solution)/shard_map/ppermute | solution.py:43
  85.5 33.9 %collective-permute-start.35 = (bf16[2,2,128,1024]{3,2,1,0:T(8,128)(2,1)S(1)}, bf16[2,2,128,1024]{3,2,1,0:T(8,128)(2,1)S(1)}, u32[]{:S(2)}, u32[]{:S(2)}) collective-permute-start(bf16[2,2,128,1024]{3,2,1,0:T(8,128)(2,1)S(1)} %join.7.refs_18_), channel_id=1, source_target_pairs={{0,1},{16,19},{1,0},{17,18},{2,3},{18,17},{3,2},{19,16},{4,5},{20,... | collective-permute-start | bytes 3145736 | tf_op jit(solution)/shard_map/ppermute | solution.py:35
  88.0 24.7 %collective-permute-start.31 = (bf16[1,2,128,1024]{3,2,1,0:T(8,128)(2,1)S(1)}, bf16[1,2,128,1024]{3,2,1,0:T(8,128)(2,1)S(1)}, u32[]{:S(2)}, u32[]{:S(2)}) collective-permute-start(bf16[1,2,128,1024]{3,2,1,0:T(8,128)(2,1)S(1)} %get-tuple-element.40), channel_id=1, source_target_pairs={{0,16},{16,0},{32,48},{48,32},{64,80},{80,64},{96,112},{112,96},{1... | collective-permute-start | bytes 1572872 | tf_op jit(solution)/shard_map/ppermute | solution.py:43
  88.0 12.4 %collective-permute-start.21 = (f32[8,128]{1,0:T(8,128)S(1)}, f32[8,128]{1,0:T(8,128)S(1)}, u32[]{:S(2)}, u32[]{:S(2)}) collective-permute-start(f32[8,128]{1,0:T(8,128)S(1)} %collective-permute-done.20.refs_21_), channel_id=1, source_target_pairs={{0,1},{16,19},{1,0},{17,18},{2,3},{18,17},{3,2},{19,16},{4,5},{20,... | collective-permute-start | bytes 12296 | tf_op jit(solution)/shard_map/ppermute | solution.py:35
  100.5 11.8 %collective-permute-start.22 = (f32[8,128]{1,0:T(8,128)S(1)}, f32[8,128]{1,0:T(8,128)S(1)}, u32[]{:S(2)}, u32[]{:S(2)}) collective-permute-start(f32[8,128]{1,0:T(8,128)S(1)} %add.100.refs_20_), channel_id=1, source_target_pairs={{0,4},{16,48},{1,5},{17,49},{2,6},{18,50},{3,7},{19,51},{4,0},{20,... | collective-permute-start | bytes 12296 | tf_op jit(solution)/shard_map/ppermute | solution.py:39
  101.9 11.2 %collective-permute-start.32 = (bf16[1,2,128,1024]{3,2,1,0:T(8,128)(2,1)S(1)}, bf16[1,2,128,1024]{3,2,1,0:T(8,128)(2,1)S(1)}, u32[]{:S(2)}, u32[]{:S(2)}) collective-permute-start(bf16[1,2,128,1024]{3,2,1,0:T(8,128)(2,1)S(1)} %join.8.refs_19_), channel_id=1, source_target_pairs={{0,8},{16,80},{1,9},{17,81},{2,10},{18,82},{3,11},{19,83},{4,12},{... | collective-permute-start | bytes 1572872 | tf_op jit(solution)/shard_map/ppermute | solution.py:35
  112.1 4.5 %collective-permute-start.29 = (bf16[1,2,128,1024]{3,2,1,0:T(8,128)(2,1)S(1)}, bf16[1,2,128,1024]{3,2,1,0:T(8,128)(2,1)S(1)}, u32[]{:S(2)}, u32[]{:S(2)}) collective-permute-start(bf16[1,2,128,1024]{3,2,1,0:T(8,128)(2,1)S(1)} %get-tuple-element.38), channel_id=1, source_target_pairs={{0,16},{16,0},{32,48},{48,32},{64,80},{80,64},{96,112},{112,96},{1... | collective-permute-start | bytes 1572872 | tf_op jit(solution)/shard_map/ppermute | solution.py:43
  112.2 7.1 %collective-permute-start.37 = (bf16[1,2,128,1024]{3,2,1,0:T(8,128)(2,1)S(1)}, bf16[1,2,128,1024]{3,2,1,0:T(8,128)(2,1)S(1)}, u32[]{:S(2)}, u32[]{:S(2)}) collective-permute-start(bf16[1,2,128,1024]{3,2,1,0:T(8,128)(2,1)S(1)} %get-tuple-element.44), channel_id=1, source_target_pairs={{0,16},{16,0},{32,48},{48,32},{64,80},{80,64},{96,112},{112,96},{1... | collective-permute-start | bytes 1572872 | tf_op jit(solution)/shard_map/ppermute | solution.py:43
  112.7 7.7 %collective-permute-start.34 = (bf16[1,2,128,1024]{3,2,1,0:T(8,128)(2,1)S(1)}, bf16[1,2,128,1024]{3,2,1,0:T(8,128)(2,1)S(1)}, u32[]{:S(2)}, u32[]{:S(2)}) collective-permute-start(bf16[1,2,128,1024]{3,2,1,0:T(8,128)(2,1)S(1)} %get-tuple-element.42), channel_id=1, source_target_pairs={{0,16},{16,0},{32,48},{48,32},{64,80},{80,64},{96,112},{112,96},{1... | collective-permute-start | bytes 1572872 | tf_op jit(solution)/shard_map/ppermute | solution.py:43
  113.0 8.8 %collective-permute-start.23 = (f32[8,128]{1,0:T(8,128)S(1)}, f32[8,128]{1,0:T(8,128)S(1)}, u32[]{:S(2)}, u32[]{:S(2)}) collective-permute-start(f32[8,128]{1,0:T(8,128)S(1)} %add.101.refs_2_), channel_id=1, source_target_pairs={{0,8},{16,80},{1,9},{17,81},{2,10},{18,82},{3,11},{19,83},{4,12},{... | collective-permute-start | bytes 12296 | tf_op jit(solution)/shard_map/ppermute | solution.py:35
  116.6 9.6 %collective-permute-start.33 = (bf16[1,2,128,1024]{3,2,1,0:T(8,128)(2,1)S(1)}, bf16[1,2,128,1024]{3,2,1,0:T(8,128)(2,1)S(1)}, u32[]{:S(2)}, u32[]{:S(2)}) collective-permute-start(bf16[1,2,128,1024]{3,2,1,0:T(8,128)(2,1)S(1)} %join.11), channel_id=1, source_target_pairs={{0,1},{16,19},{1,0},{17,18},{2,3},{18,17},{3,2},{19,16},{4,5},{20,... | collective-permute-start | bytes 1572872 | tf_op jit(solution)/shard_map/ppermute | solution.py:35
  119.3 2.9 %collective-permute-start.28 = (bf16[1,2,128,1024]{3,2,1,0:T(8,128)(2,1)S(1)}, bf16[1,2,128,1024]{3,2,1,0:T(8,128)(2,1)S(1)}, u32[]{:S(2)}, u32[]{:S(2)}) collective-permute-start(bf16[1,2,128,1024]{3,2,1,0:T(8,128)(2,1)S(1)} %get-tuple-element.36), channel_id=1, source_target_pairs={{0,16},{16,0},{32,48},{48,32},{64,80},{80,64},{96,112},{112,96},{1... | collective-permute-start | bytes 1572872 | tf_op jit(solution)/shard_map/ppermute | solution.py:43
  119.4 10.0 %collective-permute-start.30 = (bf16[1,2,128,1024]{3,2,1,0:T(8,128)(2,1)S(1)}, bf16[1,2,128,1024]{3,2,1,0:T(8,128)(2,1)S(1)}, u32[]{:S(2)}, u32[]{:S(2)}) collective-permute-start(bf16[1,2,128,1024]{3,2,1,0:T(8,128)(2,1)S(1)} %join.10), channel_id=1, source_target_pairs={{0,8},{16,80},{1,9},{17,81},{2,10},{18,82},{3,11},{19,83},{4,12},{... | collective-permute-start | bytes 1572872 | tf_op jit(solution)/shard_map/ppermute | solution.py:35
  120.4 12.4 %collective-permute-start.38 = (bf16[1,2,128,1024]{3,2,1,0:T(8,128)(2,1)S(1)}, bf16[1,2,128,1024]{3,2,1,0:T(8,128)(2,1)S(1)}, u32[]{:S(2)}, u32[]{:S(2)}) collective-permute-start(bf16[1,2,128,1024]{3,2,1,0:T(8,128)(2,1)S(1)} %join.13), channel_id=1, source_target_pairs={{0,12},{16,112},{1,13},{17,113},{2,14},{18,114},{3,15},{19,115},{4... | collective-permute-start | bytes 1572872 | tf_op jit(solution)/shard_map/ppermute | solution.py:35
  121.8 13.1 %collective-permute-start.36 = (bf16[1,2,128,1024]{3,2,1,0:T(8,128)(2,1)S(1)}, bf16[1,2,128,1024]{3,2,1,0:T(8,128)(2,1)S(1)}, u32[]{:S(2)}, u32[]{:S(2)}) collective-permute-start(bf16[1,2,128,1024]{3,2,1,0:T(8,128)(2,1)S(1)} %join.12), channel_id=1, source_target_pairs={{0,4},{16,48},{1,5},{17,49},{2,6},{18,50},{3,7},{19,51},{4,8},{20,... | collective-permute-start | bytes 1572872 | tf_op jit(solution)/shard_map/ppermute | solution.py:35
  135.2 4.1 %collective-permute-start.39 = (f32[128,1024]{1,0:T(8,128)S(1)}, f32[128,1024]{1,0:T(8,128)S(1)}, u32[]{:S(2)}, u32[]{:S(2)}) collective-permute-start(f32[128,1024]{1,0:T(8,128)S(1)} %get-tuple-element.46), channel_id=1, source_target_pairs={{0,16},{16,0},{32,48},{48,32},{64,80},{80,64},{96,112},{112,96},{1... | collective-permute-start | bytes 1572872 | tf_op jit(solution)/shard_map/ppermute | solution.py:43
  136.6 1.5 %collective-permute-start.24 = (f32[8,128]{1,0:T(8,128)S(1)}, f32[8,128]{1,0:T(8,128)S(1)}, u32[]{:S(2)}, u32[]{:S(2)}) collective-permute-start(f32[8,128]{1,0:T(8,128)S(1)} %add.102.refs_5_), channel_id=1, source_target_pairs={{0,16},{16,0},{32,48},{48,32},{64,80},{80,64},{96,112},{112,96},{1... | collective-permute-start | bytes 12296 | tf_op jit(solution)/shard_map/ppermute | solution.py:43

commit v3 on v2

v3 whole, which is shorter than its diff:
```python
import functools

import jax
import jax.numpy as jnp
from jax import lax
from jax.experimental import pallas as pl
from jax.experimental.pallas import tpu as pltpu
from jax.sharding import PartitionSpec as P

logit_scale = 40.0
log2_e = 1.4426950408889634
score_scale = logit_scale * log2_e
low = -1e30
AX = ("row", "col")
f32, bf16 = jnp.float32, jnp.bfloat16
MIB = 1024 * 1024


def lin(y, c, z, x):
    return ((y * 2 + c) * 4 + z) * 4 + x


def moves(step, turn):
    pairs = []
    for y in range(4):
        for z in range(4):
            for x in range(4):
                far_z, side = step(z, x, x ^ 1)
                pairs.append((lin(y, turn, z, x), lin(y, turn, far_z, side)))
                far_y, side = step(y, x, 3 - x)
                pairs.append((lin(y, 1 - turn, z, x), lin(far_y, 1 - turn, z, side)))
    return pairs


def hop(a, d, flip, turn=0):
    return lax.ppermute(a, AX, moves(lambda r, x, other: ((r + d) % 4, other if flip else x), turn))


def hop_xor(a, turn=0):
    return lax.ppermute(a, AX, moves(lambda r, x, other: (r ^ 1, x), turn))


def swap(a):
    return lax.ppermute(a, "row", [(i, i ^ 1) for i in range(8)])


def place():
    row, col = lax.axis_index("row"), lax.axis_index("col")
    return row // 2, row % 2, col // 4, col % 4


OFFSETS = [(0, 0), (2, 0), (3, 0), (1, 0), (0, 1), (3, 1), (1, 1), (2, 1)]


def load_copies(core, y, z, x, mine, theirs, q_dst, p_dst, sems):
    out = []
    for k, (d, flip) in enumerate(OFFSETS):
        slot = ((x % 2) ^ flip) * 4 + (z - d + 4) % 4
        far_y = (y - d + 4) % 4
        rank = (x // 2) ^ flip
        for which in range(2):
            copies = []
            q_src, p_src = (mine[k], theirs[k]) if which == 0 else (theirs[k], mine[k])
            if q_dst is not None:
                rows = pl.ds(pl.multiple_of(slot * 128, 128), 128)
                copies.append(pltpu.make_async_copy(q_src.at[which], q_dst.at[rows], sems.at[k, 0]))
            if p_dst is not None:
                for part in range(2):
                    rows = pl.ds(pl.multiple_of(far_y * 256 + (1 - part) * 128, 128), 128)
                    copies.append(
                        pltpu.make_async_copy(p_src.at[part], p_dst.at[rank, rows], sems.at[k, 1 + part])
                    )
            out.append((which, copies))
    return out


def run_copies(core, groups, start):
    for which in range(2):

        @pl.when(core == which)
        def _():
            for w, copies in groups:
                if w == which:
                    for copy in copies:
                        copy.start() if start else copy.wait()


TILE = 32


def lane_groups():
    return [(g // 8, slice(g % 8 * 128, g % 8 * 128 + 128)) for g in range(16)]


def fold(a):
    return sum(a[r : r + 8] for r in range(0, a.shape[0], 8))


def score_kernel(*refs):
    mine, theirs, (aims, sv, keep, send, qv, pt, target, row_top, row_sum, col_top, sems) = (
        refs[:8],
        refs[8:16],
        refs[16:],
    )
    y, core, z, x = place()
    groups = load_copies(core, y, z, x, mine, theirs, qv, pt, sems)
    run_copies(core, groups, True)
    for s in range(8):
        rows = slice(s * 128, s * 128 + 128)
        target[rows, :] = jnp.broadcast_to(aims[:, rows], (128, 128)).T
    run_copies(core, groups, False)
    for h in range(2):
        for n in range(2):
            cols = slice(n * 512, n * 512 + 512)
            s = score_scale * jnp.dot(qv[...], pt[h, :, cols], preferred_element_type=f32)
            sv[h, :, cols] = s
            col_top[h, :, cols] = jnp.broadcast_to(jnp.max(s, axis=0, keepdims=True), (8, 512))
            top = jnp.maximum(
                jnp.maximum(s[:, :128], s[:, 128:256]), jnp.maximum(s[:, 256:384], s[:, 384:])
            )
            row_top[...] = top if h == n == 0 else jnp.maximum(row_top[...], top)
    tops = []
    for s in range(8):
        rows = slice(s * 128, s * 128 + 128)
        top = jnp.max(row_top[rows, :].T, axis=0, keepdims=True)
        tops.append(top)
        row_top[rows, :] = jnp.broadcast_to(top, (128, 128)).T
    lanes = lax.broadcasted_iota(jnp.int32, (TILE, 128), 1).astype(f32)

    def step(i, carry):
        col_acc, hits = carry
        rows = pl.ds(pl.multiple_of(i * TILE, TILE), TILE)
        top, aim = row_top[rows, :], target[rows, :]
        total, cols = jnp.zeros((TILE, 128), f32), []
        for g, (h, at) in enumerate(lane_groups()):
            t = sv[h, rows, at]
            total = total + jnp.exp2(t - top)
            cols.append(col_acc[g] + fold(jnp.exp2(t - col_top[h, 0:1, at])))
            hits = hits + fold(jnp.where(lanes == aim - g * 128, t, 0.0))
        row_sum[rows, :] = total
        return tuple(cols), hits

    zero = jnp.zeros((8, 128), f32)
    col_acc, hits = lax.fori_loop(0, 1024 // TILE, step, ((zero,) * 16, zero))
    hits = jnp.sum(hits, axis=0, keepdims=True)

    def fill(rows_ref, cols_ref, first):
        off = 0 if first else 1024
        for s in range(8):
            at = slice(off + s * 128, off + s * 128 + 128)
            rows_ref[0:1, at] = tops[s]
            rows_ref[1:2, at] = jnp.sum(row_sum[s * 128 : s * 128 + 128, :].T, axis=0, keepdims=True)
        gap = slice(1024 - off, 2048 - off)
        rows_ref[0:1, gap] = jnp.full((1, 1024), low, f32)
        rows_ref[1:2, gap] = jnp.zeros((1, 1024), f32)
        rows_ref[2:3, :] = jnp.zeros((1, 2048), f32)
        rows_ref[2:3, :128] = hits
        for h in range(2):
            cols_ref[0:1, h * 1024 : h * 1024 + 1024] = col_top[h, 0:1, :]
        for g in range(16):
            cols_ref[1:2, g * 128 : g * 128 + 128] = jnp.sum(col_acc[g], axis=0, keepdims=True)
        cols_ref[2:3, :] = jnp.zeros((1, 2048), f32)

    @pl.when(core == 0)
    def _():
        fill(keep, send, True)

    @pl.when(core == 1)
    def _():
        fill(send, keep, False)


def slope_kernel(sv, target, own_lse, got_lse, part, slope, part_out, row_lse):
    part_out[...] = part[...]
    first = place()[1] == 0
    mine_lse, their_lse = own_lse[...], got_lse[...]
    rows_lse = jnp.where(first, mine_lse[:, :1024], their_lse[:, 1024:])
    cols_lse = jnp.where(first, their_lse, mine_lse)
    for s in range(8):
        row_lse[s * 128 : s * 128 + 128, :] = jnp.broadcast_to(
            rows_lse[:, s * 128 : s * 128 + 128], (128, 128)
        ).T
    lanes = lax.broadcasted_iota(jnp.int32, (TILE, 128), 1).astype(f32)

    def step(i, carry):
        rows = pl.ds(pl.multiple_of(i * TILE, TILE), TILE)
        aim, lse = target[rows, :], row_lse[rows, :]
        for g, (h, at) in enumerate(lane_groups()):
            t = sv[h, rows, at]
            e = 0.5 * (jnp.exp2(t - lse) + jnp.exp2(t - cols_lse[:, g * 128 : g * 128 + 128]))
            slope[h, rows, at] = jnp.where(lanes == aim - g * 128, e - 1.0, e).astype(bf16)
        return carry

    lax.fori_loop(0, 1024 // TILE, step, 0)


def grad_kernel(flip, order, n_ties, *refs):
    n = len(order)
    steps = [(g, i, d) for g, group in enumerate(order) for i, d in enumerate(group)]
    (slope, qt, pt, part), refs = refs[:4], refs[4 + n_ties :]
    keeps, sends, (part_out, gq, gp, zeros, out_sems) = refs[:n], refs[n : 2 * n], refs[2 * n :]
    part_out[...] = part[...]
    y, core, z, x = place()
    zeros[...] = jnp.zeros(zeros.shape, bf16)
    half = (x % 2) ^ flip
    rank = (x // 2) ^ flip
    rows = pl.ds(pl.multiple_of(half * 512, 512), 512)

    def send_queries(which):
        copies = []
        for k, (g, i, d) in enumerate(steps):
            to = (sends if which else keeps)[g].at[i]
            at = pl.ds(pl.multiple_of((z + d) % 4 * 128, 128), 128)
            copies.append(pltpu.make_async_copy(gq.at[at], to.at[which], out_sems.at[k, 0]))
            copies.append(pltpu.make_async_copy(zeros, to.at[1 - which], out_sems.at[k, 1]))
        return copies

    def send_passages(which, m, cut):
        copies = []
        for k, (g, i, d) in enumerate(steps):
            to = (keeps if which else sends)[g].at[i]
            for part in range(2):
                at = pl.ds(pl.multiple_of((y + d) % 4 * 256 + (1 - part) * 128, 128), 128)
                copies.append(
                    pltpu.make_async_copy(gp.at[at, cut], to.at[part, :, cut], out_sems.at[k, 2 + 2 * m + part])
                )
        return copies

    def start(make):
        for which in range(2):

            @pl.when(core == which)
            def _():
                for copy in make(which):
                    copy.start()

    for m in range(4):
        cut = slice(m * 256, m * 256 + 256)
        g = sum(
            lax.dot_general(
                slope[h, rows, :], pt[h, cut, :], (((1,), (1,)), ((), ())), preferred_element_type=f32
            )
            for h in range(2)
        )
        gq[:, cut] = (logit_scale * g).astype(bf16)
    start(send_queries)
    cuts = [slice(m * 512, m * 512 + 512) for m in range(2)]
    for m, cut in enumerate(cuts):
        g = jnp.dot(qt[...], slope[rank, :, cut], preferred_element_type=f32)
        gp[:, cut] = (logit_scale * g).astype(bf16)
        start(functools.partial(send_passages, m=m, cut=cut))

    for which in range(2):

        @pl.when(core == which)
        def _():
            for copy in send_queries(which) + [c for m, cut in enumerate(cuts) for c in send_passages(which, m, cut)]:
                copy.wait()


ANY = pl.BlockSpec(memory_space=pl.ANY)
VM = pl.BlockSpec(memory_space=pltpu.VMEM)


def arr(shape, dtype):
    return jax.ShapeDtypeStruct(shape, dtype)


def cost(flops, nbytes):
    return pl.CostEstimate(flops=flops, bytes_accessed=nbytes, transcendentals=0)


def scores_of(mine, theirs, aims):
    return pl.pallas_call(
        score_kernel,
        out_shape=(
            arr((2, 1024, 1024), f32),
            arr((3, 2048), f32),
            arr((3, 2048), f32),
            arr((1024, 1024), bf16),
            arr((2, 1024, 1024), bf16),
            arr((1024, 128), f32),
        ),
        in_specs=[ANY] * 16 + [VM],
        out_specs=(VM,) * 6,
        scratch_shapes=[
            pltpu.VMEM((1024, 128), f32),
            pltpu.VMEM((1024, 128), f32),
            pltpu.VMEM((2, 8, 1024), f32),
            pltpu.SemaphoreType.DMA((8, 3)),
        ],
        compiler_params=pltpu.CompilerParams(vmem_limit_bytes=12 * MIB),
        cost_estimate=cost(2 * 1024**2 * 2048, 16 * MIB),
        name="scores",
    )(*mine, *theirs, aims)


def flip_kernel(q, out):
    for m in range(8):
        out[:, m * 128 : m * 128 + 128] = q[m * 128 : m * 128 + 128, :].T


def flipped(q):
    return pl.pallas_call(
        flip_kernel,
        out_shape=arr(q.shape, bf16),
        in_specs=[VM],
        out_specs=VM,
        compiler_params=pltpu.CompilerParams(vmem_limit_bytes=8 * MIB),
        cost_estimate=cost(0, 4 * MIB),
        name="flip",
    )(q)


def entry_kernel(q, p, mine, send):
    first = place()[1] == 0
    flat = p[...].T
    mine[...] = jnp.where(first, q[...], flat)
    send[...] = jnp.where(first, flat, q[...])


def entry(q, p):
    return pl.pallas_call(
        entry_kernel,
        out_shape=[arr((128, 1024), bf16)] * 2,
        in_specs=[VM] * 2,
        out_specs=[VM] * 2,
        compiler_params=pltpu.CompilerParams(vmem_limit_bytes=8 * MIB),
        cost_estimate=cost(0, MIB),
        name="entry",
    )(q, p)


def finish_kernel(mine, other, grad_queries, grad_passages):
    first = place()[1] == 0
    a, b = mine[...], other[...]
    grad_queries[...] = jnp.where(first, a, b)
    grad_passages[...] = jnp.where(first, b, a).T


def finish(mine, other):
    return pl.pallas_call(
        finish_kernel,
        out_shape=[arr((128, 1024), f32), arr((1024, 128), f32)],
        in_specs=[VM] * 2,
        out_specs=[VM] * 2,
        compiler_params=pltpu.CompilerParams(vmem_limit_bytes=8 * MIB),
        cost_estimate=cost(0, 2 * MIB),
        name="finish",
    )(mine, other)


def slope_of(scores, target, own_lse, got_lse, part):
    return pl.pallas_call(
        slope_kernel,
        out_shape=[arr((2, 1024, 1024), bf16), arr((8, 128), f32)],
        in_specs=[VM] * 5,
        out_specs=[VM] * 2,
        scratch_shapes=[pltpu.VMEM((1024, 128), f32)],
        compiler_params=pltpu.CompilerParams(vmem_limit_bytes=8 * MIB),
        cost_estimate=cost(2 * 1024**2 * 2048, 12 * MIB),
        name="slope",
    )(scores, target, own_lse, got_lse, part)


def grads_of(flip, order, operands, ties):
    chunks = [arr((len(group), 2, 128, 1024), bf16) for group in order]
    return pl.pallas_call(
        functools.partial(grad_kernel, flip, order, len(ties)),
        out_shape=chunks * 2 + [arr((8, 128), f32)],
        in_specs=[VM] * len(operands) + [ANY] * len(ties),
        out_specs=[VM] * (2 * len(chunks) + 1),
        scratch_shapes=[
            pltpu.VMEM((512, 1024), bf16),
            pltpu.VMEM((1024, 1024), bf16),
            pltpu.VMEM((128, 1024), bf16),
            pltpu.SemaphoreType.DMA((4, 6)),
        ],
        compiler_params=pltpu.CompilerParams(vmem_limit_bytes=12 * MIB),
        cost_estimate=cost(2 * 1024**2 * 2048, 20 * MIB),
        name="grads_far" if flip else "grads_near",
    )(*operands, *ties)


def join_kernel(picks, *refs):
    out = refs[-1]
    parts = [r[...] if p is None else r[p : p + 1] for p, r in zip(picks, refs)]
    out[...] = sum(p.astype(f32) for p in parts).astype(bf16)


def join(terms, ties=(), pick=None):
    a, n = terms[0], len(terms)
    return pl.pallas_call(
        functools.partial(join_kernel, [None] * (n - 1) + [pick]),
        out_shape=arr(a.shape, bf16),
        in_specs=[VM] * n + [ANY] * len(ties),
        out_specs=VM,
        compiler_params=pltpu.CompilerParams(vmem_limit_bytes=8 * MIB),
        cost_estimate=cost(a.size, 6 * a.size),
        name="join",
    )(*terms, *ties)


def total_kernel(n, *refs):
    mine, other = refs[-2:]
    mine[...] = sum(r[0, 0].astype(f32) for r in refs[:n])
    other[...] = sum(r[0, 1].astype(f32) for r in refs[:n])


def total(terms, ties=()):
    return pl.pallas_call(
        functools.partial(total_kernel, len(terms)),
        out_shape=[arr((128, 1024), f32)] * 2,
        in_specs=[VM] * len(terms) + [ANY] * len(ties),
        out_specs=[VM] * 2,
        compiler_params=pltpu.CompilerParams(vmem_limit_bytes=8 * MIB),
        cost_estimate=cost(5 * 2**18, 4 * MIB),
        name="total",
    )(*terms, *ties)


def merge_kernel(last, a, b, *refs):
    top = jnp.maximum(a[0:1], b[0:1])
    total = a[1:2] * jnp.exp2(a[0:1] - top) + b[1:2] * jnp.exp2(b[0:1] - top)
    hits = a[2:3] + b[2:3]
    if last:
        lse, part = refs[-2:]
        lse[...] = top + jnp.log2(total)
        figure = jnp.sum(lse[...] - 2.0 * hits, axis=1, keepdims=True)
        part[...] = jnp.broadcast_to(figure, (8, 128))
    else:
        out = refs[-1]
        out[0:1] = top
        out[1:2] = total
        out[2:3] = hits


def merge(a, b, ties=(), last=False):
    return pl.pallas_call(
        functools.partial(merge_kernel, last),
        out_shape=[arr((1, 2048), f32), arr((8, 128), f32)] if last else arr((3, 2048), f32),
        in_specs=[VM, VM] + [ANY] * len(ties),
        out_specs=[VM, VM] if last else VM,
        compiler_params=pltpu.CompilerParams(vmem_limit_bytes=4 * MIB),
        cost_estimate=cost(0, 2**16),
        name="merge",
    )(a, b, *ties)


def shards(queries, passages, positive):
    y, core, z, x = place()
    mine, send = entry(queries, passages)
    own = jnp.stack([mine, swap(send)])
    down, up, far = hop(own, 3, False), hop(own, 1, False), hop(own, 2, False)
    across = hop(own, 0, True)
    down_across, up_across = hop(down, 0, True), hop(up, 0, True)
    far_across = hop(across, 2, False)
    chunks = [own, far, down, up, across, down_across, up_across, far_across]
    others = [swap(c) for c in chunks]

    aims = positive.reshape(4, 2, 2, 128)
    aims = jnp.where(x // 2 == 0, aims[:, 0], aims[:, 1]).transpose(1, 0, 2).reshape(1024)
    block = aims // 1024
    in_tile = (block // 4 == z) & ((block % 4 + 1) % 4 // 2 == (x + 1) % 4 // 2)
    aims = jnp.where(in_tile, block % 4 // 2 * 1024 + aims % 1024, -1)
    aims = aims.astype(f32).reshape(1, 1024)

    scores, keep, send, q_tile, p_tile, target = scores_of(chunks, others, aims)
    q_flip = flipped(q_tile)
    stats = merge(keep, swap(send))
    stats = merge(stats, hop(stats, 0, True), (q_flip,))
    stats = merge(stats, hop_xor(stats))
    own_lse, part = merge(stats, hop(stats, 2, False), last=True)
    slope, part = slope_of(scores, target, own_lse, swap(own_lse), part)

    outs = grads_of(1, ((1, 3), (2,), (0,)), (slope, q_flip, p_tile, part), ())
    part = part + hop_xor(part, 1)
    keeps, recvs = outs[:3], [swap(s) for s in outs[3:6]]
    sides, beyond = join([keeps[0], recvs[0]], (part,)), join([keeps[1], recvs[1]])
    part = part + hop(part, 2, False, 1)
    ties = (sides, beyond)
    sides, beyond = hop(sides, 0, True), hop(beyond, 2, False)
    across = [keeps[2], recvs[2]]
    outs = grads_of(0, ((1,), (3,), (2,), (0,)), (slope, q_flip, p_tile, part), ties)
    part = outs[8] + hop(outs[8], 0, True, 1)
    keeps, recvs = outs[:4], [swap(s) for s in outs[4:8]]
    up = hop(join([keeps[0], recvs[0], sides], pick=0), 1, False)
    down = hop(join([keeps[1], recvs[1], sides], pick=1), 3, False)
    across = hop(join([*across, beyond]), 0, True)
    far = hop(join([keeps[2], recvs[2]]), 2, False)
    home = join([keeps[3], recvs[3]], (part,))
    part = part + swap(part)
    mine, other = total([home, far, across, up, down], (part,))
    grad_queries, grad_passages = finish(mine, swap(other))
    loss = part[0, 0] / (32768.0 * log2_e)
    return loss, grad_queries, grad_passages


def solution(mesh):
    in_specs = (P(("row", "col"), None), P("col", "row"), P("row"))
    out_specs = (P(), P(("row", "col"), None), P("col", "row"))
    return jax.shard_map(shards, mesh=mesh, in_specs=in_specs, out_specs=out_specs, check_vma=False)
```

time: 143 us -> 138 us (0.965)
  starting transfers between devices: 53.2 us -> 70.5 us
  waiting for transfers between devices: 42.7 us -> 28.7 us
  Pallas kernels: 34.6 us -> 29.2 us
  other arithmetic: 2.68 us -> 0.89 us
    ppermute x21 -> x20, starting transfers between devices: 15.3 us -> 37.5 us  [swap(): return lax.ppermute(a, 'row', [(i, i ^ 1) for i in range(8)])]
    ppermute x17, waiting for transfers between devices: 33.4 us -> 22.4 us  [hop(): lax.ppermute(a, AX, moves(lambda r, x, other: ((r + d) % 4, other if flip...]
    pallas_call x3 -> x6, Pallas kernels: 22.9 us -> 17.3 us  [the longest x2 12 us: grads_of(): pl.pallas_call(functools.partial(grad_kernel, flip, order, len(ties)), ou...]
    ppermute x17, starting transfers between devices: 35.2 us -> 31 us  [hop(): lax.ppermute(a, AX, moves(lambda r, x, other: ((r + d) % 4, other if flip...]
    ppermute x21 -> x20, waiting for transfers between devices: 7.83 us -> 4.27 us  [swap(): return lax.ppermute(a, 'row', [(i, i ^ 1) for i in range(8)])]
  transfers between devices with their start and end apart: 40 -> 39, of which waited for: 18 -> 17; matrix products, arithmetic and copies ran while one was open for 1% -> 1% of each run, Pallas kernels for 8% -> 5%
where the time goes in v3:
time: 138 us
  starting transfers between devices  70.5 us (51%)
  Pallas kernels  29.2 us (21%)
  waiting for transfers between devices  28.7 us (21%)
  local copies, waits for them, and re-layouts  6.07 us (4%)
  between operations  2.64 us (2%)
    ppermute x20, starting transfers between devices, swap(): return lax.ppermute(a, 'row', [(i, i ^ 1) for i in range(8)])  37.5 us
    ppermute x17, starting transfers between devices, hop(): lax.ppermute(a, AX, moves(lambda r, x, other: ((r + d) % 4, other if flip...  31 us
    ppermute x17, waiting for transfers between devices, hop(): lax.ppermute(a, AX, moves(lambda r, x, other: ((r + d) % 4, other if flip...  22.4 us
    pallas_call x2, Pallas kernels, grads_of(): pl.pallas_call(functools.partial(grad_kernel, flip, order, len(ties)), ou...  12 us
    pallas_call x1, Pallas kernels, scores_of(): pl.pallas_call(score_kernel, out_shape=(arr((2, 1024, 1024), f32), arr((3...  10.2 us
    unnamed x12, local copies, waits for them, and re-layouts  5.56 us
    ppermute x20, waiting for transfers between devices, swap(): return lax.ppermute(a, 'row', [(i, i ^ 1) for i in range(8)])  4.27 us
    pallas_call x1, Pallas kernels, slope_of(): pl.pallas_call(slope_kernel, out_shape=[arr((2, 1024, 1024), bf16), arr((...  3.49 us
  transfers between devices with their start and end apart: 39, of which 17 were waited for; matrix products, arithmetic and copies ran while one was open for 1% of the time, Pallas kernels for 5%

profile of v3, /device:TPU:1, one launch (start us, length us, event | category | flops | bytes accessed | tf_op | source)
XLA Modules:
  0.0 138.0 jit_solution(5043850579693306396)
XLA Ops:
  0.6 0.9 copy-done
  1.6 0.9 copy-done.1
  2.7 1.5 %collective-permute-start = (bf16[128,1024]{1,0:T(8,128)(2,1)S(1)}, bf16[128,1024]{1,0:T(8,128)(2,1)S(1)}, u32[]{:S(2)}, u32[]{:S(2)}) collective-permute-start(bf16[128,1024]{1,0:T(8,128)(2,1)S(1)} %get-tuple-element.35), channel_id=1, source_target_pairs={{0,16},{16,0},{32,48},{48,32},{64,80},{80,64},{96,112},{112,96},{1... | collective-permute-start | bytes 786440 | tf_op jit(solution)/shard_map/ppermute | solution.py:44
  4.2 1.2 collective-permute-done
  5.4 2.6 %collective-permute-start.4 = (bf16[2,128,1024]{2,1,0:T(8,128)(2,1)S(1)}, bf16[2,128,1024]{2,1,0:T(8,128)(2,1)S(1)}, u32[]{:S(2)}, u32[]{:S(2)}) collective-permute-start(bf16[2,128,1024]{2,1,0:T(8,128)(2,1)S(1)} %pad_maximum_fusion.refs_0_), channel_id=1, source_target_pairs={{0,1},{16,19},{1,0},{17,18},{2,3},{18,17},{3,2},{19,16},{4,5},{20,... | collective-permute-start | bytes 1572872 | tf_op jit(solution)/shard_map/ppermute | solution.py:36
  8.0 1.3 collective-permute-start.3
  9.3 1.4 %collective-permute-start.2 = (bf16[2,128,1024]{2,1,0:T(8,128)(2,1)S(1)}, bf16[2,128,1024]{2,1,0:T(8,128)(2,1)S(1)}, u32[]{:S(2)}, u32[]{:S(2)}) collective-permute-start(bf16[2,128,1024]{2,1,0:T(8,128)(2,1)S(1)} %pad_maximum_fusion.refs_0_), channel_id=1, source_target_pairs={{0,12},{16,112},{1,13},{17,113},{2,14},{18,114},{3,15},{19,115},{4... | collective-permute-start | bytes 1572872 | tf_op jit(solution)/shard_map/ppermute | solution.py:36
  10.8 1.6 %collective-permute-start.1 = (bf16[2,128,1024]{2,1,0:T(8,128)(2,1)S(1)}, bf16[2,128,1024]{2,1,0:T(8,128)(2,1)S(1)}, u32[]{:S(2)}, u32[]{:S(2)}) collective-permute-start(bf16[2,128,1024]{2,1,0:T(8,128)(2,1)S(1)} %pad_maximum_fusion.refs_0_), channel_id=1, source_target_pairs={{0,8},{16,80},{1,9},{17,81},{2,10},{18,82},{3,11},{19,83},{4,12},{... | collective-permute-start | bytes 1572872 | tf_op jit(solution)/shard_map/ppermute | solution.py:36
  12.4 2.6 %collective-permute-done.4.refs_4_ = bf16[2,128,1024]{2,1,0:T(8,128)(2,1)S(1)} collective-permute-done((bf16[2,128,1024]{2,1,0:T(8,128)(2,1)S(1)}, bf16[2,128,1024]{2,1,0:T(8,128)(2,1)S(1)}, u32[]{:S(2)}, u32[]{:S(2)}) %collective-permute-start.4) | collective-permute-done | bytes 524320 | tf_op jit(solution)/shard_map/ppermute | solution.py:36
  15.0 3.0 %collective-permute-start.7 = (bf16[2,128,1024]{2,1,0:T(8,128)(2,1)S(1)}, bf16[2,128,1024]{2,1,0:T(8,128)(2,1)}, u32[]{:S(2)}, u32[]{:S(2)}) collective-permute-start(bf16[2,128,1024]{2,1,0:T(8,128)(2,1)S(1)} %collective-permute-done.4.refs_4_), channel_id=1, source_target_pairs={{0,8},{16,80},{1,9},{17,81},{2,10},{18,82},{3,11},{19,83},{4,12},{... | collective-permute-start | bytes 1572872 | tf_op jit(solution)/shard_map/ppermute | solution.py:36
  18.0 1.7 %collective-permute-start.11 = (bf16[2,128,1024]{2,1,0:T(8,128)(2,1)S(1)}, bf16[2,128,1024]{2,1,0:T(8,128)(2,1)S(1)}, u32[]{:S(2)}, u32[]{:S(2)}) collective-permute-start(bf16[2,128,1024]{2,1,0:T(8,128)(2,1)S(1)} %collective-permute-done.3.refs_3_), channel_id=1, source_target_pairs={{0,16},{16,0},{32,48},{48,32},{64,80},{80,64},{96,112},{112,96},{1... | collective-permute-start | bytes 1572872 | tf_op jit(solution)/shard_map/ppermute | solution.py:44
  19.7 1.9 %collective-permute-start.6 = (bf16[2,128,1024]{2,1,0:T(8,128)(2,1)S(1)}, bf16[2,128,1024]{2,1,0:T(8,128)(2,1)}, u32[]{:S(2)}, u32[]{:S(2)}) collective-permute-start(bf16[2,128,1024]{2,1,0:T(8,128)(2,1)S(1)} %collective-permute-done.3.refs_3_), channel_id=1, source_target_pairs={{0,1},{16,19},{1,0},{17,18},{2,3},{18,17},{3,2},{19,16},{4,5},{20,... | collective-permute-start | bytes 1572872 | tf_op jit(solution)/shard_map/ppermute | solution.py:36
  21.7 2.8 %collective-permute-done.1.refs_1_ = bf16[2,128,1024]{2,1,0:T(8,128)(2,1)S(1)} collective-permute-done((bf16[2,128,1024]{2,1,0:T(8,128)(2,1)S(1)}, bf16[2,128,1024]{2,1,0:T(8,128)(2,1)S(1)}, u32[]{:S(2)}, u32[]{:S(2)}) %collective-permute-start.1) | collective-permute-done | bytes 524320 | tf_op jit(solution)/shard_map/ppermute | solution.py:36
  24.4 1.2 collective-permute-start.5
  25.6 0.8 copy-done.2
  26.4 7.0 %collective-permute-start.10 = (bf16[2,128,1024]{2,1,0:T(8,128)(2,1)S(1)}, bf16[2,128,1024]{2,1,0:T(8,128)(2,1)}, u32[]{:S(2)}, u32[]{:S(2)}) collective-permute-start(bf16[2,128,1024]{2,1,0:T(8,128)(2,1)S(1)} %collective-permute-done.2.refs_2_), channel_id=1, source_target_pairs={{0,16},{16,0},{32,48},{48,32},{64,80},{80,64},{96,112},{112,96},{1... | collective-permute-start | bytes 1572872 | tf_op jit(solution)/shard_map/ppermute | solution.py:44
  34.7 5.1 %collective-permute-start.14 = (bf16[2,128,1024]{2,1,0:T(8,128)(2,1)}, bf16[2,128,1024]{2,1,0:T(8,128)(2,1)}, u32[]{:S(2)}, u32[]{:S(2)}) collective-permute-start(bf16[2,128,1024]{2,1,0:T(8,128)(2,1)} %collective-permute-done.6.refs_6_), channel_id=1, source_target_pairs={{0,16},{16,0},{32,48},{48,32},{64,80},{80,64},{96,112},{112,96},{1... | collective-permute-start | bytes 1572872 | tf_op jit(solution)/shard_map/ppermute | solution.py:44
  39.8 5.6 %collective-permute-start.13 = (bf16[2,128,1024]{2,1,0:T(8,128)(2,1)}, bf16[2,128,1024]{2,1,0:T(8,128)(2,1)}, u32[]{:S(2)}, u32[]{:S(2)}) collective-permute-start(bf16[2,128,1024]{2,1,0:T(8,128)(2,1)} %collective-permute-done.5.refs_5_), channel_id=1, source_target_pairs={{0,16},{16,0},{32,48},{48,32},{64,80},{80,64},{96,112},{112,96},{1... | collective-permute-start | bytes 1572872 | tf_op jit(solution)/shard_map/ppermute | solution.py:44
  46.3 1.0 collective-permute-done.13.refs_13_
  47.3 1.0 copy-done.3
  48.4 1.0 copy-done.5
  49.4 10.2 %scores.1 = (f32[2,1024,1024]{2,1,0:T(8,128)S(1)}, f32[3,2048]{1,0:T(4,128)S(1)}, f32[3,2048]{1,0:T(4,128)S(1)}, bf16[1024,1024]{1,0:T(8,128)(2,1)S(1)}, bf16[2,...) custom-call(bf16[2,128,1024]{2,1,0:T(8,128)(2,1)S(1)} %pad_maximum_fusion.refs_0_, ...), custom_call_target="tpu_custom_call" | custom-call | flops 4294967296 | bytes 16777216 | tf_op jit(solution)/shard_map/scores/pallas_call | solution.py:274
  60.2 0.9 collective-permute-done.16.b
  62.5 2.6 %collective-permute-done.17.b = f32[3,2048]{1,0:T(4,128)S(1)} collective-permute-done((f32[3,2048]{1,0:T(4,128)S(1)}, f32[3,2048]{1,0:T(4,128)S(1)}, u32[]{:S(2)}, u32[]{:S(2)}) %collective-permute-start.17) | collective-permute-done | bytes 24608 | tf_op jit(solution)/shard_map/ppermute | solution.py:36
  65.1 1.4 collective-permute-start.18
  66.5 1.5 %collective-permute-done.18.b = f32[3,2048]{1,0:T(4,128)S(1)} collective-permute-done((f32[3,2048]{1,0:T(4,128)S(1)}, f32[3,2048]{1,0:T(4,128)S(1)}, u32[]{:S(2)}, u32[]{:S(2)}) %collective-permute-start.18) | collective-permute-done | bytes 24608 | tf_op jit(solution)/shard_map/ppermute | solution.py:40
  68.0 3.0 %collective-permute-start.19 = (f32[3,2048]{1,0:T(4,128)S(1)}, f32[3,2048]{1,0:T(4,128)S(1)}, u32[]{:S(2)}, u32[]{:S(2)}) collective-permute-start(f32[3,2048]{1,0:T(4,128)S(1)} %merge.6.a), channel_id=1, source_target_pairs={{0,8},{16,80},{1,9},{17,81},{2,10},{18,82},{3,11},{19,83},{4,12},{... | collective-permute-start | bytes 73736 | tf_op jit(solution)/shard_map/ppermute | solution.py:36
  71.0 1.4 collective-permute-done.19.b
  72.4 2.8 %collective-permute-start.20 = (f32[1,2048]{1,0:T(1,128)S(1)}, f32[1,2048]{1,0:T(1,128)S(1)}, u32[]{:S(2)}, u32[]{:S(2)}) collective-permute-start(f32[1,2048]{1,0:T(1,128)S(1)} %get-tuple-element.41.own_lse), channel_id=1, source_target_pairs={{0,16},{16,0},{32,48},{48,32},{64,80},{80,64},{96,112},{112,96},{1... | collective-permute-start | bytes 24584 | tf_op jit(solution)/shard_map/ppermute | solution.py:44
  75.2 0.8 collective-permute-done.20.got_lse
  76.0 3.5 %slope.1 = (bf16[2,1024,1024]{2,1,0:T(8,128)(2,1)S(1)}, f32[8,128]{1,0:T(8,128)S(1)}) custom-call(f32[2,1024,1024]{2,1,0:T(8,128)S(1)} %get-tuple-element.36.sv, f32[1024,128]{1,0:T(8,128)S(1)} %get-tuple-element.37.target, f32[1,2048]{1,0:T(1,128)S(1)} %get-tuple-element.41.own_lse, f32[1,2048]{1,0:T(1,128)S(1)} %collective-permute-done.20.got_lse, ...), custom_call_target="tpu_custom_call" | custom-call | flops 4294967296 | bytes 12582912 | tf_op jit(solution)/shard_map/slope/pallas_call | solution.py:354
  79.5 6.3 %grads_far.1 = (bf16[2,2,128,1024]{3,2,1,0:T(8,128)(2,1)S(1)}, bf16[1,2,128,1024]{3,2,1,0:T(8,128)(2,1)S(1)}, bf16[1,2,128,1024]{3,2,1,0:T(8,128)(2,1)S(1)}, bf1...) custom-call(bf16[2,1024,1024]{2,1,0:T(8,128)(2,1)S(1)} %get-tuple-el, ...), custom_call_target="tpu_custom_call" | custom-call | flops 4294967296 | bytes 20971520 | tf_op jit(solution)/shard_map/grads_far/pallas_call | solution.py:368
  87.1 1.2 collective-permute-start.30
  89.9 3.1 %collective-permute-start.22 = (f32[8,128]{1,0:T(8,128)S(1)}, f32[8,128]{1,0:T(8,128)S(1)}, u32[]{:S(2)}, u32[]{:S(2)}) collective-permute-start(f32[8,128]{1,0:T(8,128)S(1)} %add.123.refs_2_), channel_id=1, source_target_pairs={{16,24},{0,64},{17,25},{1,65},{18,26},{2,66},{19,27},{3,67},{20,28... | collective-permute-start | bytes 12296 | tf_op jit(solution)/shard_map/ppermute | solution.py:36
  93.0 1.0 collective-permute-done.22
  94.1 5.7 %grads_near.1 = (bf16[1,2,128,1024]{3,2,1,0:T(8,128)(2,1)S(1)}, bf16[1,2,128,1024]{3,2,1,0:T(8,128)(2,1)S(1)}, bf16[1,2,128,1024]{3,2,1,0:T(8,128)(2,1)S(1)}, bf...) custom-call(bf16[2,1024,1024]{2,1,0:T(8,128)(2,1)S(1)} %get-tuple-el, ...), custom_call_target="tpu_custom_call" | custom-call | flops 4294967296 | bytes 20971520 | tf_op jit(solution)/shard_map/grads_near/pallas_call | solution.py:368
  100.2 2.9 %collective-permute-start.31 = (bf16[1,2,128,1024]{3,2,1,0:T(8,128)(2,1)S(1)}, bf16[1,2,128,1024]{3,2,1,0:T(8,128)(2,1)S(1)}, u32[]{:S(2)}, u32[]{:S(2)}) collective-permute-start(bf16[1,2,128,1024]{3,2,1,0:T(8,128)(2,1)S(1)} %join.8.refs_5_), channel_id=1, source_target_pairs={{0,8},{16,80},{1,9},{17,81},{2,10},{18,82},{3,11},{19,83},{4,12},{... | collective-permute-start | bytes 1572872 | tf_op jit(solution)/shard_map/ppermute | solution.py:36
  103.1 3.8 %collective-permute-start.28 = (bf16[1,2,128,1024]{3,2,1,0:T(8,128)(2,1)S(1)}, bf16[1,2,128,1024]{3,2,1,0:T(8,128)(2,1)S(1)}, u32[]{:S(2)}, u32[]{:S(2)}) collective-permute-start(bf16[1,2,128,1024]{3,2,1,0:T(8,128)(2,1)S(1)} %get-tuple-element.54), channel_id=1, source_target_pairs={{0,16},{16,0},{32,48},{48,32},{64,80},{80,64},{96,112},{112,96},{1... | collective-permute-start | bytes 1572872 | tf_op jit(solution)/shard_map/ppermute | solution.py:44
  107.5 2.5 %collective-permute-done.31.refs_2_ = bf16[1,2,128,1024]{3,2,1,0:T(8,128)(2,1)S(1)} collective-permute-done((bf16[1,2,128,1024]{3,2,1,0:T(8,128)(2,1)S(1)}, bf16[1,2,128,1024]{3,2,1,0:T(8,128)(2,1)S(1)}, u32[]{:S(2)}, u32[]{:S(2)}) %collective-permute-start.31) | collective-permute-done | bytes 524320 | tf_op jit(solution)/shard_map/ppermute | solution.py:36
  110.0 4.5 %collective-permute-start.26 = (f32[8,128]{1,0:T(8,128)S(1)}, f32[8,128]{1,0:T(8,128)S(1)}, u32[]{:S(2)}, u32[]{:S(2)}) collective-permute-start(f32[8,128]{1,0:T(8,128)S(1)} %add.125.refs_2_), channel_id=1, source_target_pairs={{0,16},{16,0},{32,48},{48,32},{64,80},{80,64},{96,112},{112,96},{1... | collective-permute-start | bytes 12296 | tf_op jit(solution)/shard_map/ppermute | solution.py:44
  114.8 1.1 collective-permute-start.32
  116.1 3.0 %collective-permute-start.29 = (bf16[1,2,128,1024]{3,2,1,0:T(8,128)(2,1)S(1)}, bf16[1,2,128,1024]{3,2,1,0:T(8,128)(2,1)S(1)}, u32[]{:S(2)}, u32[]{:S(2)}) collective-permute-start(bf16[1,2,128,1024]{3,2,1,0:T(8,128)(2,1)S(1)} %join.10), channel_id=1, source_target_pairs={{0,8},{16,80},{1,9},{17,81},{2,10},{18,82},{3,11},{19,83},{4,12},{... | collective-permute-start | bytes 1572872 | tf_op jit(solution)/shard_map/ppermute | solution.py:36
  120.0 2.3 %collective-permute-start.37 = (bf16[1,2,128,1024]{3,2,1,0:T(8,128)(2,1)S(1)}, bf16[1,2,128,1024]{3,2,1,0:T(8,128)(2,1)S(1)}, u32[]{:S(2)}, u32[]{:S(2)}) collective-permute-start(bf16[1,2,128,1024]{3,2,1,0:T(8,128)(2,1)S(1)} %join.13), channel_id=1, source_target_pairs={{0,12},{16,112},{1,13},{17,113},{2,14},{18,114},{3,15},{19,115},{4... | collective-permute-start | bytes 1572872 | tf_op jit(solution)/shard_map/ppermute | solution.py:36
  122.4 1.9 %collective-permute-done.32.refs_2_ = bf16[1,2,128,1024]{3,2,1,0:T(8,128)(2,1)S(1)} collective-permute-done((bf16[1,2,128,1024]{3,2,1,0:T(8,128)(2,1)S(1)}, bf16[1,2,128,1024]{3,2,1,0:T(8,128)(2,1)S(1)}, u32[]{:S(2)}, u32[]{:S(2)}) %collective-permute-start.32) | collective-permute-done | bytes 524320 | tf_op jit(solution)/shard_map/ppermute | solution.py:36
  124.4 1.6 %collective-permute-done.29.refs_1_ = bf16[1,2,128,1024]{3,2,1,0:T(8,128)(2,1)S(1)} collective-permute-done((bf16[1,2,128,1024]{3,2,1,0:T(8,128)(2,1)S(1)}, bf16[1,2,128,1024]{3,2,1,0:T(8,128)(2,1)S(1)}, u32[]{:S(2)}, u32[]{:S(2)}) %collective-permute-start.29) | collective-permute-done | bytes 524320 | tf_op jit(solution)/shard_map/ppermute | solution.py:36
  126.0 5.6 %collective-permute-done.35.refs_3_ = bf16[1,2,128,1024]{3,2,1,0:T(8,128)(2,1)S(1)} collective-permute-done((bf16[1,2,128,1024]{3,2,1,0:T(8,128)(2,1)S(1)}, bf16[1,2,128,1024]{3,2,1,0:T(8,128)(2,1)S(1)}, u32[]{:S(2)}, u32[]{:S(2)}) %collective-permute-start.35) | collective-permute-done | bytes 524320 | tf_op jit(solution)/shard_map/ppermute | solution.py:36
  132.3 2.0 %collective-permute-start.38 = (f32[128,1024]{1,0:T(8,128)S(1)}, f32[128,1024]{1,0:T(8,128)S(1)}, u32[]{:S(2)}, u32[]{:S(2)}) collective-permute-start(f32[128,1024]{1,0:T(8,128)S(1)} %get-tuple-element.62), channel_id=1, source_target_pairs={{0,16},{16,0},{32,48},{48,32},{64,80},{80,64},{96,112},{112,96},{1... | collective-permute-start | bytes 1572872 | tf_op jit(solution)/shard_map/ppermute | solution.py:44
  135.8 1.1 finish.1
  (70 shorter events, 11.4 us)
Async XLA Ops:
  0.6 1.0 copy-start
  1.6 0.9 copy-start.1
  2.7 2.7 %collective-permute-start = (bf16[128,1024]{1,0:T(8,128)(2,1)S(1)}, bf16[128,1024]{1,0:T(8,128)(2,1)S(1)}, u32[]{:S(2)}, u32[]{:S(2)}) collective-permute-start(bf16[128,1024]{1,0:T(8,128)(2,1)S(1)} %get-tuple-element.35), channel_id=1, source_target_pairs={{0,16},{16,0},{32,48},{48,32},{64,80},{80,64},{96,112},{112,96},{1... | collective-permute-start | bytes 786440 | tf_op jit(solution)/shard_map/ppermute | solution.py:44
  5.4 9.6 %collective-permute-start.4 = (bf16[2,128,1024]{2,1,0:T(8,128)(2,1)S(1)}, bf16[2,128,1024]{2,1,0:T(8,128)(2,1)S(1)}, u32[]{:S(2)}, u32[]{:S(2)}) collective-permute-start(bf16[2,128,1024]{2,1,0:T(8,128)(2,1)S(1)} %pad_maximum_fusion.refs_0_), channel_id=1, source_target_pairs={{0,1},{16,19},{1,0},{17,18},{2,3},{18,17},{3,2},{19,16},{4,5},{20,... | collective-permute-start | bytes 1572872 | tf_op jit(solution)/shard_map/ppermute | solution.py:36
  8.0 7.0 %collective-permute-start.8 = (bf16[2,128,1024]{2,1,0:T(8,128)(2,1)S(1)}, bf16[2,128,1024]{2,1,0:T(8,128)(2,1)S(1)}, u32[]{:S(2)}, u32[]{:S(2)}) collective-permute-start(bf16[2,128,1024]{2,1,0:T(8,128)(2,1)S(1)} %pad_maximum_fusion.refs_0_), channel_id=1, source_target_pairs={{0,16},{16,0},{32,48},{48,32},{64,80},{80,64},{96,112},{112,96},{1... | collective-permute-start | bytes 1572872 | tf_op jit(solution)/shard_map/ppermute | solution.py:44
  8.0 10.0 %collective-permute-start.3 = (bf16[2,128,1024]{2,1,0:T(8,128)(2,1)S(1)}, bf16[2,128,1024]{2,1,0:T(8,128)(2,1)S(1)}, u32[]{:S(2)}, u32[]{:S(2)}) collective-permute-start(bf16[2,128,1024]{2,1,0:T(8,128)(2,1)S(1)} %pad_maximum_fusion.refs_0_), channel_id=1, source_target_pairs={{0,4},{16,48},{1,5},{17,49},{2,6},{18,50},{3,7},{19,51},{4,8},{20,... | collective-permute-start | bytes 1572872 | tf_op jit(solution)/shard_map/ppermute | solution.py:36
  9.3 10.4 %collective-permute-start.2 = (bf16[2,128,1024]{2,1,0:T(8,128)(2,1)S(1)}, bf16[2,128,1024]{2,1,0:T(8,128)(2,1)S(1)}, u32[]{:S(2)}, u32[]{:S(2)}) collective-permute-start(bf16[2,128,1024]{2,1,0:T(8,128)(2,1)S(1)} %pad_maximum_fusion.refs_0_), channel_id=1, source_target_pairs={{0,12},{16,112},{1,13},{17,113},{2,14},{18,114},{3,15},{19,115},{4... | collective-permute-start | bytes 1572872 | tf_op jit(solution)/shard_map/ppermute | solution.py:36
  10.8 13.7 %collective-permute-start.1 = (bf16[2,128,1024]{2,1,0:T(8,128)(2,1)S(1)}, bf16[2,128,1024]{2,1,0:T(8,128)(2,1)S(1)}, u32[]{:S(2)}, u32[]{:S(2)}) collective-permute-start(bf16[2,128,1024]{2,1,0:T(8,128)(2,1)S(1)} %pad_maximum_fusion.refs_0_), channel_id=1, source_target_pairs={{0,8},{16,80},{1,9},{17,81},{2,10},{18,82},{3,11},{19,83},{4,12},{... | collective-permute-start | bytes 1572872 | tf_op jit(solution)/shard_map/ppermute | solution.py:36
  15.0 10.6 %collective-permute-start.12 = (bf16[2,128,1024]{2,1,0:T(8,128)(2,1)S(1)}, bf16[2,128,1024]{2,1,0:T(8,128)(2,1)S(1)}, u32[]{:S(2)}, u32[]{:S(2)}) collective-permute-start(bf16[2,128,1024]{2,1,0:T(8,128)(2,1)S(1)} %collective-permute-done.4.refs_4_), channel_id=1, source_target_pairs={{0,16},{16,0},{32,48},{48,32},{64,80},{80,64},{96,112},{112,96},{1... | collective-permute-start | bytes 1572872 | tf_op jit(solution)/shard_map/ppermute | solution.py:44
  15.0 18.4 %collective-permute-start.7 = (bf16[2,128,1024]{2,1,0:T(8,128)(2,1)S(1)}, bf16[2,128,1024]{2,1,0:T(8,128)(2,1)}, u32[]{:S(2)}, u32[]{:S(2)}) collective-permute-start(bf16[2,128,1024]{2,1,0:T(8,128)(2,1)S(1)} %collective-permute-done.4.refs_4_), channel_id=1, source_target_pairs={{0,8},{16,80},{1,9},{17,81},{2,10},{18,82},{3,11},{19,83},{4,12},{... | collective-permute-start | bytes 1572872 | tf_op jit(solution)/shard_map/ppermute | solution.py:36
  18.0 15.4 %collective-permute-start.11 = (bf16[2,128,1024]{2,1,0:T(8,128)(2,1)S(1)}, bf16[2,128,1024]{2,1,0:T(8,128)(2,1)S(1)}, u32[]{:S(2)}, u32[]{:S(2)}) collective-permute-start(bf16[2,128,1024]{2,1,0:T(8,128)(2,1)S(1)} %collective-permute-done.3.refs_3_), channel_id=1, source_target_pairs={{0,16},{16,0},{32,48},{48,32},{64,80},{80,64},{96,112},{112,96},{1... | collective-permute-start | bytes 1572872 | tf_op jit(solution)/shard_map/ppermute | solution.py:44
  19.7 15.0 %collective-permute-start.6 = (bf16[2,128,1024]{2,1,0:T(8,128)(2,1)S(1)}, bf16[2,128,1024]{2,1,0:T(8,128)(2,1)}, u32[]{:S(2)}, u32[]{:S(2)}) collective-permute-start(bf16[2,128,1024]{2,1,0:T(8,128)(2,1)S(1)} %collective-permute-done.3.refs_3_), channel_id=1, source_target_pairs={{0,1},{16,19},{1,0},{17,18},{2,3},{18,17},{3,2},{19,16},{4,5},{20,... | collective-permute-start | bytes 1572872 | tf_op jit(solution)/shard_map/ppermute | solution.py:36
  24.4 15.4 %collective-permute-start.5 = (bf16[2,128,1024]{2,1,0:T(8,128)(2,1)S(1)}, bf16[2,128,1024]{2,1,0:T(8,128)(2,1)}, u32[]{:S(2)}, u32[]{:S(2)}) collective-permute-start(bf16[2,128,1024]{2,1,0:T(8,128)(2,1)S(1)} %collective-permute-done.2.refs_2_), channel_id=1, source_target_pairs={{0,1},{16,19},{1,0},{17,18},{2,3},{18,17},{3,2},{19,16},{4,5},{20,... | collective-permute-start | bytes 1572872 | tf_op jit(solution)/shard_map/ppermute | solution.py:36
  25.6 0.8 copy-start.2
  26.4 19.9 %collective-permute-start.10 = (bf16[2,128,1024]{2,1,0:T(8,128)(2,1)S(1)}, bf16[2,128,1024]{2,1,0:T(8,128)(2,1)}, u32[]{:S(2)}, u32[]{:S(2)}) collective-permute-start(bf16[2,128,1024]{2,1,0:T(8,128)(2,1)S(1)} %collective-permute-done.2.refs_2_), channel_id=1, source_target_pairs={{0,16},{16,0},{32,48},{48,32},{64,80},{80,64},{96,112},{112,96},{1... | collective-permute-start | bytes 1572872 | tf_op jit(solution)/shard_map/ppermute | solution.py:44
  33.4 12.9 %collective-permute-start.9 = (bf16[2,128,1024]{2,1,0:T(8,128)(2,1)S(1)}, bf16[2,128,1024]{2,1,0:T(8,128)(2,1)}, u32[]{:S(2)}, u32[]{:S(2)}) collective-permute-start(bf16[2,128,1024]{2,1,0:T(8,128)(2,1)S(1)} %collective-permute-done.1.refs_1_), channel_id=1, source_target_pairs={{0,16},{16,0},{32,48},{48,32},{64,80},{80,64},{96,112},{112,96},{1... | collective-permute-start | bytes 1572872 | tf_op jit(solution)/shard_map/ppermute | solution.py:44
  33.4 0.8 copy-start.4
  34.2 12.1 %collective-permute-start.15 = (bf16[2,128,1024]{2,1,0:T(8,128)(2,1)}, bf16[2,128,1024]{2,1,0:T(8,128)(2,1)}, u32[]{:S(2)}, u32[]{:S(2)}) collective-permute-start(bf16[2,128,1024]{2,1,0:T(8,128)(2,1)} %collective-permute-done.7.refs_7_), channel_id=1, source_target_pairs={{0,16},{16,0},{32,48},{48,32},{64,80},{80,64},{96,112},{112,96},{1... | collective-permute-start | bytes 1572872 | tf_op jit(solution)/shard_map/ppermute | solution.py:44
  34.7 11.6 %collective-permute-start.14 = (bf16[2,128,1024]{2,1,0:T(8,128)(2,1)}, bf16[2,128,1024]{2,1,0:T(8,128)(2,1)}, u32[]{:S(2)}, u32[]{:S(2)}) collective-permute-start(bf16[2,128,1024]{2,1,0:T(8,128)(2,1)} %collective-permute-done.6.refs_6_), channel_id=1, source_target_pairs={{0,16},{16,0},{32,48},{48,32},{64,80},{80,64},{96,112},{112,96},{1... | collective-permute-start | bytes 1572872 | tf_op jit(solution)/shard_map/ppermute | solution.py:44
  39.8 7.5 %collective-permute-start.13 = (bf16[2,128,1024]{2,1,0:T(8,128)(2,1)}, bf16[2,128,1024]{2,1,0:T(8,128)(2,1)}, u32[]{:S(2)}, u32[]{:S(2)}) collective-permute-start(bf16[2,128,1024]{2,1,0:T(8,128)(2,1)} %collective-permute-done.5.refs_5_), channel_id=1, source_target_pairs={{0,16},{16,0},{32,48},{48,32},{64,80},{80,64},{96,112},{112,96},{1... | collective-permute-start | bytes 1572872 | tf_op jit(solution)/shard_map/ppermute | solution.py:44
  47.3 1.0 copy-start.3
  48.4 1.0 copy-start.5
  59.6 1.4 %collective-permute-start.16 = (f32[3,2048]{1,0:T(4,128)S(1)}, f32[3,2048]{1,0:T(4,128)S(1)}, u32[]{:S(2)}, u32[]{:S(2)}) collective-permute-start(f32[3,2048]{1,0:T(4,128)S(1)} %get-tuple-element.39), channel_id=1, source_target_pairs={{0,16},{16,0},{32,48},{48,32},{64,80},{80,64},{96,112},{112,96},{1... | collective-permute-start | bytes 73736 | tf_op jit(solution)/shard_map/ppermute | solution.py:44
  61.0 4.1 %collective-permute-start.17 = (f32[3,2048]{1,0:T(4,128)S(1)}, f32[3,2048]{1,0:T(4,128)S(1)}, u32[]{:S(2)}, u32[]{:S(2)}) collective-permute-start(f32[3,2048]{1,0:T(4,128)S(1)} %merge.4.a), channel_id=1, source_target_pairs={{0,1},{16,19},{1,0},{17,18},{2,3},{18,17},{3,2},{19,16},{4,5},{20,... | collective-permute-start | bytes 73736 | tf_op jit(solution)/shard_map/ppermute | solution.py:36
  65.1 2.8 %collective-permute-start.18 = (f32[3,2048]{1,0:T(4,128)S(1)}, f32[3,2048]{1,0:T(4,128)S(1)}, u32[]{:S(2)}, u32[]{:S(2)}) collective-permute-start(f32[3,2048]{1,0:T(4,128)S(1)} %merge.5.a), channel_id=1, source_target_pairs={{0,4},{16,48},{1,5},{17,49},{2,6},{18,50},{3,7},{19,51},{4,0},{20,... | collective-permute-start | bytes 73736 | tf_op jit(solution)/shard_map/ppermute | solution.py:40
  68.0 4.3 %collective-permute-start.19 = (f32[3,2048]{1,0:T(4,128)S(1)}, f32[3,2048]{1,0:T(4,128)S(1)}, u32[]{:S(2)}, u32[]{:S(2)}) collective-permute-start(f32[3,2048]{1,0:T(4,128)S(1)} %merge.6.a), channel_id=1, source_target_pairs={{0,8},{16,80},{1,9},{17,81},{2,10},{18,82},{3,11},{19,83},{4,12},{... | collective-permute-start | bytes 73736 | tf_op jit(solution)/shard_map/ppermute | solution.py:36
  72.4 3.6 %collective-permute-start.20 = (f32[1,2048]{1,0:T(1,128)S(1)}, f32[1,2048]{1,0:T(1,128)S(1)}, u32[]{:S(2)}, u32[]{:S(2)}) collective-permute-start(f32[1,2048]{1,0:T(1,128)S(1)} %get-tuple-element.41.own_lse), channel_id=1, source_target_pairs={{0,16},{16,0},{32,48},{48,32},{64,80},{80,64},{96,112},{112,96},{1... | collective-permute-start | bytes 24584 | tf_op jit(solution)/shard_map/ppermute | solution.py:44
  85.8 3.1 %collective-permute-start.23 = (bf16[2,2,128,1024]{3,2,1,0:T(8,128)(2,1)S(1)}, bf16[2,2,128,1024]{3,2,1,0:T(8,128)(2,1)S(1)}, u32[]{:S(2)}, u32[]{:S(2)}) collective-permute-start(bf16[2,2,128,1024]{3,2,1,0:T(8,128)(2,1)S(1)} %get-tuple-element.47), channel_id=1, source_target_pairs={{0,16},{16,0},{32,48},{48,32},{64,80},{80,64},{96,112},{112,96},{1... | collective-permute-start | bytes 3145736 | tf_op jit(solution)/shard_map/ppermute | solution.py:44
  86.2 7.8 %collective-permute-start.24 = (bf16[1,2,128,1024]{3,2,1,0:T(8,128)(2,1)S(1)}, bf16[1,2,128,1024]{3,2,1,0:T(8,128)(2,1)S(1)}, u32[]{:S(2)}, u32[]{:S(2)}) collective-permute-start(bf16[1,2,128,1024]{3,2,1,0:T(8,128)(2,1)S(1)} %get-tuple-element.49), channel_id=1, source_target_pairs={{0,16},{16,0},{32,48},{48,32},{64,80},{80,64},{96,112},{112,96},{1... | collective-permute-start | bytes 1572872 | tf_op jit(solution)/shard_map/ppermute | solution.py:44
  86.4 2.5 %collective-permute-start.21 = (f32[8,128]{1,0:T(8,128)S(1)}, f32[8,128]{1,0:T(8,128)S(1)}, u32[]{:S(2)}, u32[]{:S(2)}) collective-permute-start(f32[8,128]{1,0:T(8,128)S(1)} %get-tuple-element.45.refs_3_), channel_id=1, source_target_pairs={{16,20},{0,32},{17,21},{1,33},{18,22},{2,34},{19,23},{3,35},{20,16... | collective-permute-start | bytes 12296 | tf_op jit(solution)/shard_map/ppermute | solution.py:40
  87.1 19.9 %collective-permute-start.30 = (bf16[1,2,128,1024]{3,2,1,0:T(8,128)(2,1)S(1)}, bf16[1,2,128,1024]{3,2,1,0:T(8,128)(2,1)S(1)}, u32[]{:S(2)}, u32[]{:S(2)}) collective-permute-start(bf16[1,2,128,1024]{3,2,1,0:T(8,128)(2,1)S(1)} %get-tuple-element.56), channel_id=1, source_target_pairs={{0,16},{16,0},{32,48},{48,32},{64,80},{80,64},{96,112},{112,96},{1... | collective-permute-start | bytes 1572872 | tf_op jit(solution)/shard_map/ppermute | solution.py:44
  89.1 26.9 %collective-permute-start.34 = (bf16[2,2,128,1024]{3,2,1,0:T(8,128)(2,1)S(1)}, bf16[2,2,128,1024]{3,2,1,0:T(8,128)(2,1)S(1)}, u32[]{:S(2)}, u32[]{:S(2)}) collective-permute-start(bf16[2,2,128,1024]{3,2,1,0:T(8,128)(2,1)S(1)} %join.7.refs_4_), channel_id=1, source_target_pairs={{0,1},{16,19},{1,0},{17,18},{2,3},{18,17},{3,2},{19,16},{4,5},{20,... | collective-permute-start | bytes 3145736 | tf_op jit(solution)/shard_map/ppermute | solution.py:36
  89.9 4.1 %collective-permute-start.22 = (f32[8,128]{1,0:T(8,128)S(1)}, f32[8,128]{1,0:T(8,128)S(1)}, u32[]{:S(2)}, u32[]{:S(2)}) collective-permute-start(f32[8,128]{1,0:T(8,128)S(1)} %add.123.refs_2_), channel_id=1, source_target_pairs={{16,24},{0,64},{17,25},{1,65},{18,26},{2,66},{19,27},{3,67},{20,28... | collective-permute-start | bytes 12296 | tf_op jit(solution)/shard_map/ppermute | solution.py:36
  99.8 7.2 %collective-permute-start.25 = (f32[8,128]{1,0:T(8,128)S(1)}, f32[8,128]{1,0:T(8,128)S(1)}, u32[]{:S(2)}, u32[]{:S(2)}) collective-permute-start(f32[8,128]{1,0:T(8,128)S(1)} %get-tuple-element.50), channel_id=1, source_target_pairs={{16,17},{0,3},{17,16},{1,2},{18,19},{2,1},{19,18},{3,0},{20,21},{4... | collective-permute-start | bytes 12296 | tf_op jit(solution)/shard_map/ppermute | solution.py:36
  100.2 9.8 %collective-permute-start.31 = (bf16[1,2,128,1024]{3,2,1,0:T(8,128)(2,1)S(1)}, bf16[1,2,128,1024]{3,2,1,0:T(8,128)(2,1)S(1)}, u32[]{:S(2)}, u32[]{:S(2)}) collective-permute-start(bf16[1,2,128,1024]{3,2,1,0:T(8,128)(2,1)S(1)} %join.8.refs_5_), channel_id=1, source_target_pairs={{0,8},{16,80},{1,9},{17,81},{2,10},{18,82},{3,11},{19,83},{4,12},{... | collective-permute-start | bytes 1572872 | tf_op jit(solution)/shard_map/ppermute | solution.py:36
  103.1 11.6 %collective-permute-start.28 = (bf16[1,2,128,1024]{3,2,1,0:T(8,128)(2,1)S(1)}, bf16[1,2,128,1024]{3,2,1,0:T(8,128)(2,1)S(1)}, u32[]{:S(2)}, u32[]{:S(2)}) collective-permute-start(bf16[1,2,128,1024]{3,2,1,0:T(8,128)(2,1)S(1)} %get-tuple-element.54), channel_id=1, source_target_pairs={{0,16},{16,0},{32,48},{48,32},{64,80},{80,64},{96,112},{112,96},{1... | collective-permute-start | bytes 1572872 | tf_op jit(solution)/shard_map/ppermute | solution.py:44
  107.0 9.0 %collective-permute-start.33 = (bf16[1,2,128,1024]{3,2,1,0:T(8,128)(2,1)S(1)}, bf16[1,2,128,1024]{3,2,1,0:T(8,128)(2,1)S(1)}, u32[]{:S(2)}, u32[]{:S(2)}) collective-permute-start(bf16[1,2,128,1024]{3,2,1,0:T(8,128)(2,1)S(1)} %get-tuple-element.58), channel_id=1, source_target_pairs={{0,16},{16,0},{32,48},{48,32},{64,80},{80,64},{96,112},{112,96},{1... | collective-permute-start | bytes 1572872 | tf_op jit(solution)/shard_map/ppermute | solution.py:44
  107.0 12.3 %collective-permute-start.36 = (bf16[1,2,128,1024]{3,2,1,0:T(8,128)(2,1)S(1)}, bf16[1,2,128,1024]{3,2,1,0:T(8,128)(2,1)S(1)}, u32[]{:S(2)}, u32[]{:S(2)}) collective-permute-start(bf16[1,2,128,1024]{3,2,1,0:T(8,128)(2,1)S(1)} %get-tuple-element.60), channel_id=1, source_target_pairs={{0,16},{16,0},{32,48},{48,32},{64,80},{80,64},{96,112},{112,96},{1... | collective-permute-start | bytes 1572872 | tf_op jit(solution)/shard_map/ppermute | solution.py:44
  110.0 9.9 %collective-permute-start.26 = (f32[8,128]{1,0:T(8,128)S(1)}, f32[8,128]{1,0:T(8,128)S(1)}, u32[]{:S(2)}, u32[]{:S(2)}) collective-permute-start(f32[8,128]{1,0:T(8,128)S(1)} %add.125.refs_2_), channel_id=1, source_target_pairs={{0,16},{16,0},{32,48},{48,32},{64,80},{80,64},{96,112},{112,96},{1... | collective-permute-start | bytes 12296 | tf_op jit(solution)/shard_map/ppermute | solution.py:44
  114.8 9.6 %collective-permute-start.32 = (bf16[1,2,128,1024]{3,2,1,0:T(8,128)(2,1)S(1)}, bf16[1,2,128,1024]{3,2,1,0:T(8,128)(2,1)S(1)}, u32[]{:S(2)}, u32[]{:S(2)}) collective-permute-start(bf16[1,2,128,1024]{3,2,1,0:T(8,128)(2,1)S(1)} %join.11), channel_id=1, source_target_pairs={{0,1},{16,19},{1,0},{17,18},{2,3},{18,17},{3,2},{19,16},{4,5},{20,... | collective-permute-start | bytes 1572872 | tf_op jit(solution)/shard_map/ppermute | solution.py:36
  116.0 6.3 %collective-permute-start.27 = (bf16[1,2,128,1024]{3,2,1,0:T(8,128)(2,1)S(1)}, bf16[1,2,128,1024]{3,2,1,0:T(8,128)(2,1)S(1)}, u32[]{:S(2)}, u32[]{:S(2)}) collective-permute-start(bf16[1,2,128,1024]{3,2,1,0:T(8,128)(2,1)S(1)} %get-tuple-element.52), channel_id=1, source_target_pairs={{0,16},{16,0},{32,48},{48,32},{64,80},{80,64},{96,112},{112,96},{1... | collective-permute-start | bytes 1572872 | tf_op jit(solution)/shard_map/ppermute | solution.py:44
  116.1 10.0 %collective-permute-start.29 = (bf16[1,2,128,1024]{3,2,1,0:T(8,128)(2,1)S(1)}, bf16[1,2,128,1024]{3,2,1,0:T(8,128)(2,1)S(1)}, u32[]{:S(2)}, u32[]{:S(2)}) collective-permute-start(bf16[1,2,128,1024]{3,2,1,0:T(8,128)(2,1)S(1)} %join.10), channel_id=1, source_target_pairs={{0,8},{16,80},{1,9},{17,81},{2,10},{18,82},{3,11},{19,83},{4,12},{... | collective-permute-start | bytes 1572872 | tf_op jit(solution)/shard_map/ppermute | solution.py:36
  119.3 12.3 %collective-permute-start.35 = (bf16[1,2,128,1024]{3,2,1,0:T(8,128)(2,1)S(1)}, bf16[1,2,128,1024]{3,2,1,0:T(8,128)(2,1)S(1)}, u32[]{:S(2)}, u32[]{:S(2)}) collective-permute-start(bf16[1,2,128,1024]{3,2,1,0:T(8,128)(2,1)S(1)} %join.12), channel_id=1, source_target_pairs={{0,4},{16,48},{1,5},{17,49},{2,6},{18,50},{3,7},{19,51},{4,8},{20,... | collective-permute-start | bytes 1572872 | tf_op jit(solution)/shard_map/ppermute | solution.py:36
  120.0 12.0 %collective-permute-start.37 = (bf16[1,2,128,1024]{3,2,1,0:T(8,128)(2,1)S(1)}, bf16[1,2,128,1024]{3,2,1,0:T(8,128)(2,1)S(1)}, u32[]{:S(2)}, u32[]{:S(2)}) collective-permute-start(bf16[1,2,128,1024]{3,2,1,0:T(8,128)(2,1)S(1)} %join.13), channel_id=1, source_target_pairs={{0,12},{16,112},{1,13},{17,113},{2,14},{18,114},{3,15},{19,115},{4... | collective-permute-start | bytes 1572872 | tf_op jit(solution)/shard_map/ppermute | solution.py:36
  132.3 3.5 %collective-permute-start.38 = (f32[128,1024]{1,0:T(8,128)S(1)}, f32[128,1024]{1,0:T(8,128)S(1)}, u32[]{:S(2)}, u32[]{:S(2)}) collective-permute-start(f32[128,1024]{1,0:T(8,128)S(1)} %get-tuple-element.62), channel_id=1, source_target_pairs={{0,16},{16,0},{32,48},{48,32},{64,80},{80,64},{96,112},{112,96},{1... | collective-permute-start | bytes 1572872 | tf_op jit(solution)/shard_map/ppermute | solution.py:44

commit v4 on v3

--- a/solution.py
+++ b/solution.py
@@ -49,7 +49,7 @@
     return row // 2, row % 2, col // 4, col % 4
 
 
-OFFSETS = [(0, 0), (2, 0), (3, 0), (1, 0), (0, 1), (3, 1), (1, 1), (2, 1)]
+OFFSETS = [(2, 0), (1, 0), (0, 1), (3, 1), (0, 0), (3, 0), (1, 1), (2, 1)]
 
 
 def load_copies(core, y, z, x, mine, theirs, q_dst, p_dst, sems):
@@ -97,7 +97,7 @@
 
 
 def score_kernel(*refs):
-    mine, theirs, (aims, sv, keep, send, qv, pt, target, row_top, row_sum, col_top, sems) = (
+    mine, theirs, (target, sv, keep, send, qv, pt, row_top, row_sum, col_top, sems) = (
         refs[:8],
         refs[8:16],
         refs[16:],
@@ -105,9 +105,6 @@
     y, core, z, x = place()
     groups = load_copies(core, y, z, x, mine, theirs, qv, pt, sems)
     run_copies(core, groups, True)
-    for s in range(8):
-        rows = slice(s * 128, s * 128 + 128)
-        target[rows, :] = jnp.broadcast_to(aims[:, rows], (128, 128)).T
     run_copies(core, groups, False)
     for h in range(2):
         for n in range(2):
@@ -270,7 +267,7 @@
     return pl.CostEstimate(flops=flops, bytes_accessed=nbytes, transcendentals=0)
 
 
-def scores_of(mine, theirs, aims):
+def scores_of(mine, theirs, target):
     return pl.pallas_call(
         score_kernel,
         out_shape=(
@@ -279,20 +276,19 @@
             arr((3, 2048), f32),
             arr((1024, 1024), bf16),
             arr((2, 1024, 1024), bf16),
-            arr((1024, 128), f32),
         ),
         in_specs=[ANY] * 16 + [VM],
-        out_specs=(VM,) * 6,
+        out_specs=(VM,) * 5,
         scratch_shapes=[
             pltpu.VMEM((1024, 128), f32),
             pltpu.VMEM((1024, 128), f32),
             pltpu.VMEM((2, 8, 1024), f32),
             pltpu.SemaphoreType.DMA((8, 3)),
         ],
-        compiler_params=pltpu.CompilerParams(vmem_limit_bytes=12 * MIB),
+        compiler_params=pltpu.CompilerParams(vmem_limit_bytes=18 * MIB),
         cost_estimate=cost(2 * 1024**2 * 2048, 16 * MIB),
         name="scores",
-    )(*mine, *theirs, aims)
+    )(*mine, *theirs, target)
 
 
 def flip_kernel(q, out):
@@ -312,7 +308,12 @@
     )(q)
 
 
-def entry_kernel(q, p, mine, send):
+def entry_kernel(q_in, p_in, mine, send, q, p, sems):
+    copies = [pltpu.make_async_copy(q_in, q, sems.at[0]), pltpu.make_async_copy(p_in, p, sems.at[1])]
+    for copy in copies:
+        copy.start()
+    for copy in copies:
+        copy.wait()
     first = place()[1] == 0
     flat = p[...].T
     mine[...] = jnp.where(first, q[...], flat)
@@ -323,12 +324,52 @@
     return pl.pallas_call(
         entry_kernel,
         out_shape=[arr((128, 1024), bf16)] * 2,
-        in_specs=[VM] * 2,
+        in_specs=[ANY] * 2,
         out_specs=[VM] * 2,
-        compiler_params=pltpu.CompilerParams(vmem_limit_bytes=8 * MIB),
+        scratch_shapes=[pltpu.VMEM(q.shape, bf16), pltpu.VMEM(p.shape, bf16), pltpu.SemaphoreType.DMA((2,))],
+        compiler_params=pltpu.CompilerParams(vmem_limit_bytes=4 * MIB),
         cost_estimate=cost(0, MIB),
         name="entry",
     )(q, p)
+
+
+def aim_kernel(positive, out):
+    _, _, z, x = place()
+    side = (x + 1) % 4 // 2
+    for s in range(8):
+        p = positive[pl.ds(s % 4 * 4 + x // 2 * 2 + s // 4, 1), :]
+        far_z, far_x = p >> 12, (p >> 10) & 3
+        inside = (far_z == z) & ((((far_x + 1) & 3) >> 1) == side)
+        aim = jnp.where(inside, (far_x >> 1) * 1024 + (p & 1023), -1).astype(f32)
+        out[s * 128 : s * 128 + 128, :] = jnp.broadcast_to(aim, (128, 128)).T
+
+
+def aims_of(positive):
+    return pl.pallas_call(
+        aim_kernel,
+        out_shape=arr((1024, 128), f32),
+        in_specs=[VM],
+        out_specs=VM,
+        compiler_params=pltpu.CompilerParams(vmem_limit_bytes=4 * MIB),
+        cost_estimate=cost(0, MIB),
+        name="aims",
+    )(positive.reshape(16, 128))
+
+
+def after_kernel(a, *refs):
+    refs[-1][...] = a[...]
+
+
+def after(a, *ties):
+    return pl.pallas_call(
+        after_kernel,
+        out_shape=arr(a.shape, a.dtype),
+        in_specs=[VM] + [ANY] * len(ties),
+        out_specs=VM,
+        compiler_params=pltpu.CompilerParams(vmem_limit_bytes=4 * MIB),
+        cost_estimate=cost(0, 1024),
+        name="after",
+    )(a, *ties)
 
 
 def finish_kernel(mine, other, grad_queries, grad_passages):
@@ -419,10 +460,13 @@
     )(*terms, *ties)
 
 
-def merge_kernel(last, a, b, *refs):
-    top = jnp.maximum(a[0:1], b[0:1])
-    total = a[1:2] * jnp.exp2(a[0:1] - top) + b[1:2] * jnp.exp2(b[0:1] - top)
-    hits = a[2:3] + b[2:3]
+def merge_kernel(n, last, *refs):
+    ins = refs[:n]
+    top = ins[0][0:1]
+    for a in ins[1:]:
+        top = jnp.maximum(top, a[0:1])
+    total = sum(a[1:2] * jnp.exp2(a[0:1] - top) for a in ins)
+    hits = sum(a[2:3] for a in ins)
     if last:
         lse, part = refs[-2:]
         lse[...] = top + jnp.log2(total)
@@ -435,60 +479,53 @@
         out[2:3] = hits
 
 
-def merge(a, b, ties=(), last=False):
-    return pl.pallas_call(
-        functools.partial(merge_kernel, last),
+def merge(ins, ties=(), last=False):
+    return pl.pallas_call(
+        functools.partial(merge_kernel, len(ins), last),
         out_shape=[arr((1, 2048), f32), arr((8, 128), f32)] if last else arr((3, 2048), f32),
-        in_specs=[VM, VM] + [ANY] * len(ties),
+        in_specs=[VM] * len(ins) + [ANY] * len(ties),
         out_specs=[VM, VM] if last else VM,
         compiler_params=pltpu.CompilerParams(vmem_limit_bytes=4 * MIB),
         cost_estimate=cost(0, 2**16),
         name="merge",
-    )(a, b, *ties)
+    )(*ins, *ties)
 
 
 def shards(queries, passages, positive):
-    y, core, z, x = place()
     mine, send = entry(queries, passages)
     own = jnp.stack([mine, swap(send)])
     down, up, far = hop(own, 3, False), hop(own, 1, False), hop(own, 2, False)
     across = hop(own, 0, True)
     down_across, up_across = hop(down, 0, True), hop(up, 0, True)
     far_across = hop(across, 2, False)
-    chunks = [own, far, down, up, across, down_across, up_across, far_across]
+    chunks = [far, up, across, down_across, own, down, up_across, far_across]
     others = [swap(c) for c in chunks]
 
-    aims = positive.reshape(4, 2, 2, 128)
-    aims = jnp.where(x // 2 == 0, aims[:, 0], aims[:, 1]).transpose(1, 0, 2).reshape(1024)
-    block = aims // 1024
-    in_tile = (block // 4 == z) & ((block % 4 + 1) % 4 // 2 == (x + 1) % 4 // 2)
-    aims = jnp.where(in_tile, block % 4 // 2 * 1024 + aims % 1024, -1)
-    aims = aims.astype(f32).reshape(1, 1024)
-
-    scores, keep, send, q_tile, p_tile, target = scores_of(chunks, others, aims)
+    target = aims_of(positive)
+    scores, keep, send, q_tile, p_tile = scores_of(chunks, others, target)
     q_flip = flipped(q_tile)
-    stats = merge(keep, swap(send))
-    stats = merge(stats, hop(stats, 0, True), (q_flip,))
-    stats = merge(stats, hop_xor(stats))
-    own_lse, part = merge(stats, hop(stats, 2, False), last=True)
+    stats = merge([keep, swap(send)])
+    stats = merge([stats, hop(stats, 0, True)], (q_flip,))
+    own_lse, part = merge([stats, hop(stats, 2, False), hop(stats, 1, False), hop(stats, 3, False)], last=True)
     slope, part = slope_of(scores, target, own_lse, swap(own_lse), part)
 
     outs = grads_of(1, ((1, 3), (2,), (0,)), (slope, q_flip, p_tile, part), ())
     part = part + hop_xor(part, 1)
     keeps, recvs = outs[:3], [swap(s) for s in outs[3:6]]
-    sides, beyond = join([keeps[0], recvs[0]], (part,)), join([keeps[1], recvs[1]])
-    part = part + hop(part, 2, False, 1)
-    ties = (sides, beyond)
+    sides, beyond = join([keeps[0], recvs[0]]), join([keeps[1], recvs[1]])
+    ready = (sides, beyond)
     sides, beyond = hop(sides, 0, True), hop(beyond, 2, False)
     across = [keeps[2], recvs[2]]
-    outs = grads_of(0, ((1,), (3,), (2,), (0,)), (slope, q_flip, p_tile, part), ties)
-    part = outs[8] + hop(outs[8], 0, True, 1)
+    part = part + hop(part, 2, False, 1)
+    outs = grads_of(0, ((1,), (3,), (2,), (0,)), (slope, q_flip, p_tile, part), (ready[0], beyond, part))
     keeps, recvs = outs[:4], [swap(s) for s in outs[4:8]]
     up = hop(join([keeps[0], recvs[0], sides], pick=0), 1, False)
     down = hop(join([keeps[1], recvs[1], sides], pick=1), 3, False)
     across = hop(join([*across, beyond]), 0, True)
     far = hop(join([keeps[2], recvs[2]]), 2, False)
-    home = join([keeps[3], recvs[3]], (part,))
+    home = join([keeps[3], recvs[3]])
+    part = after(outs[8], across)
+    part = part + hop(part, 0, True, 1)
     part = part + swap(part)
     mine, other = total([home, far, across, up, down], (part,))
     grad_queries, grad_passages = finish(mine, swap(other))

time: 138 us -> 119 us (0.86)
  starting transfers between devices: 70.5 us -> 53.2 us
  waiting for transfers between devices: 28.7 us -> 32.2 us
  local copies, waits for them, and re-layouts: 6.07 us -> 3.1 us
    ppermute x20, starting transfers between devices: 37.5 us -> 15.2 us  [swap(): return lax.ppermute(a, 'row', [(i, i ^ 1) for i in range(8)])]
    ppermute x17 -> x19, starting transfers between devices: 31 us -> 37.7 us  [hop(): lax.ppermute(a, AX, moves(lambda r, x, other: ((r + d) % 4, other if flip...]
    ppermute x20, waiting for transfers between devices: 4.27 us -> 8.1 us  [swap(): return lax.ppermute(a, 'row', [(i, i ^ 1) for i in range(8)])]
    unnamed x12 -> x6, local copies, waits for them, and re-layouts: 5.56 us -> 2.59 us
    ppermute x2 -> x1, starting transfers between devices: 2.08 us -> 0.25 us  [hop_xor(): return lax.ppermute(a, AX, moves(lambda r, x, other: (r ^ 1, x), turn))]
    pallas_call x1, Pallas kernels: 10.2 us -> 8.77 us  [scores_of(): pl.pallas_call(score_kernel, out_shape=(arr((2, 1024, 1024), f32), arr((3...]
    ppermute x17 -> x19, waiting for transfers between devices: 22.4 us -> 21.5 us  [hop(): lax.ppermute(a, AX, moves(lambda r, x, other: ((r + d) % 4, other if flip...]
  transfers between devices with their start and end apart: 39 -> 40, of which waited for: 17 -> 19; matrix products, arithmetic and copies ran while one was open for 1% -> 0% of each run, Pallas kernels for 5% -> 7%
where the time goes in v4:
time: 119 us
  starting transfers between devices  53.2 us (45%)
  waiting for transfers between devices  32.2 us (27%)
  Pallas kernels  27.9 us (23%)
  local copies, waits for them, and re-layouts  3.1 us (3%)
  between operations  2.6 us (2%)
    ppermute x19, starting transfers between devices, hop(): lax.ppermute(a, AX, moves(lambda r, x, other: ((r + d) % 4, other if flip...  37.7 us
    ppermute x19, waiting for transfers between devices, hop(): lax.ppermute(a, AX, moves(lambda r, x, other: ((r + d) % 4, other if flip...  21.5 us
    ppermute x20, starting transfers between devices, swap(): return lax.ppermute(a, 'row', [(i, i ^ 1) for i in range(8)])  15.2 us
    pallas_call x2, Pallas kernels, grads_of(): pl.pallas_call(functools.partial(grad_kernel, flip, order, len(ties)), ou...  11.9 us
    pallas_call x1, Pallas kernels, scores_of(): pl.pallas_call(score_kernel, out_shape=(arr((2, 1024, 1024), f32), arr((3...  8.77 us
    ppermute x20, waiting for transfers between devices, swap(): return lax.ppermute(a, 'row', [(i, i ^ 1) for i in range(8)])  8.1 us
    pallas_call x1, Pallas kernels, slope_of(): pl.pallas_call(slope_kernel, out_shape=[arr((2, 1024, 1024), bf16), arr((...  3.49 us
    ppermute x1, waiting for transfers between devices, hop_xor(): return lax.ppermute(a, AX, moves(lambda r, x, other: (r ^ 1, x), turn))  2.61 us
  transfers between devices with their start and end apart: 40, of which 19 were waited for; matrix products, arithmetic and copies ran while one was open for 0% of the time, Pallas kernels for 7%

profile of v4, /device:TPU:1, one launch (start us, length us, event | category | flops | bytes accessed | tf_op | source)
XLA Modules:
  0.0 119.0 jit_solution(9864864885417405386)
XLA Ops:
  0.6 0.9 copy-done
  1.6 0.9 copy-done.1
  2.7 1.5 %collective-permute-start = (bf16[128,1024]{1,0:T(8,128)(2,1)S(1)}, bf16[128,1024]{1,0:T(8,128)(2,1)S(1)}, u32[]{:S(2)}, u32[]{:S(2)}) collective-permute-start(bf16[128,1024]{1,0:T(8,128)(2,1)S(1)} %get-tuple-element.34), channel_id=1, source_target_pairs={{0,16},{16,0},{32,48},{48,32},{64,80},{80,64},{96,112},{112,96},{1... | collective-permute-start | bytes 786440 | tf_op jit(solution)/shard_map/ppermute | solution.py:44
  4.2 1.2 collective-permute-done
  5.4 2.9 %collective-permute-start.4 = (bf16[2,128,1024]{2,1,0:T(8,128)(2,1)S(1)}, bf16[2,128,1024]{2,1,0:T(8,128)(2,1)S(1)}, u32[]{:S(2)}, u32[]{:S(2)}) collective-permute-start(bf16[2,128,1024]{2,1,0:T(8,128)(2,1)S(1)} %pad_maximum_fusion.refs_4_), channel_id=1, source_target_pairs={{0,12},{16,112},{1,13},{17,113},{2,14},{18,114},{3,15},{19,115},{4... | collective-permute-start | bytes 1572872 | tf_op jit(solution)/shard_map/ppermute | solution.py:36
  8.3 1.7 %collective-permute-start.12 = (bf16[2,128,1024]{2,1,0:T(8,128)(2,1)S(1)}, bf16[2,128,1024]{2,1,0:T(8,128)(2,1)S(1)}, u32[]{:S(2)}, u32[]{:S(2)}) collective-permute-start(bf16[2,128,1024]{2,1,0:T(8,128)(2,1)S(1)} %pad_maximum_fusion.refs_4_), channel_id=1, source_target_pairs={{0,16},{16,0},{32,48},{48,32},{64,80},{80,64},{96,112},{112,96},{1... | collective-permute-start | bytes 1572872 | tf_op jit(solution)/shard_map/ppermute | solution.py:44
  10.0 2.5 %collective-permute-start.3 = (bf16[2,128,1024]{2,1,0:T(8,128)(2,1)S(1)}, bf16[2,128,1024]{2,1,0:T(8,128)(2,1)S(1)}, u32[]{:S(2)}, u32[]{:S(2)}) collective-permute-start(bf16[2,128,1024]{2,1,0:T(8,128)(2,1)S(1)} %pad_maximum_fusion.refs_4_), channel_id=1, source_target_pairs={{0,1},{16,19},{1,0},{17,18},{2,3},{18,17},{3,2},{19,16},{4,5},{20,... | collective-permute-start | bytes 1572872 | tf_op jit(solution)/shard_map/ppermute | solution.py:36
  12.5 1.3 %collective-permute-start.2 = (bf16[2,128,1024]{2,1,0:T(8,128)(2,1)S(1)}, bf16[2,128,1024]{2,1,0:T(8,128)(2,1)S(1)}, u32[]{:S(2)}, u32[]{:S(2)}) collective-permute-start(bf16[2,128,1024]{2,1,0:T(8,128)(2,1)S(1)} %pad_maximum_fusion.refs_4_), channel_id=1, source_target_pairs={{0,4},{16,48},{1,5},{17,49},{2,6},{18,50},{3,7},{19,51},{4,8},{20,... | collective-permute-start | bytes 1572872 | tf_op jit(solution)/shard_map/ppermute | solution.py:36
  13.8 2.6 %collective-permute-start.1 = (bf16[2,128,1024]{2,1,0:T(8,128)(2,1)S(1)}, bf16[2,128,1024]{2,1,0:T(8,128)(2,1)S(1)}, u32[]{:S(2)}, u32[]{:S(2)}) collective-permute-start(bf16[2,128,1024]{2,1,0:T(8,128)(2,1)S(1)} %pad_maximum_fusion.refs_4_), channel_id=1, source_target_pairs={{0,8},{16,80},{1,9},{17,81},{2,10},{18,82},{3,11},{19,83},{4,12},{... | collective-permute-start | bytes 1572872 | tf_op jit(solution)/shard_map/ppermute | solution.py:36
  16.4 6.0 %collective-permute-start.13 = (bf16[2,128,1024]{2,1,0:T(8,128)(2,1)S(1)}, bf16[2,128,1024]{2,1,0:T(8,128)(2,1)S(1)}, u32[]{:S(2)}, u32[]{:S(2)}) collective-permute-start(bf16[2,128,1024]{2,1,0:T(8,128)(2,1)S(1)} %collective-permute-done.4.refs_5_), channel_id=1, source_target_pairs={{0,16},{16,0},{32,48},{48,32},{64,80},{80,64},{96,112},{112,96},{1... | collective-permute-start | bytes 1572872 | tf_op jit(solution)/shard_map/ppermute | solution.py:44
  22.4 2.5 %collective-permute-start.5 = (bf16[2,128,1024]{2,1,0:T(8,128)(2,1)S(1)}, bf16[2,128,1024]{2,1,0:T(8,128)(2,1)S(1)}, u32[]{:S(2)}, u32[]{:S(2)}) collective-permute-start(bf16[2,128,1024]{2,1,0:T(8,128)(2,1)S(1)} %collective-permute-done.4.refs_5_), channel_id=1, source_target_pairs={{0,1},{16,19},{1,0},{17,18},{2,3},{18,17},{3,2},{19,16},{4,5},{20,... | collective-permute-start | bytes 1572872 | tf_op jit(solution)/shard_map/ppermute | solution.py:36
  24.8 4.5 %collective-permute-start.7 = (bf16[2,128,1024]{2,1,0:T(8,128)(2,1)S(1)}, bf16[2,128,1024]{2,1,0:T(8,128)(2,1)S(1)}, u32[]{:S(2)}, u32[]{:S(2)}) collective-permute-start(bf16[2,128,1024]{2,1,0:T(8,128)(2,1)S(1)} %collective-permute-done.3.refs_2_), channel_id=1, source_target_pairs={{0,8},{16,80},{1,9},{17,81},{2,10},{18,82},{3,11},{19,83},{4,12},{... | collective-permute-start | bytes 1572872 | tf_op jit(solution)/shard_map/ppermute | solution.py:36
  29.5 2.3 %collective-permute-done.5.refs_3_ = bf16[2,128,1024]{2,1,0:T(8,128)(2,1)S(1)} collective-permute-done((bf16[2,128,1024]{2,1,0:T(8,128)(2,1)S(1)}, bf16[2,128,1024]{2,1,0:T(8,128)(2,1)S(1)}, u32[]{:S(2)}, u32[]{:S(2)}) %collective-permute-start.5) | collective-permute-done | bytes 524320 | tf_op jit(solution)/shard_map/ppermute | solution.py:36
  31.9 0.5 collective-permute-start.11
  32.4 3.5 %collective-permute-done.7.refs_7_ = bf16[2,128,1024]{2,1,0:T(8,128)(2,1)S(1)} collective-permute-done((bf16[2,128,1024]{2,1,0:T(8,128)(2,1)S(1)}, bf16[2,128,1024]{2,1,0:T(8,128)(2,1)S(1)}, u32[]{:S(2)}, u32[]{:S(2)}) %collective-permute-start.7) | collective-permute-done | bytes 524320 | tf_op jit(solution)/shard_map/ppermute | solution.py:36
  36.2 2.4 %collective-permute-done.6.refs_6_ = bf16[2,128,1024]{2,1,0:T(8,128)(2,1)S(1)} collective-permute-done((bf16[2,128,1024]{2,1,0:T(8,128)(2,1)S(1)}, bf16[2,128,1024]{2,1,0:T(8,128)(2,1)S(1)}, u32[]{:S(2)}, u32[]{:S(2)}) %collective-permute-start.6) | collective-permute-done | bytes 524320 | tf_op jit(solution)/shard_map/ppermute | solution.py:36
  38.6 0.7 copy-done.2
  39.5 1.0 collective-permute-done.14.refs_14_
  40.5 8.8 %scores.1 = (f32[2,1024,1024]{2,1,0:T(8,128)S(1)}, f32[3,2048]{1,0:T(4,128)S(1)}, f32[3,2048]{1,0:T(4,128)S(1)}, bf16[1024,1024]{1,0:T(8,128)(2,1)S(1)}, bf16[2,1024,1024]{2,1,0:T(8,128)(2,1)S(1)}) custom-call(bf16[2,128,1024]{2,1,0:T(8,128)(2,1)S(1)} %collective-permute-done.1.refs_0_, bf16[2,128,1024]{2,1,0:T(8,128)(2,1)S(1)} %collective-permute-done.2.refs_1_, ...), custom_call_target="tpu_custom_call" | custom-call | flops 4294967296 | bytes 16777216 | tf_op jit(solution)/shard_map/scores/pallas_call | solution.py:271
  49.4 1.1 collective-permute-done.16.refs_1_
  50.6 1.2 collective-permute-start.17
  51.7 0.7 flip.1.refs_2_.refs_1_
  52.4 2.2 %collective-permute-done.17.refs_1_ = f32[3,2048]{1,0:T(4,128)S(1)} collective-permute-done((f32[3,2048]{1,0:T(4,128)S(1)}, f32[3,2048]{1,0:T(4,128)S(1)}, u32[]{:S(2)}, u32[]{:S(2)}) %collective-permute-start.17) | collective-permute-done | bytes 24608 | tf_op jit(solution)/shard_map/ppermute | solution.py:36
  54.6 2.8 %collective-permute-start.20 = (f32[3,2048]{1,0:T(4,128)S(1)}, f32[3,2048]{1,0:T(4,128)S(1)}, u32[]{:S(2)}, u32[]{:S(2)}) collective-permute-start(f32[3,2048]{1,0:T(4,128)S(1)} %merge.4.refs_0_), channel_id=1, source_target_pairs={{0,12},{16,112},{1,13},{17,113},{2,14},{18,114},{3,15},{19,115},{4... | collective-permute-start | bytes 73736 | tf_op jit(solution)/shard_map/ppermute | solution.py:36
  57.4 1.6 %collective-permute-start.18 = (f32[3,2048]{1,0:T(4,128)S(1)}, f32[3,2048]{1,0:T(4,128)S(1)}, u32[]{:S(2)}, u32[]{:S(2)}) collective-permute-start(f32[3,2048]{1,0:T(4,128)S(1)} %merge.4.refs_0_), channel_id=1, source_target_pairs={{0,8},{16,80},{1,9},{17,81},{2,10},{18,82},{3,11},{19,83},{4,12},{... | collective-permute-start | bytes 73736 | tf_op jit(solution)/shard_map/ppermute | solution.py:36
  59.1 2.6 %collective-permute-done.19.refs_2_ = f32[3,2048]{1,0:T(4,128)S(1)} collective-permute-done((f32[3,2048]{1,0:T(4,128)S(1)}, f32[3,2048]{1,0:T(4,128)S(1)}, u32[]{:S(2)}, u32[]{:S(2)}) %collective-permute-start.19) | collective-permute-done | bytes 24608 | tf_op jit(solution)/shard_map/ppermute | solution.py:36
  62.1 0.6 collective-permute-start.21
  62.7 0.8 collective-permute-done.21.got_lse
  63.5 3.5 %slope.1 = (bf16[2,1024,1024]{2,1,0:T(8,128)(2,1)S(1)}, f32[8,128]{1,0:T(8,128)S(1)}) custom-call(f32[2,1024,1024]{2,1,0:T(8,128)S(1)} %get-tuple-element.35.sv, f32[1024,128]{1,0:T(8,128)S(1)} %aims.1.refs_16_.target, f32[1,2048]{1,0:T(1,128)S(1)} %get-tuple-element.39.own_lse, f32[1,2048]{1,0:T(1,128)S(1)} %collective-permute-done.21.got_lse, ...), custom_call_target="tpu_custom_call" | custom-call | flops 4294967296 | bytes 12582912 | tf_op jit(solution)/shard_map/slope/pallas_call | solution.py:395
  67.0 6.2 %grads_far.1 = (bf16[2,2,128,1024]{3,2,1,0:T(8,128)(2,1)S(1)}, bf16[1,2,128,1024]{3,2,1,0:T(8,128)(2,1)S(1)}, bf16[1,2,128,1024]{3,2,1,0:T(8,128)(2,1)S(1)}, bf1...) custom-call(bf16[2,1024,1024]{2,1,0:T(8,128)(2,1)S(1)} %get-tuple-el, ...), custom_call_target="tpu_custom_call" | custom-call | flops 4294967296 | bytes 20971520 | tf_op jit(solution)/shard_map/grads_far/pallas_call | solution.py:409
  73.9 2.9 %collective-permute-done.25.refs_1_ = bf16[1,2,128,1024]{3,2,1,0:T(8,128)(2,1)S(1)} collective-permute-done((bf16[1,2,128,1024]{3,2,1,0:T(8,128)(2,1)S(1)}, bf16[1,2,128,1024]{3,2,1,0:T(8,128)(2,1)S(1)}, u32[]{:S(2)}, u32[]{:S(2)}) %collective-permute-start.25) | collective-permute-done | bytes 524320 | tf_op jit(solution)/shard_map/ppermute | solution.py:44
  76.9 3.0 %collective-permute-start.26 = (bf16[1,2,128,1024]{3,2,1,0:T(8,128)(2,1)S(1)}, bf16[1,2,128,1024]{3,2,1,0:T(8,128)(2,1)S(1)}, u32[]{:S(2)}, u32[]{:S(2)}) collective-permute-start(bf16[1,2,128,1024]{3,2,1,0:T(8,128)(2,1)S(1)} %join.8), channel_id=1, source_target_pairs={{0,8},{16,80},{1,9},{17,81},{2,10},{18,82},{3,11},{19,83},{4,12},{... | collective-permute-start | bytes 1572872 | tf_op jit(solution)/shard_map/ppermute | solution.py:36
  80.1 2.6 %collective-permute-start.35 = (bf16[2,2,128,1024]{3,2,1,0:T(8,128)(2,1)S(1)}, bf16[2,2,128,1024]{3,2,1,0:T(8,128)(2,1)S(1)}, u32[]{:S(2)}, u32[]{:S(2)}) collective-permute-start(bf16[2,2,128,1024]{3,2,1,0:T(8,128)(2,1)S(1)} %join.7.refs_4_), channel_id=1, source_target_pairs={{0,1},{16,19},{1,0},{17,18},{2,3},{18,17},{3,2},{19,16},{4,5},{20,... | collective-permute-start | bytes 3145736 | tf_op jit(solution)/shard_map/ppermute | solution.py:36
  82.9 2.6 %collective-permute-done.22 = f32[8,128]{1,0:T(8,128)S(1)} collective-permute-done((f32[8,128]{1,0:T(8,128)S(1)}, f32[8,128]{1,0:T(8,128)S(1)}, u32[]{:S(2)}, u32[]{:S(2)}) %collective-permute-start.22) | collective-permute-done | bytes 4128 | tf_op jit(solution)/shard_map/ppermute | solution.py:40
  85.5 2.6 %collective-permute-start.23 = (f32[8,128]{1,0:T(8,128)S(1)}, f32[8,128]{1,0:T(8,128)S(1)}, u32[]{:S(2)}, u32[]{:S(2)}) collective-permute-start(f32[8,128]{1,0:T(8,128)S(1)} %add.12), channel_id=1, source_target_pairs={{16,24},{0,64},{17,25},{1,65},{18,26},{2,66},{19,27},{3,67},{20,28... | collective-permute-start | bytes 12296 | tf_op jit(solution)/shard_map/ppermute | solution.py:36
  88.2 1.3 %collective-permute-done.23 = f32[8,128]{1,0:T(8,128)S(1)} collective-permute-done((f32[8,128]{1,0:T(8,128)S(1)}, f32[8,128]{1,0:T(8,128)S(1)}, u32[]{:S(2)}, u32[]{:S(2)}) %collective-permute-start.23) | collective-permute-done | bytes 4128 | tf_op jit(solution)/shard_map/ppermute | solution.py:36
  89.5 5.7 %grads_near.1 = (bf16[1,2,128,1024]{3,2,1,0:T(8,128)(2,1)S(1)}, bf16[1,2,128,1024]{3,2,1,0:T(8,128)(2,1)S(1)}, bf16[1,2,128,1024]{3,2,1,0:T(8,128)(2,1)S(1)}, bf...) custom-call(bf16[2,1024,1024]{2,1,0:T(8,128)(2,1)S(1)} %get-tuple-el, ...), custom_call_target="tpu_custom_call" | custom-call | flops 4294967296 | bytes 20971520 | tf_op jit(solution)/shard_map/grads_near/pallas_call | solution.py:409
  96.1 1.7 %collective-permute-start.28 = (bf16[1,2,128,1024]{3,2,1,0:T(8,128)(2,1)S(1)}, bf16[1,2,128,1024]{3,2,1,0:T(8,128)(2,1)S(1)}, u32[]{:S(2)}, u32[]{:S(2)}) collective-permute-start(bf16[1,2,128,1024]{3,2,1,0:T(8,128)(2,1)S(1)} %join.9), channel_id=1, source_target_pairs={{0,1},{16,19},{1,0},{17,18},{2,3},{18,17},{3,2},{19,16},{4,5},{20,... | collective-permute-start | bytes 1572872 | tf_op jit(solution)/shard_map/ppermute | solution.py:36
  97.9 3.0 %collective-permute-start.33 = (bf16[1,2,128,1024]{3,2,1,0:T(8,128)(2,1)S(1)}, bf16[1,2,128,1024]{3,2,1,0:T(8,128)(2,1)S(1)}, u32[]{:S(2)}, u32[]{:S(2)}) collective-permute-start(bf16[1,2,128,1024]{3,2,1,0:T(8,128)(2,1)S(1)} %join.11), channel_id=1, source_target_pairs={{0,8},{16,80},{1,9},{17,81},{2,10},{18,82},{3,11},{19,83},{4,12},{... | collective-permute-start | bytes 1572872 | tf_op jit(solution)/shard_map/ppermute | solution.py:36
  101.8 2.3 %collective-permute-start.38 = (bf16[1,2,128,1024]{3,2,1,0:T(8,128)(2,1)S(1)}, bf16[1,2,128,1024]{3,2,1,0:T(8,128)(2,1)S(1)}, u32[]{:S(2)}, u32[]{:S(2)}) collective-permute-start(bf16[1,2,128,1024]{3,2,1,0:T(8,128)(2,1)S(1)} %join.13), channel_id=1, source_target_pairs={{0,12},{16,112},{1,13},{17,113},{2,14},{18,114},{3,15},{19,115},{4... | collective-permute-start | bytes 1572872 | tf_op jit(solution)/shard_map/ppermute | solution.py:36
  104.1 1.8 %collective-permute-done.28.refs_0_.refs_2_ = bf16[1,2,128,1024]{3,2,1,0:T(8,128)(2,1)S(1)} collective-permute-done((bf16[1,2,128,1024]{3,2,1,0:T(8,128)(2,1)S(1)}, bf16[1,2,128,1024]{3,2,1,0:T(8,128)(2,1)S(1)}, u32[]{:S(2)}, u32[]{:S(2)}) %collective-permute-start.28) | collective-permute-done | bytes 524320 | tf_op jit(solution)/shard_map/ppermute | solution.py:36
  105.9 2.7 %collective-permute-done.29 = f32[8,128]{1,0:T(8,128)S(1)} collective-permute-done((f32[8,128]{1,0:T(8,128)S(1)}, f32[8,128]{1,0:T(8,128)S(1)}, u32[]{:S(2)}, u32[]{:S(2)}) %collective-permute-start.29) | collective-permute-done | bytes 4128 | tf_op jit(solution)/shard_map/ppermute | solution.py:36
  108.7 2.1 %collective-permute-start.30 = (f32[8,128]{1,0:T(8,128)S(1)}, f32[8,128]{1,0:T(8,128)S(1)}, u32[]{:S(2)}, u32[]{:S(2)}) collective-permute-start(f32[8,128]{1,0:T(8,128)S(1)} %add.14), channel_id=1, source_target_pairs={{0,16},{16,0},{32,48},{48,32},{64,80},{80,64},{96,112},{112,96},{1... | collective-permute-start | bytes 12296 | tf_op jit(solution)/shard_map/ppermute | solution.py:44
  110.9 0.7 collective-permute-done.30
  111.6 1.8 %collective-permute-done.36.refs_3_ = bf16[1,2,128,1024]{3,2,1,0:T(8,128)(2,1)S(1)} collective-permute-done((bf16[1,2,128,1024]{3,2,1,0:T(8,128)(2,1)S(1)}, bf16[1,2,128,1024]{3,2,1,0:T(8,128)(2,1)S(1)}, u32[]{:S(2)}, u32[]{:S(2)}) %collective-permute-start.36) | collective-permute-done | bytes 524320 | tf_op jit(solution)/shard_map/ppermute | solution.py:36
  114.2 1.1 collective-permute-start.39
  115.3 0.5 slice.3
  116.8 1.1 finish.1
  (64 shorter events, 5.9 us)
Async XLA Ops:
  0.6 1.0 copy-start
  1.6 0.9 copy-start.1
  2.7 2.7 %collective-permute-start = (bf16[128,1024]{1,0:T(8,128)(2,1)S(1)}, bf16[128,1024]{1,0:T(8,128)(2,1)S(1)}, u32[]{:S(2)}, u32[]{:S(2)}) collective-permute-start(bf16[128,1024]{1,0:T(8,128)(2,1)S(1)} %get-tuple-element.34), channel_id=1, source_target_pairs={{0,16},{16,0},{32,48},{48,32},{64,80},{80,64},{96,112},{112,96},{1... | collective-permute-start | bytes 786440 | tf_op jit(solution)/shard_map/ppermute | solution.py:44
  5.4 11.0 %collective-permute-start.4 = (bf16[2,128,1024]{2,1,0:T(8,128)(2,1)S(1)}, bf16[2,128,1024]{2,1,0:T(8,128)(2,1)S(1)}, u32[]{:S(2)}, u32[]{:S(2)}) collective-permute-start(bf16[2,128,1024]{2,1,0:T(8,128)(2,1)S(1)} %pad_maximum_fusion.refs_4_), channel_id=1, source_target_pairs={{0,12},{16,112},{1,13},{17,113},{2,14},{18,114},{3,15},{19,115},{4... | collective-permute-start | bytes 1572872 | tf_op jit(solution)/shard_map/ppermute | solution.py:36
  8.3 14.0 %collective-permute-start.12 = (bf16[2,128,1024]{2,1,0:T(8,128)(2,1)S(1)}, bf16[2,128,1024]{2,1,0:T(8,128)(2,1)S(1)}, u32[]{:S(2)}, u32[]{:S(2)}) collective-permute-start(bf16[2,128,1024]{2,1,0:T(8,128)(2,1)S(1)} %pad_maximum_fusion.refs_4_), channel_id=1, source_target_pairs={{0,16},{16,0},{32,48},{48,32},{64,80},{80,64},{96,112},{112,96},{1... | collective-permute-start | bytes 1572872 | tf_op jit(solution)/shard_map/ppermute | solution.py:44
  10.0 14.8 %collective-permute-start.3 = (bf16[2,128,1024]{2,1,0:T(8,128)(2,1)S(1)}, bf16[2,128,1024]{2,1,0:T(8,128)(2,1)S(1)}, u32[]{:S(2)}, u32[]{:S(2)}) collective-permute-start(bf16[2,128,1024]{2,1,0:T(8,128)(2,1)S(1)} %pad_maximum_fusion.refs_4_), channel_id=1, source_target_pairs={{0,1},{16,19},{1,0},{17,18},{2,3},{18,17},{3,2},{19,16},{4,5},{20,... | collective-permute-start | bytes 1572872 | tf_op jit(solution)/shard_map/ppermute | solution.py:36
  12.5 12.4 %collective-permute-start.2 = (bf16[2,128,1024]{2,1,0:T(8,128)(2,1)S(1)}, bf16[2,128,1024]{2,1,0:T(8,128)(2,1)S(1)}, u32[]{:S(2)}, u32[]{:S(2)}) collective-permute-start(bf16[2,128,1024]{2,1,0:T(8,128)(2,1)S(1)} %pad_maximum_fusion.refs_4_), channel_id=1, source_target_pairs={{0,4},{16,48},{1,5},{17,49},{2,6},{18,50},{3,7},{19,51},{4,8},{20,... | collective-permute-start | bytes 1572872 | tf_op jit(solution)/shard_map/ppermute | solution.py:36
  13.8 15.6 %collective-permute-start.1 = (bf16[2,128,1024]{2,1,0:T(8,128)(2,1)S(1)}, bf16[2,128,1024]{2,1,0:T(8,128)(2,1)S(1)}, u32[]{:S(2)}, u32[]{:S(2)}) collective-permute-start(bf16[2,128,1024]{2,1,0:T(8,128)(2,1)S(1)} %pad_maximum_fusion.refs_4_), channel_id=1, source_target_pairs={{0,8},{16,80},{1,9},{17,81},{2,10},{18,82},{3,11},{19,83},{4,12},{... | collective-permute-start | bytes 1572872 | tf_op jit(solution)/shard_map/ppermute | solution.py:36
  16.4 13.1 %collective-permute-start.13 = (bf16[2,128,1024]{2,1,0:T(8,128)(2,1)S(1)}, bf16[2,128,1024]{2,1,0:T(8,128)(2,1)S(1)}, u32[]{:S(2)}, u32[]{:S(2)}) collective-permute-start(bf16[2,128,1024]{2,1,0:T(8,128)(2,1)S(1)} %collective-permute-done.4.refs_5_), channel_id=1, source_target_pairs={{0,16},{16,0},{32,48},{48,32},{64,80},{80,64},{96,112},{112,96},{1... | collective-permute-start | bytes 1572872 | tf_op jit(solution)/shard_map/ppermute | solution.py:44
  22.4 9.5 %collective-permute-start.5 = (bf16[2,128,1024]{2,1,0:T(8,128)(2,1)S(1)}, bf16[2,128,1024]{2,1,0:T(8,128)(2,1)S(1)}, u32[]{:S(2)}, u32[]{:S(2)}) collective-permute-start(bf16[2,128,1024]{2,1,0:T(8,128)(2,1)S(1)} %collective-permute-done.4.refs_5_), channel_id=1, source_target_pairs={{0,1},{16,19},{1,0},{17,18},{2,3},{18,17},{3,2},{19,16},{4,5},{20,... | collective-permute-start | bytes 1572872 | tf_op jit(solution)/shard_map/ppermute | solution.py:36
  24.8 7.1 %collective-permute-start.10 = (bf16[2,128,1024]{2,1,0:T(8,128)(2,1)S(1)}, bf16[2,128,1024]{2,1,0:T(8,128)(2,1)S(1)}, u32[]{:S(2)}, u32[]{:S(2)}) collective-permute-start(bf16[2,128,1024]{2,1,0:T(8,128)(2,1)S(1)} %collective-permute-done.3.refs_2_), channel_id=1, source_target_pairs={{0,16},{16,0},{32,48},{48,32},{64,80},{80,64},{96,112},{112,96},{1... | collective-permute-start | bytes 1572872 | tf_op jit(solution)/shard_map/ppermute | solution.py:44
  24.8 11.1 %collective-permute-start.7 = (bf16[2,128,1024]{2,1,0:T(8,128)(2,1)S(1)}, bf16[2,128,1024]{2,1,0:T(8,128)(2,1)S(1)}, u32[]{:S(2)}, u32[]{:S(2)}) collective-permute-start(bf16[2,128,1024]{2,1,0:T(8,128)(2,1)S(1)} %collective-permute-done.3.refs_2_), channel_id=1, source_target_pairs={{0,8},{16,80},{1,9},{17,81},{2,10},{18,82},{3,11},{19,83},{4,12},{... | collective-permute-start | bytes 1572872 | tf_op jit(solution)/shard_map/ppermute | solution.py:36
  29.3 9.2 %collective-permute-start.6 = (bf16[2,128,1024]{2,1,0:T(8,128)(2,1)S(1)}, bf16[2,128,1024]{2,1,0:T(8,128)(2,1)S(1)}, u32[]{:S(2)}, u32[]{:S(2)}) collective-permute-start(bf16[2,128,1024]{2,1,0:T(8,128)(2,1)S(1)} %collective-permute-done.2.refs_1_), channel_id=1, source_target_pairs={{0,1},{16,19},{1,0},{17,18},{2,3},{18,17},{3,2},{19,16},{4,5},{20,... | collective-permute-start | bytes 1572872 | tf_op jit(solution)/shard_map/ppermute | solution.py:36
  29.5 9.9 %collective-permute-start.9 = (bf16[2,128,1024]{2,1,0:T(8,128)(2,1)S(1)}, bf16[2,128,1024]{2,1,0:T(8,128)(2,1)S(1)}, u32[]{:S(2)}, u32[]{:S(2)}) collective-permute-start(bf16[2,128,1024]{2,1,0:T(8,128)(2,1)S(1)} %collective-permute-done.2.refs_1_), channel_id=1, source_target_pairs={{0,16},{16,0},{32,48},{48,32},{64,80},{80,64},{96,112},{112,96},{1... | collective-permute-start | bytes 1572872 | tf_op jit(solution)/shard_map/ppermute | solution.py:44
  31.9 7.6 %collective-permute-start.8 = (bf16[2,128,1024]{2,1,0:T(8,128)(2,1)S(1)}, bf16[2,128,1024]{2,1,0:T(8,128)(2,1)S(1)}, u32[]{:S(2)}, u32[]{:S(2)}) collective-permute-start(bf16[2,128,1024]{2,1,0:T(8,128)(2,1)S(1)} %collective-permute-done.1.refs_0_), channel_id=1, source_target_pairs={{0,16},{16,0},{32,48},{48,32},{64,80},{80,64},{96,112},{112,96},{1... | collective-permute-start | bytes 1572872 | tf_op jit(solution)/shard_map/ppermute | solution.py:44
  31.9 7.6 %collective-permute-start.11 = (bf16[2,128,1024]{2,1,0:T(8,128)(2,1)S(1)}, bf16[2,128,1024]{2,1,0:T(8,128)(2,1)S(1)}, u32[]{:S(2)}, u32[]{:S(2)}) collective-permute-start(bf16[2,128,1024]{2,1,0:T(8,128)(2,1)S(1)} %collective-permute-done.5.refs_3_), channel_id=1, source_target_pairs={{0,16},{16,0},{32,48},{48,32},{64,80},{80,64},{96,112},{112,96},{1... | collective-permute-start | bytes 1572872 | tf_op jit(solution)/shard_map/ppermute | solution.py:44
  35.9 3.6 %collective-permute-start.15 = (bf16[2,128,1024]{2,1,0:T(8,128)(2,1)S(1)}, bf16[2,128,1024]{2,1,0:T(8,128)(2,1)S(1)}, u32[]{:S(2)}, u32[]{:S(2)}) collective-permute-start(bf16[2,128,1024]{2,1,0:T(8,128)(2,1)S(1)} %collective-permute-done.7.refs_7_), channel_id=1, source_target_pairs={{0,16},{16,0},{32,48},{48,32},{64,80},{80,64},{96,112},{112,96},{1... | collective-permute-start | bytes 1572872 | tf_op jit(solution)/shard_map/ppermute | solution.py:44
  38.6 1.9 %collective-permute-start.14 = (bf16[2,128,1024]{2,1,0:T(8,128)(2,1)S(1)}, bf16[2,128,1024]{2,1,0:T(8,128)(2,1)S(1)}, u32[]{:S(2)}, u32[]{:S(2)}) collective-permute-start(bf16[2,128,1024]{2,1,0:T(8,128)(2,1)S(1)} %collective-permute-done.6.refs_6_), channel_id=1, source_target_pairs={{0,16},{16,0},{32,48},{48,32},{64,80},{80,64},{96,112},{112,96},{1... | collective-permute-start | bytes 1572872 | tf_op jit(solution)/shard_map/ppermute | solution.py:44
  38.6 0.7 copy-start.2
  49.3 1.3 %collective-permute-start.16 = (f32[3,2048]{1,0:T(4,128)S(1)}, f32[3,2048]{1,0:T(4,128)S(1)}, u32[]{:S(2)}, u32[]{:S(2)}) collective-permute-start(f32[3,2048]{1,0:T(4,128)S(1)} %get-tuple-element.37), channel_id=1, source_target_pairs={{0,16},{16,0},{32,48},{48,32},{64,80},{80,64},{96,112},{112,96},{1... | collective-permute-start | bytes 73736 | tf_op jit(solution)/shard_map/ppermute | solution.py:44
  50.6 4.1 %collective-permute-start.17 = (f32[3,2048]{1,0:T(4,128)S(1)}, f32[3,2048]{1,0:T(4,128)S(1)}, u32[]{:S(2)}, u32[]{:S(2)}) collective-permute-start(f32[3,2048]{1,0:T(4,128)S(1)} %merge.3.refs_0_), channel_id=1, source_target_pairs={{0,1},{16,19},{1,0},{17,18},{2,3},{18,17},{3,2},{19,16},{4,5},{20,... | collective-permute-start | bytes 73736 | tf_op jit(solution)/shard_map/ppermute | solution.py:36
  54.6 4.4 %collective-permute-start.20 = (f32[3,2048]{1,0:T(4,128)S(1)}, f32[3,2048]{1,0:T(4,128)S(1)}, u32[]{:S(2)}, u32[]{:S(2)}) collective-permute-start(f32[3,2048]{1,0:T(4,128)S(1)} %merge.4.refs_0_), channel_id=1, source_target_pairs={{0,12},{16,112},{1,13},{17,113},{2,14},{18,114},{3,15},{19,115},{4... | collective-permute-start | bytes 73736 | tf_op jit(solution)/shard_map/ppermute | solution.py:36
  57.4 4.3 %collective-permute-start.19 = (f32[3,2048]{1,0:T(4,128)S(1)}, f32[3,2048]{1,0:T(4,128)S(1)}, u32[]{:S(2)}, u32[]{:S(2)}) collective-permute-start(f32[3,2048]{1,0:T(4,128)S(1)} %merge.4.refs_0_), channel_id=1, source_target_pairs={{0,4},{16,48},{1,5},{17,49},{2,6},{18,50},{3,7},{19,51},{4,8},{20,... | collective-permute-start | bytes 73736 | tf_op jit(solution)/shard_map/ppermute | solution.py:36
  57.4 4.6 %collective-permute-start.18 = (f32[3,2048]{1,0:T(4,128)S(1)}, f32[3,2048]{1,0:T(4,128)S(1)}, u32[]{:S(2)}, u32[]{:S(2)}) collective-permute-start(f32[3,2048]{1,0:T(4,128)S(1)} %merge.4.refs_0_), channel_id=1, source_target_pairs={{0,8},{16,80},{1,9},{17,81},{2,10},{18,82},{3,11},{19,83},{4,12},{... | collective-permute-start | bytes 73736 | tf_op jit(solution)/shard_map/ppermute | solution.py:36
  62.1 1.4 %collective-permute-start.21 = (f32[1,2048]{1,0:T(1,128)S(1)}, f32[1,2048]{1,0:T(1,128)S(1)}, u32[]{:S(2)}, u32[]{:S(2)}) collective-permute-start(f32[1,2048]{1,0:T(1,128)S(1)} %get-tuple-element.39.own_lse), channel_id=1, source_target_pairs={{0,16},{16,0},{32,48},{48,32},{64,80},{80,64},{96,112},{112,96},{1... | collective-permute-start | bytes 24584 | tf_op jit(solution)/shard_map/ppermute | solution.py:44
  73.3 6.6 %collective-permute-start.24 = (bf16[2,2,128,1024]{3,2,1,0:T(8,128)(2,1)S(1)}, bf16[2,2,128,1024]{3,2,1,0:T(8,128)(2,1)S(1)}, u32[]{:S(2)}, u32[]{:S(2)}) collective-permute-start(bf16[2,2,128,1024]{3,2,1,0:T(8,128)(2,1)S(1)} %get-tuple-element.45), channel_id=1, source_target_pairs={{0,16},{16,0},{32,48},{48,32},{64,80},{80,64},{96,112},{112,96},{1... | collective-permute-start | bytes 3145736 | tf_op jit(solution)/shard_map/ppermute | solution.py:44
  73.7 3.1 %collective-permute-start.25 = (bf16[1,2,128,1024]{3,2,1,0:T(8,128)(2,1)S(1)}, bf16[1,2,128,1024]{3,2,1,0:T(8,128)(2,1)S(1)}, u32[]{:S(2)}, u32[]{:S(2)}) collective-permute-start(bf16[1,2,128,1024]{3,2,1,0:T(8,128)(2,1)S(1)} %get-tuple-element.47), channel_id=1, source_target_pairs={{0,16},{16,0},{32,48},{48,32},{64,80},{80,64},{96,112},{112,96},{1... | collective-permute-start | bytes 1572872 | tf_op jit(solution)/shard_map/ppermute | solution.py:44
  76.9 12.6 %collective-permute-start.26 = (bf16[1,2,128,1024]{3,2,1,0:T(8,128)(2,1)S(1)}, bf16[1,2,128,1024]{3,2,1,0:T(8,128)(2,1)S(1)}, u32[]{:S(2)}, u32[]{:S(2)}) collective-permute-start(bf16[1,2,128,1024]{3,2,1,0:T(8,128)(2,1)S(1)} %join.8), channel_id=1, source_target_pairs={{0,8},{16,80},{1,9},{17,81},{2,10},{18,82},{3,11},{19,83},{4,12},{... | collective-permute-start | bytes 1572872 | tf_op jit(solution)/shard_map/ppermute | solution.py:36
  80.1 20.8 %collective-permute-start.35 = (bf16[2,2,128,1024]{3,2,1,0:T(8,128)(2,1)S(1)}, bf16[2,2,128,1024]{3,2,1,0:T(8,128)(2,1)S(1)}, u32[]{:S(2)}, u32[]{:S(2)}) collective-permute-start(bf16[2,2,128,1024]{3,2,1,0:T(8,128)(2,1)S(1)} %join.7.refs_4_), channel_id=1, source_target_pairs={{0,1},{16,19},{1,0},{17,18},{2,3},{18,17},{3,2},{19,16},{4,5},{20,... | collective-permute-start | bytes 3145736 | tf_op jit(solution)/shard_map/ppermute | solution.py:36
  82.7 2.9 %collective-permute-start.22 = (f32[8,128]{1,0:T(8,128)S(1)}, f32[8,128]{1,0:T(8,128)S(1)}, u32[]{:S(2)}, u32[]{:S(2)}) collective-permute-start(f32[8,128]{1,0:T(8,128)S(1)} %get-tuple-element.43.refs_3_), channel_id=1, source_target_pairs={{16,20},{0,32},{17,21},{1,33},{18,22},{2,34},{19,23},{3,35},{20,16... | collective-permute-start | bytes 12296 | tf_op jit(solution)/shard_map/ppermute | solution.py:40
  85.5 4.0 %collective-permute-start.23 = (f32[8,128]{1,0:T(8,128)S(1)}, f32[8,128]{1,0:T(8,128)S(1)}, u32[]{:S(2)}, u32[]{:S(2)}) collective-permute-start(f32[8,128]{1,0:T(8,128)S(1)} %add.12), channel_id=1, source_target_pairs={{16,24},{0,64},{17,25},{1,65},{18,26},{2,66},{19,27},{3,67},{20,28... | collective-permute-start | bytes 12296 | tf_op jit(solution)/shard_map/ppermute | solution.py:36
  88.2 7.7 %collective-permute-start.27 = (bf16[1,2,128,1024]{3,2,1,0:T(8,128)(2,1)S(1)}, bf16[1,2,128,1024]{3,2,1,0:T(8,128)(2,1)S(1)}, u32[]{:S(2)}, u32[]{:S(2)}) collective-permute-start(bf16[1,2,128,1024]{3,2,1,0:T(8,128)(2,1)S(1)} %get-tuple-element.50), channel_id=1, source_target_pairs={{0,16},{16,0},{32,48},{48,32},{64,80},{80,64},{96,112},{112,96},{1... | collective-permute-start | bytes 1572872 | tf_op jit(solution)/shard_map/ppermute | solution.py:44
  95.2 2.6 %collective-permute-start.32 = (bf16[1,2,128,1024]{3,2,1,0:T(8,128)(2,1)S(1)}, bf16[1,2,128,1024]{3,2,1,0:T(8,128)(2,1)S(1)}, u32[]{:S(2)}, u32[]{:S(2)}) collective-permute-start(bf16[1,2,128,1024]{3,2,1,0:T(8,128)(2,1)S(1)} %get-tuple-element.54), channel_id=1, source_target_pairs={{0,16},{16,0},{32,48},{48,32},{64,80},{80,64},{96,112},{112,96},{1... | collective-permute-start | bytes 1572872 | tf_op jit(solution)/shard_map/ppermute | solution.py:44
  95.3 2.6 %collective-permute-start.34 = (bf16[1,2,128,1024]{3,2,1,0:T(8,128)(2,1)S(1)}, bf16[1,2,128,1024]{3,2,1,0:T(8,128)(2,1)S(1)}, u32[]{:S(2)}, u32[]{:S(2)}) collective-permute-start(bf16[1,2,128,1024]{3,2,1,0:T(8,128)(2,1)S(1)} %get-tuple-element.56), channel_id=1, source_target_pairs={{0,16},{16,0},{32,48},{48,32},{64,80},{80,64},{96,112},{112,96},{1... | collective-permute-start | bytes 1572872 | tf_op jit(solution)/shard_map/ppermute | solution.py:44
  95.8 5.8 %collective-permute-start.37 = (bf16[1,2,128,1024]{3,2,1,0:T(8,128)(2,1)S(1)}, bf16[1,2,128,1024]{3,2,1,0:T(8,128)(2,1)S(1)}, u32[]{:S(2)}, u32[]{:S(2)}) collective-permute-start(bf16[1,2,128,1024]{3,2,1,0:T(8,128)(2,1)S(1)} %get-tuple-element.58), channel_id=1, source_target_pairs={{0,16},{16,0},{32,48},{48,32},{64,80},{80,64},{96,112},{112,96},{1... | collective-permute-start | bytes 1572872 | tf_op jit(solution)/shard_map/ppermute | solution.py:44
  96.1 9.8 %collective-permute-start.28 = (bf16[1,2,128,1024]{3,2,1,0:T(8,128)(2,1)S(1)}, bf16[1,2,128,1024]{3,2,1,0:T(8,128)(2,1)S(1)}, u32[]{:S(2)}, u32[]{:S(2)}) collective-permute-start(bf16[1,2,128,1024]{3,2,1,0:T(8,128)(2,1)S(1)} %join.9), channel_id=1, source_target_pairs={{0,1},{16,19},{1,0},{17,18},{2,3},{18,17},{3,2},{19,16},{4,5},{20,... | collective-permute-start | bytes 1572872 | tf_op jit(solution)/shard_map/ppermute | solution.py:36
  97.7 13.1 %collective-permute-start.31 = (bf16[1,2,128,1024]{3,2,1,0:T(8,128)(2,1)S(1)}, bf16[1,2,128,1024]{3,2,1,0:T(8,128)(2,1)S(1)}, u32[]{:S(2)}, u32[]{:S(2)}) collective-permute-start(bf16[1,2,128,1024]{3,2,1,0:T(8,128)(2,1)S(1)} %get-tuple-element.52), channel_id=1, source_target_pairs={{0,16},{16,0},{32,48},{48,32},{64,80},{80,64},{96,112},{112,96},{1... | collective-permute-start | bytes 1572872 | tf_op jit(solution)/shard_map/ppermute | solution.py:44
  97.9 13.7 %collective-permute-start.33 = (bf16[1,2,128,1024]{3,2,1,0:T(8,128)(2,1)S(1)}, bf16[1,2,128,1024]{3,2,1,0:T(8,128)(2,1)S(1)}, u32[]{:S(2)}, u32[]{:S(2)}) collective-permute-start(bf16[1,2,128,1024]{3,2,1,0:T(8,128)(2,1)S(1)} %join.11), channel_id=1, source_target_pairs={{0,8},{16,80},{1,9},{17,81},{2,10},{18,82},{3,11},{19,83},{4,12},{... | collective-permute-start | bytes 1572872 | tf_op jit(solution)/shard_map/ppermute | solution.py:36
  101.1 12.3 %collective-permute-start.36 = (bf16[1,2,128,1024]{3,2,1,0:T(8,128)(2,1)S(1)}, bf16[1,2,128,1024]{3,2,1,0:T(8,128)(2,1)S(1)}, u32[]{:S(2)}, u32[]{:S(2)}) collective-permute-start(bf16[1,2,128,1024]{3,2,1,0:T(8,128)(2,1)S(1)} %join.12), channel_id=1, source_target_pairs={{0,4},{16,48},{1,5},{17,49},{2,6},{18,50},{3,7},{19,51},{4,8},{20,... | collective-permute-start | bytes 1572872 | tf_op jit(solution)/shard_map/ppermute | solution.py:36
  101.8 12.1 %collective-permute-start.38 = (bf16[1,2,128,1024]{3,2,1,0:T(8,128)(2,1)S(1)}, bf16[1,2,128,1024]{3,2,1,0:T(8,128)(2,1)S(1)}, u32[]{:S(2)}, u32[]{:S(2)}) collective-permute-start(bf16[1,2,128,1024]{3,2,1,0:T(8,128)(2,1)S(1)} %join.13), channel_id=1, source_target_pairs={{0,12},{16,112},{1,13},{17,113},{2,14},{18,114},{3,15},{19,115},{4... | collective-permute-start | bytes 1572872 | tf_op jit(solution)/shard_map/ppermute | solution.py:36
  105.9 2.8 %collective-permute-start.29 = (f32[8,128]{1,0:T(8,128)S(1)}, f32[8,128]{1,0:T(8,128)S(1)}, u32[]{:S(2)}, u32[]{:S(2)}) collective-permute-start(f32[8,128]{1,0:T(8,128)S(1)} %after.1), channel_id=1, source_target_pairs={{16,17},{0,3},{17,16},{1,2},{18,19},{2,1},{19,18},{3,0},{20,21},{4... | collective-permute-start | bytes 12296 | tf_op jit(solution)/shard_map/ppermute | solution.py:36
  108.7 3.0 %collective-permute-start.30 = (f32[8,128]{1,0:T(8,128)S(1)}, f32[8,128]{1,0:T(8,128)S(1)}, u32[]{:S(2)}, u32[]{:S(2)}) collective-permute-start(f32[8,128]{1,0:T(8,128)S(1)} %add.14), channel_id=1, source_target_pairs={{0,16},{16,0},{32,48},{48,32},{64,80},{80,64},{96,112},{112,96},{1... | collective-permute-start | bytes 12296 | tf_op jit(solution)/shard_map/ppermute | solution.py:44
  114.2 2.7 %collective-permute-start.39 = (f32[128,1024]{1,0:T(8,128)S(1)}, f32[128,1024]{1,0:T(8,128)S(1)}, u32[]{:S(2)}, u32[]{:S(2)}) collective-permute-start(f32[128,1024]{1,0:T(8,128)S(1)} %get-tuple-element.60), channel_id=1, source_target_pairs={{0,16},{16,0},{32,48},{48,32},{64,80},{80,64},{96,112},{112,96},{1... | collective-permute-start | bytes 1572872 | tf_op jit(solution)/shard_map/ppermute | solution.py:44

commit v5 on v4

--- a/solution.py
+++ b/solution.py
@@ -167,8 +167,7 @@
         fill(send, keep, False)
 
 
-def slope_kernel(sv, target, own_lse, got_lse, part, slope, part_out, row_lse):
-    part_out[...] = part[...]
+def slope_kernel(sv, target, own_lse, got_lse, slope, row_lse):
     first = place()[1] == 0
     mine_lse, their_lse = own_lse[...], got_lse[...]
     rows_lse = jnp.where(first, mine_lse[:, :1024], their_lse[:, 1024:])
@@ -194,9 +193,9 @@
 def grad_kernel(flip, order, n_ties, *refs):
     n = len(order)
     steps = [(g, i, d) for g, group in enumerate(order) for i, d in enumerate(group)]
-    (slope, qt, pt, part), refs = refs[:4], refs[4 + n_ties :]
+    (slope, qt, pt, part, far_part), refs = refs[:5], refs[5 + n_ties :]
     keeps, sends, (part_out, gq, gp, zeros, out_sems) = refs[:n], refs[n : 2 * n], refs[2 * n :]
-    part_out[...] = part[...]
+    part_out[...] = part[...] + far_part[...]
     y, core, z, x = place()
     zeros[...] = jnp.zeros(zeros.shape, bf16)
     half = (x % 2) ^ flip
@@ -391,17 +390,17 @@
     )(mine, other)
 
 
-def slope_of(scores, target, own_lse, got_lse, part):
+def slope_of(scores, target, own_lse, got_lse):
     return pl.pallas_call(
         slope_kernel,
-        out_shape=[arr((2, 1024, 1024), bf16), arr((8, 128), f32)],
-        in_specs=[VM] * 5,
-        out_specs=[VM] * 2,
+        out_shape=arr((2, 1024, 1024), bf16),
+        in_specs=[VM] * 4,
+        out_specs=VM,
         scratch_shapes=[pltpu.VMEM((1024, 128), f32)],
         compiler_params=pltpu.CompilerParams(vmem_limit_bytes=8 * MIB),
         cost_estimate=cost(2 * 1024**2 * 2048, 12 * MIB),
         name="slope",
-    )(scores, target, own_lse, got_lse, part)
+    )(scores, target, own_lse, got_lse)
 
 
 def grads_of(flip, order, operands, ties):
@@ -507,24 +506,24 @@
     stats = merge([keep, swap(send)])
     stats = merge([stats, hop(stats, 0, True)], (q_flip,))
     own_lse, part = merge([stats, hop(stats, 2, False), hop(stats, 1, False), hop(stats, 3, False)], last=True)
-    slope, part = slope_of(scores, target, own_lse, swap(own_lse), part)
-
-    outs = grads_of(1, ((1, 3), (2,), (0,)), (slope, q_flip, p_tile, part), ())
-    part = part + hop_xor(part, 1)
-    keeps, recvs = outs[:3], [swap(s) for s in outs[3:6]]
+    slope = slope_of(scores, target, own_lse, swap(own_lse))
+
+    outs = grads_of(1, ((1, 3), (2,), (0,)), (slope, q_flip, p_tile, part, hop_xor(part, 1)), ())
+    keeps, recvs, part = outs[:3], [swap(s) for s in outs[3:6]], outs[6]
     sides, beyond = join([keeps[0], recvs[0]]), join([keeps[1], recvs[1]])
     ready = (sides, beyond)
     sides, beyond = hop(sides, 0, True), hop(beyond, 2, False)
     across = [keeps[2], recvs[2]]
-    part = part + hop(part, 2, False, 1)
-    outs = grads_of(0, ((1,), (3,), (2,), (0,)), (slope, q_flip, p_tile, part), (ready[0], beyond, part))
+    outs = grads_of(0, ((1,), (3,), (2,), (0,)), (slope, q_flip, p_tile, part, hop(part, 2, False, 1)), ready)
+    part = outs[8]
     keeps, recvs = outs[:4], [swap(s) for s in outs[4:8]]
-    up = hop(join([keeps[0], recvs[0], sides], pick=0), 1, False)
-    down = hop(join([keeps[1], recvs[1], sides], pick=1), 3, False)
-    across = hop(join([*across, beyond]), 0, True)
-    far = hop(join([keeps[2], recvs[2]]), 2, False)
+    far = join([keeps[2], recvs[2]])
+    up = join([keeps[0], recvs[0], sides], (far,), pick=0)
+    down = join([keeps[1], recvs[1], sides], (far,), pick=1)
+    across = hop(join([*across, beyond], (far,)), 0, True)
+    far, up, down = hop(far, 2, False), hop(up, 1, False), hop(down, 3, False)
     home = join([keeps[3], recvs[3]])
-    part = after(outs[8], across)
+    part = after(part, far)
     part = part + hop(part, 0, True, 1)
     part = part + swap(part)
     mine, other = total([home, far, across, up, down], (part,))

time: 119 us -> 113 us (0.950)
  waiting for transfers between devices: 32.2 us -> 25.5 us
    ppermute x20, waiting for transfers between devices: 8.1 us -> 5.39 us  [swap(): return lax.ppermute(a, 'row', [(i, i ^ 1) for i in range(8)])]
    ppermute x1, waiting for transfers between devices: 2.61 us -> 0.01 us  [hop_xor(): return lax.ppermute(a, AX, moves(lambda r, x, other: (r ^ 1, x), turn))]
    ppermute x19, waiting for transfers between devices: 21.5 us -> 20.1 us  [hop(): lax.ppermute(a, AX, moves(lambda r, x, other: ((r + d) % 4, other if flip...]
  transfers between devices with their start and end apart: 40 -> 40, of which waited for: 19 -> 16; matrix products, arithmetic and copies ran while one was open for 0% -> 0% of each run, Pallas kernels for 7% -> 10%
where the time goes in v5:
time: 113 us
  starting transfers between devices  54.3 us (48%)
  Pallas kernels  27.3 us (24%)
  waiting for transfers between devices  25.5 us (23%)
  local copies, waits for them, and re-layouts  3.1 us (3%)
  between operations  2.64 us (2%)
    ppermute x19, starting transfers between devices, hop(): lax.ppermute(a, AX, moves(lambda r, x, other: ((r + d) % 4, other if flip...  38.3 us
    ppermute x19, waiting for transfers between devices, hop(): lax.ppermute(a, AX, moves(lambda r, x, other: ((r + d) % 4, other if flip...  20.1 us
    ppermute x20, starting transfers between devices, swap(): return lax.ppermute(a, 'row', [(i, i ^ 1) for i in range(8)])  15.8 us
    pallas_call x2, Pallas kernels, grads_of(): pl.pallas_call(functools.partial(grad_kernel, flip, order, len(ties)), ou...  11.3 us
    pallas_call x1, Pallas kernels, scores_of(): pl.pallas_call(score_kernel, out_shape=(arr((2, 1024, 1024), f32), arr((3...  8.77 us
    ppermute x20, waiting for transfers between devices, swap(): return lax.ppermute(a, 'row', [(i, i ^ 1) for i in range(8)])  5.39 us
    pallas_call x1, Pallas kernels, slope_of(): pl.pallas_call(slope_kernel, out_shape=arr((2, 1024, 1024), bf16), in_spe...  3.49 us
    unnamed x6, local copies, waits for them, and re-layouts  2.59 us
  transfers between devices with their start and end apart: 40, of which 16 were waited for; matrix products, arithmetic and copies ran while one was open for 0% of the time, Pallas kernels for 10%

profile of v5, /device:TPU:1, one launch (start us, length us, event | category | flops | bytes accessed | tf_op | source)
XLA Modules:
  0.0 112.9 jit_solution(15809880126379746579)
XLA Ops:
  0.6 0.9 copy-done
  1.6 0.9 copy-done.1
  2.7 1.5 %collective-permute-start = (bf16[128,1024]{1,0:T(8,128)(2,1)S(1)}, bf16[128,1024]{1,0:T(8,128)(2,1)S(1)}, u32[]{:S(2)}, u32[]{:S(2)}) collective-permute-start(bf16[128,1024]{1,0:T(8,128)(2,1)S(1)} %get-tuple-element.33), channel_id=1, source_target_pairs={{0,16},{16,0},{32,48},{48,32},{64,80},{80,64},{96,112},{112,96},{1... | collective-permute-start | bytes 786440 | tf_op jit(solution)/shard_map/ppermute | solution.py:44
  4.2 1.2 %collective-permute-done = bf16[128,1024]{1,0:T(8,128)(2,1)S(1)} collective-permute-done((bf16[128,1024]{1,0:T(8,128)(2,1)S(1)}, bf16[128,1024]{1,0:T(8,128)(2,1)S(1)}, u32[]{:S(2)}, u32[]{:S(2)}) %collective-permute-start) | collective-permute-done | bytes 262176 | tf_op jit(solution)/shard_map/ppermute | solution.py:44
  5.4 2.9 %collective-permute-start.4 = (bf16[2,128,1024]{2,1,0:T(8,128)(2,1)S(1)}, bf16[2,128,1024]{2,1,0:T(8,128)(2,1)S(1)}, u32[]{:S(2)}, u32[]{:S(2)}) collective-permute-start(bf16[2,128,1024]{2,1,0:T(8,128)(2,1)S(1)} %pad_maximum_fusion.refs_4_), channel_id=1, source_target_pairs={{0,12},{16,112},{1,13},{17,113},{2,14},{18,114},{3,15},{19,115},{4... | collective-permute-start | bytes 1572872 | tf_op jit(solution)/shard_map/ppermute | solution.py:36
  8.3 1.7 %collective-permute-start.12 = (bf16[2,128,1024]{2,1,0:T(8,128)(2,1)S(1)}, bf16[2,128,1024]{2,1,0:T(8,128)(2,1)S(1)}, u32[]{:S(2)}, u32[]{:S(2)}) collective-permute-start(bf16[2,128,1024]{2,1,0:T(8,128)(2,1)S(1)} %pad_maximum_fusion.refs_4_), channel_id=1, source_target_pairs={{0,16},{16,0},{32,48},{48,32},{64,80},{80,64},{96,112},{112,96},{1... | collective-permute-start | bytes 1572872 | tf_op jit(solution)/shard_map/ppermute | solution.py:44
  10.0 2.5 %collective-permute-start.3 = (bf16[2,128,1024]{2,1,0:T(8,128)(2,1)S(1)}, bf16[2,128,1024]{2,1,0:T(8,128)(2,1)S(1)}, u32[]{:S(2)}, u32[]{:S(2)}) collective-permute-start(bf16[2,128,1024]{2,1,0:T(8,128)(2,1)S(1)} %pad_maximum_fusion.refs_4_), channel_id=1, source_target_pairs={{0,1},{16,19},{1,0},{17,18},{2,3},{18,17},{3,2},{19,16},{4,5},{20,... | collective-permute-start | bytes 1572872 | tf_op jit(solution)/shard_map/ppermute | solution.py:36
  12.5 1.3 %collective-permute-start.2 = (bf16[2,128,1024]{2,1,0:T(8,128)(2,1)S(1)}, bf16[2,128,1024]{2,1,0:T(8,128)(2,1)S(1)}, u32[]{:S(2)}, u32[]{:S(2)}) collective-permute-start(bf16[2,128,1024]{2,1,0:T(8,128)(2,1)S(1)} %pad_maximum_fusion.refs_4_), channel_id=1, source_target_pairs={{0,4},{16,48},{1,5},{17,49},{2,6},{18,50},{3,7},{19,51},{4,8},{20,... | collective-permute-start | bytes 1572872 | tf_op jit(solution)/shard_map/ppermute | solution.py:36
  13.8 2.6 %collective-permute-start.1 = (bf16[2,128,1024]{2,1,0:T(8,128)(2,1)S(1)}, bf16[2,128,1024]{2,1,0:T(8,128)(2,1)S(1)}, u32[]{:S(2)}, u32[]{:S(2)}) collective-permute-start(bf16[2,128,1024]{2,1,0:T(8,128)(2,1)S(1)} %pad_maximum_fusion.refs_4_), channel_id=1, source_target_pairs={{0,8},{16,80},{1,9},{17,81},{2,10},{18,82},{3,11},{19,83},{4,12},{... | collective-permute-start | bytes 1572872 | tf_op jit(solution)/shard_map/ppermute | solution.py:36
  16.4 6.0 %collective-permute-start.13 = (bf16[2,128,1024]{2,1,0:T(8,128)(2,1)S(1)}, bf16[2,128,1024]{2,1,0:T(8,128)(2,1)S(1)}, u32[]{:S(2)}, u32[]{:S(2)}) collective-permute-start(bf16[2,128,1024]{2,1,0:T(8,128)(2,1)S(1)} %collective-permute-done.4.refs_5_), channel_id=1, source_target_pairs={{0,16},{16,0},{32,48},{48,32},{64,80},{80,64},{96,112},{112,96},{1... | collective-permute-start | bytes 1572872 | tf_op jit(solution)/shard_map/ppermute | solution.py:44
  22.4 2.5 %collective-permute-start.5 = (bf16[2,128,1024]{2,1,0:T(8,128)(2,1)S(1)}, bf16[2,128,1024]{2,1,0:T(8,128)(2,1)S(1)}, u32[]{:S(2)}, u32[]{:S(2)}) collective-permute-start(bf16[2,128,1024]{2,1,0:T(8,128)(2,1)S(1)} %collective-permute-done.4.refs_5_), channel_id=1, source_target_pairs={{0,1},{16,19},{1,0},{17,18},{2,3},{18,17},{3,2},{19,16},{4,5},{20,... | collective-permute-start | bytes 1572872 | tf_op jit(solution)/shard_map/ppermute | solution.py:36
  24.8 4.5 %collective-permute-start.7 = (bf16[2,128,1024]{2,1,0:T(8,128)(2,1)S(1)}, bf16[2,128,1024]{2,1,0:T(8,128)(2,1)S(1)}, u32[]{:S(2)}, u32[]{:S(2)}) collective-permute-start(bf16[2,128,1024]{2,1,0:T(8,128)(2,1)S(1)} %collective-permute-done.3.refs_2_), channel_id=1, source_target_pairs={{0,8},{16,80},{1,9},{17,81},{2,10},{18,82},{3,11},{19,83},{4,12},{... | collective-permute-start | bytes 1572872 | tf_op jit(solution)/shard_map/ppermute | solution.py:36
  29.5 2.3 %collective-permute-done.5.refs_3_ = bf16[2,128,1024]{2,1,0:T(8,128)(2,1)S(1)} collective-permute-done((bf16[2,128,1024]{2,1,0:T(8,128)(2,1)S(1)}, bf16[2,128,1024]{2,1,0:T(8,128)(2,1)S(1)}, u32[]{:S(2)}, u32[]{:S(2)}) %collective-permute-start.5) | collective-permute-done | bytes 524320 | tf_op jit(solution)/shard_map/ppermute | solution.py:36
  31.9 0.5 collective-permute-start.11
  32.4 3.5 %collective-permute-done.7.refs_7_ = bf16[2,128,1024]{2,1,0:T(8,128)(2,1)S(1)} collective-permute-done((bf16[2,128,1024]{2,1,0:T(8,128)(2,1)S(1)}, bf16[2,128,1024]{2,1,0:T(8,128)(2,1)S(1)}, u32[]{:S(2)}, u32[]{:S(2)}) %collective-permute-start.7) | collective-permute-done | bytes 524320 | tf_op jit(solution)/shard_map/ppermute | solution.py:36
  36.2 2.4 %collective-permute-done.6.refs_6_ = bf16[2,128,1024]{2,1,0:T(8,128)(2,1)S(1)} collective-permute-done((bf16[2,128,1024]{2,1,0:T(8,128)(2,1)S(1)}, bf16[2,128,1024]{2,1,0:T(8,128)(2,1)S(1)}, u32[]{:S(2)}, u32[]{:S(2)}) %collective-permute-start.6) | collective-permute-done | bytes 524320 | tf_op jit(solution)/shard_map/ppermute | solution.py:36
  38.6 0.7 copy-done.2
  39.5 1.0 collective-permute-done.14.refs_14_
  40.5 8.8 %scores.1 = (f32[2,1024,1024]{2,1,0:T(8,128)S(1)}, f32[3,2048]{1,0:T(4,128)S(1)}, f32[3,2048]{1,0:T(4,128)S(1)}, bf16[1024,1024]{1,0:T(8,128)(2,1)S(1)}, bf16[2,1024,1024]{2,1,0:T(8,128)(2,1)S(1)}) custom-call(bf16[2,128,1024]{2,1,0:T(8,128)(2,1)S(1)} %collective-permute-done.1.refs_0_, bf16[2,128,1024]{2,1,0:T(8,128)(2,1)S(1)} %collective-permute-done.2.refs_1_, ...), custom_call_target="tpu_custom_call" | custom-call | flops 4294967296 | bytes 16777216 | tf_op jit(solution)/shard_map/scores/pallas_call | solution.py:270
  49.4 1.1 collective-permute-done.16.refs_1_
  50.6 1.2 %collective-permute-start.17 = (f32[3,2048]{1,0:T(4,128)S(1)}, f32[3,2048]{1,0:T(4,128)S(1)}, u32[]{:S(2)}, u32[]{:S(2)}) collective-permute-start(f32[3,2048]{1,0:T(4,128)S(1)} %merge.3.refs_0_), channel_id=1, source_target_pairs={{0,1},{16,19},{1,0},{17,18},{2,3},{18,17},{3,2},{19,16},{4,5},{20,... | collective-permute-start | bytes 73736 | tf_op jit(solution)/shard_map/ppermute | solution.py:36
  51.7 0.7 flip.1.refs_2_.refs_1_
  52.4 2.2 %collective-permute-done.17.refs_1_ = f32[3,2048]{1,0:T(4,128)S(1)} collective-permute-done((f32[3,2048]{1,0:T(4,128)S(1)}, f32[3,2048]{1,0:T(4,128)S(1)}, u32[]{:S(2)}, u32[]{:S(2)}) %collective-permute-start.17) | collective-permute-done | bytes 24608 | tf_op jit(solution)/shard_map/ppermute | solution.py:36
  54.6 2.8 %collective-permute-start.20 = (f32[3,2048]{1,0:T(4,128)S(1)}, f32[3,2048]{1,0:T(4,128)S(1)}, u32[]{:S(2)}, u32[]{:S(2)}) collective-permute-start(f32[3,2048]{1,0:T(4,128)S(1)} %merge.4.refs_0_), channel_id=1, source_target_pairs={{0,12},{16,112},{1,13},{17,113},{2,14},{18,114},{3,15},{19,115},{4... | collective-permute-start | bytes 73736 | tf_op jit(solution)/shard_map/ppermute | solution.py:36
  57.4 1.6 %collective-permute-start.18 = (f32[3,2048]{1,0:T(4,128)S(1)}, f32[3,2048]{1,0:T(4,128)S(1)}, u32[]{:S(2)}, u32[]{:S(2)}) collective-permute-start(f32[3,2048]{1,0:T(4,128)S(1)} %merge.4.refs_0_), channel_id=1, source_target_pairs={{0,8},{16,80},{1,9},{17,81},{2,10},{18,82},{3,11},{19,83},{4,12},{... | collective-permute-start | bytes 73736 | tf_op jit(solution)/shard_map/ppermute | solution.py:36
  59.1 2.6 %collective-permute-done.19.refs_2_ = f32[3,2048]{1,0:T(4,128)S(1)} collective-permute-done((f32[3,2048]{1,0:T(4,128)S(1)}, f32[3,2048]{1,0:T(4,128)S(1)}, u32[]{:S(2)}, u32[]{:S(2)}) %collective-permute-start.19) | collective-permute-done | bytes 24608 | tf_op jit(solution)/shard_map/ppermute | solution.py:36
  62.1 0.6 collective-permute-start.21
  62.9 0.6 collective-permute-done.21.got_lse
  63.5 3.5 %slope.1.refs_0_ = bf16[2,1024,1024]{2,1,0:T(8,128)(2,1)S(1)} custom-call(f32[2,1024,1024]{2,1,0:T(8,128)S(1)} %get-tuple-element.34.sv, f32[1024,128]{1,0:T(8,128)S(1)} %aims.1.refs_16_.target, f32[1,2048]{1,0:T(1,128)S(1)} %get-tuple-element.38.own_lse, f32[1,2048]{1,0:T(1,128)S(1)} %collective-permute-done.21.got_lse), custom_call_target="tpu_custom_call" | custom-call | flops 4294967296 | bytes 12582912 | tf_op jit(solution)/shard_map/slope/pallas_call | solution.py:394
  67.0 5.6 %grads_far.1 = (bf16[2,2,128,1024]{3,2,1,0:T(8,128)(2,1)S(1)}, bf16[1,2,128,1024]{3,2,1,0:T(8,128)(2,1)S(1)}, bf16[1,2,128,1024]{3,2,1,0:T(8,128)(2,1)S(1)}, bf1...) custom-call(bf16[2,1024,1024]{2,1,0:T(8,128)(2,1)S(1)} %slope.1.refs, ...), custom_call_target="tpu_custom_call" | custom-call | flops 4294967296 | bytes 20971520 | tf_op jit(solution)/shard_map/grads_far/pallas_call | solution.py:408
  72.7 0.9 collective-permute-start.24
  73.7 2.8 %collective-permute-start.23 = (f32[8,128]{1,0:T(8,128)S(1)}, f32[8,128]{1,0:T(8,128)S(1)}, u32[]{:S(2)}, u32[]{:S(2)}) collective-permute-start(f32[8,128]{1,0:T(8,128)S(1)} %get-tuple-element.41.refs_3_), channel_id=1, source_target_pairs={{16,24},{0,64},{17,25},{1,65},{18,26},{2,66},{19,27},{3,67},{20,28... | collective-permute-start | bytes 12296 | tf_op jit(solution)/shard_map/ppermute | solution.py:36
  77.0 2.6 %collective-permute-start.35 = (bf16[2,2,128,1024]{3,2,1,0:T(8,128)(2,1)S(1)}, bf16[2,2,128,1024]{3,2,1,0:T(8,128)(2,1)S(1)}, u32[]{:S(2)}, u32[]{:S(2)}) collective-permute-start(bf16[2,2,128,1024]{3,2,1,0:T(8,128)(2,1)S(1)} %join.7.refs_5_), channel_id=1, source_target_pairs={{0,1},{16,19},{1,0},{17,18},{2,3},{18,17},{3,2},{19,16},{4,5},{20,... | collective-permute-start | bytes 3145736 | tf_op jit(solution)/shard_map/ppermute | solution.py:36
  79.6 5.6 %grads_near.1 = (bf16[1,2,128,1024]{3,2,1,0:T(8,128)(2,1)S(1)}, bf16[1,2,128,1024]{3,2,1,0:T(8,128)(2,1)S(1)}, bf16[1,2,128,1024]{3,2,1,0:T(8,128)(2,1)S(1)}, bf...) custom-call(bf16[2,1024,1024]{2,1,0:T(8,128)(2,1)S(1)} %slope.1.refs, ...), custom_call_target="tpu_custom_call" | custom-call | flops 4294967296 | bytes 20971520 | tf_op jit(solution)/shard_map/grads_near/pallas_call | solution.py:408
  85.8 2.8 %collective-permute-start.32 = (bf16[1,2,128,1024]{3,2,1,0:T(8,128)(2,1)S(1)}, bf16[1,2,128,1024]{3,2,1,0:T(8,128)(2,1)S(1)}, u32[]{:S(2)}, u32[]{:S(2)}) collective-permute-start(bf16[1,2,128,1024]{3,2,1,0:T(8,128)(2,1)S(1)} %join.8.refs_6_), channel_id=1, source_target_pairs={{0,8},{16,80},{1,9},{17,81},{2,10},{18,82},{3,11},{19,83},{4,12},{... | collective-permute-start | bytes 1572872 | tf_op jit(solution)/shard_map/ppermute | solution.py:36
  89.3 3.1 %collective-permute-start.27 = (bf16[1,2,128,1024]{3,2,1,0:T(8,128)(2,1)S(1)}, bf16[1,2,128,1024]{3,2,1,0:T(8,128)(2,1)S(1)}, u32[]{:S(2)}, u32[]{:S(2)}) collective-permute-start(bf16[1,2,128,1024]{3,2,1,0:T(8,128)(2,1)S(1)} %join.9.refs_3_), channel_id=1, source_target_pairs={{0,8},{16,80},{1,9},{17,81},{2,10},{18,82},{3,11},{19,83},{4,12},{... | collective-permute-start | bytes 1572872 | tf_op jit(solution)/shard_map/ppermute | solution.py:36
  92.3 3.3 %collective-permute-done.32.refs_2_ = bf16[1,2,128,1024]{3,2,1,0:T(8,128)(2,1)S(1)} collective-permute-done((bf16[1,2,128,1024]{3,2,1,0:T(8,128)(2,1)S(1)}, bf16[1,2,128,1024]{3,2,1,0:T(8,128)(2,1)S(1)}, u32[]{:S(2)}, u32[]{:S(2)}) %collective-permute-start.32) | collective-permute-done | bytes 524320 | tf_op jit(solution)/shard_map/ppermute | solution.py:36
  95.6 0.9 collective-permute-start.30
  96.8 2.1 %collective-permute-start.33 = (bf16[1,2,128,1024]{3,2,1,0:T(8,128)(2,1)S(1)}, bf16[1,2,128,1024]{3,2,1,0:T(8,128)(2,1)S(1)}, u32[]{:S(2)}, u32[]{:S(2)}) collective-permute-start(bf16[1,2,128,1024]{3,2,1,0:T(8,128)(2,1)S(1)} %join.11), channel_id=1, source_target_pairs={{0,1},{16,19},{1,0},{17,18},{2,3},{18,17},{3,2},{19,16},{4,5},{20,... | collective-permute-start | bytes 1572872 | tf_op jit(solution)/shard_map/ppermute | solution.py:36
  99.1 0.9 collective-permute-start.36
  100.1 2.0 %collective-permute-start.38 = (bf16[1,2,128,1024]{3,2,1,0:T(8,128)(2,1)S(1)}, bf16[1,2,128,1024]{3,2,1,0:T(8,128)(2,1)S(1)}, u32[]{:S(2)}, u32[]{:S(2)}) collective-permute-start(bf16[1,2,128,1024]{3,2,1,0:T(8,128)(2,1)S(1)} %join.13), channel_id=1, source_target_pairs={{0,12},{16,112},{1,13},{17,113},{2,14},{18,114},{3,15},{19,115},{4... | collective-permute-start | bytes 1572872 | tf_op jit(solution)/shard_map/ppermute | solution.py:36
  102.1 2.9 %collective-permute-done.28 = f32[8,128]{1,0:T(8,128)S(1)} collective-permute-done((f32[8,128]{1,0:T(8,128)S(1)}, f32[8,128]{1,0:T(8,128)S(1)}, u32[]{:S(2)}, u32[]{:S(2)}) %collective-permute-start.28) | collective-permute-done | bytes 4128 | tf_op jit(solution)/shard_map/ppermute | solution.py:36
  105.0 2.1 %collective-permute-start.29 = (f32[8,128]{1,0:T(8,128)S(1)}, f32[8,128]{1,0:T(8,128)S(1)}, u32[]{:S(2)}, u32[]{:S(2)}) collective-permute-start(f32[8,128]{1,0:T(8,128)S(1)} %add.6), channel_id=1, source_target_pairs={{0,16},{16,0},{32,48},{48,32},{64,80},{80,64},{96,112},{112,96},{1... | collective-permute-start | bytes 12296 | tf_op jit(solution)/shard_map/ppermute | solution.py:44
  107.2 0.7 collective-permute-done.29
  107.9 0.5 collective-permute-done.36.refs_3_
  108.8 0.5 slice.3
  110.0 0.7 collective-permute-done.39.other
  110.7 1.1 finish.1
  (62 shorter events, 4.7 us)
Async XLA Ops:
  0.6 1.0 copy-start
  1.6 0.9 copy-start.1
  2.7 2.7 %collective-permute-start = (bf16[128,1024]{1,0:T(8,128)(2,1)S(1)}, bf16[128,1024]{1,0:T(8,128)(2,1)S(1)}, u32[]{:S(2)}, u32[]{:S(2)}) collective-permute-start(bf16[128,1024]{1,0:T(8,128)(2,1)S(1)} %get-tuple-element.33), channel_id=1, source_target_pairs={{0,16},{16,0},{32,48},{48,32},{64,80},{80,64},{96,112},{112,96},{1... | collective-permute-start | bytes 786440 | tf_op jit(solution)/shard_map/ppermute | solution.py:44
  5.4 11.0 %collective-permute-start.4 = (bf16[2,128,1024]{2,1,0:T(8,128)(2,1)S(1)}, bf16[2,128,1024]{2,1,0:T(8,128)(2,1)S(1)}, u32[]{:S(2)}, u32[]{:S(2)}) collective-permute-start(bf16[2,128,1024]{2,1,0:T(8,128)(2,1)S(1)} %pad_maximum_fusion.refs_4_), channel_id=1, source_target_pairs={{0,12},{16,112},{1,13},{17,113},{2,14},{18,114},{3,15},{19,115},{4... | collective-permute-start | bytes 1572872 | tf_op jit(solution)/shard_map/ppermute | solution.py:36
  8.3 14.0 %collective-permute-start.12 = (bf16[2,128,1024]{2,1,0:T(8,128)(2,1)S(1)}, bf16[2,128,1024]{2,1,0:T(8,128)(2,1)S(1)}, u32[]{:S(2)}, u32[]{:S(2)}) collective-permute-start(bf16[2,128,1024]{2,1,0:T(8,128)(2,1)S(1)} %pad_maximum_fusion.refs_4_), channel_id=1, source_target_pairs={{0,16},{16,0},{32,48},{48,32},{64,80},{80,64},{96,112},{112,96},{1... | collective-permute-start | bytes 1572872 | tf_op jit(solution)/shard_map/ppermute | solution.py:44
  10.0 14.8 %collective-permute-start.3 = (bf16[2,128,1024]{2,1,0:T(8,128)(2,1)S(1)}, bf16[2,128,1024]{2,1,0:T(8,128)(2,1)S(1)}, u32[]{:S(2)}, u32[]{:S(2)}) collective-permute-start(bf16[2,128,1024]{2,1,0:T(8,128)(2,1)S(1)} %pad_maximum_fusion.refs_4_), channel_id=1, source_target_pairs={{0,1},{16,19},{1,0},{17,18},{2,3},{18,17},{3,2},{19,16},{4,5},{20,... | collective-permute-start | bytes 1572872 | tf_op jit(solution)/shard_map/ppermute | solution.py:36
  12.5 12.4 %collective-permute-start.2 = (bf16[2,128,1024]{2,1,0:T(8,128)(2,1)S(1)}, bf16[2,128,1024]{2,1,0:T(8,128)(2,1)S(1)}, u32[]{:S(2)}, u32[]{:S(2)}) collective-permute-start(bf16[2,128,1024]{2,1,0:T(8,128)(2,1)S(1)} %pad_maximum_fusion.refs_4_), channel_id=1, source_target_pairs={{0,4},{16,48},{1,5},{17,49},{2,6},{18,50},{3,7},{19,51},{4,8},{20,... | collective-permute-start | bytes 1572872 | tf_op jit(solution)/shard_map/ppermute | solution.py:36
  13.8 15.6 %collective-permute-start.1 = (bf16[2,128,1024]{2,1,0:T(8,128)(2,1)S(1)}, bf16[2,128,1024]{2,1,0:T(8,128)(2,1)S(1)}, u32[]{:S(2)}, u32[]{:S(2)}) collective-permute-start(bf16[2,128,1024]{2,1,0:T(8,128)(2,1)S(1)} %pad_maximum_fusion.refs_4_), channel_id=1, source_target_pairs={{0,8},{16,80},{1,9},{17,81},{2,10},{18,82},{3,11},{19,83},{4,12},{... | collective-permute-start | bytes 1572872 | tf_op jit(solution)/shard_map/ppermute | solution.py:36
  16.4 13.1 %collective-permute-start.13 = (bf16[2,128,1024]{2,1,0:T(8,128)(2,1)S(1)}, bf16[2,128,1024]{2,1,0:T(8,128)(2,1)S(1)}, u32[]{:S(2)}, u32[]{:S(2)}) collective-permute-start(bf16[2,128,1024]{2,1,0:T(8,128)(2,1)S(1)} %collective-permute-done.4.refs_5_), channel_id=1, source_target_pairs={{0,16},{16,0},{32,48},{48,32},{64,80},{80,64},{96,112},{112,96},{1... | collective-permute-start | bytes 1572872 | tf_op jit(solution)/shard_map/ppermute | solution.py:44
  22.4 9.5 %collective-permute-start.5 = (bf16[2,128,1024]{2,1,0:T(8,128)(2,1)S(1)}, bf16[2,128,1024]{2,1,0:T(8,128)(2,1)S(1)}, u32[]{:S(2)}, u32[]{:S(2)}) collective-permute-start(bf16[2,128,1024]{2,1,0:T(8,128)(2,1)S(1)} %collective-permute-done.4.refs_5_), channel_id=1, source_target_pairs={{0,1},{16,19},{1,0},{17,18},{2,3},{18,17},{3,2},{19,16},{4,5},{20,... | collective-permute-start | bytes 1572872 | tf_op jit(solution)/shard_map/ppermute | solution.py:36
  24.8 7.1 %collective-permute-start.10 = (bf16[2,128,1024]{2,1,0:T(8,128)(2,1)S(1)}, bf16[2,128,1024]{2,1,0:T(8,128)(2,1)S(1)}, u32[]{:S(2)}, u32[]{:S(2)}) collective-permute-start(bf16[2,128,1024]{2,1,0:T(8,128)(2,1)S(1)} %collective-permute-done.3.refs_2_), channel_id=1, source_target_pairs={{0,16},{16,0},{32,48},{48,32},{64,80},{80,64},{96,112},{112,96},{1... | collective-permute-start | bytes 1572872 | tf_op jit(solution)/shard_map/ppermute | solution.py:44
  24.8 11.1 %collective-permute-start.7 = (bf16[2,128,1024]{2,1,0:T(8,128)(2,1)S(1)}, bf16[2,128,1024]{2,1,0:T(8,128)(2,1)S(1)}, u32[]{:S(2)}, u32[]{:S(2)}) collective-permute-start(bf16[2,128,1024]{2,1,0:T(8,128)(2,1)S(1)} %collective-permute-done.3.refs_2_), channel_id=1, source_target_pairs={{0,8},{16,80},{1,9},{17,81},{2,10},{18,82},{3,11},{19,83},{4,12},{... | collective-permute-start | bytes 1572872 | tf_op jit(solution)/shard_map/ppermute | solution.py:36
  29.3 9.2 %collective-permute-start.6 = (bf16[2,128,1024]{2,1,0:T(8,128)(2,1)S(1)}, bf16[2,128,1024]{2,1,0:T(8,128)(2,1)S(1)}, u32[]{:S(2)}, u32[]{:S(2)}) collective-permute-start(bf16[2,128,1024]{2,1,0:T(8,128)(2,1)S(1)} %collective-permute-done.2.refs_1_), channel_id=1, source_target_pairs={{0,1},{16,19},{1,0},{17,18},{2,3},{18,17},{3,2},{19,16},{4,5},{20,... | collective-permute-start | bytes 1572872 | tf_op jit(solution)/shard_map/ppermute | solution.py:36
  29.5 9.9 %collective-permute-start.9 = (bf16[2,128,1024]{2,1,0:T(8,128)(2,1)S(1)}, bf16[2,128,1024]{2,1,0:T(8,128)(2,1)S(1)}, u32[]{:S(2)}, u32[]{:S(2)}) collective-permute-start(bf16[2,128,1024]{2,1,0:T(8,128)(2,1)S(1)} %collective-permute-done.2.refs_1_), channel_id=1, source_target_pairs={{0,16},{16,0},{32,48},{48,32},{64,80},{80,64},{96,112},{112,96},{1... | collective-permute-start | bytes 1572872 | tf_op jit(solution)/shard_map/ppermute | solution.py:44
  31.9 7.6 %collective-permute-start.8 = (bf16[2,128,1024]{2,1,0:T(8,128)(2,1)S(1)}, bf16[2,128,1024]{2,1,0:T(8,128)(2,1)S(1)}, u32[]{:S(2)}, u32[]{:S(2)}) collective-permute-start(bf16[2,128,1024]{2,1,0:T(8,128)(2,1)S(1)} %collective-permute-done.1.refs_0_), channel_id=1, source_target_pairs={{0,16},{16,0},{32,48},{48,32},{64,80},{80,64},{96,112},{112,96},{1... | collective-permute-start | bytes 1572872 | tf_op jit(solution)/shard_map/ppermute | solution.py:44
  31.9 7.6 %collective-permute-start.11 = (bf16[2,128,1024]{2,1,0:T(8,128)(2,1)S(1)}, bf16[2,128,1024]{2,1,0:T(8,128)(2,1)S(1)}, u32[]{:S(2)}, u32[]{:S(2)}) collective-permute-start(bf16[2,128,1024]{2,1,0:T(8,128)(2,1)S(1)} %collective-permute-done.5.refs_3_), channel_id=1, source_target_pairs={{0,16},{16,0},{32,48},{48,32},{64,80},{80,64},{96,112},{112,96},{1... | collective-permute-start | bytes 1572872 | tf_op jit(solution)/shard_map/ppermute | solution.py:44
  35.9 3.6 %collective-permute-start.15 = (bf16[2,128,1024]{2,1,0:T(8,128)(2,1)S(1)}, bf16[2,128,1024]{2,1,0:T(8,128)(2,1)S(1)}, u32[]{:S(2)}, u32[]{:S(2)}) collective-permute-start(bf16[2,128,1024]{2,1,0:T(8,128)(2,1)S(1)} %collective-permute-done.7.refs_7_), channel_id=1, source_target_pairs={{0,16},{16,0},{32,48},{48,32},{64,80},{80,64},{96,112},{112,96},{1... | collective-permute-start | bytes 1572872 | tf_op jit(solution)/shard_map/ppermute | solution.py:44
  38.6 1.9 %collective-permute-start.14 = (bf16[2,128,1024]{2,1,0:T(8,128)(2,1)S(1)}, bf16[2,128,1024]{2,1,0:T(8,128)(2,1)S(1)}, u32[]{:S(2)}, u32[]{:S(2)}) collective-permute-start(bf16[2,128,1024]{2,1,0:T(8,128)(2,1)S(1)} %collective-permute-done.6.refs_6_), channel_id=1, source_target_pairs={{0,16},{16,0},{32,48},{48,32},{64,80},{80,64},{96,112},{112,96},{1... | collective-permute-start | bytes 1572872 | tf_op jit(solution)/shard_map/ppermute | solution.py:44
  38.6 0.7 copy-start.2
  49.3 1.3 %collective-permute-start.16 = (f32[3,2048]{1,0:T(4,128)S(1)}, f32[3,2048]{1,0:T(4,128)S(1)}, u32[]{:S(2)}, u32[]{:S(2)}) collective-permute-start(f32[3,2048]{1,0:T(4,128)S(1)} %get-tuple-element.36), channel_id=1, source_target_pairs={{0,16},{16,0},{32,48},{48,32},{64,80},{80,64},{96,112},{112,96},{1... | collective-permute-start | bytes 73736 | tf_op jit(solution)/shard_map/ppermute | solution.py:44
  50.6 4.1 %collective-permute-start.17 = (f32[3,2048]{1,0:T(4,128)S(1)}, f32[3,2048]{1,0:T(4,128)S(1)}, u32[]{:S(2)}, u32[]{:S(2)}) collective-permute-start(f32[3,2048]{1,0:T(4,128)S(1)} %merge.3.refs_0_), channel_id=1, source_target_pairs={{0,1},{16,19},{1,0},{17,18},{2,3},{18,17},{3,2},{19,16},{4,5},{20,... | collective-permute-start | bytes 73736 | tf_op jit(solution)/shard_map/ppermute | solution.py:36
  54.6 4.4 %collective-permute-start.20 = (f32[3,2048]{1,0:T(4,128)S(1)}, f32[3,2048]{1,0:T(4,128)S(1)}, u32[]{:S(2)}, u32[]{:S(2)}) collective-permute-start(f32[3,2048]{1,0:T(4,128)S(1)} %merge.4.refs_0_), channel_id=1, source_target_pairs={{0,12},{16,112},{1,13},{17,113},{2,14},{18,114},{3,15},{19,115},{4... | collective-permute-start | bytes 73736 | tf_op jit(solution)/shard_map/ppermute | solution.py:36
  57.4 4.3 %collective-permute-start.19 = (f32[3,2048]{1,0:T(4,128)S(1)}, f32[3,2048]{1,0:T(4,128)S(1)}, u32[]{:S(2)}, u32[]{:S(2)}) collective-permute-start(f32[3,2048]{1,0:T(4,128)S(1)} %merge.4.refs_0_), channel_id=1, source_target_pairs={{0,4},{16,48},{1,5},{17,49},{2,6},{18,50},{3,7},{19,51},{4,8},{20,... | collective-permute-start | bytes 73736 | tf_op jit(solution)/shard_map/ppermute | solution.py:36
  57.4 4.6 %collective-permute-start.18 = (f32[3,2048]{1,0:T(4,128)S(1)}, f32[3,2048]{1,0:T(4,128)S(1)}, u32[]{:S(2)}, u32[]{:S(2)}) collective-permute-start(f32[3,2048]{1,0:T(4,128)S(1)} %merge.4.refs_0_), channel_id=1, source_target_pairs={{0,8},{16,80},{1,9},{17,81},{2,10},{18,82},{3,11},{19,83},{4,12},{... | collective-permute-start | bytes 73736 | tf_op jit(solution)/shard_map/ppermute | solution.py:36
  62.1 1.4 %collective-permute-start.21 = (f32[1,2048]{1,0:T(1,128)S(1)}, f32[1,2048]{1,0:T(1,128)S(1)}, u32[]{:S(2)}, u32[]{:S(2)}) collective-permute-start(f32[1,2048]{1,0:T(1,128)S(1)} %get-tuple-element.38.own_lse), channel_id=1, source_target_pairs={{0,16},{16,0},{32,48},{48,32},{64,80},{80,64},{96,112},{112,96},{1... | collective-permute-start | bytes 24584 | tf_op jit(solution)/shard_map/ppermute | solution.py:44
  62.7 4.3 %collective-permute-start.22 = (f32[8,128]{1,0:T(8,128)S(1)}, f32[8,128]{1,0:T(8,128)S(1)}, u32[]{:S(2)}, u32[]{:S(2)}) collective-permute-start(f32[8,128]{1,0:T(8,128)S(1)} %get-tuple-element.40.refs_3_), channel_id=1, source_target_pairs={{16,20},{0,32},{17,21},{1,33},{18,22},{2,34},{19,23},{3,35},{20,16... | collective-permute-start | bytes 12296 | tf_op jit(solution)/shard_map/ppermute | solution.py:40
  72.7 4.1 %collective-permute-start.24 = (bf16[2,2,128,1024]{3,2,1,0:T(8,128)(2,1)S(1)}, bf16[2,2,128,1024]{3,2,1,0:T(8,128)(2,1)S(1)}, u32[]{:S(2)}, u32[]{:S(2)}) collective-permute-start(bf16[2,2,128,1024]{3,2,1,0:T(8,128)(2,1)S(1)} %get-tuple-element.43), channel_id=1, source_target_pairs={{0,16},{16,0},{32,48},{48,32},{64,80},{80,64},{96,112},{112,96},{1... | collective-permute-start | bytes 3145736 | tf_op jit(solution)/shard_map/ppermute | solution.py:44
  73.6 3.0 %collective-permute-start.25 = (bf16[1,2,128,1024]{3,2,1,0:T(8,128)(2,1)S(1)}, bf16[1,2,128,1024]{3,2,1,0:T(8,128)(2,1)S(1)}, u32[]{:S(2)}, u32[]{:S(2)}) collective-permute-start(bf16[1,2,128,1024]{3,2,1,0:T(8,128)(2,1)S(1)} %get-tuple-element.45), channel_id=1, source_target_pairs={{0,16},{16,0},{32,48},{48,32},{64,80},{80,64},{96,112},{112,96},{1... | collective-permute-start | bytes 1572872 | tf_op jit(solution)/shard_map/ppermute | solution.py:44
  73.7 5.9 %collective-permute-start.23 = (f32[8,128]{1,0:T(8,128)S(1)}, f32[8,128]{1,0:T(8,128)S(1)}, u32[]{:S(2)}, u32[]{:S(2)}) collective-permute-start(f32[8,128]{1,0:T(8,128)S(1)} %get-tuple-element.41.refs_3_), channel_id=1, source_target_pairs={{16,24},{0,64},{17,25},{1,65},{18,26},{2,66},{19,27},{3,67},{20,28... | collective-permute-start | bytes 12296 | tf_op jit(solution)/shard_map/ppermute | solution.py:36
  77.0 21.9 %collective-permute-start.35 = (bf16[2,2,128,1024]{3,2,1,0:T(8,128)(2,1)S(1)}, bf16[2,2,128,1024]{3,2,1,0:T(8,128)(2,1)S(1)}, u32[]{:S(2)}, u32[]{:S(2)}) collective-permute-start(bf16[2,2,128,1024]{3,2,1,0:T(8,128)(2,1)S(1)} %join.7.refs_5_), channel_id=1, source_target_pairs={{0,1},{16,19},{1,0},{17,18},{2,3},{18,17},{3,2},{19,16},{4,5},{20,... | collective-permute-start | bytes 3145736 | tf_op jit(solution)/shard_map/ppermute | solution.py:36
  85.2 3.8 %collective-permute-start.26 = (bf16[1,2,128,1024]{3,2,1,0:T(8,128)(2,1)S(1)}, bf16[1,2,128,1024]{3,2,1,0:T(8,128)(2,1)S(1)}, u32[]{:S(2)}, u32[]{:S(2)}) collective-permute-start(bf16[1,2,128,1024]{3,2,1,0:T(8,128)(2,1)S(1)} %get-tuple-element.48), channel_id=1, source_target_pairs={{0,16},{16,0},{32,48},{48,32},{64,80},{80,64},{96,112},{112,96},{1... | collective-permute-start | bytes 1572872 | tf_op jit(solution)/shard_map/ppermute | solution.py:44
  85.3 4.0 %collective-permute-start.31 = (bf16[1,2,128,1024]{3,2,1,0:T(8,128)(2,1)S(1)}, bf16[1,2,128,1024]{3,2,1,0:T(8,128)(2,1)S(1)}, u32[]{:S(2)}, u32[]{:S(2)}) collective-permute-start(bf16[1,2,128,1024]{3,2,1,0:T(8,128)(2,1)S(1)} %get-tuple-element.52), channel_id=1, source_target_pairs={{0,16},{16,0},{32,48},{48,32},{64,80},{80,64},{96,112},{112,96},{1... | collective-permute-start | bytes 1572872 | tf_op jit(solution)/shard_map/ppermute | solution.py:44
  85.8 9.8 %collective-permute-start.32 = (bf16[1,2,128,1024]{3,2,1,0:T(8,128)(2,1)S(1)}, bf16[1,2,128,1024]{3,2,1,0:T(8,128)(2,1)S(1)}, u32[]{:S(2)}, u32[]{:S(2)}) collective-permute-start(bf16[1,2,128,1024]{3,2,1,0:T(8,128)(2,1)S(1)} %join.8.refs_6_), channel_id=1, source_target_pairs={{0,8},{16,80},{1,9},{17,81},{2,10},{18,82},{3,11},{19,83},{4,12},{... | collective-permute-start | bytes 1572872 | tf_op jit(solution)/shard_map/ppermute | solution.py:36
  88.6 8.1 %collective-permute-start.34 = (bf16[1,2,128,1024]{3,2,1,0:T(8,128)(2,1)S(1)}, bf16[1,2,128,1024]{3,2,1,0:T(8,128)(2,1)S(1)}, u32[]{:S(2)}, u32[]{:S(2)}) collective-permute-start(bf16[1,2,128,1024]{3,2,1,0:T(8,128)(2,1)S(1)} %get-tuple-element.54), channel_id=1, source_target_pairs={{0,16},{16,0},{32,48},{48,32},{64,80},{80,64},{96,112},{112,96},{1... | collective-permute-start | bytes 1572872 | tf_op jit(solution)/shard_map/ppermute | solution.py:44
  89.0 11.0 %collective-permute-start.37 = (bf16[1,2,128,1024]{3,2,1,0:T(8,128)(2,1)S(1)}, bf16[1,2,128,1024]{3,2,1,0:T(8,128)(2,1)S(1)}, u32[]{:S(2)}, u32[]{:S(2)}) collective-permute-start(bf16[1,2,128,1024]{3,2,1,0:T(8,128)(2,1)S(1)} %get-tuple-element.56), channel_id=1, source_target_pairs={{0,16},{16,0},{32,48},{48,32},{64,80},{80,64},{96,112},{112,96},{1... | collective-permute-start | bytes 1572872 | tf_op jit(solution)/shard_map/ppermute | solution.py:44
  89.3 12.8 %collective-permute-start.27 = (bf16[1,2,128,1024]{3,2,1,0:T(8,128)(2,1)S(1)}, bf16[1,2,128,1024]{3,2,1,0:T(8,128)(2,1)S(1)}, u32[]{:S(2)}, u32[]{:S(2)}) collective-permute-start(bf16[1,2,128,1024]{3,2,1,0:T(8,128)(2,1)S(1)} %join.9.refs_3_), channel_id=1, source_target_pairs={{0,8},{16,80},{1,9},{17,81},{2,10},{18,82},{3,11},{19,83},{4,12},{... | collective-permute-start | bytes 1572872 | tf_op jit(solution)/shard_map/ppermute | solution.py:36
  95.6 11.4 %collective-permute-start.30 = (bf16[1,2,128,1024]{3,2,1,0:T(8,128)(2,1)S(1)}, bf16[1,2,128,1024]{3,2,1,0:T(8,128)(2,1)S(1)}, u32[]{:S(2)}, u32[]{:S(2)}) collective-permute-start(bf16[1,2,128,1024]{3,2,1,0:T(8,128)(2,1)S(1)} %get-tuple-element.50), channel_id=1, source_target_pairs={{0,16},{16,0},{32,48},{48,32},{64,80},{80,64},{96,112},{112,96},{1... | collective-permute-start | bytes 1572872 | tf_op jit(solution)/shard_map/ppermute | solution.py:44
  96.8 11.1 %collective-permute-start.33 = (bf16[1,2,128,1024]{3,2,1,0:T(8,128)(2,1)S(1)}, bf16[1,2,128,1024]{3,2,1,0:T(8,128)(2,1)S(1)}, u32[]{:S(2)}, u32[]{:S(2)}) collective-permute-start(bf16[1,2,128,1024]{3,2,1,0:T(8,128)(2,1)S(1)} %join.11), channel_id=1, source_target_pairs={{0,1},{16,19},{1,0},{17,18},{2,3},{18,17},{3,2},{19,16},{4,5},{20,... | collective-permute-start | bytes 1572872 | tf_op jit(solution)/shard_map/ppermute | solution.py:36
  99.1 9.3 %collective-permute-start.36 = (bf16[1,2,128,1024]{3,2,1,0:T(8,128)(2,1)S(1)}, bf16[1,2,128,1024]{3,2,1,0:T(8,128)(2,1)S(1)}, u32[]{:S(2)}, u32[]{:S(2)}) collective-permute-start(bf16[1,2,128,1024]{3,2,1,0:T(8,128)(2,1)S(1)} %join.12), channel_id=1, source_target_pairs={{0,4},{16,48},{1,5},{17,49},{2,6},{18,50},{3,7},{19,51},{4,8},{20,... | collective-permute-start | bytes 1572872 | tf_op jit(solution)/shard_map/ppermute | solution.py:36
  100.1 8.3 %collective-permute-start.38 = (bf16[1,2,128,1024]{3,2,1,0:T(8,128)(2,1)S(1)}, bf16[1,2,128,1024]{3,2,1,0:T(8,128)(2,1)S(1)}, u32[]{:S(2)}, u32[]{:S(2)}) collective-permute-start(bf16[1,2,128,1024]{3,2,1,0:T(8,128)(2,1)S(1)} %join.13), channel_id=1, source_target_pairs={{0,12},{16,112},{1,13},{17,113},{2,14},{18,114},{3,15},{19,115},{4... | collective-permute-start | bytes 1572872 | tf_op jit(solution)/shard_map/ppermute | solution.py:36
  102.1 2.9 %collective-permute-start.28 = (f32[8,128]{1,0:T(8,128)S(1)}, f32[8,128]{1,0:T(8,128)S(1)}, u32[]{:S(2)}, u32[]{:S(2)}) collective-permute-start(f32[8,128]{1,0:T(8,128)S(1)} %after.1), channel_id=1, source_target_pairs={{16,17},{0,3},{17,16},{1,2},{18,19},{2,1},{19,18},{3,0},{20,21},{4... | collective-permute-start | bytes 12296 | tf_op jit(solution)/shard_map/ppermute | solution.py:36
  105.0 2.9 %collective-permute-start.29 = (f32[8,128]{1,0:T(8,128)S(1)}, f32[8,128]{1,0:T(8,128)S(1)}, u32[]{:S(2)}, u32[]{:S(2)}) collective-permute-start(f32[8,128]{1,0:T(8,128)S(1)} %add.6), channel_id=1, source_target_pairs={{0,16},{16,0},{32,48},{48,32},{64,80},{80,64},{96,112},{112,96},{1... | collective-permute-start | bytes 12296 | tf_op jit(solution)/shard_map/ppermute | solution.py:44
  108.7 2.0 %collective-permute-start.39 = (f32[128,1024]{1,0:T(8,128)S(1)}, f32[128,1024]{1,0:T(8,128)S(1)}, u32[]{:S(2)}, u32[]{:S(2)}) collective-permute-start(f32[128,1024]{1,0:T(8,128)S(1)} %get-tuple-element.58), channel_id=1, source_target_pairs={{0,16},{16,0},{32,48},{48,32},{64,80},{80,64},{96,112},{112,96},{1... | collective-permute-start | bytes 1572872 | tf_op jit(solution)/shard_map/ppermute | solution.py:44

commit v6 on v5

--- a/solution.py
+++ b/solution.py
@@ -49,7 +49,7 @@
     return row // 2, row % 2, col // 4, col % 4
 
 
-OFFSETS = [(2, 0), (1, 0), (0, 1), (3, 1), (0, 0), (3, 0), (1, 1), (2, 1)]
+OFFSETS = [(0, 0), (3, 1), (2, 0), (3, 0), (2, 1), (1, 1), (1, 0), (0, 1)]
 
 
 def load_copies(core, y, z, x, mine, theirs, q_dst, p_dst, sems):
@@ -190,23 +190,42 @@
     lax.fori_loop(0, 1024 // TILE, step, 0)
 
 
-def grad_kernel(flip, order, n_ties, *refs):
+def grad_kernel(flip, order, n_parts, n_ties, *refs):
     n = len(order)
     steps = [(g, i, d) for g, group in enumerate(order) for i, d in enumerate(group)]
-    (slope, qt, pt, part, far_part), refs = refs[:5], refs[5 + n_ties :]
+    (slope, qt, pt), parts, refs = refs[:3], refs[3 : 3 + n_parts], refs[3 + n_parts + n_ties :]
     keeps, sends, (part_out, gq, gp, zeros, out_sems) = refs[:n], refs[n : 2 * n], refs[2 * n :]
-    part_out[...] = part[...] + far_part[...]
+    part_out[...] = sum((p[...] for p in parts), jnp.zeros((8, 128), f32))
     y, core, z, x = place()
     zeros[...] = jnp.zeros(zeros.shape, bf16)
     half = (x % 2) ^ flip
     rank = (x // 2) ^ flip
-    rows = pl.ds(pl.multiple_of(half * 512, 512), 512)
+    whole = len(steps) == 4
+
+    def q_rows(k, d):
+        return (z + d) % 4 * 128 if whole else k * 128
+
+    def p_rows(k, d):
+        return (y + d) % 4 * 256 if whole else k * 256
+
+    def slope_rows(h):
+        if whole:
+            return slope[h, pl.ds(pl.multiple_of(half * 512, 512), 512), :]
+        starts = [pl.multiple_of(half * 512 + (z + d) % 4 * 128, 128) for _, _, d in steps]
+        return jnp.concatenate([slope[h, pl.ds(r, 128), :] for r in starts], axis=0)
+
+    def q_flip_rows():
+        if whole:
+            return qt[...]
+        starts = [pl.multiple_of((y + d) % 4 * 256, 256) for _, _, d in steps]
+        return jnp.concatenate([qt[pl.ds(r, 256), :] for r in starts], axis=0)
+
 
     def send_queries(which):
         copies = []
         for k, (g, i, d) in enumerate(steps):
             to = (sends if which else keeps)[g].at[i]
-            at = pl.ds(pl.multiple_of((z + d) % 4 * 128, 128), 128)
+            at = pl.ds(pl.multiple_of(q_rows(k, d), 128), 128)
             copies.append(pltpu.make_async_copy(gq.at[at], to.at[which], out_sems.at[k, 0]))
             copies.append(pltpu.make_async_copy(zeros, to.at[1 - which], out_sems.at[k, 1]))
         return copies
@@ -216,7 +235,7 @@
         for k, (g, i, d) in enumerate(steps):
             to = (keeps if which else sends)[g].at[i]
             for part in range(2):
-                at = pl.ds(pl.multiple_of((y + d) % 4 * 256 + (1 - part) * 128, 128), 128)
+                at = pl.ds(pl.multiple_of(p_rows(k, d) + (1 - part) * 128, 128), 128)
                 copies.append(
                     pltpu.make_async_copy(gp.at[at, cut], to.at[part, :, cut], out_sems.at[k, 2 + 2 * m + part])
                 )
@@ -234,7 +253,7 @@
         cut = slice(m * 256, m * 256 + 256)
         g = sum(
             lax.dot_general(
-                slope[h, rows, :], pt[h, cut, :], (((1,), (1,)), ((), ())), preferred_element_type=f32
+                slope_rows(h), pt[h, cut, :], (((1,), (1,)), ((), ())), preferred_element_type=f32
             )
             for h in range(2)
         )
@@ -242,7 +261,7 @@
     start(send_queries)
     cuts = [slice(m * 512, m * 512 + 512) for m in range(2)]
     for m, cut in enumerate(cuts):
-        g = jnp.dot(qt[...], slope[rank, :, cut], preferred_element_type=f32)
+        g = jnp.dot(q_flip_rows(), slope[rank, :, cut], preferred_element_type=f32)
         gp[:, cut] = (logit_scale * g).astype(bf16)
         start(functools.partial(send_passages, m=m, cut=cut))
 
@@ -403,21 +422,23 @@
     )(scores, target, own_lse, got_lse)
 
 
-def grads_of(flip, order, operands, ties):
+def grads_of(flip, order, operands, parts, ties):
+    n = sum(len(group) for group in order)
+    operands = (*operands, *parts)
     chunks = [arr((len(group), 2, 128, 1024), bf16) for group in order]
     return pl.pallas_call(
-        functools.partial(grad_kernel, flip, order, len(ties)),
+        functools.partial(grad_kernel, flip, order, len(parts), len(ties)),
         out_shape=chunks * 2 + [arr((8, 128), f32)],
         in_specs=[VM] * len(operands) + [ANY] * len(ties),
         out_specs=[VM] * (2 * len(chunks) + 1),
         scratch_shapes=[
-            pltpu.VMEM((512, 1024), bf16),
-            pltpu.VMEM((1024, 1024), bf16),
+            pltpu.VMEM((n * 128, 1024), bf16),
+            pltpu.VMEM((n * 256, 1024), bf16),
             pltpu.VMEM((128, 1024), bf16),
-            pltpu.SemaphoreType.DMA((4, 6)),
+            pltpu.SemaphoreType.DMA((n, 6)),
         ],
         compiler_params=pltpu.CompilerParams(vmem_limit_bytes=12 * MIB),
-        cost_estimate=cost(2 * 1024**2 * 2048, 20 * MIB),
+        cost_estimate=cost(n * 1024**3, n * 5 * MIB),
         name="grads_far" if flip else "grads_near",
     )(*operands, *ties)
 
@@ -497,7 +518,7 @@
     across = hop(own, 0, True)
     down_across, up_across = hop(down, 0, True), hop(up, 0, True)
     far_across = hop(across, 2, False)
-    chunks = [far, up, across, down_across, own, down, up_across, far_across]
+    chunks = [own, down_across, far, down, far_across, up_across, up, across]
     others = [swap(c) for c in chunks]
 
     target = aims_of(positive)
@@ -508,21 +529,23 @@
     own_lse, part = merge([stats, hop(stats, 2, False), hop(stats, 1, False), hop(stats, 3, False)], last=True)
     slope = slope_of(scores, target, own_lse, swap(own_lse))
 
-    outs = grads_of(1, ((1, 3), (2,), (0,)), (slope, q_flip, p_tile, part, hop_xor(part, 1)), ())
-    keeps, recvs, part = outs[:3], [swap(s) for s in outs[3:6]], outs[6]
-    sides, beyond = join([keeps[0], recvs[0]]), join([keeps[1], recvs[1]])
+    tiles = (slope, q_flip, p_tile)
+    outs = grads_of(1, ((1, 3),), tiles, (part, hop_xor(part, 1)), ())
+    sides, part = join([outs[0], swap(outs[1])]), outs[2]
+    outs = grads_of(1, ((2,), (0,)), tiles, (part,), ())
+    moved = hop(part, 2, False, 1)
+    beyond, across, part = join([outs[0], swap(outs[2])]), [outs[1], swap(outs[3])], outs[4]
     ready = (sides, beyond)
     sides, beyond = hop(sides, 0, True), hop(beyond, 2, False)
-    across = [keeps[2], recvs[2]]
-    outs = grads_of(0, ((1,), (3,), (2,), (0,)), (slope, q_flip, p_tile, part, hop(part, 2, False, 1)), ready)
-    part = outs[8]
-    keeps, recvs = outs[:4], [swap(s) for s in outs[4:8]]
-    far = join([keeps[2], recvs[2]])
-    up = join([keeps[0], recvs[0], sides], (far,), pick=0)
-    down = join([keeps[1], recvs[1], sides], (far,), pick=1)
-    across = hop(join([*across, beyond], (far,)), 0, True)
+    outs = grads_of(0, ((2,), (0,)), tiles, (part, moved), ready)
+    far = join([outs[0], swap(outs[2])])
+    home = join([outs[1], swap(outs[3])])
+    outs = grads_of(0, ((1,), (3,)), tiles, (outs[4],), ())
+    part = outs[4]
+    up = join([outs[0], swap(outs[2]), sides], (), pick=0)
+    down = join([outs[1], swap(outs[3]), sides], (), pick=1)
+    across = hop(join([*across, beyond], ()), 0, True)
     far, up, down = hop(far, 2, False), hop(up, 1, False), hop(down, 3, False)
-    home = join([keeps[3], recvs[3]])
     part = after(part, far)
     part = part + hop(part, 0, True, 1)
     part = part + swap(part)

time: 113 us -> 110 us (0.973)
  waiting for transfers between devices: 25.5 us -> 21.3 us
    ppermute x19, starting transfers between devices: 38.3 us -> 35.3 us  [hop(): lax.ppermute(a, AX, moves(lambda r, x, other: ((r + d) % 4, other if flip...]
    ppermute x19, waiting for transfers between devices: 20.1 us -> 17.3 us  [hop(): lax.ppermute(a, AX, moves(lambda r, x, other: ((r + d) % 4, other if flip...]
    ppermute x20, starting transfers between devices: 15.8 us -> 18.4 us  [swap(): return lax.ppermute(a, 'row', [(i, i ^ 1) for i in range(8)])]
    ppermute x20, waiting for transfers between devices: 5.39 us -> 3.99 us  [swap(): return lax.ppermute(a, 'row', [(i, i ^ 1) for i in range(8)])]
    pallas_call x2 -> x4, Pallas kernels: 11.3 us -> 12.3 us  [grads_of(): pl.pallas_call(functools.partial(grad_kernel, flip, order, len(parts), le...]
  transfers between devices with their start and end apart: 40 -> 40, of which waited for: 16 -> 17; matrix products, arithmetic and copies ran while one was open for 0% -> 0% of each run, Pallas kernels for 10% -> 13%
where the time goes in v6:
time: 110 us
  starting transfers between devices  54.2 us (49%)
  Pallas kernels  28.2 us (26%)
  waiting for transfers between devices  21.3 us (19%)
  local copies, waits for them, and re-layouts  3.1 us (3%)
  between operations  2.67 us (2%)
    ppermute x19, starting transfers between devices, hop(): lax.ppermute(a, AX, moves(lambda r, x, other: ((r + d) % 4, other if flip...  35.3 us
    ppermute x20, starting transfers between devices, swap(): return lax.ppermute(a, 'row', [(i, i ^ 1) for i in range(8)])  18.4 us
    ppermute x19, waiting for transfers between devices, hop(): lax.ppermute(a, AX, moves(lambda r, x, other: ((r + d) % 4, other if flip...  17.3 us
    pallas_call x4, Pallas kernels, grads_of(): pl.pallas_call(functools.partial(grad_kernel, flip, order, len(parts), le...  12.3 us
    pallas_call x1, Pallas kernels, scores_of(): pl.pallas_call(score_kernel, out_shape=(arr((2, 1024, 1024), f32), arr((3...  8.75 us
    ppermute x20, waiting for transfers between devices, swap(): return lax.ppermute(a, 'row', [(i, i ^ 1) for i in range(8)])  3.99 us
    pallas_call x1, Pallas kernels, slope_of(): pl.pallas_call(slope_kernel, out_shape=arr((2, 1024, 1024), bf16), in_spe...  3.49 us
    unnamed x6, local copies, waits for them, and re-layouts  2.59 us
  transfers between devices with their start and end apart: 40, of which 17 were waited for; matrix products, arithmetic and copies ran while one was open for 0% of the time, Pallas kernels for 13%

profile of v6, /device:TPU:1, one launch (start us, length us, event | category | flops | bytes accessed | tf_op | source)
XLA Modules:
  0.0 109.6 jit_solution(11637438886555898619)
XLA Ops:
  0.6 0.9 copy-done
  1.6 0.9 copy-done.1
  2.7 1.5 %collective-permute-start = (bf16[128,1024]{1,0:T(8,128)(2,1)S(1)}, bf16[128,1024]{1,0:T(8,128)(2,1)S(1)}, u32[]{:S(2)}, u32[]{:S(2)}) collective-permute-start(bf16[128,1024]{1,0:T(8,128)(2,1)S(1)} %get-tuple-element.35), channel_id=1, source_target_pairs={{0,16},{16,0},{32,48},{48,32},{64,80},{80,64},{96,112},{112,96},{1... | collective-permute-start | bytes 786440 | tf_op jit(solution)/shard_map/ppermute | solution.py:44
  4.2 1.2 %collective-permute-done = bf16[128,1024]{1,0:T(8,128)(2,1)S(1)} collective-permute-done((bf16[128,1024]{1,0:T(8,128)(2,1)S(1)}, bf16[128,1024]{1,0:T(8,128)(2,1)S(1)}, u32[]{:S(2)}, u32[]{:S(2)}) %collective-permute-start) | collective-permute-done | bytes 262176 | tf_op jit(solution)/shard_map/ppermute | solution.py:44
  5.4 1.4 %collective-permute-start.6 = (bf16[2,128,1024]{2,1,0:T(8,128)(2,1)S(1)}, bf16[2,128,1024]{2,1,0:T(8,128)(2,1)S(1)}, u32[]{:S(2)}, u32[]{:S(2)}) collective-permute-start(bf16[2,128,1024]{2,1,0:T(8,128)(2,1)S(1)} %pad_maximum_fusion.refs_0_), channel_id=1, source_target_pairs={{0,4},{16,48},{1,5},{17,49},{2,6},{18,50},{3,7},{19,51},{4,8},{20,... | collective-permute-start | bytes 1572872 | tf_op jit(solution)/shard_map/ppermute | solution.py:36
  6.9 1.0 collective-permute-start.8
  7.9 2.5 %collective-permute-start.4 = (bf16[2,128,1024]{2,1,0:T(8,128)(2,1)S(1)}, bf16[2,128,1024]{2,1,0:T(8,128)(2,1)S(1)}, u32[]{:S(2)}, u32[]{:S(2)}) collective-permute-start(bf16[2,128,1024]{2,1,0:T(8,128)(2,1)S(1)} %pad_maximum_fusion.refs_0_), channel_id=1, source_target_pairs={{0,1},{16,19},{1,0},{17,18},{2,3},{18,17},{3,2},{19,16},{4,5},{20,... | collective-permute-start | bytes 1572872 | tf_op jit(solution)/shard_map/ppermute | solution.py:36
  10.4 2.9 %collective-permute-start.3 = (bf16[2,128,1024]{2,1,0:T(8,128)(2,1)S(1)}, bf16[2,128,1024]{2,1,0:T(8,128)(2,1)S(1)}, u32[]{:S(2)}, u32[]{:S(2)}) collective-permute-start(bf16[2,128,1024]{2,1,0:T(8,128)(2,1)S(1)} %pad_maximum_fusion.refs_0_), channel_id=1, source_target_pairs={{0,8},{16,80},{1,9},{17,81},{2,10},{18,82},{3,11},{19,83},{4,12},{... | collective-permute-start | bytes 1572872 | tf_op jit(solution)/shard_map/ppermute | solution.py:36
  13.3 0.8 collective-permute-start.1
  14.0 1.1 %collective-permute-done.6.refs_6_ = bf16[2,128,1024]{2,1,0:T(8,128)(2,1)S(1)} collective-permute-done((bf16[2,128,1024]{2,1,0:T(8,128)(2,1)S(1)}, bf16[2,128,1024]{2,1,0:T(8,128)(2,1)S(1)}, u32[]{:S(2)}, u32[]{:S(2)}) %collective-permute-start.6) | collective-permute-done | bytes 524320 | tf_op jit(solution)/shard_map/ppermute | solution.py:36
  15.2 2.0 %collective-permute-start.14 = (bf16[2,128,1024]{2,1,0:T(8,128)(2,1)S(1)}, bf16[2,128,1024]{2,1,0:T(8,128)(2,1)S(1)}, u32[]{:S(2)}, u32[]{:S(2)}) collective-permute-start(bf16[2,128,1024]{2,1,0:T(8,128)(2,1)S(1)} %collective-permute-done.6.refs_6_), channel_id=1, source_target_pairs={{0,16},{16,0},{32,48},{48,32},{64,80},{80,64},{96,112},{112,96},{1... | collective-permute-start | bytes 1572872 | tf_op jit(solution)/shard_map/ppermute | solution.py:44
  17.2 2.5 %collective-permute-start.7 = (bf16[2,128,1024]{2,1,0:T(8,128)(2,1)S(1)}, bf16[2,128,1024]{2,1,0:T(8,128)(2,1)S(1)}, u32[]{:S(2)}, u32[]{:S(2)}) collective-permute-start(bf16[2,128,1024]{2,1,0:T(8,128)(2,1)S(1)} %collective-permute-done.6.refs_6_), channel_id=1, source_target_pairs={{0,1},{16,19},{1,0},{17,18},{2,3},{18,17},{3,2},{19,16},{4,5},{20,... | collective-permute-start | bytes 1572872 | tf_op jit(solution)/shard_map/ppermute | solution.py:36
  19.7 2.3 %collective-permute-done.3.refs_2_ = bf16[2,128,1024]{2,1,0:T(8,128)(2,1)S(1)} collective-permute-done((bf16[2,128,1024]{2,1,0:T(8,128)(2,1)S(1)}, bf16[2,128,1024]{2,1,0:T(8,128)(2,1)S(1)}, u32[]{:S(2)}, u32[]{:S(2)}) %collective-permute-start.3) | collective-permute-done | bytes 524320 | tf_op jit(solution)/shard_map/ppermute | solution.py:36
  22.0 3.0 %collective-permute-start.5 = (bf16[2,128,1024]{2,1,0:T(8,128)(2,1)S(1)}, bf16[2,128,1024]{2,1,0:T(8,128)(2,1)S(1)}, u32[]{:S(2)}, u32[]{:S(2)}) collective-permute-start(bf16[2,128,1024]{2,1,0:T(8,128)(2,1)S(1)} %collective-permute-done.4.refs_7_), channel_id=1, source_target_pairs={{0,8},{16,80},{1,9},{17,81},{2,10},{18,82},{3,11},{19,83},{4,12},{... | collective-permute-start | bytes 1572872 | tf_op jit(solution)/shard_map/ppermute | solution.py:36
  25.0 1.2 %collective-permute-done.1.refs_3_ = bf16[2,128,1024]{2,1,0:T(8,128)(2,1)S(1)} collective-permute-done((bf16[2,128,1024]{2,1,0:T(8,128)(2,1)S(1)}, bf16[2,128,1024]{2,1,0:T(8,128)(2,1)S(1)}, u32[]{:S(2)}, u32[]{:S(2)}) %collective-permute-start.1) | collective-permute-done | bytes 524320 | tf_op jit(solution)/shard_map/ppermute | solution.py:36
  26.4 1.5 %collective-permute-start.11 = (bf16[2,128,1024]{2,1,0:T(8,128)(2,1)S(1)}, bf16[2,128,1024]{2,1,0:T(8,128)(2,1)S(1)}, u32[]{:S(2)}, u32[]{:S(2)}) collective-permute-start(bf16[2,128,1024]{2,1,0:T(8,128)(2,1)S(1)} %collective-permute-done.1.refs_3_), channel_id=1, source_target_pairs={{0,16},{16,0},{32,48},{48,32},{64,80},{80,64},{96,112},{112,96},{1... | collective-permute-start | bytes 1572872 | tf_op jit(solution)/shard_map/ppermute | solution.py:44
  28.4 3.5 %collective-permute-done.5.refs_4_ = bf16[2,128,1024]{2,1,0:T(8,128)(2,1)S(1)} collective-permute-done((bf16[2,128,1024]{2,1,0:T(8,128)(2,1)S(1)}, bf16[2,128,1024]{2,1,0:T(8,128)(2,1)S(1)}, u32[]{:S(2)}, u32[]{:S(2)}) %collective-permute-start.5) | collective-permute-done | bytes 524320 | tf_op jit(solution)/shard_map/ppermute | solution.py:36
  31.9 3.0 %collective-permute-start.12 = (bf16[2,128,1024]{2,1,0:T(8,128)(2,1)S(1)}, bf16[2,128,1024]{2,1,0:T(8,128)(2,1)S(1)}, u32[]{:S(2)}, u32[]{:S(2)}) collective-permute-start(bf16[2,128,1024]{2,1,0:T(8,128)(2,1)S(1)} %collective-permute-done.5.refs_4_), channel_id=1, source_target_pairs={{0,16},{16,0},{32,48},{48,32},{64,80},{80,64},{96,112},{112,96},{1... | collective-permute-start | bytes 1572872 | tf_op jit(solution)/shard_map/ppermute | solution.py:44
  35.4 1.4 %collective-permute-start.9 = (bf16[2,128,1024]{2,1,0:T(8,128)(2,1)S(1)}, bf16[2,128,1024]{2,1,0:T(8,128)(2,1)S(1)}, u32[]{:S(2)}, u32[]{:S(2)}) collective-permute-start(bf16[2,128,1024]{2,1,0:T(8,128)(2,1)S(1)} %collective-permute-done.2.refs_1_), channel_id=1, source_target_pairs={{0,16},{16,0},{32,48},{48,32},{64,80},{80,64},{96,112},{112,96},{1... | collective-permute-start | bytes 1572872 | tf_op jit(solution)/shard_map/ppermute | solution.py:44
  36.8 0.7 copy-done.2
  37.8 0.6 collective-permute-done.9.refs_9_
  38.4 8.7 %scores.1 = (f32[2,1024,1024]{2,1,0:T(8,128)S(1)}, f32[3,2048]{1,0:T(4,128)S(1)}, f32[3,2048]{1,0:T(4,128)S(1)}, bf16[1024,1024]{1,0:T(8,128)(2,1)S(1)}, bf16[2,1024,1024]{2,1,0:T(8,128)(2,1)S(1)}) custom-call(bf16[2,128,1024]{2,1,0:T(8,128)(2,1)S(1)} %pad_maximum_fusion.refs_0_, bf16[2,128,1024]{2,1,0:T(8,128)(2,1)S(1)} %collective-permute-done.2.refs_1_, ...), custom_call_target="tpu_custom_call" | custom-call | flops 4294967296 | bytes 16777216 | tf_op jit(solution)/shard_map/scores/pallas_call | solution.py:289
  47.6 0.9 collective-permute-done.16.refs_1_
  48.4 1.4 %collective-permute-start.17 = (f32[3,2048]{1,0:T(4,128)S(1)}, f32[3,2048]{1,0:T(4,128)S(1)}, u32[]{:S(2)}, u32[]{:S(2)}) collective-permute-start(f32[3,2048]{1,0:T(4,128)S(1)} %merge.3.refs_0_), channel_id=1, source_target_pairs={{0,1},{16,19},{1,0},{17,18},{2,3},{18,17},{3,2},{19,16},{4,5},{20,... | collective-permute-start | bytes 73736 | tf_op jit(solution)/shard_map/ppermute | solution.py:36
  49.8 0.7 flip.1.refs_2_.refs_1_
  50.5 2.0 %collective-permute-done.17.refs_1_ = f32[3,2048]{1,0:T(4,128)S(1)} collective-permute-done((f32[3,2048]{1,0:T(4,128)S(1)}, f32[3,2048]{1,0:T(4,128)S(1)}, u32[]{:S(2)}, u32[]{:S(2)}) %collective-permute-start.17) | collective-permute-done | bytes 24608 | tf_op jit(solution)/shard_map/ppermute | solution.py:36
  52.5 2.8 %collective-permute-start.20 = (f32[3,2048]{1,0:T(4,128)S(1)}, f32[3,2048]{1,0:T(4,128)S(1)}, u32[]{:S(2)}, u32[]{:S(2)}) collective-permute-start(f32[3,2048]{1,0:T(4,128)S(1)} %merge.4.refs_0_), channel_id=1, source_target_pairs={{0,12},{16,112},{1,13},{17,113},{2,14},{18,114},{3,15},{19,115},{4... | collective-permute-start | bytes 73736 | tf_op jit(solution)/shard_map/ppermute | solution.py:36
  55.3 1.6 %collective-permute-start.18 = (f32[3,2048]{1,0:T(4,128)S(1)}, f32[3,2048]{1,0:T(4,128)S(1)}, u32[]{:S(2)}, u32[]{:S(2)}) collective-permute-start(f32[3,2048]{1,0:T(4,128)S(1)} %merge.4.refs_0_), channel_id=1, source_target_pairs={{0,8},{16,80},{1,9},{17,81},{2,10},{18,82},{3,11},{19,83},{4,12},{... | collective-permute-start | bytes 73736 | tf_op jit(solution)/shard_map/ppermute | solution.py:36
  57.0 2.6 %collective-permute-done.19.refs_2_ = f32[3,2048]{1,0:T(4,128)S(1)} collective-permute-done((f32[3,2048]{1,0:T(4,128)S(1)}, f32[3,2048]{1,0:T(4,128)S(1)}, u32[]{:S(2)}, u32[]{:S(2)}) %collective-permute-start.19) | collective-permute-done | bytes 24608 | tf_op jit(solution)/shard_map/ppermute | solution.py:36
  61.3 3.5 %slope.1.refs_0_ = bf16[2,1024,1024]{2,1,0:T(8,128)(2,1)S(1)} custom-call(f32[2,1024,1024]{2,1,0:T(8,128)S(1)} %get-tuple-element.36.sv, f32[1024,128]{1,0:T(8,128)S(1)} %aims.1.refs_16_.target, f32[1,2048]{1,0:T(1,128)S(1)} %get-tuple-element.40.own_lse, f32[1,2048]{1,0:T(1,128)S(1)} %collective-permute-done.21.got_lse), custom_call_target="tpu_custom_call" | custom-call | flops 4294967296 | bytes 12582912 | tf_op jit(solution)/shard_map/slope/pallas_call | solution.py:413
  64.8 3.1 %grads_far.2 = (bf16[2,2,128,1024]{3,2,1,0:T(8,128)(2,1)S(1)}, bf16[2,2,128,1024]{3,2,1,0:T(8,128)(2,1)S(1)}, f32[8,128]{1,0:T(8,128)S(1)}) custom-call(bf16[2,1024,1024]{2,1,0:T(8,128)(2,1)S(1)} %slope.1.refs_0_, bf16[1024,1024]{1,0:T(8,128)(2,1)S(1)} %flip.1.refs_2_.refs_1_, bf16[2,1024,1024]{2,1,0:T(8,128)(2,1)S(1)} %get-tuple-element.41.refs_2_, ...), custom_call_target="tpu_custom_call" | custom-call | flops 2147483648 | bytes 10485760 | tf_op jit(solution)/shard_map/grads_far/pallas_call | solution.py:429
  67.8 0.9 collective-permute-start.24
  68.8 3.1 %grads_far.3 = (bf16[1,2,128,1024]{3,2,1,0:T(8,128)(2,1)S(1)}, bf16[1,2,128,1024]{3,2,1,0:T(8,128)(2,1)S(1)}, bf16[1,2,128,1024]{3,2,1,0:T(8,128)(2,1)S(1)}, bf1...) custom-call(bf16[2,1024,1024]{2,1,0:T(8,128)(2,1)S(1)} %slope.1.refs_0_, bf16[1024,1024]{1,0:T(8,128)(2,1)S(1)} %flip.1.refs_2_.refs_1_, ...), custom_call_target="tpu_custom_call" | custom-call | flops 2147483648 | bytes 10485760 | tf_op jit(solution)/shard_map/grads_far/pallas_call | solution.py:429
  71.9 2.7 %collective-permute-start.23 = (f32[8,128]{1,0:T(8,128)S(1)}, f32[8,128]{1,0:T(8,128)S(1)}, u32[]{:S(2)}, u32[]{:S(2)}) collective-permute-start(f32[8,128]{1,0:T(8,128)S(1)} %get-tuple-element.43.refs_3_), channel_id=1, source_target_pairs={{16,24},{0,64},{17,25},{1,65},{18,26},{2,66},{19,27},{3,67},{20,28... | collective-permute-start | bytes 12296 | tf_op jit(solution)/shard_map/ppermute | solution.py:36
  75.0 2.5 %collective-permute-start.35 = (bf16[2,2,128,1024]{3,2,1,0:T(8,128)(2,1)S(1)}, bf16[2,2,128,1024]{3,2,1,0:T(8,128)(2,1)S(1)}, u32[]{:S(2)}, u32[]{:S(2)}) collective-permute-start(bf16[2,2,128,1024]{3,2,1,0:T(8,128)(2,1)S(1)} %join.7.refs_5_), channel_id=1, source_target_pairs={{0,1},{16,19},{1,0},{17,18},{2,3},{18,17},{3,2},{19,16},{4,5},{20,... | collective-permute-start | bytes 3145736 | tf_op jit(solution)/shard_map/ppermute | solution.py:36
  77.5 3.1 %grads_near.2 = (bf16[1,2,128,1024]{3,2,1,0:T(8,128)(2,1)S(1)}, bf16[1,2,128,1024]{3,2,1,0:T(8,128)(2,1)S(1)}, bf16[1,2,128,1024]{3,2,1,0:T(8,128)(2,1)S(1)}, bf...) custom-call(bf16[2,1024,1024]{2,1,0:T(8,128)(2,1)S(1)} %slope.1.refs_0_, bf16[1024,1024]{1,0:T(8,128)(2,1)S(1)} %flip.1.refs_2_.refs_1_, ...), custom_call_target="tpu_custom_call" | custom-call | flops 2147483648 | bytes 10485760 | tf_op jit(solution)/shard_map/grads_near/pallas_call | solution.py:429
  81.2 3.2 %collective-permute-start.32 = (bf16[1,2,128,1024]{3,2,1,0:T(8,128)(2,1)S(1)}, bf16[1,2,128,1024]{3,2,1,0:T(8,128)(2,1)S(1)}, u32[]{:S(2)}, u32[]{:S(2)}) collective-permute-start(bf16[1,2,128,1024]{3,2,1,0:T(8,128)(2,1)S(1)} %join.8.refs_6_), channel_id=1, source_target_pairs={{0,8},{16,80},{1,9},{17,81},{2,10},{18,82},{3,11},{19,83},{4,12},{... | collective-permute-start | bytes 1572872 | tf_op jit(solution)/shard_map/ppermute | solution.py:36
  84.5 3.1 %grads_near.3 = (bf16[1,2,128,1024]{3,2,1,0:T(8,128)(2,1)S(1)}, bf16[1,2,128,1024]{3,2,1,0:T(8,128)(2,1)S(1)}, bf16[1,2,128,1024]{3,2,1,0:T(8,128)(2,1)S(1)}, bf...) custom-call(bf16[2,1024,1024]{2,1,0:T(8,128)(2,1)S(1)} %slope.1.refs_0_, bf16[1024,1024]{1,0:T(8,128)(2,1)S(1)} %flip.1.refs_2_.refs_1_, ...), custom_call_target="tpu_custom_call" | custom-call | flops 2147483648 | bytes 10485760 | tf_op jit(solution)/shard_map/grads_near/pallas_call | solution.py:429
  88.5 2.3 %collective-permute-start.27 = (bf16[1,2,128,1024]{3,2,1,0:T(8,128)(2,1)S(1)}, bf16[1,2,128,1024]{3,2,1,0:T(8,128)(2,1)S(1)}, u32[]{:S(2)}, u32[]{:S(2)}) collective-permute-start(bf16[1,2,128,1024]{3,2,1,0:T(8,128)(2,1)S(1)} %join.9), channel_id=1, source_target_pairs={{0,8},{16,80},{1,9},{17,81},{2,10},{18,82},{3,11},{19,83},{4,12},{... | collective-permute-start | bytes 1572872 | tf_op jit(solution)/shard_map/ppermute | solution.py:36
  91.3 0.7 collective-permute-start.30
  92.2 2.2 %collective-permute-start.33 = (bf16[1,2,128,1024]{3,2,1,0:T(8,128)(2,1)S(1)}, bf16[1,2,128,1024]{3,2,1,0:T(8,128)(2,1)S(1)}, u32[]{:S(2)}, u32[]{:S(2)}) collective-permute-start(bf16[1,2,128,1024]{3,2,1,0:T(8,128)(2,1)S(1)} %join.11), channel_id=1, source_target_pairs={{0,1},{16,19},{1,0},{17,18},{2,3},{18,17},{3,2},{19,16},{4,5},{20,... | collective-permute-start | bytes 1572872 | tf_op jit(solution)/shard_map/ppermute | solution.py:36
  94.5 0.9 collective-permute-start.36
  95.6 2.0 %collective-permute-start.38 = (bf16[1,2,128,1024]{3,2,1,0:T(8,128)(2,1)S(1)}, bf16[1,2,128,1024]{3,2,1,0:T(8,128)(2,1)S(1)}, u32[]{:S(2)}, u32[]{:S(2)}) collective-permute-start(bf16[1,2,128,1024]{3,2,1,0:T(8,128)(2,1)S(1)} %join.13), channel_id=1, source_target_pairs={{0,12},{16,112},{1,13},{17,113},{2,14},{18,114},{3,15},{19,115},{4... | collective-permute-start | bytes 1572872 | tf_op jit(solution)/shard_map/ppermute | solution.py:36
  97.6 0.8 collective-permute-done.27.refs_0_.refs_1_
  98.8 2.4 %collective-permute-done.28 = f32[8,128]{1,0:T(8,128)S(1)} collective-permute-done((f32[8,128]{1,0:T(8,128)S(1)}, f32[8,128]{1,0:T(8,128)S(1)}, u32[]{:S(2)}, u32[]{:S(2)}) %collective-permute-start.28) | collective-permute-done | bytes 4128 | tf_op jit(solution)/shard_map/ppermute | solution.py:36
  101.1 3.1 %collective-permute-start.29 = (f32[8,128]{1,0:T(8,128)S(1)}, f32[8,128]{1,0:T(8,128)S(1)}, u32[]{:S(2)}, u32[]{:S(2)}) collective-permute-start(f32[8,128]{1,0:T(8,128)S(1)} %add.6), channel_id=1, source_target_pairs={{0,16},{16,0},{32,48},{48,32},{64,80},{80,64},{96,112},{112,96},{1... | collective-permute-start | bytes 12296 | tf_op jit(solution)/shard_map/ppermute | solution.py:44
  104.4 0.7 collective-permute-done.29
  107.4 1.1 finish.1
  (64 shorter events, 9.2 us)
Async XLA Ops:
  0.6 1.0 copy-start
  1.6 0.9 copy-start.1
  2.7 2.7 %collective-permute-start = (bf16[128,1024]{1,0:T(8,128)(2,1)S(1)}, bf16[128,1024]{1,0:T(8,128)(2,1)S(1)}, u32[]{:S(2)}, u32[]{:S(2)}) collective-permute-start(bf16[128,1024]{1,0:T(8,128)(2,1)S(1)} %get-tuple-element.35), channel_id=1, source_target_pairs={{0,16},{16,0},{32,48},{48,32},{64,80},{80,64},{96,112},{112,96},{1... | collective-permute-start | bytes 786440 | tf_op jit(solution)/shard_map/ppermute | solution.py:44
  5.4 9.8 %collective-permute-start.6 = (bf16[2,128,1024]{2,1,0:T(8,128)(2,1)S(1)}, bf16[2,128,1024]{2,1,0:T(8,128)(2,1)S(1)}, u32[]{:S(2)}, u32[]{:S(2)}) collective-permute-start(bf16[2,128,1024]{2,1,0:T(8,128)(2,1)S(1)} %pad_maximum_fusion.refs_0_), channel_id=1, source_target_pairs={{0,4},{16,48},{1,5},{17,49},{2,6},{18,50},{3,7},{19,51},{4,8},{20,... | collective-permute-start | bytes 1572872 | tf_op jit(solution)/shard_map/ppermute | solution.py:36
  6.9 10.3 %collective-permute-start.8 = (bf16[2,128,1024]{2,1,0:T(8,128)(2,1)S(1)}, bf16[2,128,1024]{2,1,0:T(8,128)(2,1)S(1)}, u32[]{:S(2)}, u32[]{:S(2)}) collective-permute-start(bf16[2,128,1024]{2,1,0:T(8,128)(2,1)S(1)} %pad_maximum_fusion.refs_0_), channel_id=1, source_target_pairs={{0,16},{16,0},{32,48},{48,32},{64,80},{80,64},{96,112},{112,96},{1... | collective-permute-start | bytes 1572872 | tf_op jit(solution)/shard_map/ppermute | solution.py:44
  7.9 11.8 %collective-permute-start.4 = (bf16[2,128,1024]{2,1,0:T(8,128)(2,1)S(1)}, bf16[2,128,1024]{2,1,0:T(8,128)(2,1)S(1)}, u32[]{:S(2)}, u32[]{:S(2)}) collective-permute-start(bf16[2,128,1024]{2,1,0:T(8,128)(2,1)S(1)} %pad_maximum_fusion.refs_0_), channel_id=1, source_target_pairs={{0,1},{16,19},{1,0},{17,18},{2,3},{18,17},{3,2},{19,16},{4,5},{20,... | collective-permute-start | bytes 1572872 | tf_op jit(solution)/shard_map/ppermute | solution.py:36
  10.4 11.6 %collective-permute-start.3 = (bf16[2,128,1024]{2,1,0:T(8,128)(2,1)S(1)}, bf16[2,128,1024]{2,1,0:T(8,128)(2,1)S(1)}, u32[]{:S(2)}, u32[]{:S(2)}) collective-permute-start(bf16[2,128,1024]{2,1,0:T(8,128)(2,1)S(1)} %pad_maximum_fusion.refs_0_), channel_id=1, source_target_pairs={{0,8},{16,80},{1,9},{17,81},{2,10},{18,82},{3,11},{19,83},{4,12},{... | collective-permute-start | bytes 1572872 | tf_op jit(solution)/shard_map/ppermute | solution.py:36
  13.3 12.9 %collective-permute-start.1 = (bf16[2,128,1024]{2,1,0:T(8,128)(2,1)S(1)}, bf16[2,128,1024]{2,1,0:T(8,128)(2,1)S(1)}, u32[]{:S(2)}, u32[]{:S(2)}) collective-permute-start(bf16[2,128,1024]{2,1,0:T(8,128)(2,1)S(1)} %pad_maximum_fusion.refs_0_), channel_id=1, source_target_pairs={{0,12},{16,112},{1,13},{17,113},{2,14},{18,114},{3,15},{19,115},{4... | collective-permute-start | bytes 1572872 | tf_op jit(solution)/shard_map/ppermute | solution.py:36
  15.2 11.2 %collective-permute-start.14 = (bf16[2,128,1024]{2,1,0:T(8,128)(2,1)S(1)}, bf16[2,128,1024]{2,1,0:T(8,128)(2,1)S(1)}, u32[]{:S(2)}, u32[]{:S(2)}) collective-permute-start(bf16[2,128,1024]{2,1,0:T(8,128)(2,1)S(1)} %collective-permute-done.6.refs_6_), channel_id=1, source_target_pairs={{0,16},{16,0},{32,48},{48,32},{64,80},{80,64},{96,112},{112,96},{1... | collective-permute-start | bytes 1572872 | tf_op jit(solution)/shard_map/ppermute | solution.py:44
  17.2 10.7 %collective-permute-start.7 = (bf16[2,128,1024]{2,1,0:T(8,128)(2,1)S(1)}, bf16[2,128,1024]{2,1,0:T(8,128)(2,1)S(1)}, u32[]{:S(2)}, u32[]{:S(2)}) collective-permute-start(bf16[2,128,1024]{2,1,0:T(8,128)(2,1)S(1)} %collective-permute-done.6.refs_6_), channel_id=1, source_target_pairs={{0,1},{16,19},{1,0},{17,18},{2,3},{18,17},{3,2},{19,16},{4,5},{20,... | collective-permute-start | bytes 1572872 | tf_op jit(solution)/shard_map/ppermute | solution.py:36
  19.6 8.3 %collective-permute-start.15 = (bf16[2,128,1024]{2,1,0:T(8,128)(2,1)S(1)}, bf16[2,128,1024]{2,1,0:T(8,128)(2,1)S(1)}, u32[]{:S(2)}, u32[]{:S(2)}) collective-permute-start(bf16[2,128,1024]{2,1,0:T(8,128)(2,1)S(1)} %collective-permute-done.4.refs_7_), channel_id=1, source_target_pairs={{0,16},{16,0},{32,48},{48,32},{64,80},{80,64},{96,112},{112,96},{1... | collective-permute-start | bytes 1572872 | tf_op jit(solution)/shard_map/ppermute | solution.py:44
  22.0 9.9 %collective-permute-start.5 = (bf16[2,128,1024]{2,1,0:T(8,128)(2,1)S(1)}, bf16[2,128,1024]{2,1,0:T(8,128)(2,1)S(1)}, u32[]{:S(2)}, u32[]{:S(2)}) collective-permute-start(bf16[2,128,1024]{2,1,0:T(8,128)(2,1)S(1)} %collective-permute-done.4.refs_7_), channel_id=1, source_target_pairs={{0,8},{16,80},{1,9},{17,81},{2,10},{18,82},{3,11},{19,83},{4,12},{... | collective-permute-start | bytes 1572872 | tf_op jit(solution)/shard_map/ppermute | solution.py:36
  26.2 9.2 %collective-permute-start.2 = (bf16[2,128,1024]{2,1,0:T(8,128)(2,1)S(1)}, bf16[2,128,1024]{2,1,0:T(8,128)(2,1)S(1)}, u32[]{:S(2)}, u32[]{:S(2)}) collective-permute-start(bf16[2,128,1024]{2,1,0:T(8,128)(2,1)S(1)} %collective-permute-done.1.refs_3_), channel_id=1, source_target_pairs={{0,1},{16,19},{1,0},{17,18},{2,3},{18,17},{3,2},{19,16},{4,5},{20,... | collective-permute-start | bytes 1572872 | tf_op jit(solution)/shard_map/ppermute | solution.py:36
  26.4 11.3 %collective-permute-start.11 = (bf16[2,128,1024]{2,1,0:T(8,128)(2,1)S(1)}, bf16[2,128,1024]{2,1,0:T(8,128)(2,1)S(1)}, u32[]{:S(2)}, u32[]{:S(2)}) collective-permute-start(bf16[2,128,1024]{2,1,0:T(8,128)(2,1)S(1)} %collective-permute-done.1.refs_3_), channel_id=1, source_target_pairs={{0,16},{16,0},{32,48},{48,32},{64,80},{80,64},{96,112},{112,96},{1... | collective-permute-start | bytes 1572872 | tf_op jit(solution)/shard_map/ppermute | solution.py:44
  27.9 9.9 %collective-permute-start.10 = (bf16[2,128,1024]{2,1,0:T(8,128)(2,1)S(1)}, bf16[2,128,1024]{2,1,0:T(8,128)(2,1)S(1)}, u32[]{:S(2)}, u32[]{:S(2)}) collective-permute-start(bf16[2,128,1024]{2,1,0:T(8,128)(2,1)S(1)} %collective-permute-done.3.refs_2_), channel_id=1, source_target_pairs={{0,16},{16,0},{32,48},{48,32},{64,80},{80,64},{96,112},{112,96},{1... | collective-permute-start | bytes 1572872 | tf_op jit(solution)/shard_map/ppermute | solution.py:44
  28.0 9.8 %collective-permute-start.13 = (bf16[2,128,1024]{2,1,0:T(8,128)(2,1)S(1)}, bf16[2,128,1024]{2,1,0:T(8,128)(2,1)S(1)}, u32[]{:S(2)}, u32[]{:S(2)}) collective-permute-start(bf16[2,128,1024]{2,1,0:T(8,128)(2,1)S(1)} %collective-permute-done.7.refs_5_), channel_id=1, source_target_pairs={{0,16},{16,0},{32,48},{48,32},{64,80},{80,64},{96,112},{112,96},{1... | collective-permute-start | bytes 1572872 | tf_op jit(solution)/shard_map/ppermute | solution.py:44
  31.9 5.9 %collective-permute-start.12 = (bf16[2,128,1024]{2,1,0:T(8,128)(2,1)S(1)}, bf16[2,128,1024]{2,1,0:T(8,128)(2,1)S(1)}, u32[]{:S(2)}, u32[]{:S(2)}) collective-permute-start(bf16[2,128,1024]{2,1,0:T(8,128)(2,1)S(1)} %collective-permute-done.5.refs_4_), channel_id=1, source_target_pairs={{0,16},{16,0},{32,48},{48,32},{64,80},{80,64},{96,112},{112,96},{1... | collective-permute-start | bytes 1572872 | tf_op jit(solution)/shard_map/ppermute | solution.py:44
  35.4 2.9 %collective-permute-start.9 = (bf16[2,128,1024]{2,1,0:T(8,128)(2,1)S(1)}, bf16[2,128,1024]{2,1,0:T(8,128)(2,1)S(1)}, u32[]{:S(2)}, u32[]{:S(2)}) collective-permute-start(bf16[2,128,1024]{2,1,0:T(8,128)(2,1)S(1)} %collective-permute-done.2.refs_1_), channel_id=1, source_target_pairs={{0,16},{16,0},{32,48},{48,32},{64,80},{80,64},{96,112},{112,96},{1... | collective-permute-start | bytes 1572872 | tf_op jit(solution)/shard_map/ppermute | solution.py:44
  36.8 0.7 copy-start.2
  47.1 1.3 %collective-permute-start.16 = (f32[3,2048]{1,0:T(4,128)S(1)}, f32[3,2048]{1,0:T(4,128)S(1)}, u32[]{:S(2)}, u32[]{:S(2)}) collective-permute-start(f32[3,2048]{1,0:T(4,128)S(1)} %get-tuple-element.38), channel_id=1, source_target_pairs={{0,16},{16,0},{32,48},{48,32},{64,80},{80,64},{96,112},{112,96},{1... | collective-permute-start | bytes 73736 | tf_op jit(solution)/shard_map/ppermute | solution.py:44
  48.4 4.1 %collective-permute-start.17 = (f32[3,2048]{1,0:T(4,128)S(1)}, f32[3,2048]{1,0:T(4,128)S(1)}, u32[]{:S(2)}, u32[]{:S(2)}) collective-permute-start(f32[3,2048]{1,0:T(4,128)S(1)} %merge.3.refs_0_), channel_id=1, source_target_pairs={{0,1},{16,19},{1,0},{17,18},{2,3},{18,17},{3,2},{19,16},{4,5},{20,... | collective-permute-start | bytes 73736 | tf_op jit(solution)/shard_map/ppermute | solution.py:36
  52.5 4.5 %collective-permute-start.20 = (f32[3,2048]{1,0:T(4,128)S(1)}, f32[3,2048]{1,0:T(4,128)S(1)}, u32[]{:S(2)}, u32[]{:S(2)}) collective-permute-start(f32[3,2048]{1,0:T(4,128)S(1)} %merge.4.refs_0_), channel_id=1, source_target_pairs={{0,12},{16,112},{1,13},{17,113},{2,14},{18,114},{3,15},{19,115},{4... | collective-permute-start | bytes 73736 | tf_op jit(solution)/shard_map/ppermute | solution.py:36
  55.3 4.3 %collective-permute-start.19 = (f32[3,2048]{1,0:T(4,128)S(1)}, f32[3,2048]{1,0:T(4,128)S(1)}, u32[]{:S(2)}, u32[]{:S(2)}) collective-permute-start(f32[3,2048]{1,0:T(4,128)S(1)} %merge.4.refs_0_), channel_id=1, source_target_pairs={{0,4},{16,48},{1,5},{17,49},{2,6},{18,50},{3,7},{19,51},{4,8},{20,... | collective-permute-start | bytes 73736 | tf_op jit(solution)/shard_map/ppermute | solution.py:36
  55.3 4.6 %collective-permute-start.18 = (f32[3,2048]{1,0:T(4,128)S(1)}, f32[3,2048]{1,0:T(4,128)S(1)}, u32[]{:S(2)}, u32[]{:S(2)}) collective-permute-start(f32[3,2048]{1,0:T(4,128)S(1)} %merge.4.refs_0_), channel_id=1, source_target_pairs={{0,8},{16,80},{1,9},{17,81},{2,10},{18,82},{3,11},{19,83},{4,12},{... | collective-permute-start | bytes 73736 | tf_op jit(solution)/shard_map/ppermute | solution.py:36
  60.0 1.3 %collective-permute-start.21 = (f32[1,2048]{1,0:T(1,128)S(1)}, f32[1,2048]{1,0:T(1,128)S(1)}, u32[]{:S(2)}, u32[]{:S(2)}) collective-permute-start(f32[1,2048]{1,0:T(1,128)S(1)} %get-tuple-element.40.own_lse), channel_id=1, source_target_pairs={{0,16},{16,0},{32,48},{48,32},{64,80},{80,64},{96,112},{112,96},{1... | collective-permute-start | bytes 24584 | tf_op jit(solution)/shard_map/ppermute | solution.py:44
  60.4 4.3 %collective-permute-start.22 = (f32[8,128]{1,0:T(8,128)S(1)}, f32[8,128]{1,0:T(8,128)S(1)}, u32[]{:S(2)}, u32[]{:S(2)}) collective-permute-start(f32[8,128]{1,0:T(8,128)S(1)} %get-tuple-element.42.refs_3_), channel_id=1, source_target_pairs={{16,20},{0,32},{17,21},{1,33},{18,22},{2,34},{19,23},{3,35},{20,16... | collective-permute-start | bytes 12296 | tf_op jit(solution)/shard_map/ppermute | solution.py:40
  67.8 6.9 %collective-permute-start.24 = (bf16[2,2,128,1024]{3,2,1,0:T(8,128)(2,1)S(1)}, bf16[2,2,128,1024]{3,2,1,0:T(8,128)(2,1)S(1)}, u32[]{:S(2)}, u32[]{:S(2)}) collective-permute-start(bf16[2,2,128,1024]{3,2,1,0:T(8,128)(2,1)S(1)} %get-tuple-element.46), channel_id=1, source_target_pairs={{0,16},{16,0},{32,48},{48,32},{64,80},{80,64},{96,112},{112,96},{1... | collective-permute-start | bytes 3145736 | tf_op jit(solution)/shard_map/ppermute | solution.py:44
  71.8 2.8 %collective-permute-start.25 = (bf16[1,2,128,1024]{3,2,1,0:T(8,128)(2,1)S(1)}, bf16[1,2,128,1024]{3,2,1,0:T(8,128)(2,1)S(1)}, u32[]{:S(2)}, u32[]{:S(2)}) collective-permute-start(bf16[1,2,128,1024]{3,2,1,0:T(8,128)(2,1)S(1)} %get-tuple-element.48), channel_id=1, source_target_pairs={{0,16},{16,0},{32,48},{48,32},{64,80},{80,64},{96,112},{112,96},{1... | collective-permute-start | bytes 1572872 | tf_op jit(solution)/shard_map/ppermute | solution.py:44
  71.9 5.6 %collective-permute-start.23 = (f32[8,128]{1,0:T(8,128)S(1)}, f32[8,128]{1,0:T(8,128)S(1)}, u32[]{:S(2)}, u32[]{:S(2)}) collective-permute-start(f32[8,128]{1,0:T(8,128)S(1)} %get-tuple-element.43.refs_3_), channel_id=1, source_target_pairs={{16,24},{0,64},{17,25},{1,65},{18,26},{2,66},{19,27},{3,67},{20,28... | collective-permute-start | bytes 12296 | tf_op jit(solution)/shard_map/ppermute | solution.py:36
  75.0 19.4 %collective-permute-start.35 = (bf16[2,2,128,1024]{3,2,1,0:T(8,128)(2,1)S(1)}, bf16[2,2,128,1024]{3,2,1,0:T(8,128)(2,1)S(1)}, u32[]{:S(2)}, u32[]{:S(2)}) collective-permute-start(bf16[2,2,128,1024]{3,2,1,0:T(8,128)(2,1)S(1)} %join.7.refs_5_), channel_id=1, source_target_pairs={{0,1},{16,19},{1,0},{17,18},{2,3},{18,17},{3,2},{19,16},{4,5},{20,... | collective-permute-start | bytes 3145736 | tf_op jit(solution)/shard_map/ppermute | solution.py:36
  80.6 7.2 %collective-permute-start.26 = (bf16[1,2,128,1024]{3,2,1,0:T(8,128)(2,1)S(1)}, bf16[1,2,128,1024]{3,2,1,0:T(8,128)(2,1)S(1)}, u32[]{:S(2)}, u32[]{:S(2)}) collective-permute-start(bf16[1,2,128,1024]{3,2,1,0:T(8,128)(2,1)S(1)} %get-tuple-element.52), channel_id=1, source_target_pairs={{0,16},{16,0},{32,48},{48,32},{64,80},{80,64},{96,112},{112,96},{1... | collective-permute-start | bytes 1572872 | tf_op jit(solution)/shard_map/ppermute | solution.py:44
  80.7 7.8 %collective-permute-start.31 = (bf16[1,2,128,1024]{3,2,1,0:T(8,128)(2,1)S(1)}, bf16[1,2,128,1024]{3,2,1,0:T(8,128)(2,1)S(1)}, u32[]{:S(2)}, u32[]{:S(2)}) collective-permute-start(bf16[1,2,128,1024]{3,2,1,0:T(8,128)(2,1)S(1)} %get-tuple-element.56), channel_id=1, source_target_pairs={{0,16},{16,0},{32,48},{48,32},{64,80},{80,64},{96,112},{112,96},{1... | collective-permute-start | bytes 1572872 | tf_op jit(solution)/shard_map/ppermute | solution.py:44
  81.2 10.1 %collective-permute-start.32 = (bf16[1,2,128,1024]{3,2,1,0:T(8,128)(2,1)S(1)}, bf16[1,2,128,1024]{3,2,1,0:T(8,128)(2,1)S(1)}, u32[]{:S(2)}, u32[]{:S(2)}) collective-permute-start(bf16[1,2,128,1024]{3,2,1,0:T(8,128)(2,1)S(1)} %join.8.refs_6_), channel_id=1, source_target_pairs={{0,8},{16,80},{1,9},{17,81},{2,10},{18,82},{3,11},{19,83},{4,12},{... | collective-permute-start | bytes 1572872 | tf_op jit(solution)/shard_map/ppermute | solution.py:36
  87.5 4.7 %collective-permute-start.34 = (bf16[1,2,128,1024]{3,2,1,0:T(8,128)(2,1)S(1)}, bf16[1,2,128,1024]{3,2,1,0:T(8,128)(2,1)S(1)}, u32[]{:S(2)}, u32[]{:S(2)}) collective-permute-start(bf16[1,2,128,1024]{3,2,1,0:T(8,128)(2,1)S(1)} %get-tuple-element.58), channel_id=1, source_target_pairs={{0,16},{16,0},{32,48},{48,32},{64,80},{80,64},{96,112},{112,96},{1... | collective-permute-start | bytes 1572872 | tf_op jit(solution)/shard_map/ppermute | solution.py:44
  87.9 7.6 %collective-permute-start.37 = (bf16[1,2,128,1024]{3,2,1,0:T(8,128)(2,1)S(1)}, bf16[1,2,128,1024]{3,2,1,0:T(8,128)(2,1)S(1)}, u32[]{:S(2)}, u32[]{:S(2)}) collective-permute-start(bf16[1,2,128,1024]{3,2,1,0:T(8,128)(2,1)S(1)} %get-tuple-element.60), channel_id=1, source_target_pairs={{0,16},{16,0},{32,48},{48,32},{64,80},{80,64},{96,112},{112,96},{1... | collective-permute-start | bytes 1572872 | tf_op jit(solution)/shard_map/ppermute | solution.py:44
  88.5 9.9 %collective-permute-start.27 = (bf16[1,2,128,1024]{3,2,1,0:T(8,128)(2,1)S(1)}, bf16[1,2,128,1024]{3,2,1,0:T(8,128)(2,1)S(1)}, u32[]{:S(2)}, u32[]{:S(2)}) collective-permute-start(bf16[1,2,128,1024]{3,2,1,0:T(8,128)(2,1)S(1)} %join.9), channel_id=1, source_target_pairs={{0,8},{16,80},{1,9},{17,81},{2,10},{18,82},{3,11},{19,83},{4,12},{... | collective-permute-start | bytes 1572872 | tf_op jit(solution)/shard_map/ppermute | solution.py:36
  91.3 13.0 %collective-permute-start.30 = (bf16[1,2,128,1024]{3,2,1,0:T(8,128)(2,1)S(1)}, bf16[1,2,128,1024]{3,2,1,0:T(8,128)(2,1)S(1)}, u32[]{:S(2)}, u32[]{:S(2)}) collective-permute-start(bf16[1,2,128,1024]{3,2,1,0:T(8,128)(2,1)S(1)} %get-tuple-element.54), channel_id=1, source_target_pairs={{0,16},{16,0},{32,48},{48,32},{64,80},{80,64},{96,112},{112,96},{1... | collective-permute-start | bytes 1572872 | tf_op jit(solution)/shard_map/ppermute | solution.py:44
  92.2 12.9 %collective-permute-start.33 = (bf16[1,2,128,1024]{3,2,1,0:T(8,128)(2,1)S(1)}, bf16[1,2,128,1024]{3,2,1,0:T(8,128)(2,1)S(1)}, u32[]{:S(2)}, u32[]{:S(2)}) collective-permute-start(bf16[1,2,128,1024]{3,2,1,0:T(8,128)(2,1)S(1)} %join.11), channel_id=1, source_target_pairs={{0,1},{16,19},{1,0},{17,18},{2,3},{18,17},{3,2},{19,16},{4,5},{20,... | collective-permute-start | bytes 1572872 | tf_op jit(solution)/shard_map/ppermute | solution.py:36
  94.5 10.6 %collective-permute-start.36 = (bf16[1,2,128,1024]{3,2,1,0:T(8,128)(2,1)S(1)}, bf16[1,2,128,1024]{3,2,1,0:T(8,128)(2,1)S(1)}, u32[]{:S(2)}, u32[]{:S(2)}) collective-permute-start(bf16[1,2,128,1024]{3,2,1,0:T(8,128)(2,1)S(1)} %join.12), channel_id=1, source_target_pairs={{0,4},{16,48},{1,5},{17,49},{2,6},{18,50},{3,7},{19,51},{4,8},{20,... | collective-permute-start | bytes 1572872 | tf_op jit(solution)/shard_map/ppermute | solution.py:36
  95.6 9.5 %collective-permute-start.38 = (bf16[1,2,128,1024]{3,2,1,0:T(8,128)(2,1)S(1)}, bf16[1,2,128,1024]{3,2,1,0:T(8,128)(2,1)S(1)}, u32[]{:S(2)}, u32[]{:S(2)}) collective-permute-start(bf16[1,2,128,1024]{3,2,1,0:T(8,128)(2,1)S(1)} %join.13), channel_id=1, source_target_pairs={{0,12},{16,112},{1,13},{17,113},{2,14},{18,114},{3,15},{19,115},{4... | collective-permute-start | bytes 1572872 | tf_op jit(solution)/shard_map/ppermute | solution.py:36
  98.4 2.8 %collective-permute-start.28 = (f32[8,128]{1,0:T(8,128)S(1)}, f32[8,128]{1,0:T(8,128)S(1)}, u32[]{:S(2)}, u32[]{:S(2)}) collective-permute-start(f32[8,128]{1,0:T(8,128)S(1)} %after.1), channel_id=1, source_target_pairs={{16,17},{0,3},{17,16},{1,2},{18,19},{2,1},{19,18},{3,0},{20,21},{4... | collective-permute-start | bytes 12296 | tf_op jit(solution)/shard_map/ppermute | solution.py:36
  101.1 3.9 %collective-permute-start.29 = (f32[8,128]{1,0:T(8,128)S(1)}, f32[8,128]{1,0:T(8,128)S(1)}, u32[]{:S(2)}, u32[]{:S(2)}) collective-permute-start(f32[8,128]{1,0:T(8,128)S(1)} %add.6), channel_id=1, source_target_pairs={{0,16},{16,0},{32,48},{48,32},{64,80},{80,64},{96,112},{112,96},{1... | collective-permute-start | bytes 12296 | tf_op jit(solution)/shard_map/ppermute | solution.py:44
  105.4 2.0 %collective-permute-start.39 = (f32[128,1024]{1,0:T(8,128)S(1)}, f32[128,1024]{1,0:T(8,128)S(1)}, u32[]{:S(2)}, u32[]{:S(2)}) collective-permute-start(f32[128,1024]{1,0:T(8,128)S(1)} %get-tuple-element.62), channel_id=1, source_target_pairs={{0,16},{16,0},{32,48},{48,32},{64,80},{80,64},{96,112},{112,96},{1... | collective-permute-start | bytes 1572872 | tf_op jit(solution)/shard_map/ppermute | solution.py:44

commit v7 on v6

--- a/solution.py
+++ b/solution.py
@@ -49,7 +49,7 @@
     return row // 2, row % 2, col // 4, col % 4
 
 
-OFFSETS = [(0, 0), (3, 1), (2, 0), (3, 0), (2, 1), (1, 1), (1, 0), (0, 1)]
+OFFSETS = [(3, 1), (2, 1), (2, 0), (0, 0), (0, 1), (1, 1), (3, 0), (1, 0)]
 
 
 def load_copies(core, y, z, x, mine, theirs, q_dst, p_dst, sems):
@@ -138,7 +138,7 @@
         return tuple(cols), hits
 
     zero = jnp.zeros((8, 128), f32)
-    col_acc, hits = lax.fori_loop(0, 1024 // TILE, step, ((zero,) * 16, zero))
+    col_acc, hits = lax.fori_loop(0, 1024 // TILE, step, ((zero,) * 16, zero), unroll=2)
     hits = jnp.sum(hits, axis=0, keepdims=True)
 
     def fill(rows_ref, cols_ref, first):
@@ -187,7 +187,7 @@
             slope[h, rows, at] = jnp.where(lanes == aim - g * 128, e - 1.0, e).astype(bf16)
         return carry
 
-    lax.fori_loop(0, 1024 // TILE, step, 0)
+    lax.fori_loop(0, 1024 // TILE, step, 0, unroll=2)
 
 
 def grad_kernel(flip, order, n_parts, n_ties, *refs):
@@ -518,7 +518,7 @@
     across = hop(own, 0, True)
     down_across, up_across = hop(down, 0, True), hop(up, 0, True)
     far_across = hop(across, 2, False)
-    chunks = [own, down_across, far, down, far_across, up_across, up, across]
+    chunks = [down_across, far_across, far, own, across, up_across, down, up]
     others = [swap(c) for c in chunks]
 
     target = aims_of(positive)
@@ -533,9 +533,9 @@
     outs = grads_of(1, ((1, 3),), tiles, (part, hop_xor(part, 1)), ())
     sides, part = join([outs[0], swap(outs[1])]), outs[2]
     outs = grads_of(1, ((2,), (0,)), tiles, (part,), ())
-    moved = hop(part, 2, False, 1)
     beyond, across, part = join([outs[0], swap(outs[2])]), [outs[1], swap(outs[3])], outs[4]
     ready = (sides, beyond)
+    moved = hop(after(part, ready[0]), 2, False, 1)
     sides, beyond = hop(sides, 0, True), hop(beyond, 2, False)
     outs = grads_of(0, ((2,), (0,)), tiles, (part, moved), ready)
     far = join([outs[0], swap(outs[2])])

time: 110 us -> 110 us (level)
    ppermute x19, starting transfers between devices: 35.3 us -> 38.9 us  [hop(): lax.ppermute(a, AX, moves(lambda r, x, other: ((r + d) % 4, other if flip...]
    ppermute x20, starting transfers between devices: 18.4 us -> 15 us  [swap(): return lax.ppermute(a, 'row', [(i, i ^ 1) for i in range(8)])]
  transfers between devices with their start and end apart: 40 -> 40, of which waited for: 17 -> 15; matrix products, arithmetic and copies ran while one was open for 0% -> 0% of each run, Pallas kernels for 13% -> 14%
where the time goes in v7:
time: 110 us; the launch traced here: 109 us
  starting transfers between devices  54.7 us (50%)
  Pallas kernels  28.3 us (26%)
  waiting for transfers between devices  20.6 us (19%)
  local copies, waits for them, and re-layouts  3.1 us (3%)
  between operations  2.66 us (2%)
    ppermute x19, starting transfers between devices, hop(): lax.ppermute(a, AX, moves(lambda r, x, other: ((r + d) % 4, other if flip...  38.9 us
    ppermute x19, waiting for transfers between devices, hop(): lax.ppermute(a, AX, moves(lambda r, x, other: ((r + d) % 4, other if flip...  16.8 us
    ppermute x20, starting transfers between devices, swap(): return lax.ppermute(a, 'row', [(i, i ^ 1) for i in range(8)])  15 us
    pallas_call x4, Pallas kernels, grads_of(): pl.pallas_call(functools.partial(grad_kernel, flip, order, len(parts), le...  12.5 us
    pallas_call x1, Pallas kernels, scores_of(): pl.pallas_call(score_kernel, out_shape=(arr((2, 1024, 1024), f32), arr((3...  8.56 us
    ppermute x20, waiting for transfers between devices, swap(): return lax.ppermute(a, 'row', [(i, i ^ 1) for i in range(8)])  3.81 us
    pallas_call x1, Pallas kernels, slope_of(): pl.pallas_call(slope_kernel, out_shape=arr((2, 1024, 1024), bf16), in_spe...  3.5 us
    unnamed x6, local copies, waits for them, and re-layouts  2.59 us
  transfers between devices with their start and end apart: 40, of which 15 were waited for; matrix products, arithmetic and copies ran while one was open for 0% of the time, Pallas kernels for 14%

profile of v7, /device:TPU:1, one launch (start us, length us, event | category | flops | bytes accessed | tf_op | source)
XLA Modules:
  0.0 109.4 jit_solution(12339867844944023277)
XLA Ops:
  0.6 0.9 copy-done
  1.6 0.9 copy-done.1
  2.7 1.5 %collective-permute-start = (bf16[128,1024]{1,0:T(8,128)(2,1)S(1)}, bf16[128,1024]{1,0:T(8,128)(2,1)S(1)}, u32[]{:S(2)}, u32[]{:S(2)}) collective-permute-start(bf16[128,1024]{1,0:T(8,128)(2,1)S(1)} %get-tuple-element.35), channel_id=1, source_target_pairs={{0,16},{16,0},{32,48},{48,32},{64,80},{80,64},{96,112},{112,96},{1... | collective-permute-start | bytes 786440 | tf_op jit(solution)/shard_map/ppermute | solution.py:44
  4.2 1.2 %collective-permute-done = bf16[128,1024]{1,0:T(8,128)(2,1)S(1)} collective-permute-done((bf16[128,1024]{1,0:T(8,128)(2,1)S(1)}, bf16[128,1024]{1,0:T(8,128)(2,1)S(1)}, u32[]{:S(2)}, u32[]{:S(2)}) %collective-permute-start) | collective-permute-done | bytes 262176 | tf_op jit(solution)/shard_map/ppermute | solution.py:44
  5.4 1.4 %collective-permute-start.6 = (bf16[2,128,1024]{2,1,0:T(8,128)(2,1)S(1)}, bf16[2,128,1024]{2,1,0:T(8,128)(2,1)S(1)}, u32[]{:S(2)}, u32[]{:S(2)}) collective-permute-start(bf16[2,128,1024]{2,1,0:T(8,128)(2,1)S(1)} %pad_maximum_fusion.refs_3_), channel_id=1, source_target_pairs={{0,4},{16,48},{1,5},{17,49},{2,6},{18,50},{3,7},{19,51},{4,8},{20,... | collective-permute-start | bytes 1572872 | tf_op jit(solution)/shard_map/ppermute | solution.py:36
  6.9 1.0 collective-permute-start.11
  7.9 2.9 %collective-permute-start.5 = (bf16[2,128,1024]{2,1,0:T(8,128)(2,1)S(1)}, bf16[2,128,1024]{2,1,0:T(8,128)(2,1)S(1)}, u32[]{:S(2)}, u32[]{:S(2)}) collective-permute-start(bf16[2,128,1024]{2,1,0:T(8,128)(2,1)S(1)} %pad_maximum_fusion.refs_3_), channel_id=1, source_target_pairs={{0,8},{16,80},{1,9},{17,81},{2,10},{18,82},{3,11},{19,83},{4,12},{... | collective-permute-start | bytes 1572872 | tf_op jit(solution)/shard_map/ppermute | solution.py:36
  10.8 2.5 %collective-permute-start.3 = (bf16[2,128,1024]{2,1,0:T(8,128)(2,1)S(1)}, bf16[2,128,1024]{2,1,0:T(8,128)(2,1)S(1)}, u32[]{:S(2)}, u32[]{:S(2)}) collective-permute-start(bf16[2,128,1024]{2,1,0:T(8,128)(2,1)S(1)} %pad_maximum_fusion.refs_3_), channel_id=1, source_target_pairs={{0,1},{16,19},{1,0},{17,18},{2,3},{18,17},{3,2},{19,16},{4,5},{20,... | collective-permute-start | bytes 1572872 | tf_op jit(solution)/shard_map/ppermute | solution.py:36
  13.3 0.8 collective-permute-start.1
  14.0 1.1 %collective-permute-done.6.refs_7_ = bf16[2,128,1024]{2,1,0:T(8,128)(2,1)S(1)} collective-permute-done((bf16[2,128,1024]{2,1,0:T(8,128)(2,1)S(1)}, bf16[2,128,1024]{2,1,0:T(8,128)(2,1)S(1)}, u32[]{:S(2)}, u32[]{:S(2)}) %collective-permute-start.6) | collective-permute-done | bytes 524320 | tf_op jit(solution)/shard_map/ppermute | solution.py:36
  15.2 2.0 %collective-permute-start.15 = (bf16[2,128,1024]{2,1,0:T(8,128)(2,1)S(1)}, bf16[2,128,1024]{2,1,0:T(8,128)(2,1)S(1)}, u32[]{:S(2)}, u32[]{:S(2)}) collective-permute-start(bf16[2,128,1024]{2,1,0:T(8,128)(2,1)S(1)} %collective-permute-done.6.refs_7_), channel_id=1, source_target_pairs={{0,16},{16,0},{32,48},{48,32},{64,80},{80,64},{96,112},{112,96},{1... | collective-permute-start | bytes 1572872 | tf_op jit(solution)/shard_map/ppermute | solution.py:44
  17.2 2.5 %collective-permute-start.7 = (bf16[2,128,1024]{2,1,0:T(8,128)(2,1)S(1)}, bf16[2,128,1024]{2,1,0:T(8,128)(2,1)S(1)}, u32[]{:S(2)}, u32[]{:S(2)}) collective-permute-start(bf16[2,128,1024]{2,1,0:T(8,128)(2,1)S(1)} %collective-permute-done.6.refs_7_), channel_id=1, source_target_pairs={{0,1},{16,19},{1,0},{17,18},{2,3},{18,17},{3,2},{19,16},{4,5},{20,... | collective-permute-start | bytes 1572872 | tf_op jit(solution)/shard_map/ppermute | solution.py:36
  19.6 2.3 %collective-permute-done.5.refs_2_ = bf16[2,128,1024]{2,1,0:T(8,128)(2,1)S(1)} collective-permute-done((bf16[2,128,1024]{2,1,0:T(8,128)(2,1)S(1)}, bf16[2,128,1024]{2,1,0:T(8,128)(2,1)S(1)}, u32[]{:S(2)}, u32[]{:S(2)}) %collective-permute-start.5) | collective-permute-done | bytes 524320 | tf_op jit(solution)/shard_map/ppermute | solution.py:36
  22.0 2.3 %collective-permute-start.10 = (bf16[2,128,1024]{2,1,0:T(8,128)(2,1)S(1)}, bf16[2,128,1024]{2,1,0:T(8,128)(2,1)S(1)}, u32[]{:S(2)}, u32[]{:S(2)}) collective-permute-start(bf16[2,128,1024]{2,1,0:T(8,128)(2,1)S(1)} %collective-permute-done.5.refs_2_), channel_id=1, source_target_pairs={{0,16},{16,0},{32,48},{48,32},{64,80},{80,64},{96,112},{112,96},{1... | collective-permute-start | bytes 1572872 | tf_op jit(solution)/shard_map/ppermute | solution.py:44
  24.2 2.9 %collective-permute-start.4 = (bf16[2,128,1024]{2,1,0:T(8,128)(2,1)S(1)}, bf16[2,128,1024]{2,1,0:T(8,128)(2,1)S(1)}, u32[]{:S(2)}, u32[]{:S(2)}) collective-permute-start(bf16[2,128,1024]{2,1,0:T(8,128)(2,1)S(1)} %collective-permute-done.3.refs_4_), channel_id=1, source_target_pairs={{0,8},{16,80},{1,9},{17,81},{2,10},{18,82},{3,11},{19,83},{4,12},{... | collective-permute-start | bytes 1572872 | tf_op jit(solution)/shard_map/ppermute | solution.py:36
  27.2 2.5 %collective-permute-start.2 = (bf16[2,128,1024]{2,1,0:T(8,128)(2,1)S(1)}, bf16[2,128,1024]{2,1,0:T(8,128)(2,1)S(1)}, u32[]{:S(2)}, u32[]{:S(2)}) collective-permute-start(bf16[2,128,1024]{2,1,0:T(8,128)(2,1)S(1)} %collective-permute-done.1.refs_6_), channel_id=1, source_target_pairs={{0,1},{16,19},{1,0},{17,18},{2,3},{18,17},{3,2},{19,16},{4,5},{20,... | collective-permute-start | bytes 1572872 | tf_op jit(solution)/shard_map/ppermute | solution.py:36
  30.2 3.8 %collective-permute-done.4.refs_1_ = bf16[2,128,1024]{2,1,0:T(8,128)(2,1)S(1)} collective-permute-done((bf16[2,128,1024]{2,1,0:T(8,128)(2,1)S(1)}, bf16[2,128,1024]{2,1,0:T(8,128)(2,1)S(1)}, u32[]{:S(2)}, u32[]{:S(2)}) %collective-permute-start.4) | collective-permute-done | bytes 524320 | tf_op jit(solution)/shard_map/ppermute | solution.py:36
  34.1 0.9 collective-permute-start.9
  34.9 1.5 %collective-permute-done.2.refs_0_ = bf16[2,128,1024]{2,1,0:T(8,128)(2,1)S(1)} collective-permute-done((bf16[2,128,1024]{2,1,0:T(8,128)(2,1)S(1)}, bf16[2,128,1024]{2,1,0:T(8,128)(2,1)S(1)}, u32[]{:S(2)}, u32[]{:S(2)}) %collective-permute-start.2) | collective-permute-done | bytes 524320 | tf_op jit(solution)/shard_map/ppermute | solution.py:36
  36.8 0.7 copy-done.2
  37.8 0.6 collective-permute-done.8.refs_8_
  38.4 8.6 %scores.1 = (f32[2,1024,1024]{2,1,0:T(8,128)S(1)}, f32[3,2048]{1,0:T(4,128)S(1)}, f32[3,2048]{1,0:T(4,128)S(1)}, bf16[1024,1024]{1,0:T(8,128)(2,1)S(1)}, bf16[2,1024,1024]{2,1,0:T(8,128)(2,1)S(1)}) custom-call(bf16[2,128,1024]{2,1,0:T(8,128)(2,1)S(1)} %collective-permute-done.2.refs_0_, bf16[2,128,1024]{2,1,0:T(8,128)(2,1)S(1)} %collective-permute-done.4.refs_1_, ...), custom_call_target="tpu_custom_call" | custom-call | flops 4294967296 | bytes 16777216 | tf_op jit(solution)/shard_map/scores/pallas_call | solution.py:289
  47.4 0.9 collective-permute-done.16.refs_1_
  48.2 2.5 %collective-permute-start.17 = (f32[3,2048]{1,0:T(4,128)S(1)}, f32[3,2048]{1,0:T(4,128)S(1)}, u32[]{:S(2)}, u32[]{:S(2)}) collective-permute-start(f32[3,2048]{1,0:T(4,128)S(1)} %merge.3.refs_0_), channel_id=1, source_target_pairs={{0,1},{16,19},{1,0},{17,18},{2,3},{18,17},{3,2},{19,16},{4,5},{20,... | collective-permute-start | bytes 73736 | tf_op jit(solution)/shard_map/ppermute | solution.py:36
  50.7 0.7 flip.1.refs_2_.refs_1_
  51.4 0.9 collective-permute-done.17.refs_1_
  52.3 2.8 %collective-permute-start.20 = (f32[3,2048]{1,0:T(4,128)S(1)}, f32[3,2048]{1,0:T(4,128)S(1)}, u32[]{:S(2)}, u32[]{:S(2)}) collective-permute-start(f32[3,2048]{1,0:T(4,128)S(1)} %merge.4.refs_0_), channel_id=1, source_target_pairs={{0,12},{16,112},{1,13},{17,113},{2,14},{18,114},{3,15},{19,115},{4... | collective-permute-start | bytes 73736 | tf_op jit(solution)/shard_map/ppermute | solution.py:36
  55.1 1.6 %collective-permute-start.18 = (f32[3,2048]{1,0:T(4,128)S(1)}, f32[3,2048]{1,0:T(4,128)S(1)}, u32[]{:S(2)}, u32[]{:S(2)}) collective-permute-start(f32[3,2048]{1,0:T(4,128)S(1)} %merge.4.refs_0_), channel_id=1, source_target_pairs={{0,8},{16,80},{1,9},{17,81},{2,10},{18,82},{3,11},{19,83},{4,12},{... | collective-permute-start | bytes 73736 | tf_op jit(solution)/shard_map/ppermute | solution.py:36
  56.7 2.6 %collective-permute-done.19.refs_2_ = f32[3,2048]{1,0:T(4,128)S(1)} collective-permute-done((f32[3,2048]{1,0:T(4,128)S(1)}, f32[3,2048]{1,0:T(4,128)S(1)}, u32[]{:S(2)}, u32[]{:S(2)}) %collective-permute-start.19) | collective-permute-done | bytes 24608 | tf_op jit(solution)/shard_map/ppermute | solution.py:36
  60.2 0.8 collective-permute-start.22
  61.1 3.5 %slope.1.refs_0_ = bf16[2,1024,1024]{2,1,0:T(8,128)(2,1)S(1)} custom-call(f32[2,1024,1024]{2,1,0:T(8,128)S(1)} %get-tuple-element.36.sv, f32[1024,128]{1,0:T(8,128)S(1)} %aims.1.refs_16_.target, f32[1,2048]{1,0:T(1,128)S(1)} %get-tuple-element.40.own_lse, f32[1,2048]{1,0:T(1,128)S(1)} %collective-permute-done.21.got_lse), custom_call_target="tpu_custom_call" | custom-call | flops 4294967296 | bytes 12582912 | tf_op jit(solution)/shard_map/slope/pallas_call | solution.py:413
  64.6 3.1 %grads_far.2 = (bf16[2,2,128,1024]{3,2,1,0:T(8,128)(2,1)S(1)}, bf16[2,2,128,1024]{3,2,1,0:T(8,128)(2,1)S(1)}, f32[8,128]{1,0:T(8,128)S(1)}) custom-call(bf16[2,1024,1024]{2,1,0:T(8,128)(2,1)S(1)} %slope.1.refs_0_, bf16[1024,1024]{1,0:T(8,128)(2,1)S(1)} %flip.1.refs_2_.refs_1_, bf16[2,1024,1024]{2,1,0:T(8,128)(2,1)S(1)} %get-tuple-element.41.refs_2_, ...), custom_call_target="tpu_custom_call" | custom-call | flops 2147483648 | bytes 10485760 | tf_op jit(solution)/shard_map/grads_far/pallas_call | solution.py:429
  67.6 0.9 collective-permute-start.23
  68.6 3.1 %grads_far.3 = (bf16[1,2,128,1024]{3,2,1,0:T(8,128)(2,1)S(1)}, bf16[1,2,128,1024]{3,2,1,0:T(8,128)(2,1)S(1)}, bf16[1,2,128,1024]{3,2,1,0:T(8,128)(2,1)S(1)}, bf1...) custom-call(bf16[2,1024,1024]{2,1,0:T(8,128)(2,1)S(1)} %slope.1.refs_0_, bf16[1024,1024]{1,0:T(8,128)(2,1)S(1)} %flip.1.refs_2_.refs_1_, ...), custom_call_target="tpu_custom_call" | custom-call | flops 2147483648 | bytes 10485760 | tf_op jit(solution)/shard_map/grads_far/pallas_call | solution.py:429
  72.0 2.7 %collective-permute-start.24 = (f32[8,128]{1,0:T(8,128)S(1)}, f32[8,128]{1,0:T(8,128)S(1)}, u32[]{:S(2)}, u32[]{:S(2)}) collective-permute-start(f32[8,128]{1,0:T(8,128)S(1)} %after.2), channel_id=1, source_target_pairs={{16,24},{0,64},{17,25},{1,65},{18,26},{2,66},{19,27},{3,67},{20,28... | collective-permute-start | bytes 12296 | tf_op jit(solution)/shard_map/ppermute | solution.py:36
  74.8 2.5 %collective-permute-start.35 = (bf16[2,2,128,1024]{3,2,1,0:T(8,128)(2,1)S(1)}, bf16[2,2,128,1024]{3,2,1,0:T(8,128)(2,1)S(1)}, u32[]{:S(2)}, u32[]{:S(2)}) collective-permute-start(bf16[2,2,128,1024]{3,2,1,0:T(8,128)(2,1)S(1)} %join.7.refs_0_.refs_5_), channel_id=1, source_target_pairs={{0,1},{16,19},{1,0},{17,18},{2,3},{18,17},{3,2},{19,16},{4,5},{20,... | collective-permute-start | bytes 3145736 | tf_op jit(solution)/shard_map/ppermute | solution.py:36
  77.4 3.1 %grads_near.2 = (bf16[1,2,128,1024]{3,2,1,0:T(8,128)(2,1)S(1)}, bf16[1,2,128,1024]{3,2,1,0:T(8,128)(2,1)S(1)}, bf16[1,2,128,1024]{3,2,1,0:T(8,128)(2,1)S(1)}, bf...) custom-call(bf16[2,1024,1024]{2,1,0:T(8,128)(2,1)S(1)} %slope.1.refs_0_, bf16[1024,1024]{1,0:T(8,128)(2,1)S(1)} %flip.1.refs_2_.refs_1_, ...), custom_call_target="tpu_custom_call" | custom-call | flops 2147483648 | bytes 10485760 | tf_op jit(solution)/shard_map/grads_near/pallas_call | solution.py:429
  81.0 3.3 %collective-permute-start.32 = (bf16[1,2,128,1024]{3,2,1,0:T(8,128)(2,1)S(1)}, bf16[1,2,128,1024]{3,2,1,0:T(8,128)(2,1)S(1)}, u32[]{:S(2)}, u32[]{:S(2)}) collective-permute-start(bf16[1,2,128,1024]{3,2,1,0:T(8,128)(2,1)S(1)} %join.8.refs_6_), channel_id=1, source_target_pairs={{0,8},{16,80},{1,9},{17,81},{2,10},{18,82},{3,11},{19,83},{4,12},{... | collective-permute-start | bytes 1572872 | tf_op jit(solution)/shard_map/ppermute | solution.py:36
  84.4 3.3 %grads_near.3 = (bf16[1,2,128,1024]{3,2,1,0:T(8,128)(2,1)S(1)}, bf16[1,2,128,1024]{3,2,1,0:T(8,128)(2,1)S(1)}, bf16[1,2,128,1024]{3,2,1,0:T(8,128)(2,1)S(1)}, bf...) custom-call(bf16[2,1024,1024]{2,1,0:T(8,128)(2,1)S(1)} %slope.1.refs_0_, bf16[1024,1024]{1,0:T(8,128)(2,1)S(1)} %flip.1.refs_2_.refs_1_, ...), custom_call_target="tpu_custom_call" | custom-call | flops 2147483648 | bytes 10485760 | tf_op jit(solution)/shard_map/grads_near/pallas_call | solution.py:429
  88.4 2.4 %collective-permute-start.27 = (bf16[1,2,128,1024]{3,2,1,0:T(8,128)(2,1)S(1)}, bf16[1,2,128,1024]{3,2,1,0:T(8,128)(2,1)S(1)}, u32[]{:S(2)}, u32[]{:S(2)}) collective-permute-start(bf16[1,2,128,1024]{3,2,1,0:T(8,128)(2,1)S(1)} %join.9), channel_id=1, source_target_pairs={{0,8},{16,80},{1,9},{17,81},{2,10},{18,82},{3,11},{19,83},{4,12},{... | collective-permute-start | bytes 1572872 | tf_op jit(solution)/shard_map/ppermute | solution.py:36
  91.4 2.1 %collective-permute-start.33 = (bf16[1,2,128,1024]{3,2,1,0:T(8,128)(2,1)S(1)}, bf16[1,2,128,1024]{3,2,1,0:T(8,128)(2,1)S(1)}, u32[]{:S(2)}, u32[]{:S(2)}) collective-permute-start(bf16[1,2,128,1024]{3,2,1,0:T(8,128)(2,1)S(1)} %join.11), channel_id=1, source_target_pairs={{0,1},{16,19},{1,0},{17,18},{2,3},{18,17},{3,2},{19,16},{4,5},{20,... | collective-permute-start | bytes 1572872 | tf_op jit(solution)/shard_map/ppermute | solution.py:36
  94.5 2.2 %collective-permute-start.38 = (bf16[1,2,128,1024]{3,2,1,0:T(8,128)(2,1)S(1)}, bf16[1,2,128,1024]{3,2,1,0:T(8,128)(2,1)S(1)}, u32[]{:S(2)}, u32[]{:S(2)}) collective-permute-start(bf16[1,2,128,1024]{3,2,1,0:T(8,128)(2,1)S(1)} %join.13), channel_id=1, source_target_pairs={{0,12},{16,112},{1,13},{17,113},{2,14},{18,114},{3,15},{19,115},{4... | collective-permute-start | bytes 1572872 | tf_op jit(solution)/shard_map/ppermute | solution.py:36
  96.8 1.5 %collective-permute-done.27.refs_0_.refs_1_ = bf16[1,2,128,1024]{3,2,1,0:T(8,128)(2,1)S(1)} collective-permute-done((bf16[1,2,128,1024]{3,2,1,0:T(8,128)(2,1)S(1)}, bf16[1,2,128,1024]{3,2,1,0:T(8,128)(2,1)S(1)}, u32[]{:S(2)}, u32[]{:S(2)}) %collective-permute-start.27) | collective-permute-done | bytes 524320 | tf_op jit(solution)/shard_map/ppermute | solution.py:36
  98.3 0.6 collective-permute-start.28
  98.9 2.3 %collective-permute-done.28 = f32[8,128]{1,0:T(8,128)S(1)} collective-permute-done((f32[8,128]{1,0:T(8,128)S(1)}, f32[8,128]{1,0:T(8,128)S(1)}, u32[]{:S(2)}, u32[]{:S(2)}) %collective-permute-start.28) | collective-permute-done | bytes 4128 | tf_op jit(solution)/shard_map/ppermute | solution.py:36
  101.1 2.9 %collective-permute-start.29 = (f32[8,128]{1,0:T(8,128)S(1)}, f32[8,128]{1,0:T(8,128)S(1)}, u32[]{:S(2)}, u32[]{:S(2)}) collective-permute-start(f32[8,128]{1,0:T(8,128)S(1)} %add.6), channel_id=1, source_target_pairs={{0,16},{16,0},{32,48},{48,32},{64,80},{80,64},{96,112},{112,96},{1... | collective-permute-start | bytes 12296 | tf_op jit(solution)/shard_map/ppermute | solution.py:44
  104.2 0.7 collective-permute-done.29
  107.2 1.1 finish.1
  (65 shorter events, 7.9 us)
Async XLA Ops:
  0.6 1.0 copy-start
  1.6 0.9 copy-start.1
  2.7 2.7 %collective-permute-start = (bf16[128,1024]{1,0:T(8,128)(2,1)S(1)}, bf16[128,1024]{1,0:T(8,128)(2,1)S(1)}, u32[]{:S(2)}, u32[]{:S(2)}) collective-permute-start(bf16[128,1024]{1,0:T(8,128)(2,1)S(1)} %get-tuple-element.35), channel_id=1, source_target_pairs={{0,16},{16,0},{32,48},{48,32},{64,80},{80,64},{96,112},{112,96},{1... | collective-permute-start | bytes 786440 | tf_op jit(solution)/shard_map/ppermute | solution.py:44
  5.4 9.8 %collective-permute-start.6 = (bf16[2,128,1024]{2,1,0:T(8,128)(2,1)S(1)}, bf16[2,128,1024]{2,1,0:T(8,128)(2,1)S(1)}, u32[]{:S(2)}, u32[]{:S(2)}) collective-permute-start(bf16[2,128,1024]{2,1,0:T(8,128)(2,1)S(1)} %pad_maximum_fusion.refs_3_), channel_id=1, source_target_pairs={{0,4},{16,48},{1,5},{17,49},{2,6},{18,50},{3,7},{19,51},{4,8},{20,... | collective-permute-start | bytes 1572872 | tf_op jit(solution)/shard_map/ppermute | solution.py:36
  6.9 10.3 %collective-permute-start.11 = (bf16[2,128,1024]{2,1,0:T(8,128)(2,1)S(1)}, bf16[2,128,1024]{2,1,0:T(8,128)(2,1)S(1)}, u32[]{:S(2)}, u32[]{:S(2)}) collective-permute-start(bf16[2,128,1024]{2,1,0:T(8,128)(2,1)S(1)} %pad_maximum_fusion.refs_3_), channel_id=1, source_target_pairs={{0,16},{16,0},{32,48},{48,32},{64,80},{80,64},{96,112},{112,96},{1... | collective-permute-start | bytes 1572872 | tf_op jit(solution)/shard_map/ppermute | solution.py:44
  7.9 14.1 %collective-permute-start.5 = (bf16[2,128,1024]{2,1,0:T(8,128)(2,1)S(1)}, bf16[2,128,1024]{2,1,0:T(8,128)(2,1)S(1)}, u32[]{:S(2)}, u32[]{:S(2)}) collective-permute-start(bf16[2,128,1024]{2,1,0:T(8,128)(2,1)S(1)} %pad_maximum_fusion.refs_3_), channel_id=1, source_target_pairs={{0,8},{16,80},{1,9},{17,81},{2,10},{18,82},{3,11},{19,83},{4,12},{... | collective-permute-start | bytes 1572872 | tf_op jit(solution)/shard_map/ppermute | solution.py:36
  10.8 13.4 %collective-permute-start.3 = (bf16[2,128,1024]{2,1,0:T(8,128)(2,1)S(1)}, bf16[2,128,1024]{2,1,0:T(8,128)(2,1)S(1)}, u32[]{:S(2)}, u32[]{:S(2)}) collective-permute-start(bf16[2,128,1024]{2,1,0:T(8,128)(2,1)S(1)} %pad_maximum_fusion.refs_3_), channel_id=1, source_target_pairs={{0,1},{16,19},{1,0},{17,18},{2,3},{18,17},{3,2},{19,16},{4,5},{20,... | collective-permute-start | bytes 1572872 | tf_op jit(solution)/shard_map/ppermute | solution.py:36
  13.3 13.9 %collective-permute-start.1 = (bf16[2,128,1024]{2,1,0:T(8,128)(2,1)S(1)}, bf16[2,128,1024]{2,1,0:T(8,128)(2,1)S(1)}, u32[]{:S(2)}, u32[]{:S(2)}) collective-permute-start(bf16[2,128,1024]{2,1,0:T(8,128)(2,1)S(1)} %pad_maximum_fusion.refs_3_), channel_id=1, source_target_pairs={{0,12},{16,112},{1,13},{17,113},{2,14},{18,114},{3,15},{19,115},{4... | collective-permute-start | bytes 1572872 | tf_op jit(solution)/shard_map/ppermute | solution.py:36
  15.2 14.4 %collective-permute-start.15 = (bf16[2,128,1024]{2,1,0:T(8,128)(2,1)S(1)}, bf16[2,128,1024]{2,1,0:T(8,128)(2,1)S(1)}, u32[]{:S(2)}, u32[]{:S(2)}) collective-permute-start(bf16[2,128,1024]{2,1,0:T(8,128)(2,1)S(1)} %collective-permute-done.6.refs_7_), channel_id=1, source_target_pairs={{0,16},{16,0},{32,48},{48,32},{64,80},{80,64},{96,112},{112,96},{1... | collective-permute-start | bytes 1572872 | tf_op jit(solution)/shard_map/ppermute | solution.py:44
  17.2 12.5 %collective-permute-start.7 = (bf16[2,128,1024]{2,1,0:T(8,128)(2,1)S(1)}, bf16[2,128,1024]{2,1,0:T(8,128)(2,1)S(1)}, u32[]{:S(2)}, u32[]{:S(2)}) collective-permute-start(bf16[2,128,1024]{2,1,0:T(8,128)(2,1)S(1)} %collective-permute-done.6.refs_7_), channel_id=1, source_target_pairs={{0,1},{16,19},{1,0},{17,18},{2,3},{18,17},{3,2},{19,16},{4,5},{20,... | collective-permute-start | bytes 1572872 | tf_op jit(solution)/shard_map/ppermute | solution.py:36
  22.0 8.2 %collective-permute-start.10 = (bf16[2,128,1024]{2,1,0:T(8,128)(2,1)S(1)}, bf16[2,128,1024]{2,1,0:T(8,128)(2,1)S(1)}, u32[]{:S(2)}, u32[]{:S(2)}) collective-permute-start(bf16[2,128,1024]{2,1,0:T(8,128)(2,1)S(1)} %collective-permute-done.5.refs_2_), channel_id=1, source_target_pairs={{0,16},{16,0},{32,48},{48,32},{64,80},{80,64},{96,112},{112,96},{1... | collective-permute-start | bytes 1572872 | tf_op jit(solution)/shard_map/ppermute | solution.py:44
  24.2 9.8 %collective-permute-start.4 = (bf16[2,128,1024]{2,1,0:T(8,128)(2,1)S(1)}, bf16[2,128,1024]{2,1,0:T(8,128)(2,1)S(1)}, u32[]{:S(2)}, u32[]{:S(2)}) collective-permute-start(bf16[2,128,1024]{2,1,0:T(8,128)(2,1)S(1)} %collective-permute-done.3.refs_4_), channel_id=1, source_target_pairs={{0,8},{16,80},{1,9},{17,81},{2,10},{18,82},{3,11},{19,83},{4,12},{... | collective-permute-start | bytes 1572872 | tf_op jit(solution)/shard_map/ppermute | solution.py:36
  27.2 9.2 %collective-permute-start.2 = (bf16[2,128,1024]{2,1,0:T(8,128)(2,1)S(1)}, bf16[2,128,1024]{2,1,0:T(8,128)(2,1)S(1)}, u32[]{:S(2)}, u32[]{:S(2)}) collective-permute-start(bf16[2,128,1024]{2,1,0:T(8,128)(2,1)S(1)} %collective-permute-done.1.refs_6_), channel_id=1, source_target_pairs={{0,1},{16,19},{1,0},{17,18},{2,3},{18,17},{3,2},{19,16},{4,5},{20,... | collective-permute-start | bytes 1572872 | tf_op jit(solution)/shard_map/ppermute | solution.py:36
  29.6 8.1 %collective-permute-start.12 = (bf16[2,128,1024]{2,1,0:T(8,128)(2,1)S(1)}, bf16[2,128,1024]{2,1,0:T(8,128)(2,1)S(1)}, u32[]{:S(2)}, u32[]{:S(2)}) collective-permute-start(bf16[2,128,1024]{2,1,0:T(8,128)(2,1)S(1)} %collective-permute-done.3.refs_4_), channel_id=1, source_target_pairs={{0,16},{16,0},{32,48},{48,32},{64,80},{80,64},{96,112},{112,96},{1... | collective-permute-start | bytes 1572872 | tf_op jit(solution)/shard_map/ppermute | solution.py:44
  29.6 8.1 %collective-permute-start.14 = (bf16[2,128,1024]{2,1,0:T(8,128)(2,1)S(1)}, bf16[2,128,1024]{2,1,0:T(8,128)(2,1)S(1)}, u32[]{:S(2)}, u32[]{:S(2)}) collective-permute-start(bf16[2,128,1024]{2,1,0:T(8,128)(2,1)S(1)} %collective-permute-done.1.refs_6_), channel_id=1, source_target_pairs={{0,16},{16,0},{32,48},{48,32},{64,80},{80,64},{96,112},{112,96},{1... | collective-permute-start | bytes 1572872 | tf_op jit(solution)/shard_map/ppermute | solution.py:44
  30.2 7.6 %collective-permute-start.13 = (bf16[2,128,1024]{2,1,0:T(8,128)(2,1)S(1)}, bf16[2,128,1024]{2,1,0:T(8,128)(2,1)S(1)}, u32[]{:S(2)}, u32[]{:S(2)}) collective-permute-start(bf16[2,128,1024]{2,1,0:T(8,128)(2,1)S(1)} %collective-permute-done.7.refs_5_), channel_id=1, source_target_pairs={{0,16},{16,0},{32,48},{48,32},{64,80},{80,64},{96,112},{112,96},{1... | collective-permute-start | bytes 1572872 | tf_op jit(solution)/shard_map/ppermute | solution.py:44
  34.1 3.7 %collective-permute-start.9 = (bf16[2,128,1024]{2,1,0:T(8,128)(2,1)S(1)}, bf16[2,128,1024]{2,1,0:T(8,128)(2,1)S(1)}, u32[]{:S(2)}, u32[]{:S(2)}) collective-permute-start(bf16[2,128,1024]{2,1,0:T(8,128)(2,1)S(1)} %collective-permute-done.4.refs_1_), channel_id=1, source_target_pairs={{0,16},{16,0},{32,48},{48,32},{64,80},{80,64},{96,112},{112,96},{1... | collective-permute-start | bytes 1572872 | tf_op jit(solution)/shard_map/ppermute | solution.py:44
  36.4 2.0 %collective-permute-start.8 = (bf16[2,128,1024]{2,1,0:T(8,128)(2,1)S(1)}, bf16[2,128,1024]{2,1,0:T(8,128)(2,1)S(1)}, u32[]{:S(2)}, u32[]{:S(2)}) collective-permute-start(bf16[2,128,1024]{2,1,0:T(8,128)(2,1)S(1)} %collective-permute-done.2.refs_0_), channel_id=1, source_target_pairs={{0,16},{16,0},{32,48},{48,32},{64,80},{80,64},{96,112},{112,96},{1... | collective-permute-start | bytes 1572872 | tf_op jit(solution)/shard_map/ppermute | solution.py:44
  36.8 0.7 copy-start.2
  46.9 1.3 %collective-permute-start.16 = (f32[3,2048]{1,0:T(4,128)S(1)}, f32[3,2048]{1,0:T(4,128)S(1)}, u32[]{:S(2)}, u32[]{:S(2)}) collective-permute-start(f32[3,2048]{1,0:T(4,128)S(1)} %get-tuple-element.38), channel_id=1, source_target_pairs={{0,16},{16,0},{32,48},{48,32},{64,80},{80,64},{96,112},{112,96},{1... | collective-permute-start | bytes 73736 | tf_op jit(solution)/shard_map/ppermute | solution.py:44
  48.2 4.1 %collective-permute-start.17 = (f32[3,2048]{1,0:T(4,128)S(1)}, f32[3,2048]{1,0:T(4,128)S(1)}, u32[]{:S(2)}, u32[]{:S(2)}) collective-permute-start(f32[3,2048]{1,0:T(4,128)S(1)} %merge.3.refs_0_), channel_id=1, source_target_pairs={{0,1},{16,19},{1,0},{17,18},{2,3},{18,17},{3,2},{19,16},{4,5},{20,... | collective-permute-start | bytes 73736 | tf_op jit(solution)/shard_map/ppermute | solution.py:36
  52.3 4.4 %collective-permute-start.20 = (f32[3,2048]{1,0:T(4,128)S(1)}, f32[3,2048]{1,0:T(4,128)S(1)}, u32[]{:S(2)}, u32[]{:S(2)}) collective-permute-start(f32[3,2048]{1,0:T(4,128)S(1)} %merge.4.refs_0_), channel_id=1, source_target_pairs={{0,12},{16,112},{1,13},{17,113},{2,14},{18,114},{3,15},{19,115},{4... | collective-permute-start | bytes 73736 | tf_op jit(solution)/shard_map/ppermute | solution.py:36
  55.1 4.3 %collective-permute-start.19 = (f32[3,2048]{1,0:T(4,128)S(1)}, f32[3,2048]{1,0:T(4,128)S(1)}, u32[]{:S(2)}, u32[]{:S(2)}) collective-permute-start(f32[3,2048]{1,0:T(4,128)S(1)} %merge.4.refs_0_), channel_id=1, source_target_pairs={{0,4},{16,48},{1,5},{17,49},{2,6},{18,50},{3,7},{19,51},{4,8},{20,... | collective-permute-start | bytes 73736 | tf_op jit(solution)/shard_map/ppermute | solution.py:36
  55.1 4.6 %collective-permute-start.18 = (f32[3,2048]{1,0:T(4,128)S(1)}, f32[3,2048]{1,0:T(4,128)S(1)}, u32[]{:S(2)}, u32[]{:S(2)}) collective-permute-start(f32[3,2048]{1,0:T(4,128)S(1)} %merge.4.refs_0_), channel_id=1, source_target_pairs={{0,8},{16,80},{1,9},{17,81},{2,10},{18,82},{3,11},{19,83},{4,12},{... | collective-permute-start | bytes 73736 | tf_op jit(solution)/shard_map/ppermute | solution.py:36
  59.8 1.3 %collective-permute-start.21 = (f32[1,2048]{1,0:T(1,128)S(1)}, f32[1,2048]{1,0:T(1,128)S(1)}, u32[]{:S(2)}, u32[]{:S(2)}) collective-permute-start(f32[1,2048]{1,0:T(1,128)S(1)} %get-tuple-element.40.own_lse), channel_id=1, source_target_pairs={{0,16},{16,0},{32,48},{48,32},{64,80},{80,64},{96,112},{112,96},{1... | collective-permute-start | bytes 24584 | tf_op jit(solution)/shard_map/ppermute | solution.py:44
  60.2 4.3 %collective-permute-start.22 = (f32[8,128]{1,0:T(8,128)S(1)}, f32[8,128]{1,0:T(8,128)S(1)}, u32[]{:S(2)}, u32[]{:S(2)}) collective-permute-start(f32[8,128]{1,0:T(8,128)S(1)} %get-tuple-element.42.refs_3_), channel_id=1, source_target_pairs={{16,20},{0,32},{17,21},{1,33},{18,22},{2,34},{19,23},{3,35},{20,16... | collective-permute-start | bytes 12296 | tf_op jit(solution)/shard_map/ppermute | solution.py:40
  67.6 4.1 %collective-permute-start.23 = (bf16[2,2,128,1024]{3,2,1,0:T(8,128)(2,1)S(1)}, bf16[2,2,128,1024]{3,2,1,0:T(8,128)(2,1)S(1)}, u32[]{:S(2)}, u32[]{:S(2)}) collective-permute-start(bf16[2,2,128,1024]{3,2,1,0:T(8,128)(2,1)S(1)} %get-tuple-element.46), channel_id=1, source_target_pairs={{0,16},{16,0},{32,48},{48,32},{64,80},{80,64},{96,112},{112,96},{1... | collective-permute-start | bytes 3145736 | tf_op jit(solution)/shard_map/ppermute | solution.py:44
  71.7 3.0 %collective-permute-start.25 = (bf16[1,2,128,1024]{3,2,1,0:T(8,128)(2,1)S(1)}, bf16[1,2,128,1024]{3,2,1,0:T(8,128)(2,1)S(1)}, u32[]{:S(2)}, u32[]{:S(2)}) collective-permute-start(bf16[1,2,128,1024]{3,2,1,0:T(8,128)(2,1)S(1)} %get-tuple-element.48), channel_id=1, source_target_pairs={{0,16},{16,0},{32,48},{48,32},{64,80},{80,64},{96,112},{112,96},{1... | collective-permute-start | bytes 1572872 | tf_op jit(solution)/shard_map/ppermute | solution.py:44
  72.0 5.4 %collective-permute-start.24 = (f32[8,128]{1,0:T(8,128)S(1)}, f32[8,128]{1,0:T(8,128)S(1)}, u32[]{:S(2)}, u32[]{:S(2)}) collective-permute-start(f32[8,128]{1,0:T(8,128)S(1)} %after.2), channel_id=1, source_target_pairs={{16,24},{0,64},{17,25},{1,65},{18,26},{2,66},{19,27},{3,67},{20,28... | collective-permute-start | bytes 12296 | tf_op jit(solution)/shard_map/ppermute | solution.py:36
  74.8 18.7 %collective-permute-start.35 = (bf16[2,2,128,1024]{3,2,1,0:T(8,128)(2,1)S(1)}, bf16[2,2,128,1024]{3,2,1,0:T(8,128)(2,1)S(1)}, u32[]{:S(2)}, u32[]{:S(2)}) collective-permute-start(bf16[2,2,128,1024]{3,2,1,0:T(8,128)(2,1)S(1)} %join.7.refs_0_.refs_5_), channel_id=1, source_target_pairs={{0,1},{16,19},{1,0},{17,18},{2,3},{18,17},{3,2},{19,16},{4,5},{20,... | collective-permute-start | bytes 3145736 | tf_op jit(solution)/shard_map/ppermute | solution.py:36
  80.4 7.3 %collective-permute-start.26 = (bf16[1,2,128,1024]{3,2,1,0:T(8,128)(2,1)S(1)}, bf16[1,2,128,1024]{3,2,1,0:T(8,128)(2,1)S(1)}, u32[]{:S(2)}, u32[]{:S(2)}) collective-permute-start(bf16[1,2,128,1024]{3,2,1,0:T(8,128)(2,1)S(1)} %get-tuple-element.52), channel_id=1, source_target_pairs={{0,16},{16,0},{32,48},{48,32},{64,80},{80,64},{96,112},{112,96},{1... | collective-permute-start | bytes 1572872 | tf_op jit(solution)/shard_map/ppermute | solution.py:44
  80.9 7.5 %collective-permute-start.31 = (bf16[1,2,128,1024]{3,2,1,0:T(8,128)(2,1)S(1)}, bf16[1,2,128,1024]{3,2,1,0:T(8,128)(2,1)S(1)}, u32[]{:S(2)}, u32[]{:S(2)}) collective-permute-start(bf16[1,2,128,1024]{3,2,1,0:T(8,128)(2,1)S(1)} %get-tuple-element.56), channel_id=1, source_target_pairs={{0,16},{16,0},{32,48},{48,32},{64,80},{80,64},{96,112},{112,96},{1... | collective-permute-start | bytes 1572872 | tf_op jit(solution)/shard_map/ppermute | solution.py:44
  81.0 10.2 %collective-permute-start.32 = (bf16[1,2,128,1024]{3,2,1,0:T(8,128)(2,1)S(1)}, bf16[1,2,128,1024]{3,2,1,0:T(8,128)(2,1)S(1)}, u32[]{:S(2)}, u32[]{:S(2)}) collective-permute-start(bf16[1,2,128,1024]{3,2,1,0:T(8,128)(2,1)S(1)} %join.8.refs_6_), channel_id=1, source_target_pairs={{0,8},{16,80},{1,9},{17,81},{2,10},{18,82},{3,11},{19,83},{4,12},{... | collective-permute-start | bytes 1572872 | tf_op jit(solution)/shard_map/ppermute | solution.py:36
  87.6 5.9 %collective-permute-start.34 = (bf16[1,2,128,1024]{3,2,1,0:T(8,128)(2,1)S(1)}, bf16[1,2,128,1024]{3,2,1,0:T(8,128)(2,1)S(1)}, u32[]{:S(2)}, u32[]{:S(2)}) collective-permute-start(bf16[1,2,128,1024]{3,2,1,0:T(8,128)(2,1)S(1)} %get-tuple-element.58), channel_id=1, source_target_pairs={{0,16},{16,0},{32,48},{48,32},{64,80},{80,64},{96,112},{112,96},{1... | collective-permute-start | bytes 1572872 | tf_op jit(solution)/shard_map/ppermute | solution.py:44
  87.7 6.6 %collective-permute-start.37 = (bf16[1,2,128,1024]{3,2,1,0:T(8,128)(2,1)S(1)}, bf16[1,2,128,1024]{3,2,1,0:T(8,128)(2,1)S(1)}, u32[]{:S(2)}, u32[]{:S(2)}) collective-permute-start(bf16[1,2,128,1024]{3,2,1,0:T(8,128)(2,1)S(1)} %get-tuple-element.60), channel_id=1, source_target_pairs={{0,16},{16,0},{32,48},{48,32},{64,80},{80,64},{96,112},{112,96},{1... | collective-permute-start | bytes 1572872 | tf_op jit(solution)/shard_map/ppermute | solution.py:44
  88.4 9.9 %collective-permute-start.27 = (bf16[1,2,128,1024]{3,2,1,0:T(8,128)(2,1)S(1)}, bf16[1,2,128,1024]{3,2,1,0:T(8,128)(2,1)S(1)}, u32[]{:S(2)}, u32[]{:S(2)}) collective-permute-start(bf16[1,2,128,1024]{3,2,1,0:T(8,128)(2,1)S(1)} %join.9), channel_id=1, source_target_pairs={{0,8},{16,80},{1,9},{17,81},{2,10},{18,82},{3,11},{19,83},{4,12},{... | collective-permute-start | bytes 1572872 | tf_op jit(solution)/shard_map/ppermute | solution.py:36
  91.4 13.5 %collective-permute-start.33 = (bf16[1,2,128,1024]{3,2,1,0:T(8,128)(2,1)S(1)}, bf16[1,2,128,1024]{3,2,1,0:T(8,128)(2,1)S(1)}, u32[]{:S(2)}, u32[]{:S(2)}) collective-permute-start(bf16[1,2,128,1024]{3,2,1,0:T(8,128)(2,1)S(1)} %join.11), channel_id=1, source_target_pairs={{0,1},{16,19},{1,0},{17,18},{2,3},{18,17},{3,2},{19,16},{4,5},{20,... | collective-permute-start | bytes 1572872 | tf_op jit(solution)/shard_map/ppermute | solution.py:36
  93.6 10.5 %collective-permute-start.30 = (bf16[1,2,128,1024]{3,2,1,0:T(8,128)(2,1)S(1)}, bf16[1,2,128,1024]{3,2,1,0:T(8,128)(2,1)S(1)}, u32[]{:S(2)}, u32[]{:S(2)}) collective-permute-start(bf16[1,2,128,1024]{3,2,1,0:T(8,128)(2,1)S(1)} %get-tuple-element.54), channel_id=1, source_target_pairs={{0,16},{16,0},{32,48},{48,32},{64,80},{80,64},{96,112},{112,96},{1... | collective-permute-start | bytes 1572872 | tf_op jit(solution)/shard_map/ppermute | solution.py:44
  93.8 11.1 %collective-permute-start.36 = (bf16[1,2,128,1024]{3,2,1,0:T(8,128)(2,1)S(1)}, bf16[1,2,128,1024]{3,2,1,0:T(8,128)(2,1)S(1)}, u32[]{:S(2)}, u32[]{:S(2)}) collective-permute-start(bf16[1,2,128,1024]{3,2,1,0:T(8,128)(2,1)S(1)} %join.12), channel_id=1, source_target_pairs={{0,4},{16,48},{1,5},{17,49},{2,6},{18,50},{3,7},{19,51},{4,8},{20,... | collective-permute-start | bytes 1572872 | tf_op jit(solution)/shard_map/ppermute | solution.py:36
  94.5 10.4 %collective-permute-start.38 = (bf16[1,2,128,1024]{3,2,1,0:T(8,128)(2,1)S(1)}, bf16[1,2,128,1024]{3,2,1,0:T(8,128)(2,1)S(1)}, u32[]{:S(2)}, u32[]{:S(2)}) collective-permute-start(bf16[1,2,128,1024]{3,2,1,0:T(8,128)(2,1)S(1)} %join.13), channel_id=1, source_target_pairs={{0,12},{16,112},{1,13},{17,113},{2,14},{18,114},{3,15},{19,115},{4... | collective-permute-start | bytes 1572872 | tf_op jit(solution)/shard_map/ppermute | solution.py:36
  98.3 2.9 %collective-permute-start.28 = (f32[8,128]{1,0:T(8,128)S(1)}, f32[8,128]{1,0:T(8,128)S(1)}, u32[]{:S(2)}, u32[]{:S(2)}) collective-permute-start(f32[8,128]{1,0:T(8,128)S(1)} %after.3), channel_id=1, source_target_pairs={{16,17},{0,3},{17,16},{1,2},{18,19},{2,1},{19,18},{3,0},{20,21},{4... | collective-permute-start | bytes 12296 | tf_op jit(solution)/shard_map/ppermute | solution.py:36
  101.1 3.7 %collective-permute-start.29 = (f32[8,128]{1,0:T(8,128)S(1)}, f32[8,128]{1,0:T(8,128)S(1)}, u32[]{:S(2)}, u32[]{:S(2)}) collective-permute-start(f32[8,128]{1,0:T(8,128)S(1)} %add.6), channel_id=1, source_target_pairs={{0,16},{16,0},{32,48},{48,32},{64,80},{80,64},{96,112},{112,96},{1... | collective-permute-start | bytes 12296 | tf_op jit(solution)/shard_map/ppermute | solution.py:44
  105.2 2.0 %collective-permute-start.39 = (f32[128,1024]{1,0:T(8,128)S(1)}, f32[128,1024]{1,0:T(8,128)S(1)}, u32[]{:S(2)}, u32[]{:S(2)}) collective-permute-start(f32[128,1024]{1,0:T(8,128)S(1)} %get-tuple-element.62), channel_id=1, source_target_pairs={{0,16},{16,0},{32,48},{48,32},{64,80},{80,64},{96,112},{112,96},{1... | collective-permute-start | bytes 1572872 | tf_op jit(solution)/shard_map/ppermute | solution.py:44

commit v8 on v7

--- a/solution.py
+++ b/solution.py
@@ -104,9 +104,14 @@
     )
     y, core, z, x = place()
     groups = load_copies(core, y, z, x, mine, theirs, qv, pt, sems)
-    run_copies(core, groups, True)
-    run_copies(core, groups, False)
-    for h in range(2):
+    flips = [flip for _, flip in OFFSETS for _ in range(2)]
+    early = [(w, c[:1] if flip else c) for flip, (w, c) in zip(flips, groups)]
+    late = [(w, c[1:]) for flip, (w, c) in zip(flips, groups) if flip]
+    run_copies(core, early, True)
+    run_copies(core, late, True)
+    for flip, copies in enumerate((early, late)):
+        run_copies(core, copies, False)
+        h = (x // 2) ^ flip
         for n in range(2):
             cols = slice(n * 512, n * 512 + 512)
             s = score_scale * jnp.dot(qv[...], pt[h, :, cols], preferred_element_type=f32)
@@ -115,7 +120,7 @@
             top = jnp.maximum(
                 jnp.maximum(s[:, :128], s[:, 128:256]), jnp.maximum(s[:, 256:384], s[:, 384:])
             )
-            row_top[...] = top if h == n == 0 else jnp.maximum(row_top[...], top)
+            row_top[...] = top if flip == n == 0 else jnp.maximum(row_top[...], top)
     tops = []
     for s in range(8):
         rows = slice(s * 128, s * 128 + 128)

time: 110 us -> 110 us (level)
  transfers between devices with their start and end apart: 40 -> 40, of which waited for: 15 -> 16; matrix products, arithmetic and copies ran while one was open for 0% -> 0% of each run, Pallas kernels for 14% -> 14%
where the time goes in v8:
time: 110 us
  starting transfers between devices  54.7 us (50%)
  Pallas kernels  28.5 us (26%)
  waiting for transfers between devices  20.6 us (19%)
  local copies, waits for them, and re-layouts  3.1 us (3%)
  between operations  2.66 us (2%)
    ppermute x19, starting transfers between devices, hop(): lax.ppermute(a, AX, moves(lambda r, x, other: ((r + d) % 4, other if flip...  38.9 us
    ppermute x19, waiting for transfers between devices, hop(): lax.ppermute(a, AX, moves(lambda r, x, other: ((r + d) % 4, other if flip...  16.8 us
    ppermute x20, starting transfers between devices, swap(): return lax.ppermute(a, 'row', [(i, i ^ 1) for i in range(8)])  15 us
    pallas_call x4, Pallas kernels, grads_of(): pl.pallas_call(functools.partial(grad_kernel, flip, order, len(parts), le...  12.5 us
    pallas_call x1, Pallas kernels, scores_of(): pl.pallas_call(score_kernel, out_shape=(arr((2, 1024, 1024), f32), arr((3...  8.74 us
    ppermute x20, waiting for transfers between devices, swap(): return lax.ppermute(a, 'row', [(i, i ^ 1) for i in range(8)])  3.82 us
    pallas_call x1, Pallas kernels, slope_of(): pl.pallas_call(slope_kernel, out_shape=arr((2, 1024, 1024), bf16), in_spe...  3.5 us
    unnamed x6, local copies, waits for them, and re-layouts  2.59 us
  transfers between devices with their start and end apart: 40, of which 16 were waited for; matrix products, arithmetic and copies ran while one was open for 0% of the time, Pallas kernels for 14%

profile of v8, /device:TPU:1, one launch (start us, length us, event | category | flops | bytes accessed | tf_op | source)
XLA Modules:
  0.0 109.6 jit_solution(10185660657460918525)
XLA Ops:
  0.6 0.9 copy-done
  1.6 0.9 copy-done.1
  2.7 1.5 %collective-permute-start = (bf16[128,1024]{1,0:T(8,128)(2,1)S(1)}, bf16[128,1024]{1,0:T(8,128)(2,1)S(1)}, u32[]{:S(2)}, u32[]{:S(2)}) collective-permute-start(bf16[128,1024]{1,0:T(8,128)(2,1)S(1)} %get-tuple-element.35), channel_id=1, source_target_pairs={{0,16},{16,0},{32,48},{48,32},{64,80},{80,64},{96,112},{112,96},{1... | collective-permute-start | bytes 786440 | tf_op jit(solution)/shard_map/ppermute | solution.py:44
  4.2 1.2 %collective-permute-done = bf16[128,1024]{1,0:T(8,128)(2,1)S(1)} collective-permute-done((bf16[128,1024]{1,0:T(8,128)(2,1)S(1)}, bf16[128,1024]{1,0:T(8,128)(2,1)S(1)}, u32[]{:S(2)}, u32[]{:S(2)}) %collective-permute-start) | collective-permute-done | bytes 262176 | tf_op jit(solution)/shard_map/ppermute | solution.py:44
  5.4 1.4 %collective-permute-start.6 = (bf16[2,128,1024]{2,1,0:T(8,128)(2,1)S(1)}, bf16[2,128,1024]{2,1,0:T(8,128)(2,1)S(1)}, u32[]{:S(2)}, u32[]{:S(2)}) collective-permute-start(bf16[2,128,1024]{2,1,0:T(8,128)(2,1)S(1)} %pad_maximum_fusion.refs_3_), channel_id=1, source_target_pairs={{0,4},{16,48},{1,5},{17,49},{2,6},{18,50},{3,7},{19,51},{4,8},{20,... | collective-permute-start | bytes 1572872 | tf_op jit(solution)/shard_map/ppermute | solution.py:36
  6.9 1.0 collective-permute-start.11
  7.9 2.9 %collective-permute-start.5 = (bf16[2,128,1024]{2,1,0:T(8,128)(2,1)S(1)}, bf16[2,128,1024]{2,1,0:T(8,128)(2,1)S(1)}, u32[]{:S(2)}, u32[]{:S(2)}) collective-permute-start(bf16[2,128,1024]{2,1,0:T(8,128)(2,1)S(1)} %pad_maximum_fusion.refs_3_), channel_id=1, source_target_pairs={{0,8},{16,80},{1,9},{17,81},{2,10},{18,82},{3,11},{19,83},{4,12},{... | collective-permute-start | bytes 1572872 | tf_op jit(solution)/shard_map/ppermute | solution.py:36
  10.8 2.5 %collective-permute-start.3 = (bf16[2,128,1024]{2,1,0:T(8,128)(2,1)S(1)}, bf16[2,128,1024]{2,1,0:T(8,128)(2,1)S(1)}, u32[]{:S(2)}, u32[]{:S(2)}) collective-permute-start(bf16[2,128,1024]{2,1,0:T(8,128)(2,1)S(1)} %pad_maximum_fusion.refs_3_), channel_id=1, source_target_pairs={{0,1},{16,19},{1,0},{17,18},{2,3},{18,17},{3,2},{19,16},{4,5},{20,... | collective-permute-start | bytes 1572872 | tf_op jit(solution)/shard_map/ppermute | solution.py:36
  13.3 0.8 collective-permute-start.1
  14.0 1.1 %collective-permute-done.6.refs_7_ = bf16[2,128,1024]{2,1,0:T(8,128)(2,1)S(1)} collective-permute-done((bf16[2,128,1024]{2,1,0:T(8,128)(2,1)S(1)}, bf16[2,128,1024]{2,1,0:T(8,128)(2,1)S(1)}, u32[]{:S(2)}, u32[]{:S(2)}) %collective-permute-start.6) | collective-permute-done | bytes 524320 | tf_op jit(solution)/shard_map/ppermute | solution.py:36
  15.2 2.0 %collective-permute-start.15 = (bf16[2,128,1024]{2,1,0:T(8,128)(2,1)S(1)}, bf16[2,128,1024]{2,1,0:T(8,128)(2,1)S(1)}, u32[]{:S(2)}, u32[]{:S(2)}) collective-permute-start(bf16[2,128,1024]{2,1,0:T(8,128)(2,1)S(1)} %collective-permute-done.6.refs_7_), channel_id=1, source_target_pairs={{0,16},{16,0},{32,48},{48,32},{64,80},{80,64},{96,112},{112,96},{1... | collective-permute-start | bytes 1572872 | tf_op jit(solution)/shard_map/ppermute | solution.py:44
  17.2 2.5 %collective-permute-start.7 = (bf16[2,128,1024]{2,1,0:T(8,128)(2,1)S(1)}, bf16[2,128,1024]{2,1,0:T(8,128)(2,1)S(1)}, u32[]{:S(2)}, u32[]{:S(2)}) collective-permute-start(bf16[2,128,1024]{2,1,0:T(8,128)(2,1)S(1)} %collective-permute-done.6.refs_7_), channel_id=1, source_target_pairs={{0,1},{16,19},{1,0},{17,18},{2,3},{18,17},{3,2},{19,16},{4,5},{20,... | collective-permute-start | bytes 1572872 | tf_op jit(solution)/shard_map/ppermute | solution.py:36
  19.6 2.3 %collective-permute-done.5.refs_2_ = bf16[2,128,1024]{2,1,0:T(8,128)(2,1)S(1)} collective-permute-done((bf16[2,128,1024]{2,1,0:T(8,128)(2,1)S(1)}, bf16[2,128,1024]{2,1,0:T(8,128)(2,1)S(1)}, u32[]{:S(2)}, u32[]{:S(2)}) %collective-permute-start.5) | collective-permute-done | bytes 524320 | tf_op jit(solution)/shard_map/ppermute | solution.py:36
  22.0 2.3 %collective-permute-start.10 = (bf16[2,128,1024]{2,1,0:T(8,128)(2,1)S(1)}, bf16[2,128,1024]{2,1,0:T(8,128)(2,1)S(1)}, u32[]{:S(2)}, u32[]{:S(2)}) collective-permute-start(bf16[2,128,1024]{2,1,0:T(8,128)(2,1)S(1)} %collective-permute-done.5.refs_2_), channel_id=1, source_target_pairs={{0,16},{16,0},{32,48},{48,32},{64,80},{80,64},{96,112},{112,96},{1... | collective-permute-start | bytes 1572872 | tf_op jit(solution)/shard_map/ppermute | solution.py:44
  24.2 2.9 %collective-permute-start.4 = (bf16[2,128,1024]{2,1,0:T(8,128)(2,1)S(1)}, bf16[2,128,1024]{2,1,0:T(8,128)(2,1)S(1)}, u32[]{:S(2)}, u32[]{:S(2)}) collective-permute-start(bf16[2,128,1024]{2,1,0:T(8,128)(2,1)S(1)} %collective-permute-done.3.refs_4_), channel_id=1, source_target_pairs={{0,8},{16,80},{1,9},{17,81},{2,10},{18,82},{3,11},{19,83},{4,12},{... | collective-permute-start | bytes 1572872 | tf_op jit(solution)/shard_map/ppermute | solution.py:36
  27.2 2.5 %collective-permute-start.2 = (bf16[2,128,1024]{2,1,0:T(8,128)(2,1)S(1)}, bf16[2,128,1024]{2,1,0:T(8,128)(2,1)S(1)}, u32[]{:S(2)}, u32[]{:S(2)}) collective-permute-start(bf16[2,128,1024]{2,1,0:T(8,128)(2,1)S(1)} %collective-permute-done.1.refs_6_), channel_id=1, source_target_pairs={{0,1},{16,19},{1,0},{17,18},{2,3},{18,17},{3,2},{19,16},{4,5},{20,... | collective-permute-start | bytes 1572872 | tf_op jit(solution)/shard_map/ppermute | solution.py:36
  30.2 3.8 %collective-permute-done.4.refs_1_ = bf16[2,128,1024]{2,1,0:T(8,128)(2,1)S(1)} collective-permute-done((bf16[2,128,1024]{2,1,0:T(8,128)(2,1)S(1)}, bf16[2,128,1024]{2,1,0:T(8,128)(2,1)S(1)}, u32[]{:S(2)}, u32[]{:S(2)}) %collective-permute-start.4) | collective-permute-done | bytes 524320 | tf_op jit(solution)/shard_map/ppermute | solution.py:36
  34.1 0.9 collective-permute-start.9
  34.9 1.5 %collective-permute-done.2.refs_0_ = bf16[2,128,1024]{2,1,0:T(8,128)(2,1)S(1)} collective-permute-done((bf16[2,128,1024]{2,1,0:T(8,128)(2,1)S(1)}, bf16[2,128,1024]{2,1,0:T(8,128)(2,1)S(1)}, u32[]{:S(2)}, u32[]{:S(2)}) %collective-permute-start.2) | collective-permute-done | bytes 524320 | tf_op jit(solution)/shard_map/ppermute | solution.py:36
  36.8 0.7 copy-done.2
  37.8 0.6 collective-permute-done.8.refs_8_
  38.4 8.7 %scores.1 = (f32[2,1024,1024]{2,1,0:T(8,128)S(1)}, f32[3,2048]{1,0:T(4,128)S(1)}, f32[3,2048]{1,0:T(4,128)S(1)}, bf16[1024,1024]{1,0:T(8,128)(2,1)S(1)}, bf16[2,1024,1024]{2,1,0:T(8,128)(2,1)S(1)}) custom-call(bf16[2,128,1024]{2,1,0:T(8,128)(2,1)S(1)} %collective-permute-done.2.refs_0_, bf16[2,128,1024]{2,1,0:T(8,128)(2,1)S(1)} %collective-permute-done.4.refs_1_, ...), custom_call_target="tpu_custom_call" | custom-call | flops 4294967296 | bytes 16777216 | tf_op jit(solution)/shard_map/scores/pallas_call | solution.py:294
  47.6 0.9 collective-permute-done.16.refs_1_
  48.4 2.5 %collective-permute-start.17 = (f32[3,2048]{1,0:T(4,128)S(1)}, f32[3,2048]{1,0:T(4,128)S(1)}, u32[]{:S(2)}, u32[]{:S(2)}) collective-permute-start(f32[3,2048]{1,0:T(4,128)S(1)} %merge.3.refs_0_), channel_id=1, source_target_pairs={{0,1},{16,19},{1,0},{17,18},{2,3},{18,17},{3,2},{19,16},{4,5},{20,... | collective-permute-start | bytes 73736 | tf_op jit(solution)/shard_map/ppermute | solution.py:36
  50.9 0.7 flip.1.refs_2_.refs_1_
  51.6 0.9 collective-permute-done.17.refs_1_
  52.5 2.8 %collective-permute-start.20 = (f32[3,2048]{1,0:T(4,128)S(1)}, f32[3,2048]{1,0:T(4,128)S(1)}, u32[]{:S(2)}, u32[]{:S(2)}) collective-permute-start(f32[3,2048]{1,0:T(4,128)S(1)} %merge.4.refs_0_), channel_id=1, source_target_pairs={{0,12},{16,112},{1,13},{17,113},{2,14},{18,114},{3,15},{19,115},{4... | collective-permute-start | bytes 73736 | tf_op jit(solution)/shard_map/ppermute | solution.py:36
  55.3 1.6 %collective-permute-start.18 = (f32[3,2048]{1,0:T(4,128)S(1)}, f32[3,2048]{1,0:T(4,128)S(1)}, u32[]{:S(2)}, u32[]{:S(2)}) collective-permute-start(f32[3,2048]{1,0:T(4,128)S(1)} %merge.4.refs_0_), channel_id=1, source_target_pairs={{0,8},{16,80},{1,9},{17,81},{2,10},{18,82},{3,11},{19,83},{4,12},{... | collective-permute-start | bytes 73736 | tf_op jit(solution)/shard_map/ppermute | solution.py:36
  56.9 2.6 %collective-permute-done.19.refs_2_ = f32[3,2048]{1,0:T(4,128)S(1)} collective-permute-done((f32[3,2048]{1,0:T(4,128)S(1)}, f32[3,2048]{1,0:T(4,128)S(1)}, u32[]{:S(2)}, u32[]{:S(2)}) %collective-permute-start.19) | collective-permute-done | bytes 24608 | tf_op jit(solution)/shard_map/ppermute | solution.py:36
  60.4 0.8 collective-permute-start.22
  61.3 3.5 %slope.1.refs_0_ = bf16[2,1024,1024]{2,1,0:T(8,128)(2,1)S(1)} custom-call(f32[2,1024,1024]{2,1,0:T(8,128)S(1)} %get-tuple-element.36.sv, f32[1024,128]{1,0:T(8,128)S(1)} %aims.1.refs_16_.target, f32[1,2048]{1,0:T(1,128)S(1)} %get-tuple-element.40.own_lse, f32[1,2048]{1,0:T(1,128)S(1)} %collective-permute-done.21.got_lse), custom_call_target="tpu_custom_call" | custom-call | flops 4294967296 | bytes 12582912 | tf_op jit(solution)/shard_map/slope/pallas_call | solution.py:418
  64.8 3.1 %grads_far.2 = (bf16[2,2,128,1024]{3,2,1,0:T(8,128)(2,1)S(1)}, bf16[2,2,128,1024]{3,2,1,0:T(8,128)(2,1)S(1)}, f32[8,128]{1,0:T(8,128)S(1)}) custom-call(bf16[2,1024,1024]{2,1,0:T(8,128)(2,1)S(1)} %slope.1.refs_0_, bf16[1024,1024]{1,0:T(8,128)(2,1)S(1)} %flip.1.refs_2_.refs_1_, bf16[2,1024,1024]{2,1,0:T(8,128)(2,1)S(1)} %get-tuple-element.41.refs_2_, ...), custom_call_target="tpu_custom_call" | custom-call | flops 2147483648 | bytes 10485760 | tf_op jit(solution)/shard_map/grads_far/pallas_call | solution.py:434
  67.8 0.9 collective-permute-start.23
  68.8 3.1 %grads_far.3 = (bf16[1,2,128,1024]{3,2,1,0:T(8,128)(2,1)S(1)}, bf16[1,2,128,1024]{3,2,1,0:T(8,128)(2,1)S(1)}, bf16[1,2,128,1024]{3,2,1,0:T(8,128)(2,1)S(1)}, bf1...) custom-call(bf16[2,1024,1024]{2,1,0:T(8,128)(2,1)S(1)} %slope.1.refs_0_, bf16[1024,1024]{1,0:T(8,128)(2,1)S(1)} %flip.1.refs_2_.refs_1_, ...), custom_call_target="tpu_custom_call" | custom-call | flops 2147483648 | bytes 10485760 | tf_op jit(solution)/shard_map/grads_far/pallas_call | solution.py:434
  72.2 2.7 %collective-permute-start.24 = (f32[8,128]{1,0:T(8,128)S(1)}, f32[8,128]{1,0:T(8,128)S(1)}, u32[]{:S(2)}, u32[]{:S(2)}) collective-permute-start(f32[8,128]{1,0:T(8,128)S(1)} %after.2), channel_id=1, source_target_pairs={{16,24},{0,64},{17,25},{1,65},{18,26},{2,66},{19,27},{3,67},{20,28... | collective-permute-start | bytes 12296 | tf_op jit(solution)/shard_map/ppermute | solution.py:36
  75.0 2.5 %collective-permute-start.35 = (bf16[2,2,128,1024]{3,2,1,0:T(8,128)(2,1)S(1)}, bf16[2,2,128,1024]{3,2,1,0:T(8,128)(2,1)S(1)}, u32[]{:S(2)}, u32[]{:S(2)}) collective-permute-start(bf16[2,2,128,1024]{3,2,1,0:T(8,128)(2,1)S(1)} %join.7.refs_0_.refs_5_), channel_id=1, source_target_pairs={{0,1},{16,19},{1,0},{17,18},{2,3},{18,17},{3,2},{19,16},{4,5},{20,... | collective-permute-start | bytes 3145736 | tf_op jit(solution)/shard_map/ppermute | solution.py:36
  77.6 3.1 %grads_near.2 = (bf16[1,2,128,1024]{3,2,1,0:T(8,128)(2,1)S(1)}, bf16[1,2,128,1024]{3,2,1,0:T(8,128)(2,1)S(1)}, bf16[1,2,128,1024]{3,2,1,0:T(8,128)(2,1)S(1)}, bf...) custom-call(bf16[2,1024,1024]{2,1,0:T(8,128)(2,1)S(1)} %slope.1.refs_0_, bf16[1024,1024]{1,0:T(8,128)(2,1)S(1)} %flip.1.refs_2_.refs_1_, ...), custom_call_target="tpu_custom_call" | custom-call | flops 2147483648 | bytes 10485760 | tf_op jit(solution)/shard_map/grads_near/pallas_call | solution.py:434
  81.2 3.3 %collective-permute-start.32 = (bf16[1,2,128,1024]{3,2,1,0:T(8,128)(2,1)S(1)}, bf16[1,2,128,1024]{3,2,1,0:T(8,128)(2,1)S(1)}, u32[]{:S(2)}, u32[]{:S(2)}) collective-permute-start(bf16[1,2,128,1024]{3,2,1,0:T(8,128)(2,1)S(1)} %join.8.refs_6_), channel_id=1, source_target_pairs={{0,8},{16,80},{1,9},{17,81},{2,10},{18,82},{3,11},{19,83},{4,12},{... | collective-permute-start | bytes 1572872 | tf_op jit(solution)/shard_map/ppermute | solution.py:36
  84.5 3.3 %grads_near.3 = (bf16[1,2,128,1024]{3,2,1,0:T(8,128)(2,1)S(1)}, bf16[1,2,128,1024]{3,2,1,0:T(8,128)(2,1)S(1)}, bf16[1,2,128,1024]{3,2,1,0:T(8,128)(2,1)S(1)}, bf...) custom-call(bf16[2,1024,1024]{2,1,0:T(8,128)(2,1)S(1)} %slope.1.refs_0_, bf16[1024,1024]{1,0:T(8,128)(2,1)S(1)} %flip.1.refs_2_.refs_1_, ...), custom_call_target="tpu_custom_call" | custom-call | flops 2147483648 | bytes 10485760 | tf_op jit(solution)/shard_map/grads_near/pallas_call | solution.py:434
  88.6 2.4 %collective-permute-start.27 = (bf16[1,2,128,1024]{3,2,1,0:T(8,128)(2,1)S(1)}, bf16[1,2,128,1024]{3,2,1,0:T(8,128)(2,1)S(1)}, u32[]{:S(2)}, u32[]{:S(2)}) collective-permute-start(bf16[1,2,128,1024]{3,2,1,0:T(8,128)(2,1)S(1)} %join.9), channel_id=1, source_target_pairs={{0,8},{16,80},{1,9},{17,81},{2,10},{18,82},{3,11},{19,83},{4,12},{... | collective-permute-start | bytes 1572872 | tf_op jit(solution)/shard_map/ppermute | solution.py:36
  91.6 2.1 %collective-permute-start.33 = (bf16[1,2,128,1024]{3,2,1,0:T(8,128)(2,1)S(1)}, bf16[1,2,128,1024]{3,2,1,0:T(8,128)(2,1)S(1)}, u32[]{:S(2)}, u32[]{:S(2)}) collective-permute-start(bf16[1,2,128,1024]{3,2,1,0:T(8,128)(2,1)S(1)} %join.11), channel_id=1, source_target_pairs={{0,1},{16,19},{1,0},{17,18},{2,3},{18,17},{3,2},{19,16},{4,5},{20,... | collective-permute-start | bytes 1572872 | tf_op jit(solution)/shard_map/ppermute | solution.py:36
  94.7 2.3 %collective-permute-start.38 = (bf16[1,2,128,1024]{3,2,1,0:T(8,128)(2,1)S(1)}, bf16[1,2,128,1024]{3,2,1,0:T(8,128)(2,1)S(1)}, u32[]{:S(2)}, u32[]{:S(2)}) collective-permute-start(bf16[1,2,128,1024]{3,2,1,0:T(8,128)(2,1)S(1)} %join.13), channel_id=1, source_target_pairs={{0,12},{16,112},{1,13},{17,113},{2,14},{18,114},{3,15},{19,115},{4... | collective-permute-start | bytes 1572872 | tf_op jit(solution)/shard_map/ppermute | solution.py:36
  97.0 1.5 %collective-permute-done.27.refs_0_.refs_1_ = bf16[1,2,128,1024]{3,2,1,0:T(8,128)(2,1)S(1)} collective-permute-done((bf16[1,2,128,1024]{3,2,1,0:T(8,128)(2,1)S(1)}, bf16[1,2,128,1024]{3,2,1,0:T(8,128)(2,1)S(1)}, u32[]{:S(2)}, u32[]{:S(2)}) %collective-permute-start.27) | collective-permute-done | bytes 524320 | tf_op jit(solution)/shard_map/ppermute | solution.py:36
  98.5 0.6 collective-permute-start.28
  99.1 2.3 %collective-permute-done.28 = f32[8,128]{1,0:T(8,128)S(1)} collective-permute-done((f32[8,128]{1,0:T(8,128)S(1)}, f32[8,128]{1,0:T(8,128)S(1)}, u32[]{:S(2)}, u32[]{:S(2)}) %collective-permute-start.28) | collective-permute-done | bytes 4128 | tf_op jit(solution)/shard_map/ppermute | solution.py:36
  101.3 2.9 %collective-permute-start.29 = (f32[8,128]{1,0:T(8,128)S(1)}, f32[8,128]{1,0:T(8,128)S(1)}, u32[]{:S(2)}, u32[]{:S(2)}) collective-permute-start(f32[8,128]{1,0:T(8,128)S(1)} %add.6), channel_id=1, source_target_pairs={{0,16},{16,0},{32,48},{48,32},{64,80},{80,64},{96,112},{112,96},{1... | collective-permute-start | bytes 12296 | tf_op jit(solution)/shard_map/ppermute | solution.py:44
  104.4 0.7 collective-permute-done.29
  107.4 1.1 finish.1
  (65 shorter events, 8.0 us)
Async XLA Ops:
  0.6 1.0 copy-start
  1.6 0.9 copy-start.1
  2.7 2.7 %collective-permute-start = (bf16[128,1024]{1,0:T(8,128)(2,1)S(1)}, bf16[128,1024]{1,0:T(8,128)(2,1)S(1)}, u32[]{:S(2)}, u32[]{:S(2)}) collective-permute-start(bf16[128,1024]{1,0:T(8,128)(2,1)S(1)} %get-tuple-element.35), channel_id=1, source_target_pairs={{0,16},{16,0},{32,48},{48,32},{64,80},{80,64},{96,112},{112,96},{1... | collective-permute-start | bytes 786440 | tf_op jit(solution)/shard_map/ppermute | solution.py:44
  5.4 9.8 %collective-permute-start.6 = (bf16[2,128,1024]{2,1,0:T(8,128)(2,1)S(1)}, bf16[2,128,1024]{2,1,0:T(8,128)(2,1)S(1)}, u32[]{:S(2)}, u32[]{:S(2)}) collective-permute-start(bf16[2,128,1024]{2,1,0:T(8,128)(2,1)S(1)} %pad_maximum_fusion.refs_3_), channel_id=1, source_target_pairs={{0,4},{16,48},{1,5},{17,49},{2,6},{18,50},{3,7},{19,51},{4,8},{20,... | collective-permute-start | bytes 1572872 | tf_op jit(solution)/shard_map/ppermute | solution.py:36
  6.9 10.3 %collective-permute-start.11 = (bf16[2,128,1024]{2,1,0:T(8,128)(2,1)S(1)}, bf16[2,128,1024]{2,1,0:T(8,128)(2,1)S(1)}, u32[]{:S(2)}, u32[]{:S(2)}) collective-permute-start(bf16[2,128,1024]{2,1,0:T(8,128)(2,1)S(1)} %pad_maximum_fusion.refs_3_), channel_id=1, source_target_pairs={{0,16},{16,0},{32,48},{48,32},{64,80},{80,64},{96,112},{112,96},{1... | collective-permute-start | bytes 1572872 | tf_op jit(solution)/shard_map/ppermute | solution.py:44
  7.9 14.1 %collective-permute-start.5 = (bf16[2,128,1024]{2,1,0:T(8,128)(2,1)S(1)}, bf16[2,128,1024]{2,1,0:T(8,128)(2,1)S(1)}, u32[]{:S(2)}, u32[]{:S(2)}) collective-permute-start(bf16[2,128,1024]{2,1,0:T(8,128)(2,1)S(1)} %pad_maximum_fusion.refs_3_), channel_id=1, source_target_pairs={{0,8},{16,80},{1,9},{17,81},{2,10},{18,82},{3,11},{19,83},{4,12},{... | collective-permute-start | bytes 1572872 | tf_op jit(solution)/shard_map/ppermute | solution.py:36
  10.8 13.4 %collective-permute-start.3 = (bf16[2,128,1024]{2,1,0:T(8,128)(2,1)S(1)}, bf16[2,128,1024]{2,1,0:T(8,128)(2,1)S(1)}, u32[]{:S(2)}, u32[]{:S(2)}) collective-permute-start(bf16[2,128,1024]{2,1,0:T(8,128)(2,1)S(1)} %pad_maximum_fusion.refs_3_), channel_id=1, source_target_pairs={{0,1},{16,19},{1,0},{17,18},{2,3},{18,17},{3,2},{19,16},{4,5},{20,... | collective-permute-start | bytes 1572872 | tf_op jit(solution)/shard_map/ppermute | solution.py:36
  13.3 13.9 %collective-permute-start.1 = (bf16[2,128,1024]{2,1,0:T(8,128)(2,1)S(1)}, bf16[2,128,1024]{2,1,0:T(8,128)(2,1)S(1)}, u32[]{:S(2)}, u32[]{:S(2)}) collective-permute-start(bf16[2,128,1024]{2,1,0:T(8,128)(2,1)S(1)} %pad_maximum_fusion.refs_3_), channel_id=1, source_target_pairs={{0,12},{16,112},{1,13},{17,113},{2,14},{18,114},{3,15},{19,115},{4... | collective-permute-start | bytes 1572872 | tf_op jit(solution)/shard_map/ppermute | solution.py:36
  15.2 14.4 %collective-permute-start.15 = (bf16[2,128,1024]{2,1,0:T(8,128)(2,1)S(1)}, bf16[2,128,1024]{2,1,0:T(8,128)(2,1)S(1)}, u32[]{:S(2)}, u32[]{:S(2)}) collective-permute-start(bf16[2,128,1024]{2,1,0:T(8,128)(2,1)S(1)} %collective-permute-done.6.refs_7_), channel_id=1, source_target_pairs={{0,16},{16,0},{32,48},{48,32},{64,80},{80,64},{96,112},{112,96},{1... | collective-permute-start | bytes 1572872 | tf_op jit(solution)/shard_map/ppermute | solution.py:44
  17.2 12.5 %collective-permute-start.7 = (bf16[2,128,1024]{2,1,0:T(8,128)(2,1)S(1)}, bf16[2,128,1024]{2,1,0:T(8,128)(2,1)S(1)}, u32[]{:S(2)}, u32[]{:S(2)}) collective-permute-start(bf16[2,128,1024]{2,1,0:T(8,128)(2,1)S(1)} %collective-permute-done.6.refs_7_), channel_id=1, source_target_pairs={{0,1},{16,19},{1,0},{17,18},{2,3},{18,17},{3,2},{19,16},{4,5},{20,... | collective-permute-start | bytes 1572872 | tf_op jit(solution)/shard_map/ppermute | solution.py:36
  22.0 8.2 %collective-permute-start.10 = (bf16[2,128,1024]{2,1,0:T(8,128)(2,1)S(1)}, bf16[2,128,1024]{2,1,0:T(8,128)(2,1)S(1)}, u32[]{:S(2)}, u32[]{:S(2)}) collective-permute-start(bf16[2,128,1024]{2,1,0:T(8,128)(2,1)S(1)} %collective-permute-done.5.refs_2_), channel_id=1, source_target_pairs={{0,16},{16,0},{32,48},{48,32},{64,80},{80,64},{96,112},{112,96},{1... | collective-permute-start | bytes 1572872 | tf_op jit(solution)/shard_map/ppermute | solution.py:44
  24.2 9.8 %collective-permute-start.4 = (bf16[2,128,1024]{2,1,0:T(8,128)(2,1)S(1)}, bf16[2,128,1024]{2,1,0:T(8,128)(2,1)S(1)}, u32[]{:S(2)}, u32[]{:S(2)}) collective-permute-start(bf16[2,128,1024]{2,1,0:T(8,128)(2,1)S(1)} %collective-permute-done.3.refs_4_), channel_id=1, source_target_pairs={{0,8},{16,80},{1,9},{17,81},{2,10},{18,82},{3,11},{19,83},{4,12},{... | collective-permute-start | bytes 1572872 | tf_op jit(solution)/shard_map/ppermute | solution.py:36
  27.2 9.2 %collective-permute-start.2 = (bf16[2,128,1024]{2,1,0:T(8,128)(2,1)S(1)}, bf16[2,128,1024]{2,1,0:T(8,128)(2,1)S(1)}, u32[]{:S(2)}, u32[]{:S(2)}) collective-permute-start(bf16[2,128,1024]{2,1,0:T(8,128)(2,1)S(1)} %collective-permute-done.1.refs_6_), channel_id=1, source_target_pairs={{0,1},{16,19},{1,0},{17,18},{2,3},{18,17},{3,2},{19,16},{4,5},{20,... | collective-permute-start | bytes 1572872 | tf_op jit(solution)/shard_map/ppermute | solution.py:36
  29.6 8.1 %collective-permute-start.12 = (bf16[2,128,1024]{2,1,0:T(8,128)(2,1)S(1)}, bf16[2,128,1024]{2,1,0:T(8,128)(2,1)S(1)}, u32[]{:S(2)}, u32[]{:S(2)}) collective-permute-start(bf16[2,128,1024]{2,1,0:T(8,128)(2,1)S(1)} %collective-permute-done.3.refs_4_), channel_id=1, source_target_pairs={{0,16},{16,0},{32,48},{48,32},{64,80},{80,64},{96,112},{112,96},{1... | collective-permute-start | bytes 1572872 | tf_op jit(solution)/shard_map/ppermute | solution.py:44
  29.6 8.1 %collective-permute-start.14 = (bf16[2,128,1024]{2,1,0:T(8,128)(2,1)S(1)}, bf16[2,128,1024]{2,1,0:T(8,128)(2,1)S(1)}, u32[]{:S(2)}, u32[]{:S(2)}) collective-permute-start(bf16[2,128,1024]{2,1,0:T(8,128)(2,1)S(1)} %collective-permute-done.1.refs_6_), channel_id=1, source_target_pairs={{0,16},{16,0},{32,48},{48,32},{64,80},{80,64},{96,112},{112,96},{1... | collective-permute-start | bytes 1572872 | tf_op jit(solution)/shard_map/ppermute | solution.py:44
  30.2 7.6 %collective-permute-start.13 = (bf16[2,128,1024]{2,1,0:T(8,128)(2,1)S(1)}, bf16[2,128,1024]{2,1,0:T(8,128)(2,1)S(1)}, u32[]{:S(2)}, u32[]{:S(2)}) collective-permute-start(bf16[2,128,1024]{2,1,0:T(8,128)(2,1)S(1)} %collective-permute-done.7.refs_5_), channel_id=1, source_target_pairs={{0,16},{16,0},{32,48},{48,32},{64,80},{80,64},{96,112},{112,96},{1... | collective-permute-start | bytes 1572872 | tf_op jit(solution)/shard_map/ppermute | solution.py:44
  34.1 3.7 %collective-permute-start.9 = (bf16[2,128,1024]{2,1,0:T(8,128)(2,1)S(1)}, bf16[2,128,1024]{2,1,0:T(8,128)(2,1)S(1)}, u32[]{:S(2)}, u32[]{:S(2)}) collective-permute-start(bf16[2,128,1024]{2,1,0:T(8,128)(2,1)S(1)} %collective-permute-done.4.refs_1_), channel_id=1, source_target_pairs={{0,16},{16,0},{32,48},{48,32},{64,80},{80,64},{96,112},{112,96},{1... | collective-permute-start | bytes 1572872 | tf_op jit(solution)/shard_map/ppermute | solution.py:44
  36.4 2.0 %collective-permute-start.8 = (bf16[2,128,1024]{2,1,0:T(8,128)(2,1)S(1)}, bf16[2,128,1024]{2,1,0:T(8,128)(2,1)S(1)}, u32[]{:S(2)}, u32[]{:S(2)}) collective-permute-start(bf16[2,128,1024]{2,1,0:T(8,128)(2,1)S(1)} %collective-permute-done.2.refs_0_), channel_id=1, source_target_pairs={{0,16},{16,0},{32,48},{48,32},{64,80},{80,64},{96,112},{112,96},{1... | collective-permute-start | bytes 1572872 | tf_op jit(solution)/shard_map/ppermute | solution.py:44
  36.8 0.7 copy-start.2
  47.1 1.3 %collective-permute-start.16 = (f32[3,2048]{1,0:T(4,128)S(1)}, f32[3,2048]{1,0:T(4,128)S(1)}, u32[]{:S(2)}, u32[]{:S(2)}) collective-permute-start(f32[3,2048]{1,0:T(4,128)S(1)} %get-tuple-element.38), channel_id=1, source_target_pairs={{0,16},{16,0},{32,48},{48,32},{64,80},{80,64},{96,112},{112,96},{1... | collective-permute-start | bytes 73736 | tf_op jit(solution)/shard_map/ppermute | solution.py:44
  48.4 4.1 %collective-permute-start.17 = (f32[3,2048]{1,0:T(4,128)S(1)}, f32[3,2048]{1,0:T(4,128)S(1)}, u32[]{:S(2)}, u32[]{:S(2)}) collective-permute-start(f32[3,2048]{1,0:T(4,128)S(1)} %merge.3.refs_0_), channel_id=1, source_target_pairs={{0,1},{16,19},{1,0},{17,18},{2,3},{18,17},{3,2},{19,16},{4,5},{20,... | collective-permute-start | bytes 73736 | tf_op jit(solution)/shard_map/ppermute | solution.py:36
  52.5 4.4 %collective-permute-start.20 = (f32[3,2048]{1,0:T(4,128)S(1)}, f32[3,2048]{1,0:T(4,128)S(1)}, u32[]{:S(2)}, u32[]{:S(2)}) collective-permute-start(f32[3,2048]{1,0:T(4,128)S(1)} %merge.4.refs_0_), channel_id=1, source_target_pairs={{0,12},{16,112},{1,13},{17,113},{2,14},{18,114},{3,15},{19,115},{4... | collective-permute-start | bytes 73736 | tf_op jit(solution)/shard_map/ppermute | solution.py:36
  55.3 4.3 %collective-permute-start.19 = (f32[3,2048]{1,0:T(4,128)S(1)}, f32[3,2048]{1,0:T(4,128)S(1)}, u32[]{:S(2)}, u32[]{:S(2)}) collective-permute-start(f32[3,2048]{1,0:T(4,128)S(1)} %merge.4.refs_0_), channel_id=1, source_target_pairs={{0,4},{16,48},{1,5},{17,49},{2,6},{18,50},{3,7},{19,51},{4,8},{20,... | collective-permute-start | bytes 73736 | tf_op jit(solution)/shard_map/ppermute | solution.py:36
  55.3 4.6 %collective-permute-start.18 = (f32[3,2048]{1,0:T(4,128)S(1)}, f32[3,2048]{1,0:T(4,128)S(1)}, u32[]{:S(2)}, u32[]{:S(2)}) collective-permute-start(f32[3,2048]{1,0:T(4,128)S(1)} %merge.4.refs_0_), channel_id=1, source_target_pairs={{0,8},{16,80},{1,9},{17,81},{2,10},{18,82},{3,11},{19,83},{4,12},{... | collective-permute-start | bytes 73736 | tf_op jit(solution)/shard_map/ppermute | solution.py:36
  60.0 1.3 %collective-permute-start.21 = (f32[1,2048]{1,0:T(1,128)S(1)}, f32[1,2048]{1,0:T(1,128)S(1)}, u32[]{:S(2)}, u32[]{:S(2)}) collective-permute-start(f32[1,2048]{1,0:T(1,128)S(1)} %get-tuple-element.40.own_lse), channel_id=1, source_target_pairs={{0,16},{16,0},{32,48},{48,32},{64,80},{80,64},{96,112},{112,96},{1... | collective-permute-start | bytes 24584 | tf_op jit(solution)/shard_map/ppermute | solution.py:44
  60.4 4.3 %collective-permute-start.22 = (f32[8,128]{1,0:T(8,128)S(1)}, f32[8,128]{1,0:T(8,128)S(1)}, u32[]{:S(2)}, u32[]{:S(2)}) collective-permute-start(f32[8,128]{1,0:T(8,128)S(1)} %get-tuple-element.42.refs_3_), channel_id=1, source_target_pairs={{16,20},{0,32},{17,21},{1,33},{18,22},{2,34},{19,23},{3,35},{20,16... | collective-permute-start | bytes 12296 | tf_op jit(solution)/shard_map/ppermute | solution.py:40
  67.8 4.1 %collective-permute-start.23 = (bf16[2,2,128,1024]{3,2,1,0:T(8,128)(2,1)S(1)}, bf16[2,2,128,1024]{3,2,1,0:T(8,128)(2,1)S(1)}, u32[]{:S(2)}, u32[]{:S(2)}) collective-permute-start(bf16[2,2,128,1024]{3,2,1,0:T(8,128)(2,1)S(1)} %get-tuple-element.46), channel_id=1, source_target_pairs={{0,16},{16,0},{32,48},{48,32},{64,80},{80,64},{96,112},{112,96},{1... | collective-permute-start | bytes 3145736 | tf_op jit(solution)/shard_map/ppermute | solution.py:44
  71.8 3.1 %collective-permute-start.25 = (bf16[1,2,128,1024]{3,2,1,0:T(8,128)(2,1)S(1)}, bf16[1,2,128,1024]{3,2,1,0:T(8,128)(2,1)S(1)}, u32[]{:S(2)}, u32[]{:S(2)}) collective-permute-start(bf16[1,2,128,1024]{3,2,1,0:T(8,128)(2,1)S(1)} %get-tuple-element.48), channel_id=1, source_target_pairs={{0,16},{16,0},{32,48},{48,32},{64,80},{80,64},{96,112},{112,96},{1... | collective-permute-start | bytes 1572872 | tf_op jit(solution)/shard_map/ppermute | solution.py:44
  72.2 5.4 %collective-permute-start.24 = (f32[8,128]{1,0:T(8,128)S(1)}, f32[8,128]{1,0:T(8,128)S(1)}, u32[]{:S(2)}, u32[]{:S(2)}) collective-permute-start(f32[8,128]{1,0:T(8,128)S(1)} %after.2), channel_id=1, source_target_pairs={{16,24},{0,64},{17,25},{1,65},{18,26},{2,66},{19,27},{3,67},{20,28... | collective-permute-start | bytes 12296 | tf_op jit(solution)/shard_map/ppermute | solution.py:36
  75.0 18.7 %collective-permute-start.35 = (bf16[2,2,128,1024]{3,2,1,0:T(8,128)(2,1)S(1)}, bf16[2,2,128,1024]{3,2,1,0:T(8,128)(2,1)S(1)}, u32[]{:S(2)}, u32[]{:S(2)}) collective-permute-start(bf16[2,2,128,1024]{3,2,1,0:T(8,128)(2,1)S(1)} %join.7.refs_0_.refs_5_), channel_id=1, source_target_pairs={{0,1},{16,19},{1,0},{17,18},{2,3},{18,17},{3,2},{19,16},{4,5},{20,... | collective-permute-start | bytes 3145736 | tf_op jit(solution)/shard_map/ppermute | solution.py:36
  80.6 7.3 %collective-permute-start.26 = (bf16[1,2,128,1024]{3,2,1,0:T(8,128)(2,1)S(1)}, bf16[1,2,128,1024]{3,2,1,0:T(8,128)(2,1)S(1)}, u32[]{:S(2)}, u32[]{:S(2)}) collective-permute-start(bf16[1,2,128,1024]{3,2,1,0:T(8,128)(2,1)S(1)} %get-tuple-element.52), channel_id=1, source_target_pairs={{0,16},{16,0},{32,48},{48,32},{64,80},{80,64},{96,112},{112,96},{1... | collective-permute-start | bytes 1572872 | tf_op jit(solution)/shard_map/ppermute | solution.py:44
  81.0 7.5 %collective-permute-start.31 = (bf16[1,2,128,1024]{3,2,1,0:T(8,128)(2,1)S(1)}, bf16[1,2,128,1024]{3,2,1,0:T(8,128)(2,1)S(1)}, u32[]{:S(2)}, u32[]{:S(2)}) collective-permute-start(bf16[1,2,128,1024]{3,2,1,0:T(8,128)(2,1)S(1)} %get-tuple-element.56), channel_id=1, source_target_pairs={{0,16},{16,0},{32,48},{48,32},{64,80},{80,64},{96,112},{112,96},{1... | collective-permute-start | bytes 1572872 | tf_op jit(solution)/shard_map/ppermute | solution.py:44
  81.2 10.2 %collective-permute-start.32 = (bf16[1,2,128,1024]{3,2,1,0:T(8,128)(2,1)S(1)}, bf16[1,2,128,1024]{3,2,1,0:T(8,128)(2,1)S(1)}, u32[]{:S(2)}, u32[]{:S(2)}) collective-permute-start(bf16[1,2,128,1024]{3,2,1,0:T(8,128)(2,1)S(1)} %join.8.refs_6_), channel_id=1, source_target_pairs={{0,8},{16,80},{1,9},{17,81},{2,10},{18,82},{3,11},{19,83},{4,12},{... | collective-permute-start | bytes 1572872 | tf_op jit(solution)/shard_map/ppermute | solution.py:36
  87.8 5.9 %collective-permute-start.34 = (bf16[1,2,128,1024]{3,2,1,0:T(8,128)(2,1)S(1)}, bf16[1,2,128,1024]{3,2,1,0:T(8,128)(2,1)S(1)}, u32[]{:S(2)}, u32[]{:S(2)}) collective-permute-start(bf16[1,2,128,1024]{3,2,1,0:T(8,128)(2,1)S(1)} %get-tuple-element.58), channel_id=1, source_target_pairs={{0,16},{16,0},{32,48},{48,32},{64,80},{80,64},{96,112},{112,96},{1... | collective-permute-start | bytes 1572872 | tf_op jit(solution)/shard_map/ppermute | solution.py:44
  87.9 6.6 %collective-permute-start.37 = (bf16[1,2,128,1024]{3,2,1,0:T(8,128)(2,1)S(1)}, bf16[1,2,128,1024]{3,2,1,0:T(8,128)(2,1)S(1)}, u32[]{:S(2)}, u32[]{:S(2)}) collective-permute-start(bf16[1,2,128,1024]{3,2,1,0:T(8,128)(2,1)S(1)} %get-tuple-element.60), channel_id=1, source_target_pairs={{0,16},{16,0},{32,48},{48,32},{64,80},{80,64},{96,112},{112,96},{1... | collective-permute-start | bytes 1572872 | tf_op jit(solution)/shard_map/ppermute | solution.py:44
  88.6 9.9 %collective-permute-start.27 = (bf16[1,2,128,1024]{3,2,1,0:T(8,128)(2,1)S(1)}, bf16[1,2,128,1024]{3,2,1,0:T(8,128)(2,1)S(1)}, u32[]{:S(2)}, u32[]{:S(2)}) collective-permute-start(bf16[1,2,128,1024]{3,2,1,0:T(8,128)(2,1)S(1)} %join.9), channel_id=1, source_target_pairs={{0,8},{16,80},{1,9},{17,81},{2,10},{18,82},{3,11},{19,83},{4,12},{... | collective-permute-start | bytes 1572872 | tf_op jit(solution)/shard_map/ppermute | solution.py:36
  91.6 13.5 %collective-permute-start.33 = (bf16[1,2,128,1024]{3,2,1,0:T(8,128)(2,1)S(1)}, bf16[1,2,128,1024]{3,2,1,0:T(8,128)(2,1)S(1)}, u32[]{:S(2)}, u32[]{:S(2)}) collective-permute-start(bf16[1,2,128,1024]{3,2,1,0:T(8,128)(2,1)S(1)} %join.11), channel_id=1, source_target_pairs={{0,1},{16,19},{1,0},{17,18},{2,3},{18,17},{3,2},{19,16},{4,5},{20,... | collective-permute-start | bytes 1572872 | tf_op jit(solution)/shard_map/ppermute | solution.py:36
  93.7 10.5 %collective-permute-start.30 = (bf16[1,2,128,1024]{3,2,1,0:T(8,128)(2,1)S(1)}, bf16[1,2,128,1024]{3,2,1,0:T(8,128)(2,1)S(1)}, u32[]{:S(2)}, u32[]{:S(2)}) collective-permute-start(bf16[1,2,128,1024]{3,2,1,0:T(8,128)(2,1)S(1)} %get-tuple-element.54), channel_id=1, source_target_pairs={{0,16},{16,0},{32,48},{48,32},{64,80},{80,64},{96,112},{112,96},{1... | collective-permute-start | bytes 1572872 | tf_op jit(solution)/shard_map/ppermute | solution.py:44
  94.0 11.1 %collective-permute-start.36 = (bf16[1,2,128,1024]{3,2,1,0:T(8,128)(2,1)S(1)}, bf16[1,2,128,1024]{3,2,1,0:T(8,128)(2,1)S(1)}, u32[]{:S(2)}, u32[]{:S(2)}) collective-permute-start(bf16[1,2,128,1024]{3,2,1,0:T(8,128)(2,1)S(1)} %join.12), channel_id=1, source_target_pairs={{0,4},{16,48},{1,5},{17,49},{2,6},{18,50},{3,7},{19,51},{4,8},{20,... | collective-permute-start | bytes 1572872 | tf_op jit(solution)/shard_map/ppermute | solution.py:36
  94.7 10.4 %collective-permute-start.38 = (bf16[1,2,128,1024]{3,2,1,0:T(8,128)(2,1)S(1)}, bf16[1,2,128,1024]{3,2,1,0:T(8,128)(2,1)S(1)}, u32[]{:S(2)}, u32[]{:S(2)}) collective-permute-start(bf16[1,2,128,1024]{3,2,1,0:T(8,128)(2,1)S(1)} %join.13), channel_id=1, source_target_pairs={{0,12},{16,112},{1,13},{17,113},{2,14},{18,114},{3,15},{19,115},{4... | collective-permute-start | bytes 1572872 | tf_op jit(solution)/shard_map/ppermute | solution.py:36
  98.5 2.9 %collective-permute-start.28 = (f32[8,128]{1,0:T(8,128)S(1)}, f32[8,128]{1,0:T(8,128)S(1)}, u32[]{:S(2)}, u32[]{:S(2)}) collective-permute-start(f32[8,128]{1,0:T(8,128)S(1)} %after.3), channel_id=1, source_target_pairs={{16,17},{0,3},{17,16},{1,2},{18,19},{2,1},{19,18},{3,0},{20,21},{4... | collective-permute-start | bytes 12296 | tf_op jit(solution)/shard_map/ppermute | solution.py:36
  101.3 3.7 %collective-permute-start.29 = (f32[8,128]{1,0:T(8,128)S(1)}, f32[8,128]{1,0:T(8,128)S(1)}, u32[]{:S(2)}, u32[]{:S(2)}) collective-permute-start(f32[8,128]{1,0:T(8,128)S(1)} %add.6), channel_id=1, source_target_pairs={{0,16},{16,0},{32,48},{48,32},{64,80},{80,64},{96,112},{112,96},{1... | collective-permute-start | bytes 12296 | tf_op jit(solution)/shard_map/ppermute | solution.py:44
  105.4 2.0 %collective-permute-start.39 = (f32[128,1024]{1,0:T(8,128)S(1)}, f32[128,1024]{1,0:T(8,128)S(1)}, u32[]{:S(2)}, u32[]{:S(2)}) collective-permute-start(f32[128,1024]{1,0:T(8,128)S(1)} %get-tuple-element.62), channel_id=1, source_target_pairs={{0,16},{16,0},{32,48},{48,32},{64,80},{80,64},{96,112},{112,96},{1... | collective-permute-start | bytes 1572872 | tf_op jit(solution)/shard_map/ppermute | solution.py:44
